TPU v7x, 32 devices: a whole 2x2x4 slice. The times are simulated.
32 devices in a mesh: seq: 4 (over y, x), batch: 8 (over z, core).
Axes of the slice: x: 2, y: 2, z: 4, core: 2. Of those that a mesh axis runs over, the one named last changes fastest.
Arguments:
- tokens: bfloat16 [32, 1024, 768], P('batch', 'seq'), may hold values from -6 to 6
- cotangent: bfloat16 [32, 1024, 768], P('batch', 'seq'), may hold values from -6 to 6
- doc_lengths: int32 [32, 8], P('batch'), may hold values from 1 to 1017, as said below
- w_query: bfloat16 [768, 768], replicated, may hold values from -0.21875 to 0.21875
- w_key: bfloat16 [768, 768], replicated, may hold values from -0.21875 to 0.21875
- w_value: bfloat16 [768, 768], replicated, may hold values from -0.21875 to 0.21875
- w_out: bfloat16 [768, 768], replicated, may hold values from -1.25 to 1.25
- w_in: bfloat16 [768, 3072], replicated, may hold values from -0.21875 to 0.21875
- w_back: bfloat16 [3072, 768], replicated, may hold values from -0.109375 to 0.109375
- gain_one: float32 [768], replicated, may hold values from 0.5 to 1.5
- shift_one: float32 [768], replicated, may hold values from -1.8 to 1.8
- gain_two: float32 [768], replicated, may hold values from 0.5 to 1.5
- shift_two: float32 [768], replicated, may hold values from -1.8 to 1.8
Outputs:
- layer_out: bfloat16 [32, 1024, 768], P('batch', 'seq')
- grad_tokens: float32 [32, 1024, 768], P('batch', 'seq')
- grad_query: float32 [768, 768], P('seq')
- grad_key: float32 [768, 768], P('seq')
- grad_value: float32 [768, 768], P('seq')
- grad_out: float32 [768, 768], P('seq')
- grad_in: float32 [768, 3072], P('seq')
- grad_back: float32 [3072, 768], P('seq')
- grad_gain_one: float32 [768], P('seq')
- grad_shift_one: float32 [768], P('seq')
- grad_gain_two: float32 [768], P('seq')
- grad_shift_two: float32 [768], P('seq')
Inputs may be any that keep to these rules, and one draw needn't show every extreme that they name: `doc_lengths`: each row holds the lengths of its 8 documents in order, each 1 or more, summing to 1024. Among the 4 rows of each index of batch, one holds a document of 1017 positions followed by documents of one position; the other rows are cut at distinct places drawn evenly.
All inputs are finite; a program needn't handle non-finite values.
Results may differ from a plain program's by a relative error of at most 0.0085.
Values sent between devices are 32-bit elements; how exact they have to be, the bound alone decides.
No kernel may reach another device: no remote copies, remote signals or barrier semaphores. Data moves between devices by JAX's collectives and lax.ppermute only.
A program may use at most 256 MiB of HBM per device.

v0:
```python
from functools import partial

import jax
import jax.numpy as jnp
from jax import lax
from jax.sharding import PartitionSpec as P

HEADS = 12
HEAD_DIM = 64


half_pi = 1.5707963267948966
norm_eps = 1e-05
highest = lax.Precision.HIGHEST


def entering(part, axis, combine, identity, reverse):
    count = lax.axis_size(axis)
    place = lax.axis_index(axis)
    ahead = count - 1 - place if reverse else place
    gathered = jax.tree.map(lambda a: lax.all_gather(a, axis), part)
    state = jax.tree.map(lambda a, e: jnp.zeros_like(a) + jnp.asarray(e, a.dtype), part, identity)

    def one(step, state):
        source = count - 1 - step if reverse else step
        return combine(
            state, jax.tree.map(lambda a: lax.dynamic_index_in_dim(a, source, 0, False), gathered)
        )

    return lax.fori_loop(0, ahead, one, state)


def doc_tables(lengths, positions):
    doc_ends = jnp.cumsum(lengths, axis=-1)
    starts = doc_ends - lengths
    inside = (
        (positions[None, :, None] >= starts[:, None, :])
        & (positions[None, :, None] < doc_ends[:, None, :])
    ).astype(jnp.int32)
    doc_begin = jnp.sum(inside * starts[:, None, :], axis=-1)
    doc_span = jnp.sum(inside * lengths[:, None, :], axis=-1)
    return (doc_begin, doc_span)


def norm_parts(summed):
    centered = summed - jnp.mean(summed, axis=-1, keepdims=True)
    inv_scale = lax.rsqrt(jnp.mean(centered * centered, axis=-1, keepdims=True) + norm_eps)
    return (centered * inv_scale, inv_scale)


def norm_back(grad_norm, normed, inv_scale):
    return inv_scale * (
        grad_norm
        - jnp.mean(grad_norm, axis=-1, keepdims=True)
        - normed * jnp.mean(grad_norm * normed, axis=-1, keepdims=True)
    )


def combine_state(earlier, latter):
    factor = latter[2]
    return (
        latter[0] + factor[:, None, None] * earlier[0],
        latter[1] + factor[:, None] * earlier[1],
        earlier[2] * latter[2],
    )


def body(
    tokens,
    cotangent,
    doc_lengths,
    w_query,
    w_key,
    w_value,
    w_out,
    w_in,
    w_back,
    gain_one,
    shift_one,
    gain_two,
    shift_two,
):
    row_count, tok_count, model_width = tokens.shape
    head_count = HEADS
    head_size = HEAD_DIM
    flat_count = row_count * tok_count
    first_place = lax.axis_index("seq") * tok_count
    positions = first_place + jnp.arange(tok_count, dtype=jnp.int32)
    doc_begin, doc_span = doc_tables(doc_lengths, positions)
    doc_pos = positions[None, :] - doc_begin
    angles = half_pi * doc_pos.astype(jnp.float32) / doc_span.astype(jnp.float32)
    trig_pair = jnp.stack([jnp.cos(angles), jnp.sin(angles)], axis=1)
    reader = (doc_begin < first_place).astype(jnp.float32)
    last_begin = doc_begin[:, -1:]
    tail_mask = (doc_begin == last_begin).astype(jnp.float32)
    keep_flag = (last_begin[:, 0] < first_place).astype(jnp.float32)
    causal = jnp.arange(tok_count)[:, None] >= jnp.arange(tok_count)[None, :]
    same_doc = (doc_begin[:, :, None] == doc_begin[:, None, :]) & causal[None]
    blend = jnp.where(
        same_doc, jnp.einsum("rti,rtj->rij", trig_pair, trig_pair, precision=highest), 0.0
    )
    trig_read = trig_pair * reader[:, None, :]
    trig_tail = trig_pair * tail_mask[:, None, :]
    flat_tokens = tokens.reshape(flat_count, model_width)
    query_pre = jnp.dot(flat_tokens, w_query, preferred_element_type=jnp.float32)
    key_pre = jnp.dot(flat_tokens, w_key, preferred_element_type=jnp.float32)
    value_pre = jnp.dot(flat_tokens, w_value, preferred_element_type=jnp.float32)
    head_shape = (row_count, tok_count, head_count, head_size)
    query_heads = (
        jax.nn.softplus(query_pre).astype(jnp.bfloat16).astype(jnp.float32).reshape(head_shape)
    )
    key_heads = (
        jax.nn.softplus(key_pre).astype(jnp.bfloat16).astype(jnp.float32).reshape(head_shape)
    )
    value_heads = value_pre.astype(jnp.bfloat16).astype(jnp.float32).reshape(head_shape)
    scores = (
        jnp.einsum("rihd,rjhd->rhij", query_heads, key_heads, precision=highest) * blend[:, None]
    )
    numer = jnp.einsum("rhij,rjhd->rihd", scores, value_heads, precision=highest)
    denom = jnp.swapaxes(jnp.sum(scores, axis=-1), 1, 2)
    weighted_keys = trig_tail[:, :, :, None, None] * key_heads[:, None]
    local_mats = jnp.einsum("rtjhk,rjhv->rthkv", weighted_keys, value_heads, precision=highest)
    local_sums = jnp.sum(weighted_keys, axis=2)
    pair_shape = (row_count, 2 * head_count, head_size * head_size)
    sums_shape = (row_count, 2 * head_count * head_size)
    outgoing = (local_mats.reshape(pair_shape), local_sums.reshape(sums_shape), keep_flag)
    identity = (
        jnp.zeros(pair_shape, jnp.float32),
        jnp.zeros(sums_shape, jnp.float32),
        jnp.ones((row_count,), jnp.float32),
    )
    in_mats, in_sums, unused = entering(outgoing, "seq", combine_state, identity, False)
    in_mats = in_mats.reshape(row_count, 2, head_count, head_size, head_size)
    in_sums = in_sums.reshape(row_count, 2, head_count, head_size)
    query_read = trig_read[:, :, :, None, None] * query_heads[:, None]
    numer = numer + jnp.einsum("rtihk,rthkv->rihv", query_read, in_mats, precision=highest)
    denom = denom + jnp.einsum("rtihk,rthk->rih", query_read, in_sums, precision=highest)
    attended = numer / denom[..., None]
    att_low = attended.reshape(flat_count, model_width).astype(jnp.bfloat16)
    branch = jnp.dot(att_low, w_out, preferred_element_type=jnp.float32)
    normed_one, scale_one = norm_parts(flat_tokens.astype(jnp.float32) + branch)
    first_out = normed_one * gain_one + shift_one
    first_low = first_out.astype(jnp.bfloat16)
    hidden = jnp.dot(first_low, w_in, preferred_element_type=jnp.float32)
    active, gelu_pull = jax.vjp(partial(jax.nn.gelu, approximate=False), hidden)
    active_low = active.astype(jnp.bfloat16)
    second = jnp.dot(active_low, w_back, preferred_element_type=jnp.float32)
    normed_two, scale_two = norm_parts(first_out + second)
    layer_out = (normed_two * gain_two + shift_two).astype(jnp.bfloat16).reshape(tokens.shape)
    grad_top = cotangent.reshape(flat_count, model_width).astype(jnp.float32)
    grad_gain_two = jnp.sum(grad_top * normed_two, axis=0)
    grad_shift_two = jnp.sum(grad_top, axis=0)
    grad_mid = norm_back(grad_top * gain_two, normed_two, scale_two)
    grad_second = grad_mid.astype(jnp.bfloat16)
    grad_back = jnp.dot(active_low.T, grad_second, preferred_element_type=jnp.float32)
    grad_active = jnp.dot(grad_second, w_back.T, preferred_element_type=jnp.float32)
    grad_hidden = gelu_pull(grad_active)[0].astype(jnp.bfloat16)
    grad_in = jnp.dot(first_low.T, grad_hidden, preferred_element_type=jnp.float32)
    grad_first = grad_mid + jnp.dot(grad_hidden, w_in.T, preferred_element_type=jnp.float32)
    grad_gain_one = jnp.sum(grad_first * normed_one, axis=0)
    grad_shift_one = jnp.sum(grad_first, axis=0)
    grad_base = norm_back(grad_first * gain_one, normed_one, scale_one)
    grad_branch = grad_base.astype(jnp.bfloat16)
    grad_out = jnp.dot(att_low.T, grad_branch, preferred_element_type=jnp.float32)
    grad_att = jnp.dot(grad_branch, w_out.T, preferred_element_type=jnp.float32).reshape(head_shape)
    grad_numer = grad_att / denom[..., None]
    grad_denom = -jnp.sum(grad_att * attended, axis=-1) / denom
    grad_scores = (
        jnp.einsum("rihv,rjhv->rhij", grad_numer, value_heads, precision=highest)
        + jnp.swapaxes(grad_denom, 1, 2)[..., None]
    ) * blend[:, None]
    grad_vheads = jnp.einsum("rhij,rihv->rjhv", scores, grad_numer, precision=highest)
    grad_qheads = jnp.einsum("rhij,rjhk->rihk", grad_scores, key_heads, precision=highest)
    grad_kheads = jnp.einsum("rhij,rihk->rjhk", grad_scores, query_heads, precision=highest)
    read_inner = (
        jnp.einsum("rthkv,rihv->rtihk", in_mats, grad_numer, precision=highest)
        + grad_denom[:, None, :, :, None] * in_sums[:, :, None]
    )
    grad_qheads = grad_qheads + jnp.sum(trig_read[:, :, :, None, None] * read_inner, axis=1)
    read_mats = jnp.einsum("rtihk,rihv->rthkv", query_read, grad_numer, precision=highest)
    read_sums = jnp.einsum("rtihk,rih->rthk", query_read, grad_denom, precision=highest)
    incoming_grad = (read_mats.reshape(pair_shape), read_sums.reshape(sums_shape), keep_flag)
    out_mats, out_sums, unused_two = entering(incoming_grad, "seq", combine_state, identity, True)
    out_mats = out_mats.reshape(row_count, 2, head_count, head_size, head_size)
    out_sums = out_sums.reshape(row_count, 2, head_count, head_size)
    tail_inner = (
        jnp.einsum("rthkv,rjhv->rtjhk", out_mats, value_heads, precision=highest)
        + out_sums[:, :, None]
    )
    grad_kheads = grad_kheads + jnp.sum(trig_tail[:, :, :, None, None] * tail_inner, axis=1)
    grad_vheads = grad_vheads + jnp.einsum(
        "rtjhk,rthkv->rjhv", weighted_keys, out_mats, precision=highest
    )
    grad_qpre = (grad_qheads.reshape(flat_count, model_width) * jax.nn.sigmoid(query_pre)).astype(
        jnp.bfloat16
    )
    grad_kpre = (grad_kheads.reshape(flat_count, model_width) * jax.nn.sigmoid(key_pre)).astype(
        jnp.bfloat16
    )
    grad_vpre = grad_vheads.reshape(flat_count, model_width).astype(jnp.bfloat16)
    grad_query = jnp.dot(flat_tokens.T, grad_qpre, preferred_element_type=jnp.float32)
    grad_key = jnp.dot(flat_tokens.T, grad_kpre, preferred_element_type=jnp.float32)
    grad_value = jnp.dot(flat_tokens.T, grad_vpre, preferred_element_type=jnp.float32)
    grad_tokens = grad_base + jnp.dot(grad_qpre, w_query.T, preferred_element_type=jnp.float32)
    grad_tokens = grad_tokens + jnp.dot(grad_kpre, w_key.T, preferred_element_type=jnp.float32)
    grad_tokens = grad_tokens + jnp.dot(grad_vpre, w_value.T, preferred_element_type=jnp.float32)
    grad_tokens = grad_tokens.reshape(tokens.shape)
    shards = (
        lax.psum_scatter(grad_query, "seq", scatter_dimension=0, tiled=True),
        lax.psum_scatter(grad_key, "seq", scatter_dimension=0, tiled=True),
        lax.psum_scatter(grad_value, "seq", scatter_dimension=0, tiled=True),
        lax.psum_scatter(grad_out, "seq", scatter_dimension=0, tiled=True),
        lax.psum_scatter(grad_in, "seq", scatter_dimension=0, tiled=True),
        lax.psum_scatter(grad_back, "seq", scatter_dimension=0, tiled=True),
        lax.psum_scatter(grad_gain_one, "seq", scatter_dimension=0, tiled=True),
        lax.psum_scatter(grad_shift_one, "seq", scatter_dimension=0, tiled=True),
        lax.psum_scatter(grad_gain_two, "seq", scatter_dimension=0, tiled=True),
        lax.psum_scatter(grad_shift_two, "seq", scatter_dimension=0, tiled=True),
    )
    totals = lax.psum(
        (
            shards[0],
            shards[1],
            shards[2],
            shards[3],
            shards[4],
            shards[5],
            shards[6],
            shards[7],
            shards[8],
            shards[9],
        ),
        "batch",
    )
    return (
        layer_out,
        grad_tokens,
        totals[0],
        totals[1],
        totals[2],
        totals[3],
        totals[4],
        totals[5],
        totals[6],
        totals[7],
        totals[8],
        totals[9],
    )


def solution(mesh):
    in_specs = (
        P("batch", "seq", None),
        P("batch", "seq", None),
        P("batch", None),
        P(),
        P(),
        P(),
        P(),
        P(),
        P(),
        P(),
        P(),
        P(),
        P(),
    )
    out_specs = (
        P("batch", "seq", None),
        P("batch", "seq", None),
        P("seq", None),
        P("seq", None),
        P("seq", None),
        P("seq", None),
        P("seq", None),
        P("seq", None),
        P("seq"),
        P("seq"),
        P("seq"),
        P("seq"),
    )
    return jax.shard_map(body, mesh=mesh, in_specs=in_specs, out_specs=out_specs, check_vma=False)
```

profile of v0, /device:TPU:1, one launch (start us, length us, event | category | flops | bytes accessed | tf_op | source)
XLA Modules:
  0.0 884.6 jit_solution(7067350845526966509)
XLA Ops:
  32.0 8.8 fusion.79
  49.5 8.9 %all-reduce = f32[16]{0:T(128)S(1)} all-reduce(f32[16]{0:T(128)S(1)} %dynamic-update-slice), channel_id=2, replica_groups=mesh['seq'=4,'batch'=8] {'seq'}, use_global_device_ids=true, to_apply=%add | all-reduce | flops 16 | bytes 128
  94.7 26.2 %all-gather.4.cloned.1.call-done = f32[4,4,24,4096]{3,2,1,0:T(8,128)} async-done(((f32[1,4,24,4096]{3,2,1,0:T(8,128)}), f32[4,4,24,4096]{3,2,1,0:T(8,128)}) %all-gather.4.cloned.1.call-update) | async-done | bytes 6291472 | tf_op jit(solution)/shard_map/all_gather | solution.py:21
  123.7 10.3 %fusion.8 = f32[4,12,64,256,1]{3,2,4,1,0:T(8,128)} fusion(f32[4,256,12,64]{1,3,2,0:T(8,128)} %copy.143, f32[4,2,256]{2,1,0:T(2,128)S(1)} %get-tuple-element.295, f32[4,2,12,64,64]{4,3,2,1,0:T(8,128)} %reshape.326), kind=kOutput, calls=%fused_computation.15 | convolution fusion | flops 1209532416 | bytes 7872512 | tf_op jit(solution)/shard_map/rtihk,rthkv->rihv/dot_general | solution.py:136
  139.8 10.2 %fusion.116 = (bf16[4,256,12,64]{1,3,2,0:T(8,128)(2,1)}, f32[4,256,12,64]{1,3,2,0:T(8,128)}) fusion(f32[4,256,12]{1,2,0:T(8,128)S(1)} %fusion.108, f32[4,12,64,256,1]{3,2,4,1,0:T(8,128)} %fusion.8, f32[4,12,256,256]{2,3,1,0:T(8,128)S(1)} %copy-done.1, f32[4,256,256]{1,2,0:T(8,128)} %copy-done.6, bf16[4,256,12,64]{1,0,3,2:T(4,128)(2,1)} %copy-done.10), kind=kOutput, calls=%fused_computation.175 | convolution fusion | flops 2421424128 | bytes 23117824 | tf_op jit(solution)/shard_map/rhij,rjhd->rihd/dot_general | solution.py:119
  157.6 34.6 %multiply_convert_fusion = (bf16[1024,3072]{1,0:T(8,128)(2,1)S(1)}, f32[1024,3072]{1,0:T(8,128)}, f32[1024,3072]{1,0:T(8,128)}) fusion(bf16[768,3072]{1,0:T(8,128)(2,1)S(1)} %bitcast.203, f32[1024,768]{1,0:T(8,128)S(1)} %get-tuple-element.309, f32[768]{0:T(1024)S(1)} %copy-done.46, f32[768]{0:T(1024)S(1)} %copy-done.45, f32[1024]{0:T(1024)S(1)} %add_rsqrt_fusion.1, ...), kind=kOutput, calls=%fused_computation.20 | convolution fusion | flops 5040242688 | bytes 39335936 | tf_op jit(solution)/shard_map/dot_general | solution.py:144
  203.6 18.1 %add_convert_fusion = bf16[1024,3072]{1,0:T(8,128)(2,1)} fusion(f32[1024,3072]{1,0:T(8,128)} %get-tuple-element.289, f32[1024,3072]{1,0:T(8,128)} %get-tuple-element.310, bf16[3072,768]{1,0:T(8,128)(2,1)} %param.25, f32[1024,768]{1,0:T(8,128)} %get-tuple-element.292), kind=kOutput, calls=%fused_computation.19 | convolution fusion | flops 4876664832 | bytes 39321600 | tf_op jit(solution)/shard_map/dot_general | solution.py:156
  221.7 10.7 %multiply_reduce_fusion.2 = (f32[768]{0:T(1024)}, f32[1024]{0:T(1024)S(1)}, f32[1024]{0:T(1024)S(1)}, f32[768]{0:T(1024)}, f32[1024,768]{1,0:T(8,128)S(1)}) fusion(f32[1024,768]{1,0:T(8,128)S(1)} %get-tuple-element.309, f32[1024]{0:T(1024)S(1)} %add_rsqrt_fusion.1, f32[1024]{0:T(1024)S(1)} %broadcast_multiply_fusion.6, f32[768]{0:T(1024)S(1)} %copy-done.45, ...), kind=kOutput, calls=%fused_computation.82 | convolution fusion | flops 4839698432 | bytes 20472832 | tf_op jit(solution)/shard_map/dot_general | solution.py:159
  243.4 12.3 %fusion.74 = f32[4,2,12,64,64]{3,4,1,2,0:T(8,128)} fusion(f32[4,256,12,64]{1,3,2,0:T(8,128)} %copy.143, f32[4,2,256]{2,1,0:T(2,128)S(1)} %copy-done.44, f32[4,256,12,64]{1,0,3,2:T(4,128)} %reshape.329, f32[4,256,12]{1,2,0:T(8,128)S(1)} %copy-done.24), kind=kOutput, calls=%fused_computation.117 | convolution fusion | flops 1210318848 | bytes 7921664 | tf_op jit(solution)/shard_map/rtihk,rihv->rthkv/dot_general | solution.py:180
  284.0 8.4 fusion.29
  292.4 9.8 %bitcast_add_fusion.8 = f32[4,256,12,64]{1,3,2,0:T(8,128)} fusion(f32[4,256,12,64]{1,3,2,0:T(8,128)} %fusion.29, f32[4,12,256,256]{2,3,1,0:T(8,128)S(1)} %fusion.91, f32[4,12,256]{2,1,0:T(8,128)S(1)} %bitcast_divide_fusion.1, f32[4,256,256]{1,2,0:T(8,128)S(1)} %copy-done.7, bf16[4,256,12,64]{1,0,3,2:T(4,128)(2,1)} %copy-done.14), kind=kOutput, calls=%fused_computation.68 | convolution fusion | flops 2422996992 | bytes 21544960 | tf_op jit(solution)/shard_map/rhij,rjhk->rihk/dot_general | solution.py:173
  321.7 11.6 %all_gather.22 = f32[4,4,1536]{2,1,0:T(4,128)S(1)} all-gather(f32[1,4,1536]{2,1,0:T(4,128)} %all_gather_reshape.15), channel_id=1, replica_groups=mesh['seq'=4,'batch'=8] {'seq'}, dimensions={0}, use_global_device_ids=true | all-gather | bytes 122880 | tf_op jit(solution)/shard_map/all_gather | solution.py:21
  349.7 8.8 fusion.16
  358.5 15.1 %fusion.86 = bf16[4,256,12,64]{1,3,2,0:T(8,128)(2,1)S(1)} fusion(f32[4,12,64,256,1]{3,2,4,1,0:T(8,128)S(1)} %fusion.16, f32[4,12,256,256]{2,3,1,0:T(8,128)} %get-tuple-element.305, f32[4,256,256]{1,2,0:T(8,128)S(1)} %copy-done.8, f32[4,256,12,64]{1,0,3,2:T(4,128)S(1)} %copy-done.5, f32[4,256,12]{1,2,0:T(8,128)S(1)} %copy-done.25), kind=kOutput, calls=%fused_computation.124 | convolution fusion | flops 2421424128 | bytes 21544960 | tf_op jit(solution)/shard_map/rhij,rihv->rjhv/dot_general | solution.py:172
  388.8 10.7 %bitcast_add_fusion.7 = f32[4,256,12,64]{1,3,2,0:T(8,128)S(1)} fusion(f32[4,256,12,64]{1,3,2,0:T(8,128)S(1)} %fusion.27, f32[4,12,256,256]{2,3,1,0:T(8,128)} %copy-done.2, f32[4,12,256]{2,1,0:T(8,128)S(1)} %copy-done.36, f32[4,256,256]{1,2,0:T(8,128)S(1)} %copy-done.8, bf16[4,256,12,64]{1,0,3,2:T(4,128)(2,1)S(1)} %copy-done.13), kind=kOutput, calls=%fused_computation.67 | convolution fusion | flops 2422996992 | bytes 21544960 | tf_op jit(solution)/shard_map/rhij,rihk->rjhk/dot_general | solution.py:174
  421.2 11.2 %fusion.109 = f32[768,3072]{1,0:T(8,128)} fusion(bf16[1024,3072]{1,0:T(8,128)(2,1)} %add_convert_fusion, f32[1024,768]{1,0:T(8,128)} %copy-done.9, f32[768]{0:T(1024)S(1)} %copy-done.46, f32[768]{0:T(1024)S(1)} %copy-done.45, f32[1024]{0:T(1024)S(1)} %add_rsqrt_fusion.1, f32[1024]{0:T(1024)S(1)} %broadcast_multiply_fusion.6), kind=kOutput, calls=%fused_computation.171 | convolution fusion | flops 4835770368 | bytes 18888704 | tf_op jit(solution)/shard_map/dot_general | solution.py:158
  432.5 10.3 %fusion.103 = f32[3072,768]{1,0:T(8,128)} fusion(bf16[1024,3072]{1,0:T(8,128)(2,1)} %copy-done.63, f32[1024,768]{1,0:T(8,128)} %get-tuple-element.292), kind=kOutput, calls=%fused_computation.140 | convolution fusion | flops 4832624640 | bytes 18874368 | tf_op jit(solution)/shard_map/dot_general | solution.py:155
  447.4 14.2 %reduce-scatter.21.cloned.1.call-done = f32[192,768]{1,0:T(8,128)} async-done(((f32[768,768]{1,0:T(8,128)}), f32[192,768]{1,0:T(8,128)}) %reduce-scatter.21.cloned.1.call-update) | async-done | bytes 589840
  463.8 38.7 %reduce-scatter.13.cloned.1.call-done = f32[192,768]{1,0:T(8,128)} async-done(((f32[768,768]{1,0:T(8,128)}), f32[192,768]{1,0:T(8,128)}) %reduce-scatter.13.cloned.1.call-update) | async-done | bytes 589840 | tf_op jit(solution)/shard_map/reduce_scatter | solution.py:212
  502.5 98.1 %reduce-scatter.15.cloned.1.call-done = f32[192,3072]{1,0:T(8,128)} async-done(((f32[768,3072]{1,0:T(8,128)}), f32[192,3072]{1,0:T(8,128)}) %reduce-scatter.15.cloned.1.call-update) | async-done | bytes 2359312 | tf_op jit(solution)/shard_map/reduce_scatter | solution.py:213
  600.6 98.2 %reduce-scatter.17.cloned.1.call-done = f32[768,768]{1,0:T(8,128)} async-done(((f32[3072,768]{1,0:T(8,128)}), f32[768,768]{1,0:T(8,128)}) %reduce-scatter.17.cloned.1.call-update) | async-done | bytes 2359312 | tf_op jit(solution)/shard_map/reduce_scatter | solution.py:214
  699.7 11.3 %all-reduce.7 = (f32[768]{0:T(1024)S(1)}, f32[768]{0:T(1024)S(1)}, f32[768]{0:T(1024)S(1)}, f32[768]{0:T(1024)S(1)}) all-reduce(f32[768]{0:T(1024)S(1)} %copy-done.51, f32[768]{0:T(1024)S(1)} %copy-done.52, f32[768]{0:T(1024)S(1)} %copy-done.49, f32[768]{0:T(1024)S(1)} %copy-done.48), channel_id=9, replica_groups=mesh['seq'=4,'batch'=8] {'seq'}, use_global_device_ids=true, to_apply=%region_33.34.clone | all-reduce | flops 3072 | bytes 24576
  711.3 18.6 %all-reduce.5 = (f32[192]{0:T(256)}, f32[192]{0:T(256)}, f32[192]{0:T(256)}, f32[192]{0:T(256)}) all-reduce(f32[192]{0:T(256)S(1)} %dynamic-slice.2, f32[192]{0:T(256)S(1)} %dynamic-slice.4, f32[192]{0:T(256)S(1)} %dynamic-slice.6, f32[192]{0:T(256)S(1)} %dynamic-slice.8), channel_id=1, replica_groups=mesh['seq'=4,'batch'=8] {'batch'}, use_global_device_ids=true, to_apply=%region_34.35 | all-reduce | flops 768 | bytes 6144 | tf_op jit(solution)/shard_map/psum | solution.py:220
  737.5 128.6 %all-reduce.10.cloned.1.call-done = (f32[192,768]{0,1:T(8,128)}, f32[192,768]{0,1:T(8,128)}, f32[192,768]{0,1:T(8,128)}, f32[192,768]{1,0:T(8,128)}, f32[192,3072]{1,0:T(8,128)}, /*index=5*/f32[768,768]{1,0:T(8,128)}) async-done(((f32[192,768]{0,1:T(8,128)}, f32[192,768]{0,1:T(8,128)}, f32[192,768]{0,1:T(8,128)}, f32[192,768]{1,0:T(8,128)}, f32[192,3072]{1,0:T(8,128)}, /*index=5*/f32[768,768]{1,0:T(8,128)}), ...) | async-done | bytes 7077904 | tf_op jit(solution)/shard_map/psum | solution.py:220
  (282 shorter events, 242.0 us)
Async XLA Ops:
  7.2 54.5 %copy-start = (bf16[768,768]{1,0:T(8,128)(2,1)S(1)}, bf16[768,768]{1,0:T(8,128)(2,1)}, u32[]{:S(2)}) copy-start(bf16[768,768]{1,0:T(8,128)(2,1)} %param.20) | copy-start | bytes 3538948
  7.2 113.7 %all-gather.4.cloned.1.call-start = ((), (), s32[]{:S(2)}) async-start(), calls=%async_computation.6 | async-start | bytes 7864320 | tf_op jit(solution)/shard_map/all_gather | solution.py:21
  31.9 8.9 %copy-start.10 = (bf16[4,256,12,64]{1,0,3,2:T(4,128)(2,1)}, bf16[4,256,12,64]{1,0,3,2:T(4,128)(2,1)S(1)}, u32[]{:S(2)}) copy-start(bf16[4,256,12,64]{1,0,3,2:T(4,128)(2,1)S(1)} %reshape.323) | copy-start | bytes 4718596
  32.0 26.4 %copy-start.41 = (f32[4,2,256]{2,1,0:T(2,128)}, f32[4,2,256]{2,1,0:T(2,128)S(1)}, u32[]{:S(2)}) copy-start(f32[4,2,256]{2,1,0:T(2,128)S(1)} %get-tuple-element.294) | copy-start | bytes 24580
  32.0 102.0 %copy-start.43 = (f32[4,2,256]{2,1,0:T(2,128)}, f32[4,2,256]{2,1,0:T(2,128)S(1)}, u32[]{:S(2)}) copy-start(f32[4,2,256]{2,1,0:T(2,128)S(1)} %get-tuple-element.295) | copy-start | bytes 24580
  47.7 291.6 %all-gather.6.cloned.1.call-start = ((), (), s32[]{:S(2)}) async-start(), calls=%async_computation.7 | async-start | bytes 7864320 | tf_op jit(solution)/shard_map/all_gather | solution.py:21
  77.4 17.3 %copy-start.6 = (f32[4,256,256]{1,2,0:T(8,128)}, f32[4,256,256]{1,2,0:T(8,128)S(1)}, u32[]{:S(2)}) copy-start(f32[4,256,256]{1,2,0:T(8,128)S(1)} %copy.136) | copy-start | bytes 3145732
  94.7 44.5 %copy-start.37 = (f32[4,12,256]{2,1,0:T(8,128)}, f32[4,12,256]{2,1,0:T(8,128)S(1)}, u32[]{:S(2)}) copy-start(f32[4,12,256]{2,1,0:T(8,128)S(1)} %get-tuple-element.304) | copy-start | bytes 147460
  121.1 12.9 %copy-start.27 = (f32[4,1536]{1,0:T(4,128)}, f32[4,1536]{1,0:T(4,128)S(1)}, u32[]{:S(2)}) copy-start(f32[4,1536]{1,0:T(4,128)S(1)} %get-tuple-element.185) | copy-start | bytes 73732
  121.1 12.9 %copy-start.54 = (f32[4,4]{1,0:T(4,128)}, f32[4,4]{1,0:T(4,128)S(1)}, u32[]{:S(2)}) copy-start(f32[4,4]{1,0:T(4,128)S(1)} %get-tuple-element.537) | copy-start | bytes 196
  123.7 16.1 %copy-start.1 = (f32[4,12,256,256]{2,3,1,0:T(8,128)S(1)}, f32[4,12,256,256]{2,3,1,0:T(8,128)}, u32[]{:S(2)}) copy-start(f32[4,12,256,256]{2,3,1,0:T(8,128)} %get-tuple-element.305) | copy-start | bytes 37748740
  139.8 10.2 %copy-start.23 = (f32[4,256,12]{1,2,0:T(8,128)}, f32[4,256,12]{1,2,0:T(8,128)S(1)}, u32[]{:S(2)}) copy-start(f32[4,256,12]{1,2,0:T(8,128)S(1)} %fusion.108) | copy-start | bytes 147460
  153.3 38.9 %slice-start = ((s8[4718592]{0:T(1024)(128)(4,1)}), s8[4194304]{0:T(1024)(128)(4,1)S(1)}, s32[]{:S(2)}) async-start(s8[4718592]{0:T(1024)(128)(4,1)} %bitcast.200), calls=%async_computation.15 | async-start | bytes 8388608
  155.0 77.4 %copy-start.9 = (f32[1024,768]{1,0:T(8,128)}, f32[1024,768]{1,0:T(8,128)S(1)}, u32[]{:S(2)}) copy-start(f32[1024,768]{1,0:T(8,128)S(1)} %get-tuple-element.309) | copy-start | bytes 9437188
  157.6 34.6 %slice-start.1 = ((s8[4718592]{0:T(1024)(128)(4,1)}), s8[524288]{0:T(1024)(128)(4,1)S(1)}, s32[]{:S(2)}) async-start(s8[4718592]{0:T(1024)(128)(4,1)} %bitcast.200), calls=%async_computation.16 | async-start | bytes 1048576
  262.6 180.3 %reduce-scatter.19.cloned.1.call-start = ((), (), s32[]{:S(2)}) async-start(), calls=%async_computation.11 | async-start | bytes 2949120
  275.5 16.9 %copy-start.35 = (f32[4,12,256]{2,1,0:T(8,128)}, f32[4,12,256]{2,1,0:T(8,128)S(1)}, u32[]{:S(2)}) copy-start(f32[4,12,256]{2,1,0:T(8,128)S(1)} %bitcast_divide_fusion.1) | copy-start | bytes 147460
  333.3 111.9 %reduce-scatter.23.cloned.1.call-start = ((), (), s32[]{:S(2)}) async-start(), calls=%async_computation.13 | async-start | bytes 2949120
  382.3 79.3 %reduce-scatter.21.cloned.1.call-start = ((), (), s32[]{:S(2)}) async-start(), calls=%async_computation.12 | async-start | bytes 2949120
  415.9 86.7 %reduce-scatter.13.cloned.1.call-start = ((), (), s32[]{:S(2)}) async-start(), calls=%async_computation.8 | async-start | bytes 2949120 | tf_op jit(solution)/shard_map/reduce_scatter | solution.py:212
  421.1 179.5 %reduce-scatter.15.cloned.1.call-start = ((), (), s32[]{:S(2)}) async-start(), calls=%async_computation.9 | async-start | bytes 11796480 | tf_op jit(solution)/shard_map/reduce_scatter | solution.py:213
  432.5 266.3 %reduce-scatter.17.cloned.1.call-start = ((), (), s32[]{:S(2)}) async-start(), calls=%async_computation.10 | async-start | bytes 11796480 | tf_op jit(solution)/shard_map/reduce_scatter | solution.py:214
  442.9 423.2 %all-reduce.10.cloned.1.call-start = ((), (), s32[]{:S(2)}) async-start(), calls=%async_computation.14 | async-start | bytes 15335424 | tf_op jit(solution)/shard_map/psum | solution.py:220
  698.8 31.0 %copy-start.30 = (bf16[1024,768]{1,0:T(8,128)(2,1)S(1)}, bf16[1024,768]{1,0:T(8,128)(2,1)}, u32[]{:S(2)}) copy-start(bf16[1024,768]{1,0:T(8,128)(2,1)} %copy-done.29) | copy-start | bytes 4718596
  (53 other events, 217.3 us)
Sparse Core Ops, SparseCore 0:
  47.9 73.0 all-gather.3
  262.7 76.5 all-gather.5
  342.9 37.3 reduce-scatter.18
  383.3 37.3 reduce-scatter.22
  424.2 37.3 reduce-scatter.20
  465.1 37.3 reduce-scatter.12
  505.6 94.9 reduce-scatter.14
  603.7 95.0 reduce-scatter.16
  702.3 163.7 all-reduce.9
where the time goes:
time: 895 us; the launch traced here: 885 us
  waiting for transfers between devices  410 us (46%)
  matrix products  258 us (29%)
  local copies, waits for them, and re-layouts  110 us (12%)
  blocking collectives  56.2 us (6%)
  other arithmetic  33.2 us (4%)
  between operations  16.6 us (2%)
    psum x1, waiting for transfers between devices, body(): lax.psum((shards[0], shards[1], shards[2], shards[3], shards[4], shards[5...  129 us
    reduce_scatter x1, waiting for transfers between devices, body(): lax.psum_scatter(grad_back, 'seq', scatter_dimension=0, tiled=True)  98.2 us
    reduce_scatter x1, waiting for transfers between devices, body(): lax.psum_scatter(grad_in, 'seq', scatter_dimension=0, tiled=True)  98.1 us
    unnamed x160, local copies, waits for them, and re-layouts  43.7 us
    reduce_scatter x1, waiting for transfers between devices, body(): lax.psum_scatter(grad_out, 'seq', scatter_dimension=0, tiled=True)  38.7 us
    dot_general x1, matrix products, body(): hidden = jnp.dot(first_low, w_in, preferred_element_type=jnp.float32)  34.6 us
    all_gather x2, waiting for transfers between devices, entering(): gathered = jax.tree.map(lambda a: lax.all_gather(a, axis), part)  32.1 us
    unnamed x2, blocking collectives  20.2 us
  transfers between devices with their start and end apart: 9, of which 7 were waited for; matrix products, arithmetic and copies ran while one was open for 23% of the time, Pallas kernels for 0%

commit v1 on v0

--- a/solution.py
+++ b/solution.py
@@ -31,7 +31,9 @@
 
 
 def doc_tables(lengths, positions):
-    doc_ends = jnp.cumsum(lengths, axis=-1)
+    order = jnp.arange(lengths.shape[-1])
+    upto = (order[:, None] >= order[None, :]).astype(jnp.int32)
+    doc_ends = jnp.sum(lengths[:, None, :] * upto[None], axis=-1)
     starts = doc_ends - lengths
     inside = (
         (positions[None, :, None] >= starts[:, None, :])

time: 895 us -> 895 us (level)
  no operation moved by 1% of the time
where the time goes in v1:
time: 895 us; the launch traced here: 885 us
  waiting for transfers between devices  410 us (46%)
  matrix products  258 us (29%)
  local copies, waits for them, and re-layouts  110 us (12%)
  blocking collectives  56.2 us (6%)
  other arithmetic  33.1 us (4%)
  between operations  16.6 us (2%)
    psum x1, waiting for transfers between devices, body(): lax.psum((shards[0], shards[1], shards[2], shards[3], shards[4], shards[5...  129 us
    reduce_scatter x1, waiting for transfers between devices, body(): lax.psum_scatter(grad_back, 'seq', scatter_dimension=0, tiled=True)  98.2 us
    reduce_scatter x1, waiting for transfers between devices, body(): lax.psum_scatter(grad_in, 'seq', scatter_dimension=0, tiled=True)  98.1 us
    unnamed x160, local copies, waits for them, and re-layouts  43.6 us
    reduce_scatter x1, waiting for transfers between devices, body(): lax.psum_scatter(grad_out, 'seq', scatter_dimension=0, tiled=True)  38.7 us
    dot_general x1, matrix products, body(): hidden = jnp.dot(first_low, w_in, preferred_element_type=jnp.float32)  34.6 us
    all_gather x2, waiting for transfers between devices, entering(): gathered = jax.tree.map(lambda a: lax.all_gather(a, axis), part)  32.1 us
    unnamed x2, blocking collectives  20.2 us
  transfers between devices with their start and end apart: 9, of which 7 were waited for; matrix products, arithmetic and copies ran while one was open for 23% of the time, Pallas kernels for 0%

profile of v1, /device:TPU:1, one launch (start us, length us, event | category | flops | bytes accessed | tf_op | source)
XLA Modules:
  0.0 884.6 jit_solution(16584400238181746356)
XLA Ops:
  32.0 8.8 fusion.79
  49.5 8.9 %all-reduce = f32[16]{0:T(128)S(1)} all-reduce(f32[16]{0:T(128)S(1)} %dynamic-update-slice), channel_id=2, replica_groups=mesh['seq'=4,'batch'=8] {'seq'}, use_global_device_ids=true, to_apply=%add | all-reduce | flops 16 | bytes 128
  94.7 26.2 %all-gather.4.cloned.1.call-done = f32[4,4,24,4096]{3,2,1,0:T(8,128)} async-done(((f32[1,4,24,4096]{3,2,1,0:T(8,128)}), f32[4,4,24,4096]{3,2,1,0:T(8,128)}) %all-gather.4.cloned.1.call-update) | async-done | bytes 6291472 | tf_op jit(solution)/shard_map/all_gather | solution.py:21
  123.7 10.3 %fusion.8 = f32[4,12,64,256,1]{3,2,4,1,0:T(8,128)} fusion(f32[4,256,12,64]{1,3,2,0:T(8,128)} %copy.143, f32[4,2,256]{2,1,0:T(2,128)S(1)} %get-tuple-element.295, f32[4,2,12,64,64]{4,3,2,1,0:T(8,128)} %reshape.339), kind=kOutput, calls=%fused_computation.15 | convolution fusion | flops 1209532416 | bytes 7872512 | tf_op jit(solution)/shard_map/rtihk,rthkv->rihv/dot_general | solution.py:138
  139.8 10.2 %fusion.117 = (bf16[4,256,12,64]{1,3,2,0:T(8,128)(2,1)}, f32[4,256,12,64]{1,3,2,0:T(8,128)}) fusion(f32[4,256,12]{1,2,0:T(8,128)S(1)} %fusion.108, f32[4,12,64,256,1]{3,2,4,1,0:T(8,128)} %fusion.8, f32[4,12,256,256]{2,3,1,0:T(8,128)S(1)} %copy-done.1, f32[4,256,256]{1,2,0:T(8,128)} %copy-done.6, bf16[4,256,12,64]{1,0,3,2:T(4,128)(2,1)} %copy-done.10), kind=kOutput, calls=%fused_computation.178 | convolution fusion | flops 2421424128 | bytes 23117824 | tf_op jit(solution)/shard_map/rhij,rjhd->rihd/dot_general | solution.py:121
  157.6 34.6 %multiply_convert_fusion = (bf16[1024,3072]{1,0:T(8,128)(2,1)S(1)}, f32[1024,3072]{1,0:T(8,128)}, f32[1024,3072]{1,0:T(8,128)}) fusion(bf16[768,3072]{1,0:T(8,128)(2,1)S(1)} %bitcast.203, f32[1024,768]{1,0:T(8,128)S(1)} %get-tuple-element.309, f32[768]{0:T(1024)S(1)} %copy-done.46, f32[768]{0:T(1024)S(1)} %copy-done.45, f32[1024]{0:T(1024)S(1)} %add_rsqrt_fusion.1, ...), kind=kOutput, calls=%fused_computation.20 | convolution fusion | flops 5040242688 | bytes 39335936 | tf_op jit(solution)/shard_map/dot_general | solution.py:146
  203.7 18.1 %add_convert_fusion = bf16[1024,3072]{1,0:T(8,128)(2,1)} fusion(f32[1024,3072]{1,0:T(8,128)} %get-tuple-element.289, f32[1024,3072]{1,0:T(8,128)} %get-tuple-element.310, bf16[3072,768]{1,0:T(8,128)(2,1)} %param.25, f32[1024,768]{1,0:T(8,128)} %get-tuple-element.292), kind=kOutput, calls=%fused_computation.19 | convolution fusion | flops 4876664832 | bytes 39321600 | tf_op jit(solution)/shard_map/dot_general | solution.py:158
  221.8 10.7 %multiply_reduce_fusion.2 = (f32[768]{0:T(1024)}, f32[1024]{0:T(1024)S(1)}, f32[1024]{0:T(1024)S(1)}, f32[768]{0:T(1024)}, f32[1024,768]{1,0:T(8,128)S(1)}) fusion(f32[1024,768]{1,0:T(8,128)S(1)} %get-tuple-element.309, f32[1024]{0:T(1024)S(1)} %add_rsqrt_fusion.1, f32[1024]{0:T(1024)S(1)} %broadcast_multiply_fusion.6, f32[768]{0:T(1024)S(1)} %copy-done.45, ...), kind=kOutput, calls=%fused_computation.82 | convolution fusion | flops 4839698432 | bytes 20472832 | tf_op jit(solution)/shard_map/dot_general | solution.py:161
  243.4 12.3 %fusion.74 = f32[4,2,12,64,64]{3,4,1,2,0:T(8,128)} fusion(f32[4,256,12,64]{1,3,2,0:T(8,128)} %copy.143, f32[4,2,256]{2,1,0:T(2,128)S(1)} %copy-done.44, f32[4,256,12,64]{1,0,3,2:T(4,128)} %reshape.342, f32[4,256,12]{1,2,0:T(8,128)S(1)} %copy-done.24), kind=kOutput, calls=%fused_computation.117 | convolution fusion | flops 1210318848 | bytes 7921664 | tf_op jit(solution)/shard_map/rtihk,rihv->rthkv/dot_general | solution.py:182
  284.0 8.4 fusion.29
  292.4 9.8 %bitcast_add_fusion.8 = f32[4,256,12,64]{1,3,2,0:T(8,128)} fusion(f32[4,256,12,64]{1,3,2,0:T(8,128)} %fusion.29, f32[4,12,256,256]{2,3,1,0:T(8,128)S(1)} %fusion.91, f32[4,12,256]{2,1,0:T(8,128)S(1)} %bitcast_divide_fusion.1, f32[4,256,256]{1,2,0:T(8,128)S(1)} %copy-done.7, bf16[4,256,12,64]{1,0,3,2:T(4,128)(2,1)} %copy-done.14), kind=kOutput, calls=%fused_computation.68 | convolution fusion | flops 2422996992 | bytes 21544960 | tf_op jit(solution)/shard_map/rhij,rjhk->rihk/dot_general | solution.py:175
  321.7 11.6 %all_gather.22 = f32[4,4,1536]{2,1,0:T(4,128)S(1)} all-gather(f32[1,4,1536]{2,1,0:T(4,128)} %all_gather_reshape.15), channel_id=1, replica_groups=mesh['seq'=4,'batch'=8] {'seq'}, dimensions={0}, use_global_device_ids=true | all-gather | bytes 122880 | tf_op jit(solution)/shard_map/all_gather | solution.py:21
  349.7 8.8 fusion.16
  358.5 15.1 %fusion.86 = bf16[4,256,12,64]{1,3,2,0:T(8,128)(2,1)S(1)} fusion(f32[4,12,64,256,1]{3,2,4,1,0:T(8,128)S(1)} %fusion.16, f32[4,12,256,256]{2,3,1,0:T(8,128)} %get-tuple-element.305, f32[4,256,256]{1,2,0:T(8,128)S(1)} %copy-done.8, f32[4,256,12,64]{1,0,3,2:T(4,128)S(1)} %copy-done.5, f32[4,256,12]{1,2,0:T(8,128)S(1)} %copy-done.25), kind=kOutput, calls=%fused_computation.124 | convolution fusion | flops 2421424128 | bytes 21544960 | tf_op jit(solution)/shard_map/rhij,rihv->rjhv/dot_general | solution.py:174
  388.8 10.7 %bitcast_add_fusion.7 = f32[4,256,12,64]{1,3,2,0:T(8,128)S(1)} fusion(f32[4,256,12,64]{1,3,2,0:T(8,128)S(1)} %fusion.27, f32[4,12,256,256]{2,3,1,0:T(8,128)} %copy-done.2, f32[4,12,256]{2,1,0:T(8,128)S(1)} %copy-done.36, f32[4,256,256]{1,2,0:T(8,128)S(1)} %copy-done.8, bf16[4,256,12,64]{1,0,3,2:T(4,128)(2,1)S(1)} %copy-done.13), kind=kOutput, calls=%fused_computation.67 | convolution fusion | flops 2422996992 | bytes 21544960 | tf_op jit(solution)/shard_map/rhij,rihk->rjhk/dot_general | solution.py:176
  421.2 11.2 %fusion.110 = f32[768,3072]{1,0:T(8,128)} fusion(bf16[1024,3072]{1,0:T(8,128)(2,1)} %add_convert_fusion, f32[1024,768]{1,0:T(8,128)} %copy-done.9, f32[768]{0:T(1024)S(1)} %copy-done.46, f32[768]{0:T(1024)S(1)} %copy-done.45, f32[1024]{0:T(1024)S(1)} %add_rsqrt_fusion.1, f32[1024]{0:T(1024)S(1)} %broadcast_multiply_fusion.6), kind=kOutput, calls=%fused_computation.174 | convolution fusion | flops 4835770368 | bytes 18888704 | tf_op jit(solution)/shard_map/dot_general | solution.py:160
  432.5 10.3 %fusion.103 = f32[3072,768]{1,0:T(8,128)} fusion(bf16[1024,3072]{1,0:T(8,128)(2,1)} %copy-done.63, f32[1024,768]{1,0:T(8,128)} %get-tuple-element.292), kind=kOutput, calls=%fused_computation.140 | convolution fusion | flops 4832624640 | bytes 18874368 | tf_op jit(solution)/shard_map/dot_general | solution.py:157
  447.4 14.2 %reduce-scatter.21.cloned.1.call-done = f32[192,768]{1,0:T(8,128)} async-done(((f32[768,768]{1,0:T(8,128)}), f32[192,768]{1,0:T(8,128)}) %reduce-scatter.21.cloned.1.call-update) | async-done | bytes 589840
  463.8 38.7 %reduce-scatter.13.cloned.1.call-done = f32[192,768]{1,0:T(8,128)} async-done(((f32[768,768]{1,0:T(8,128)}), f32[192,768]{1,0:T(8,128)}) %reduce-scatter.13.cloned.1.call-update) | async-done | bytes 589840 | tf_op jit(solution)/shard_map/reduce_scatter | solution.py:214
  502.5 98.1 %reduce-scatter.15.cloned.1.call-done = f32[192,3072]{1,0:T(8,128)} async-done(((f32[768,3072]{1,0:T(8,128)}), f32[192,3072]{1,0:T(8,128)}) %reduce-scatter.15.cloned.1.call-update) | async-done | bytes 2359312 | tf_op jit(solution)/shard_map/reduce_scatter | solution.py:215
  600.6 98.2 %reduce-scatter.17.cloned.1.call-done = f32[768,768]{1,0:T(8,128)} async-done(((f32[3072,768]{1,0:T(8,128)}), f32[768,768]{1,0:T(8,128)}) %reduce-scatter.17.cloned.1.call-update) | async-done | bytes 2359312 | tf_op jit(solution)/shard_map/reduce_scatter | solution.py:216
  699.6 11.3 %all-reduce.7 = (f32[768]{0:T(1024)S(1)}, f32[768]{0:T(1024)S(1)}, f32[768]{0:T(1024)S(1)}, f32[768]{0:T(1024)S(1)}) all-reduce(f32[768]{0:T(1024)S(1)} %copy-done.51, f32[768]{0:T(1024)S(1)} %copy-done.52, f32[768]{0:T(1024)S(1)} %copy-done.49, f32[768]{0:T(1024)S(1)} %copy-done.48), channel_id=9, replica_groups=mesh['seq'=4,'batch'=8] {'seq'}, use_global_device_ids=true, to_apply=%region_33.34.clone | all-reduce | flops 3072 | bytes 24576
  711.2 18.6 %all-reduce.5 = (f32[192]{0:T(256)}, f32[192]{0:T(256)}, f32[192]{0:T(256)}, f32[192]{0:T(256)}) all-reduce(f32[192]{0:T(256)S(1)} %dynamic-slice.2, f32[192]{0:T(256)S(1)} %dynamic-slice.4, f32[192]{0:T(256)S(1)} %dynamic-slice.6, f32[192]{0:T(256)S(1)} %dynamic-slice.8), channel_id=1, replica_groups=mesh['seq'=4,'batch'=8] {'batch'}, use_global_device_ids=true, to_apply=%region_34.35 | all-reduce | flops 768 | bytes 6144 | tf_op jit(solution)/shard_map/psum | solution.py:222
  737.5 128.6 %all-reduce.10.cloned.1.call-done = (f32[192,768]{0,1:T(8,128)}, f32[192,768]{0,1:T(8,128)}, f32[192,768]{0,1:T(8,128)}, f32[192,768]{1,0:T(8,128)}, f32[192,3072]{1,0:T(8,128)}, /*index=5*/f32[768,768]{1,0:T(8,128)}) async-done(((f32[192,768]{0,1:T(8,128)}, f32[192,768]{0,1:T(8,128)}, f32[192,768]{0,1:T(8,128)}, f32[192,768]{1,0:T(8,128)}, f32[192,3072]{1,0:T(8,128)}, /*index=5*/f32[768,768]{1,0:T(8,128)}), ...) | async-done | bytes 7077904 | tf_op jit(solution)/shard_map/psum | solution.py:222
  (283 shorter events, 242.0 us)
Async XLA Ops:
  7.2 54.5 %copy-start = (bf16[768,768]{1,0:T(8,128)(2,1)S(1)}, bf16[768,768]{1,0:T(8,128)(2,1)}, u32[]{:S(2)}) copy-start(bf16[768,768]{1,0:T(8,128)(2,1)} %param.20) | copy-start | bytes 3538948
  7.2 113.7 %all-gather.4.cloned.1.call-start = ((), (), s32[]{:S(2)}) async-start(), calls=%async_computation.6 | async-start | bytes 7864320 | tf_op jit(solution)/shard_map/all_gather | solution.py:21
  31.9 8.9 %copy-start.10 = (bf16[4,256,12,64]{1,0,3,2:T(4,128)(2,1)}, bf16[4,256,12,64]{1,0,3,2:T(4,128)(2,1)S(1)}, u32[]{:S(2)}) copy-start(bf16[4,256,12,64]{1,0,3,2:T(4,128)(2,1)S(1)} %reshape.336) | copy-start | bytes 4718596
  31.9 26.4 %copy-start.41 = (f32[4,2,256]{2,1,0:T(2,128)}, f32[4,2,256]{2,1,0:T(2,128)S(1)}, u32[]{:S(2)}) copy-start(f32[4,2,256]{2,1,0:T(2,128)S(1)} %get-tuple-element.294) | copy-start | bytes 24580
  32.0 102.0 %copy-start.43 = (f32[4,2,256]{2,1,0:T(2,128)}, f32[4,2,256]{2,1,0:T(2,128)S(1)}, u32[]{:S(2)}) copy-start(f32[4,2,256]{2,1,0:T(2,128)S(1)} %get-tuple-element.295) | copy-start | bytes 24580
  47.7 291.6 %all-gather.6.cloned.1.call-start = ((), (), s32[]{:S(2)}) async-start(), calls=%async_computation.7 | async-start | bytes 7864320 | tf_op jit(solution)/shard_map/all_gather | solution.py:21
  77.4 17.3 %copy-start.6 = (f32[4,256,256]{1,2,0:T(8,128)}, f32[4,256,256]{1,2,0:T(8,128)S(1)}, u32[]{:S(2)}) copy-start(f32[4,256,256]{1,2,0:T(8,128)S(1)} %copy.136) | copy-start | bytes 3145732
  94.7 44.5 %copy-start.37 = (f32[4,12,256]{2,1,0:T(8,128)}, f32[4,12,256]{2,1,0:T(8,128)S(1)}, u32[]{:S(2)}) copy-start(f32[4,12,256]{2,1,0:T(8,128)S(1)} %get-tuple-element.304) | copy-start | bytes 147460
  121.1 12.9 %copy-start.27 = (f32[4,1536]{1,0:T(4,128)}, f32[4,1536]{1,0:T(4,128)S(1)}, u32[]{:S(2)}) copy-start(f32[4,1536]{1,0:T(4,128)S(1)} %get-tuple-element.185) | copy-start | bytes 73732
  121.1 12.9 %copy-start.54 = (f32[4,4]{1,0:T(4,128)}, f32[4,4]{1,0:T(4,128)S(1)}, u32[]{:S(2)}) copy-start(f32[4,4]{1,0:T(4,128)S(1)} %get-tuple-element.537) | copy-start | bytes 196
  123.7 16.1 %copy-start.1 = (f32[4,12,256,256]{2,3,1,0:T(8,128)S(1)}, f32[4,12,256,256]{2,3,1,0:T(8,128)}, u32[]{:S(2)}) copy-start(f32[4,12,256,256]{2,3,1,0:T(8,128)} %get-tuple-element.305) | copy-start | bytes 37748740
  139.8 10.2 %copy-start.23 = (f32[4,256,12]{1,2,0:T(8,128)}, f32[4,256,12]{1,2,0:T(8,128)S(1)}, u32[]{:S(2)}) copy-start(f32[4,256,12]{1,2,0:T(8,128)S(1)} %fusion.108) | copy-start | bytes 147460
  153.3 38.9 %slice-start = ((s8[4718592]{0:T(1024)(128)(4,1)}), s8[4194304]{0:T(1024)(128)(4,1)S(1)}, s32[]{:S(2)}) async-start(s8[4718592]{0:T(1024)(128)(4,1)} %bitcast.200), calls=%async_computation.15 | async-start | bytes 8388608
  155.0 77.4 %copy-start.9 = (f32[1024,768]{1,0:T(8,128)}, f32[1024,768]{1,0:T(8,128)S(1)}, u32[]{:S(2)}) copy-start(f32[1024,768]{1,0:T(8,128)S(1)} %get-tuple-element.309) | copy-start | bytes 9437188
  157.6 34.6 %slice-start.1 = ((s8[4718592]{0:T(1024)(128)(4,1)}), s8[524288]{0:T(1024)(128)(4,1)S(1)}, s32[]{:S(2)}) async-start(s8[4718592]{0:T(1024)(128)(4,1)} %bitcast.200), calls=%async_computation.16 | async-start | bytes 1048576
  262.6 180.3 %reduce-scatter.19.cloned.1.call-start = ((), (), s32[]{:S(2)}) async-start(), calls=%async_computation.11 | async-start | bytes 2949120
  275.5 16.9 %copy-start.35 = (f32[4,12,256]{2,1,0:T(8,128)}, f32[4,12,256]{2,1,0:T(8,128)S(1)}, u32[]{:S(2)}) copy-start(f32[4,12,256]{2,1,0:T(8,128)S(1)} %bitcast_divide_fusion.1) | copy-start | bytes 147460
  333.3 111.8 %reduce-scatter.23.cloned.1.call-start = ((), (), s32[]{:S(2)}) async-start(), calls=%async_computation.13 | async-start | bytes 2949120
  382.3 79.3 %reduce-scatter.21.cloned.1.call-start = ((), (), s32[]{:S(2)}) async-start(), calls=%async_computation.12 | async-start | bytes 2949120
  415.8 86.7 %reduce-scatter.13.cloned.1.call-start = ((), (), s32[]{:S(2)}) async-start(), calls=%async_computation.8 | async-start | bytes 2949120 | tf_op jit(solution)/shard_map/reduce_scatter | solution.py:214
  421.1 179.5 %reduce-scatter.15.cloned.1.call-start = ((), (), s32[]{:S(2)}) async-start(), calls=%async_computation.9 | async-start | bytes 11796480 | tf_op jit(solution)/shard_map/reduce_scatter | solution.py:215
  432.5 266.3 %reduce-scatter.17.cloned.1.call-start = ((), (), s32[]{:S(2)}) async-start(), calls=%async_computation.10 | async-start | bytes 11796480 | tf_op jit(solution)/shard_map/reduce_scatter | solution.py:216
  442.9 423.2 %all-reduce.10.cloned.1.call-start = ((), (), s32[]{:S(2)}) async-start(), calls=%async_computation.14 | async-start | bytes 15335424 | tf_op jit(solution)/shard_map/psum | solution.py:222
  698.8 31.0 %copy-start.30 = (bf16[1024,768]{1,0:T(8,128)(2,1)S(1)}, bf16[1024,768]{1,0:T(8,128)(2,1)}, u32[]{:S(2)}) copy-start(bf16[1024,768]{1,0:T(8,128)(2,1)} %copy-done.29) | copy-start | bytes 4718596
  (53 other events, 217.3 us)
Sparse Core Ops, SparseCore 0:
  47.8 73.0 all-gather.3
  262.7 76.5 all-gather.5
  342.9 37.3 reduce-scatter.18
  383.3 37.3 reduce-scatter.22
  424.2 37.3 reduce-scatter.20
  465.1 37.3 reduce-scatter.12
  505.6 94.9 reduce-scatter.14
  603.7 95.0 reduce-scatter.16
  702.2 163.7 all-reduce.9

commit v2 on v0

v2 whole, which is shorter than its diff:
```python
import jax
import jax.numpy as jnp
from jax import lax
from jax.experimental import pallas as pl
from jax.experimental.pallas import tpu as pltpu
from jax.sharding import PartitionSpec as P

HEADS = 12
HEAD_DIM = 64
PAIRS = HEADS // 2
HALF_HEADS = HEADS // 2
STATE_ROWS = HALF_HEADS * HEAD_DIM + 8

f32 = jnp.float32
bf16 = jnp.bfloat16
half_pi = 1.5707963267948966
norm_eps = 1e-05
VMEM_LIMIT = 58 * 1024 * 1024

NN = (((1,), (0,)), ((), ()))
NT = (((1,), (1,)), ((), ()))
TN = (((0,), (0,)), ((), ()))


def mm(a, b, dims=NN):
    return lax.dot_general(a, b, dims, preferred_element_type=f32)


COS, SIN, BEGIN, COS_READ, SIN_READ, COS_TAIL, SIN_TAIL = range(7)


def make_table(place, lens_ref, row, tok_count):
    pos = place + lax.broadcasted_iota(jnp.int32, (8, tok_count), 1)
    last = place + tok_count - 1
    start = jnp.int32(0)
    begin = jnp.zeros((8, tok_count), jnp.int32)
    span = jnp.ones((8, tok_count), jnp.int32)
    last_begin = jnp.int32(0)
    for d in range(lens_ref.shape[1]):
        length = lens_ref[row, d]
        inside = pos >= start
        begin = jnp.where(inside, start, begin)
        span = jnp.where(inside, length, span)
        last_begin = jnp.where(start <= last, start, last_begin)
        start = start + length
    angle = half_pi * (pos - begin).astype(f32) / span.astype(f32)
    cos, sin = jnp.cos(angle), jnp.sin(angle)
    reader = (begin < place).astype(f32)
    tail = (begin == last_begin).astype(f32)
    which = lax.broadcasted_iota(jnp.int32, (8, tok_count), 0)
    table = jnp.zeros((8, tok_count), f32)
    for index, value in (
        (COS, cos),
        (SIN, sin),
        (BEGIN, begin.astype(f32)),
        (COS_READ, cos * reader),
        (SIN_READ, sin * reader),
        (COS_TAIL, cos * tail),
        (SIN_TAIL, sin * tail),
    ):
        table = jnp.where(which == index, value, table)
    return table


def blend_of(table):
    columns = table.T
    tok_count = table.shape[1]
    source = lax.broadcasted_iota(jnp.int32, (tok_count, tok_count), 0)
    reader = lax.broadcasted_iota(jnp.int32, (tok_count, tok_count), 1)
    same = (columns[:, BEGIN : BEGIN + 1] == table[BEGIN : BEGIN + 1]) & (source <= reader)
    value = (
        columns[:, COS : COS + 1] * table[COS : COS + 1]
        + columns[:, SIN : SIN + 1] * table[SIN : SIN + 1]
    )
    return jnp.where(same, value, 0.0)


def trig_rows(head_rows, cos, sin):
    wide = head_rows.astype(f32)
    return jnp.concatenate([(wide * cos).astype(bf16), (wide * sin).astype(bf16)], axis=0)


def with_row(rows, extra):
    which = lax.broadcasted_iota(jnp.int32, (16, rows.shape[1]), 0)
    return jnp.concatenate([rows, jnp.where(which == 0, extra, 0.0).astype(bf16)], axis=0)


def head_slice(h):
    return slice(h * HEAD_DIM, (h + 1) * HEAD_DIM)


def put_state(state_refs, h, value):
    ref = state_refs[h // HALF_HEADS]
    place = h % HALF_HEADS
    ref[0, head_slice(place), :] = value[:HEAD_DIM]
    ref[0, HALF_HEADS * HEAD_DIM + place : HALF_HEADS * HEAD_DIM + place + 1, :] = value[
        HEAD_DIM : HEAD_DIM + 1
    ]


def take_state(state_refs, h):
    ref = state_refs[h // HALF_HEADS]
    place = h % HALF_HEADS
    mats = ref[0, head_slice(place), :].astype(bf16)
    sums = ref[0, HALF_HEADS * HEAD_DIM + place : HALF_HEADS * HEAD_DIM + place + 1, :]
    return with_row(mats, sums)


def clear_pad(state_refs):
    for ref in state_refs:
        ref[0, HALF_HEADS * HEAD_DIM :, :] = jnp.zeros((8, 2 * HEAD_DIM), f32)


def softplus_sigmoid(v):
    small = jnp.exp(-jnp.abs(v))
    soft = jnp.maximum(v, 0.0) + jnp.log1p(small)
    inverse = 1.0 / (1.0 + small)
    return soft, jnp.where(v >= 0, inverse, small * inverse)


def project_kernel(
    place_ref,
    lens_ref,
    tok_ref,
    wk_ref,
    wv_ref,
    tab_ref,
    tok_t_ref,
    k_t_ref,
    v_t_ref,
    k_ref,
    v_ref,
    sig_k_ref,
    state_a,
    state_b,
    w_t,
):
    row = pl.program_id(0)

    @pl.when(row == 0)
    def _():
        w_t[0] = wk_ref[...].T
        w_t[1] = wv_ref[...].T

    tok_t = tok_ref[0].T
    tok_t_ref[...] = tok_t
    table = make_table(place_ref[0], lens_ref, row, tok_t.shape[1])
    tab_ref[0] = table
    soft, sig = softplus_sigmoid(mm(w_t[0], tok_t))
    key_t = soft.astype(bf16)
    k_t_ref[...] = key_t
    k_ref[0] = key_t.T
    sig_k_ref[...] = sig.astype(bf16)
    value_t = mm(w_t[1], tok_t).astype(bf16)
    v_t_ref[...] = value_t
    v_ref[0] = value_t.T
    states = (state_a, state_b)
    clear_pad(states)
    cos, sin = table[COS_TAIL : COS_TAIL + 1], table[SIN_TAIL : SIN_TAIL + 1]
    for h in range(HEADS):
        keys = trig_rows(k_t_ref[head_slice(h), :], cos, sin)
        values = with_row(v_t_ref[head_slice(h), :], 1.0)
        put_state(states, h, mm(values, keys, NT))


def pair_rows(ref, pair):
    first = ref[head_slice(2 * pair), :]
    second = ref[head_slice(2 * pair + 1), :]
    nothing = jnp.zeros_like(first)
    return jnp.concatenate(
        [
            jnp.concatenate([first, nothing], axis=1),
            jnp.concatenate([nothing, second], axis=1),
        ],
        axis=0,
    )


def two_parts(v):
    high = v.astype(bf16)
    return high, (v - high.astype(f32)).astype(bf16)


def local_kernel(
    tab_ref,
    tok_t_ref,
    k_ref,
    v_t_ref,
    wq_ref,
    w_out_ref,
    w_in_ref,
    w_back_ref,
    q_t_ref,
    sig_q_ref,
    numer_ref,
    denom_ref,
    w_out_t,
    w_in_t,
    w_back_t,
    w_t,
):
    @pl.when(pl.program_id(0) == 0)
    def _():
        w_t[...] = wq_ref[...].T
        w_out_t[...] = w_out_ref[...].T

    w_in_t[...] = w_in_ref[...].T
    w_back_t[...] = w_back_ref[...].T

    soft, sig = softplus_sigmoid(mm(w_t[...], tok_t_ref[...]))
    q_t_ref[...] = soft.astype(bf16)
    sig_q_ref[...] = sig.astype(bf16)
    blend = blend_of(tab_ref[0])
    tok_count = blend.shape[0]
    denom_ref[...] = jnp.zeros_like(denom_ref)
    for pair in range(PAIRS):
        lanes = slice(pair * 2 * HEAD_DIM, (pair + 1) * 2 * HEAD_DIM)
        both = mm(k_ref[0, :, lanes], pair_rows(q_t_ref, pair))
        for side in range(2):
            h = 2 * pair + side
            high, low = two_parts(both[:, side * tok_count : (side + 1) * tok_count] * blend)
            values = with_row(v_t_ref[head_slice(h), :], 1.0)
            out = mm(values, high) + mm(values, low)
            numer_ref[head_slice(h), :] = out[:HEAD_DIM]
            denom_ref[h : h + 1, :] = out[HEAD_DIM : HEAD_DIM + 1]


def mean_rows(v):
    return jnp.sum(v, axis=0, keepdims=True) * (1.0 / v.shape[0])


def fold_lanes(v):
    total = v[:, :128]
    for at in range(128, v.shape[1], 128):
        total = total + v[:, at : at + 128]
    return total


def add_to(ref, value):
    first = pl.program_id(0) == 0

    @pl.when(first)
    def _():
        ref[...] = value

    @pl.when(jnp.logical_not(first))
    def _():
        ref[...] += value


def norm_back(grad_norm, normed, inv_scale):
    return inv_scale * (grad_norm - mean_rows(grad_norm) - normed * mean_rows(grad_norm * normed))


def forward_kernel(
    tab_ref,
    q_t_ref,
    numer_ref,
    denom_loc_ref,
    state_a,
    state_b,
    tok_t_ref,
    cot_ref,
    w_out_t,
    w_in_t,
    w_back_t,
    gain_one_ref,
    shift_one_ref,
    gain_two_ref,
    shift_two_ref,
    layer_ref,
    denom_ref,
    att_t_ref,
    att_low_ref,
    first_t_ref,
    normed_t_ref,
    scale_ref,
    active_t_ref,
    slope_t_ref,
    grad_mid_ref,
    grad_second_ref,
    grad_gain_ref,
    grad_shift_ref,
    second,
):
    table = tab_ref[0]
    cos, sin = table[COS_READ : COS_READ + 1], table[SIN_READ : SIN_READ + 1]
    states = (state_a, state_b)
    denom_ref[...] = denom_loc_ref[...]
    for h in range(HEADS):
        reads = trig_rows(q_t_ref[head_slice(h), :], cos, sin)
        more = mm(take_state(states, h), reads)
        numer = numer_ref[head_slice(h), :] + more[:HEAD_DIM]
        denom = denom_loc_ref[h : h + 1, :] + more[HEAD_DIM : HEAD_DIM + 1]
        denom_ref[h : h + 1, :] = denom
        high, low = two_parts(numer * (1.0 / denom))
        att_t_ref[head_slice(h), :] = high
        att_low_ref[head_slice(h), :] = low
    summed = tok_t_ref[...].astype(f32) + mm(w_out_t[...], att_t_ref[...])
    centered = summed - mean_rows(summed)
    inv_scale = lax.rsqrt(mean_rows(centered * centered) + norm_eps)
    scale_ref[...] = jnp.broadcast_to(inv_scale, scale_ref.shape)
    normed = centered * inv_scale
    normed_t_ref[...] = normed
    first_out = normed * gain_one_ref[...] + shift_one_ref[...]
    first_low = first_out.astype(bf16)
    first_t_ref[...] = first_low
    for at in range(0, w_in_t.shape[0], 768):
        hidden = mm(w_in_t[at : at + 768, :], first_low)
        half = 0.5 * (1.0 + lax.erf(hidden * 0.7071067811865476))
        bell = jnp.exp(hidden * hidden * -0.5) * 0.3989422804014327
        active = (hidden * half).astype(bf16)
        active_t_ref[at : at + 768, :] = active
        slope_t_ref[at : at + 768, :] = (half + hidden * bell).astype(bf16)
        part = mm(w_back_t[:, at : at + 768], active)
        if at == 0:
            second[...] = part
        else:
            second[...] += part
    summed = normed_t_ref[...] * gain_one_ref[...] + shift_one_ref[...] + second[...]
    centered = summed - mean_rows(summed)
    inv_scale = lax.rsqrt(mean_rows(centered * centered) + norm_eps)
    normed = centered * inv_scale
    layer_ref[0] = (normed * gain_two_ref[...] + shift_two_ref[...]).T.astype(bf16)
    grad_top = cot_ref[0].T.astype(f32)
    add_to(grad_gain_ref, fold_lanes(grad_top * normed))
    add_to(grad_shift_ref, fold_lanes(grad_top))
    grad_mid = norm_back(grad_top * gain_two_ref[...], normed, inv_scale)
    grad_mid_ref[...] = grad_mid
    grad_second_ref[...] = grad_mid.astype(bf16)


def backward_kernel(
    tab_ref,
    q_t_ref,
    denom_ref,
    att_t_ref,
    att_low_ref,
    normed_t_ref,
    scale_ref,
    slope_t_ref,
    grad_mid_ref,
    grad_second_ref,
    w_out_ref,
    w_in_ref,
    w_back_ref,
    gain_one_ref,
    grad_hidden_ref,
    grad_base_ref,
    grad_branch_ref,
    grad_numer_ref,
    grad_denom_ref,
    grad_gain_ref,
    grad_shift_ref,
    state_a,
    state_b,
    total,
):
    total[...] = grad_mid_ref[...]
    grad_second = grad_second_ref[...]
    for at in range(0, w_in_ref.shape[1], 768):
        grad_active = mm(w_back_ref[at : at + 768, :], grad_second)
        low = (grad_active * slope_t_ref[at : at + 768, :].astype(f32)).astype(bf16)
        grad_hidden_ref[at : at + 768, :] = low
        total[...] += mm(w_in_ref[:, at : at + 768], low)
    grad_first = total[...]
    normed = normed_t_ref[...]
    add_to(grad_gain_ref, fold_lanes(grad_first * normed))
    add_to(grad_shift_ref, fold_lanes(grad_first))
    grad_base = norm_back(grad_first * gain_one_ref[...], normed, scale_ref[0:1, :])
    grad_base_ref[...] = grad_base
    grad_branch = grad_base.astype(bf16)
    grad_branch_ref[...] = grad_branch
    total[...] = mm(w_out_ref[...], grad_branch)
    table = tab_ref[0]
    cos, sin = table[COS_READ : COS_READ + 1], table[SIN_READ : SIN_READ + 1]
    states = (state_a, state_b)
    clear_pad(states)
    grad_denom_ref[...] = jnp.zeros_like(grad_denom_ref)
    for h in range(HEADS):
        inverse = 1.0 / denom_ref[h : h + 1, :]
        grad_att = total[head_slice(h), :]
        grad_numer = (grad_att * inverse).astype(bf16)
        attended = att_t_ref[head_slice(h), :].astype(f32) + att_low_ref[head_slice(h), :].astype(f32)
        grad_denom = -jnp.sum(grad_numer.astype(f32) * attended, axis=0, keepdims=True)
        grad_denom_ref[h : h + 1, :] = grad_denom
        grad_numer_ref[head_slice(h), :] = grad_numer
        reads = trig_rows(q_t_ref[head_slice(h), :], cos, sin)
        put_state(states, h, mm(with_row(grad_numer, grad_denom), reads, NT))


def local_back_kernel(
    tab_ref,
    q_t_ref,
    k_t_ref,
    k_ref,
    v_ref,
    sig_q_ref,
    grad_numer_ref,
    grad_denom_ref,
    state_a,
    state_b,
    grad_q_ref,
    grad_k_ref,
    grad_v_ref,
):
    table = tab_ref[0]
    blend = blend_of(table)
    tok_count = blend.shape[0]
    cos, sin = table[COS_READ : COS_READ + 1], table[SIN_READ : SIN_READ + 1]
    states = (state_a, state_b)
    for pair in range(PAIRS):
        lanes = slice(pair * 2 * HEAD_DIM, (pair + 1) * 2 * HEAD_DIM)
        both = mm(k_ref[0, :, lanes], pair_rows(q_t_ref, pair))
        grads = mm(v_ref[0, :, lanes], pair_rows(grad_numer_ref, pair))
        for side in range(2):
            h = 2 * pair + side
            rows = head_slice(h)
            part = slice(side * tok_count, (side + 1) * tok_count)
            grad_denom = grad_denom_ref[h : h + 1, :]
            scores = (both[:, part] * blend).astype(bf16)
            grad_scores, rest = two_parts((grads[:, part] + grad_denom) * blend)
            grad_numer = grad_numer_ref[rows, :]
            grad_v_ref[rows, :] = mm(grad_numer, scores, NT)
            grad_k_ref[rows, :] = mm(q_t_ref[rows, :], grad_scores, NT)
            reads = mm(take_state(states, h), with_row(grad_numer, grad_denom), TN)
            grad_q = (
                mm(k_t_ref[rows, :], grad_scores)
                + mm(k_t_ref[rows, :], rest)
                + cos * reads[:HEAD_DIM]
                + sin * reads[HEAD_DIM:]
            )
            grad_q_ref[rows, :] = (grad_q * sig_q_ref[rows, :].astype(f32)).astype(bf16)


def tail_kernel(
    tab_ref,
    k_t_ref,
    v_t_ref,
    sig_k_ref,
    state_a,
    state_b,
    grad_k_in,
    grad_v_in,
    grad_kv_ref,
):
    table = tab_ref[0]
    cos, sin = table[COS_TAIL : COS_TAIL + 1], table[SIN_TAIL : SIN_TAIL + 1]
    states = (state_a, state_b)
    for h in range(HEADS):
        rows = head_slice(h)
        state = take_state(states, h)
        inner = mm(state, with_row(v_t_ref[rows, :], 1.0), TN)
        grad_k = grad_k_in[rows, :] + cos * inner[:HEAD_DIM] + sin * inner[HEAD_DIM:]
        grad_kv_ref[0, rows, :] = (grad_k * sig_k_ref[rows, :].astype(f32)).astype(bf16)
        keys = trig_rows(k_t_ref[rows, :], cos, sin)
        grad_kv_ref[1, rows, :] = (grad_v_in[rows, :] + mm(state[:HEAD_DIM], keys)).astype(bf16)


def token_kernel(gq_ref, gkv_ref, base_ref, wq_ref, wk_ref, wv_ref, out_ref):
    total = base_ref[...] + mm(wq_ref[...], gq_ref[...])
    total = total + mm(wk_ref[...], gkv_ref[0])
    total = total + mm(wv_ref[...], gkv_ref[1])
    out_ref[0] = total.T


def first_begins(lengths, count, tok_count):
    slots = lengths.shape[1]
    order = jnp.arange(slots)
    before = (order[:, None] > order[None, :]).astype(jnp.int32)
    starts = jnp.sum(lengths[:, None, :] * before[None], axis=-1)
    firsts = jnp.arange(count, dtype=jnp.int32) * tok_count
    reached = starts[:, None, :] <= firsts[None, :, None]
    return jnp.max(jnp.where(reached, starts[:, None, :], 0), axis=-1)


def pick(index, values):
    out = values[0]
    for i in range(1, len(values)):
        out = jnp.where(index == i, values[i], out)
    return out[:, None, None]


class Order:
    def __init__(self):
        self.last = None

    def tie(self, value):
        if self.last is None:
            return value
        return lax.optimization_barrier((value, self.last))[0]

    def done(self, value):
        self.last = value
        return value


def entering(order, parts, begin_first, tok_count, reverse):
    count = lax.axis_size("seq")
    place = lax.axis_index("seq")
    part_a, part_b = parts

    def covers(i, j):
        low, high = (count - 1 - j, count - 1 - i) if reverse else (i, j)
        return (begin_first[:, high] < (low + 1) * tok_count).astype(f32)

    if count != 4:
        spots = jnp.arange(count)
        mine = begin_first.T if reverse else begin_first[:, place][None]
        reach = (place if reverse else spots[:, None]) + 1
        ahead = (spots > place) if reverse else (spots < place)
        weight = ((mine < reach * tok_count) & ahead[:, None]).astype(f32)
        gathered = [lax.all_gather(p, "seq") for p in parts]
        yield
        yield
        yield tuple(jnp.sum(g * weight[:, :, None, None], axis=0) for g in gathered)
    index = count - 1 - place if reverse else place

    zero = jnp.zeros_like(begin_first[:, 0], f32)
    one = zero + 1.0
    m02, m03, m13 = covers(0, 2), covers(0, 3), covers(1, 3)
    own_a, first_a = pick(index, [m02, m13, zero, zero]), pick(index, [one, m03, zero, zero])
    own_b, first_b = pick(index, [one, zero, one, zero]), pick(index, [zero, zero, m03, one])
    end_a, then_a = pick(index, [zero, one, zero, one]), pick(index, [zero, zero, one, one])
    end_b, then_b = pick(index, [zero, zero, m02, m13]), pick(index, [zero, one, one, one])
    got_a = swap(part_a, "seq", 1)
    got_b = swap(part_b, "seq", 2)
    yield
    got_a, got_b = order.tie((got_a, got_b))
    next_a = own_a * part_a + first_a * got_a
    next_b = own_b * part_b + first_b * got_b
    order.done((next_a, next_b))
    last_a = swap(next_a, "seq", 2)
    last_b = swap(next_b, "seq", 1)
    yield
    last_a, last_b = order.tie((last_a, last_b))
    full = (end_a * got_a + then_a * last_a, end_b * got_b + then_b * last_b)
    yield order.done(full)


def take(value, index, dim):
    return lax.dynamic_index_in_dim(value, index, dim, False)


def swap(value, axis, distance):
    count = lax.axis_size(axis)
    return lax.ppermute(value, axis, [(i, i ^ distance) for i in range(count)])


def reduced(order, away, keep):
    shards, rows, columns = keep.shape
    place = lax.axis_index("seq")
    batch_place = lax.axis_index("batch")
    count = lax.axis_size("batch")
    bits = shards.bit_length() - 1
    got = swap(away, "batch", 1)
    yield
    summed = keep + order.tie(got)
    shape = (2,) * bits + (rows // 2, columns)
    parts = [summed[:, : rows // 2].reshape(shape), summed[:, rows // 2 :].reshape(shape)]
    left = [list(range(bits - 1, -1, -1)) for _ in parts]
    orders = [list(range(bits)), list(range(bits - 1, -1, -1))]
    for step in range(bits):
        aways, keeps = [], []
        for side, part in enumerate(parts):
            bit = orders[side][step]
            dim = left[side].index(bit)
            left[side].pop(dim)
            mine = (place >> bit) & 1
            aways.append(take(part, 1 - mine, dim))
            keeps.append(take(part, mine, dim))
        aways, keeps = order.done((aways, keeps))
        gots = [swap(a, "seq", 1 << orders[side][step]) for side, a in enumerate(aways)]
        yield
        parts = [k + g for k, g in zip(keeps, order.tie(gots))]
    odd = (batch_place >> 1) & 1 == 1
    away = jnp.where(odd, parts[0], parts[1])
    part = jnp.where(odd, parts[1], parts[0])
    away, part = order.done((away, part))
    got = swap(away, "batch", 2)
    yield
    part = order.done(part + order.tie(got))
    distance = 4
    while distance < count:
        got = swap(part, "batch", distance)
        yield
        part = order.done(part + order.tie(got))
        distance *= 2
    got = swap(part, "batch", 2)
    yield
    got = order.tie(got)
    mine = order.done(
        jnp.concatenate([jnp.where(odd, got, part), jnp.where(odd, part, got)], axis=0)
    )
    other = swap(mine, "batch", 1)
    yield
    other = order.tie(other)
    first = batch_place & 1 == 0
    yield order.done((jnp.where(first, mine, other), jnp.where(first, other, mine)))


def call(kernel, grid, ins, outs, scratch, flops, moved, *args):
    return pl.pallas_call(
        kernel,
        grid=grid,
        in_specs=[s for s in ins],
        out_specs=[s for s, _ in outs],
        out_shape=[jax.ShapeDtypeStruct(shape, kind) for _, (shape, kind) in outs],
        scratch_shapes=scratch,
        compiler_params=pltpu.CompilerParams(
            dimension_semantics=("arbitrary",) * len(grid), vmem_limit_bytes=VMEM_LIMIT
        ),
        cost_estimate=pl.CostEstimate(flops=flops, bytes_accessed=moved, transcendentals=0),
    )(*args)


def body(
    tokens,
    cotangent,
    doc_lengths,
    w_query,
    w_key,
    w_value,
    w_out,
    w_in,
    w_back,
    gain_one,
    shift_one,
    gain_two,
    shift_two,
):
    rows, toks, width = tokens.shape
    ff = w_in.shape[1]
    flat = rows * toks
    shards = lax.axis_size("seq")
    place = (lax.axis_index("seq") * toks).astype(jnp.int32)
    begin_first = first_begins(doc_lengths, shards, toks)
    smem = pl.BlockSpec(memory_space=pltpu.SMEM)
    whole = pl.BlockSpec(memory_space=pltpu.VMEM)
    token_major = pl.BlockSpec((1, toks, width), lambda r: (r, 0, 0))
    table_spec = pl.BlockSpec((1, 8, toks), lambda r: (r, 0, 0))
    state_spec = pl.BlockSpec((1, STATE_ROWS, 2 * HEAD_DIM), lambda r: (r, 0, 0))
    fold_spec = pl.BlockSpec((width, 128), lambda r: (0, 0))

    def feature(count):
        return pl.BlockSpec((count, toks), lambda r: (0, r))

    tok_low = (token_major, ((rows, toks, width), bf16))
    wide_low = (feature(width), ((width, flat), bf16))
    wide_full = (feature(width), ((width, flat), f32))
    ff_low = (feature(ff), ((ff, flat), bf16))
    head_rows = (feature(16), ((16, flat), f32))
    one_row = (feature(8), ((8, flat), f32))
    fold = (fold_spec, ((width, 128), f32))
    state = (state_spec, ((rows, STATE_ROWS, 2 * HEAD_DIM), f32))
    cell = 2 * flat * toks * 256
    grid = (rows,)

    order = Order()
    core = (lax.axis_index("batch") % 2).astype(jnp.int32)

    def run(kernel, ins, outs, scratch, flops, first, *args):
        return order.done(call(kernel, grid, ins, outs, scratch, flops // 4, 1_000_000, order.tie(first), *args))

    def halves(b):
        split = b.reshape(b.shape[0], 2, b.shape[1] // 2, flat)
        return [take(split, c, 1).reshape(-1, flat) for c in (1 - core, core)]

    def product(a, b):
        grad = lax.dot_general(order.tie(a), b, NT, preferred_element_type=f32)
        return order.done(grad.reshape(shards, a.shape[0] // shards, b.shape[0]))

    def reduction(a, b):
        away, keep = halves(b)
        away = product(a, away)
        return reduced(order, away, product(a, keep))

    def column(v):
        return v[:, None]

    table, tok_t, k_t, v_t, key, value, sig_k, state_a, state_b = run(
        project_kernel,
        [smem, smem, token_major, whole, whole],
        [(table_spec, ((rows, 8, toks), f32))]
        + [wide_low] * 3
        + [tok_low] * 2
        + [wide_low]
        + [state] * 2,
        [pltpu.VMEM((2, width, width), bf16)],
        4 * flat * width * width,
        place[None],
        doc_lengths,
        tokens,
        w_key,
        w_value,
    )
    states = entering(order, (state_a, state_b), begin_first, toks, False)
    next(states)
    part = ff // rows
    q_t, sig_q, numer, denom_loc, w_out_t, w_in_t, w_back_t = run(
        local_kernel,
        [
            table_spec,
            feature(width),
            token_major,
            feature(width),
            whole,
            whole,
            pl.BlockSpec((width, part), lambda r: (0, r)),
            pl.BlockSpec((part, width), lambda r: (r, 0)),
        ],
        [
            wide_low,
            wide_low,
            wide_full,
            head_rows,
            (pl.BlockSpec((width, width), lambda r: (0, 0)), ((width, width), bf16)),
            (pl.BlockSpec((part, width), lambda r: (r, 0)), ((ff, width), bf16)),
            (pl.BlockSpec((width, part), lambda r: (0, r)), ((width, ff), bf16)),
        ],
        [pltpu.VMEM((width, width), bf16)],
        2 * cell * HEADS,
        table,
        tok_t,
        key,
        v_t,
        w_query,
        w_out,
        w_in,
        w_back,
    )
    next(states)
    in_a, in_b = next(states)
    (
        layer_out,
        denom,
        att_t,
        att_low,
        first_t,
        normed_t,
        scale_one,
        active_t,
        slope_t,
        grad_mid,
        grad_second,
        fold_gain_two,
        fold_shift_two,
    ) = run(
        forward_kernel,
        [
            table_spec,
            feature(width),
            feature(width),
            feature(16),
            state_spec,
            state_spec,
            feature(width),
            token_major,
        ]
        + [whole] * 7,
        [
            tok_low,
            head_rows,
            wide_low,
            wide_low,
            wide_low,
            wide_full,
            one_row,
            ff_low,
            ff_low,
            wide_full,
            wide_low,
            fold,
            fold,
        ],
        [pltpu.VMEM((width, toks), f32)],
        2 * flat * width * (width + 2 * ff),
        table,
        q_t,
        numer,
        denom_loc,
        in_a,
        in_b,
        tok_t,
        cotangent,
        w_out_t,
        w_in_t,
        w_back_t,
        column(gain_one),
        column(shift_one),
        column(gain_two),
        column(shift_two),
    )

    back = reduction(active_t, grad_second[None])
    next(back)
    next(back)
    (
        grad_hidden,
        grad_base,
        grad_branch,
        grad_numer,
        grad_denom,
        fold_gain_one,
        fold_shift_one,
        out_a,
        out_b,
    ) = run(
        backward_kernel,
        [
            table_spec,
            feature(width),
            feature(16),
            feature(width),
            feature(width),
            feature(width),
            feature(8),
            feature(ff),
            feature(width),
            feature(width),
        ]
        + [whole] * 4,
        [ff_low, wide_full, wide_low, wide_low, head_rows, fold, fold, state, state],
        [pltpu.VMEM((width, toks), f32)],
        2 * flat * width * (width + 2 * ff),
        table,
        q_t,
        denom,
        att_t,
        att_low,
        normed_t,
        scale_one,
        slope_t,
        grad_mid,
        grad_second,
        w_out,
        w_in,
        w_back,
        column(gain_one),
    )
    back_states = entering(order, (out_a, out_b), begin_first, toks, True)
    next(back_states)
    into = reduction(first_t, grad_hidden[None])
    next(into)
    next(back)
    next(back_states)
    grad_qpre, grad_k_loc, grad_v_loc = run(
        local_back_kernel,
        [
            table_spec,
            feature(width),
            feature(width),
            token_major,
            token_major,
            feature(width),
            feature(width),
            feature(16),
            state_spec,
            state_spec,
        ],
        [wide_low, wide_full, wide_full],
        [],
        5 * cell * HEADS,
        table,
        q_t,
        k_t,
        key,
        value,
        sig_q,
        grad_numer,
        grad_denom,
        in_a,
        in_b,
    )
    share = width // shards
    small = jnp.stack(
        [
            jnp.sum(v, axis=1)
            for v in order.tie((fold_gain_one, fold_shift_one, fold_gain_two, fold_shift_two))
        ]
    )
    small = small.reshape(4, shards, share).transpose(1, 0, 2).reshape(shards, 1, 4 * share)
    small = order.done(jnp.pad(small, ((0, 0), (0, 15), (0, width - 4 * share))))

    def mixed_part(half, out_rows, query_rows):
        columns = jnp.concatenate(
            [
                lax.dot_general(a, b, NT, preferred_element_type=f32)
                for a, b in ((order.tie(att_t), out_rows), (tok_t, query_rows))
            ],
            axis=1,
        )
        cut = width // 2
        extra = lax.dynamic_slice_in_dim(small, half * cut, cut, 2)
        extra = jnp.pad(extra, ((0, 0), (0, 0), (0, cut)))
        return order.done(
            jnp.concatenate([columns.reshape(shards, share, width), extra], axis=1)
        )

    out_halves, query_halves = halves(grad_branch[None]), halves(grad_qpre[None])
    away = mixed_part(1 - core, out_halves[0], query_halves[0])
    mixed = reduced(order, away, mixed_part(core, out_halves[1], query_halves[1]))
    next(mixed)
    next(back)
    next(into)
    back_a, back_b = next(back_states)
    (grad_kv,) = run(
        tail_kernel,
        [table_spec]
        + [feature(width)] * 3
        + [state_spec] * 2
        + [feature(width)] * 2,
        [(pl.BlockSpec((2, width, toks), lambda r: (0, 0, r)), ((2, width, flat), bf16))],
        [],
        2 * cell * HEADS,
        table,
        k_t,
        v_t,
        sig_k,
        back_a,
        back_b,
        grad_k_loc,
        grad_v_loc,
    )
    last = reduction(tok_t, grad_kv)
    next(last)
    next(back)
    next(mixed)
    next(into)
    next(last)
    (grad_tokens,) = run(
        token_kernel,
        [
            feature(width),
            pl.BlockSpec((2, width, toks), lambda r: (0, 0, r)),
            feature(width),
        ]
        + [whole] * 3,
        [(token_major, ((rows, toks, width), f32))],
        [],
        6 * flat * width * width,
        grad_qpre,
        grad_kv,
        grad_base,
        w_query,
        w_key,
        w_value,
    )
    pending = [mixed, into, back, last]
    ends = {}
    while pending:
        for steps in list(pending):
            value = next(steps)
            if value is not None:
                ends[id(steps)] = value
                pending.remove(steps)

    def joined(steps, groups):
        low, high = ends[id(steps)]
        size = low.shape[1] // groups
        return [
            jnp.concatenate([v[:, g * size : (g + 1) * size] for v in (low, high)], axis=1)
            for g in range(groups)
        ]

    (total_back,), (total_in,) = joined(back, 1), joined(into, 1)
    total_out, total_query = joined(mixed, 2)
    total_key, total_value = joined(last, 2)
    vectors = total_out[share, : 4 * share].reshape(4, share)
    return (
        layer_out,
        grad_tokens,
        total_query[:share],
        total_key,
        total_value,
        total_out[:share],
        total_in,
        total_back,
        vectors[0],
        vectors[1],
        vectors[2],
        vectors[3],
    )


def solution(mesh):
    in_specs = (
        P("batch", "seq", None),
        P("batch", "seq", None),
        P("batch", None),
        P(),
        P(),
        P(),
        P(),
        P(),
        P(),
        P(),
        P(),
        P(),
        P(),
    )
    out_specs = (
        P("batch", "seq", None),
        P("batch", "seq", None),
        P("seq", None),
        P("seq", None),
        P("seq", None),
        P("seq", None),
        P("seq", None),
        P("seq", None),
        P("seq"),
        P("seq"),
        P("seq"),
        P("seq"),
    )
    return jax.shard_map(body, mesh=mesh, in_specs=in_specs, out_specs=out_specs, check_vma=False)
```

time: 895 us -> 471 us (0.53)
  waiting for transfers between devices: 410 us -> 158 us
  matrix products: 258 us -> 39.6 us
  Pallas kernels: 0 us -> 117 us
  local copies, waits for them, and re-layouts: 110 us -> 30.8 us
  starting transfers between devices: 1.01 us -> 57.9 us
  blocking collectives: 56.2 us -> 0 us
  other arithmetic: 33.2 us -> 57.7 us
  between operations: 16.6 us -> 1.73 us
    reduce_scatter x3 -> x0, waiting for transfers between devices: 235 us -> none  [the longest x1 98.2 us: body(): lax.psum_scatter(grad_back, 'seq', scatter_dimension=0, tiled=True)]
    dot_general x33 -> x10, matrix products: 258 us -> 39.6 us  [the longest x6 32.5 us: product(): grad = lax.dot_general(order.tie(a), b, NT, preferred_element_type=f32)]
    ppermute x0 -> x44, waiting for transfers between devices: none -> 158 us  [swap(): return lax.ppermute(value, axis, [(i, i ^ distance) for i in range(count)])]
    psum x1 -> x0, waiting for transfers between devices: 129 us -> none  [body(): lax.psum((shards[0], shards[1], shards[2], shards[3], shards[4], shards[5...]
    pallas_call x0 -> x7, Pallas kernels: none -> 117 us  [call(): pl.pallas_call(kernel, grid=grid, in_specs=[s for s in ins], out_specs=[s...]
    ppermute x0 -> x44, starting transfers between devices: none -> 57.9 us  [swap(): return lax.ppermute(value, axis, [(i, i ^ distance) for i in range(count)])]
    unnamed x160 -> x54, local copies, waits for them, and re-layouts: 43.7 us -> 2.27 us
    all_gather x2 -> x0, waiting for transfers between devices: 32.1 us -> none  [entering(): gathered = jax.tree.map(lambda a: lax.all_gather(a, axis), part)]
  transfers between devices with their start and end apart: 9 -> 44, of which waited for: 7 -> 20; matrix products, arithmetic and copies ran while one was open for 23% -> 21% of each run, Pallas kernels for 0% -> 11%
where the time goes in v2:
time: 471 us; the launch traced here: 462 us
  waiting for transfers between devices  158 us (34%)
  Pallas kernels  117 us (25%)
  starting transfers between devices  57.9 us (12%)
  other arithmetic  57.7 us (12%)
  matrix products  39.6 us (8%)
  local copies, waits for them, and re-layouts  30.8 us (7%)
    ppermute x44, waiting for transfers between devices, swap(): return lax.ppermute(value, axis, [(i, i ^ distance) for i in range(count)])  158 us
    pallas_call x7, Pallas kernels, call(): pl.pallas_call(kernel, grid=grid, in_specs=[s for s in ins], out_specs=[s...  117 us
    ppermute x44, starting transfers between devices, swap(): return lax.ppermute(value, axis, [(i, i ^ distance) for i in range(count)])  57.9 us
    dot_general x6, matrix products, product(): grad = lax.dot_general(order.tie(a), b, NT, preferred_element_type=f32)  32.5 us
    add x4, other arithmetic, reduced(): summed = keep + order.tie(got)  11.8 us
  transfers between devices with their start and end apart: 44, of which 20 were waited for; matrix products, arithmetic and copies ran while one was open for 21% of the time, Pallas kernels for 11%

profile of v2, /device:TPU:1, one launch (start us, length us, event | category | flops | bytes accessed | tf_op | source)
XLA Modules:
  0.0 462.2 jit_solution(17727706785959737835)
XLA Ops:
  0.6 9.9 %shard_map.220 = (f32[4,8,256]{2,1,0:T(8,128)}, bf16[768,1024]{1,0:T(8,128)(2,1)}, bf16[768,1024]{1,0:T(8,128)(2,1)}, bf16[768,1024]{1,0:T(8,128)(2,1)}, bf16[4,...) custom-call(s32[1]{0:T(128)} %bitcast.place_ref, ...), custom_call_target="tpu_custom_call" | custom-call | flops 603979776 | bytes 1000000 | tf_op jit(solution)/shard_map/pallas_call | solution.py:603
  13.9 17.6 %shard_map.221 = (bf16[768,1024]{1,0:T(8,128)(2,1)}, bf16[768,1024]{1,0:T(8,128)(2,1)}, f32[768,1024]{1,0:T(8,128)}, f32[16,1024]{1,0:T(8,128)}, bf16[768,768]{1...) custom-call(f32[4,8,256]{2,1,0:T(8,128)} %get-tuple-element.184.tab_ref, ...), custom_call_target="tpu_custom_call" | custom-call | flops 805306368 | bytes 1000000 | tf_op jit(solution)/shard_map/pallas_call | solution.py:603
  38.3 14.1 %collective-permute-done.3 = f32[4,392,128]{2,1,0:T(8,128)} collective-permute-done((f32[4,392,128]{2,1,0:T(8,128)}, f32[4,392,128]{2,1,0:T(8,128)}, u32[]{:S(2)}, u32[]{:S(2)}) %collective-permute-start.3) | collective-permute-done | bytes 802848 | tf_op jit(solution)/shard_map/ppermute | solution.py:547
  55.0 30.4 %shard_map.222 = (bf16[4,256,768]{2,1,0:T(8,128)(2,1)}, f32[16,1024]{1,0:T(8,128)}, bf16[768,1024]{1,0:T(8,128)(2,1)}, bf16[768,1024]{1,0:T(8,128)(2,1)}, bf16[7...) custom-call(f32[4,8,256]{2,1,0:T(8,128)} %get-tuple-element.184.tab_, ...), custom_call_target="tpu_custom_call" | custom-call | flops 2717908992 | bytes 1000000 | tf_op jit(solution)/shard_map/pallas_call | solution.py:603
  85.3 8.7 %fusion.8 = f32[4,768,384]{2,1,0:T(8,128)} fusion(bf16[4,768,1024]{2,1,0:T(8,128)(2,1)} %bitcast.167, bf16[1,2,384,1024]{3,2,1,0:T(8,128)(2,1)} %bitcast.157, s32[]{:T(128)S(6)} %select_n.572), kind=kOutput, calls=%fused_computation.33 | convolution fusion | flops 2415919104 | bytes 11796484 | tf_op jit(solution)/shard_map/dot_general | solution.py:670
  96.3 5.6 %fusion.6 = f32[4,768,384]{2,1,0:T(8,128)S(1)} fusion(bf16[4,768,1024]{2,1,0:T(8,128)(2,1)} %bitcast.168, bf16[1,2,384,1024]{3,2,1,0:T(8,128)(2,1)S(1)} %bitcast.158, s32[]{:T(128)S(6)} %select_n.573), kind=kOutput, calls=%fused_computation.31 | convolution fusion | flops 2415919104 | bytes 11796484 | tf_op jit(solution)/shard_map/dot_general | solution.py:670
  108.0 27.4 %shard_map.223 = (bf16[3072,1024]{1,0:T(8,128)(2,1)}, f32[768,1024]{1,0:T(8,128)}, bf16[768,1024]{1,0:T(8,128)(2,1)}, bf16[768,1024]{1,0:T(8,128)(2,1)}, f32[16,...) custom-call(f32[4,8,256]{2,1,0:T(8,128)} %get-tuple-element.184.tab_, ...), custom_call_target="tpu_custom_call" | custom-call | flops 2717908992 | bytes 1000000 | tf_op jit(solution)/shard_map/pallas_call | solution.py:603
  135.4 7.3 %fusion.2 = f32[4,192,1536]{2,1,0:T(8,128)} fusion(bf16[4,192,1024]{2,1,0:T(8,128)(2,1)} %bitcast.173, bf16[1,2,1536,1024]{3,2,1,0:T(8,128)(2,1)} %bitcast.169, s32[]{:T(128)S(6)} %select_n.572), kind=kOutput, calls=%fused_computation.2 | convolution fusion | flops 2415919104 | bytes 9437188 | tf_op jit(solution)/shard_map/dot_general | solution.py:670
  149.1 21.4 %collective-permute-done.8 = f32[2,384,384]{2,1,0:T(8,128)S(1)} collective-permute-done((f32[2,384,384]{2,1,0:T(8,128)S(1)}, f32[2,384,384]{2,1,0:T(8,128)S(1)}, u32[]{:S(2)}, u32[]{:S(2)}) %collective-permute-start.8) | collective-permute-done | bytes 1179680 | tf_op jit(solution)/shard_map/ppermute | solution.py:547
  178.9 6.7 %collective-permute-done.13 = f32[384,384]{1,0:T(8,128)} collective-permute-done((f32[384,384]{1,0:T(8,128)}, f32[384,384]{1,0:T(8,128)}, u32[]{:S(2)}, u32[]{:S(2)}) %collective-permute-start.13) | collective-permute-done | bytes 589856 | tf_op jit(solution)/shard_map/ppermute | solution.py:547
  189.8 13.0 %collective-permute-done.5 = f32[4,392,128]{2,1,0:T(8,128)} collective-permute-done((f32[4,392,128]{2,1,0:T(8,128)}, f32[4,392,128]{2,1,0:T(8,128)}, u32[]{:S(2)}, u32[]{:S(2)}) %collective-permute-start.5) | collective-permute-done | bytes 802848 | tf_op jit(solution)/shard_map/ppermute | solution.py:547
  210.7 14.1 %shard_map.224 = (bf16[768,1024]{1,0:T(8,128)(2,1)}, f32[768,1024]{1,0:T(8,128)}, f32[768,1024]{1,0:T(8,128)}) custom-call(f32[4,8,256]{2,1,0:T(8,128)} %get-tuple-element.184.tab_ref, bf16[768,1024]{1,0:T(8,128)(2,1)} %get-tuple-element.125.q_t_ref, bf16[768,1024]{1,0:T(8,128)(2,1)} %get-tuple-element.119.k_t_ref, ...), custom_call_target="tpu_custom_call" | custom-call | flops 2013265920 | bytes 1000000 | tf_op jit(solution)/shard_map/pallas_call | solution.py:603
  249.8 4.8 %add.216 = f32[4,192,1536]{2,1,0:T(8,128)S(1)} add(f32[4,192,1536]{2,1,0:T(8,128)} %fusion, f32[4,192,1536]{2,1,0:T(8,128)} %collective-permute-done.11) | non-fusion elementwise | flops 1179648 | bytes 14155776 | tf_op jit(solution)/shard_map/add | solution.py:558
  261.5 7.7 %shard_map.225.gkv_ref = bf16[2,768,1024]{2,1,0:T(8,128)(2,1)} custom-call(f32[4,8,256]{2,1,0:T(8,128)} %get-tuple-element.184.tab_ref, bf16[768,1024]{1,0:T(8,128)(2,1)} %get-tuple-element.119.k_t_ref, bf16[768,1024]{1,0:T(8,128)(2,1)} %get-tuple-element.120.v_t_ref, bf16[768,1024]{1,0:T(8,128)(2,1)} %get-tuple-element.123.sig_k_ref, ...), custom_call_target="tpu_custom_call" | custom-call | flops 805306368 | bytes 1000000 | tf_op jit(solution)/shard_map/pallas_call | solution.py:603
  297.5 10.9 %collective-permute-done.16 = f32[2,96,1536]{2,1,0:T(8,128)S(1)} collective-permute-done((f32[2,96,1536]{2,1,0:T(8,128)}, f32[2,96,1536]{2,1,0:T(8,128)S(1)}, u32[]{:S(2)}, u32[]{:S(2)}) %collective-permute-start.16) | collective-permute-done | bytes 1179680 | tf_op jit(solution)/shard_map/ppermute | solution.py:547
  318.1 9.5 %shard_map.226 = f32[4,256,768]{2,1,0:T(8,128)} custom-call(bf16[768,1024]{1,0:T(8,128)(2,1)} %get-tuple-element.192.gq_ref, bf16[2,768,1024]{2,1,0:T(8,128)(2,1)} %shard_map.225.gkv_ref, f32[768,1024]{1,0:T(8,128)} %get-tuple-element.157.base_ref, bf16[768,768]{1,0:T(8,128)(2,1)} %wq_ref.3, bf16[768,768]{1,0:T(8,128)(2,1)} %wk_ref.3, bf16[768,768]{1,0:T(8,128)(2,1)} %wv_ref.3), custom_call_target="tpu_custom_call" | custom-call | flops 905969664 | bytes 1000000 | tf_op jit(solution)/shard_map/pallas_call | solution.py:603
  341.9 5.5 %collective-permute-done.24 = f32[2,96,768]{2,1,0:T(8,128)S(1)} collective-permute-done((f32[2,96,768]{2,1,0:T(8,128)}, f32[2,96,768]{2,1,0:T(8,128)S(1)}, u32[]{:S(2)}, u32[]{:S(2)}) %collective-permute-start.24) | collective-permute-done | bytes 589856 | tf_op jit(solution)/shard_map/ppermute | solution.py:547
  354.5 8.7 %collective-permute-done.31 = f32[384,384]{1,0:T(8,128)S(1)} collective-permute-done((f32[384,384]{1,0:T(8,128)S(1)}, f32[384,384]{1,0:T(8,128)S(1)}, u32[]{:S(2)}, u32[]{:S(2)}) %collective-permute-start.31) | collective-permute-done | bytes 589856 | tf_op jit(solution)/shard_map/ppermute | solution.py:547
  374.2 5.5 %collective-permute-done.30 = f32[96,768]{1,0:T(8,128)S(1)} collective-permute-done((f32[96,768]{1,0:T(8,128)S(1)}, f32[96,768]{1,0:T(8,128)S(1)}, u32[]{:S(2)}, u32[]{:S(2)}) %collective-permute-start.30) | collective-permute-done | bytes 294944 | tf_op jit(solution)/shard_map/ppermute | solution.py:547
  380.6 10.4 %collective-permute-done.28 = f32[104,768]{1,0:T(8,128)S(1)} collective-permute-done((f32[104,768]{1,0:T(8,128)S(1)}, f32[104,768]{1,0:T(8,128)S(1)}, u32[]{:S(2)}, u32[]{:S(2)}) %collective-permute-start.28) | collective-permute-done | bytes 319520 | tf_op jit(solution)/shard_map/ppermute | solution.py:547
  391.0 6.5 %collective-permute-done.36 = f32[96,1536]{1,0:T(8,128)S(1)} collective-permute-done((f32[96,1536]{1,0:T(8,128)S(1)}, f32[96,1536]{1,0:T(8,128)S(1)}, u32[]{:S(2)}, u32[]{:S(2)}) %collective-permute-start.36) | collective-permute-done | bytes 589856 | tf_op jit(solution)/shard_map/ppermute | solution.py:547
  401.8 23.3 %collective-permute-done.34 = f32[96,768]{1,0:T(8,128)S(1)} collective-permute-done((f32[96,768]{1,0:T(8,128)}, f32[96,768]{1,0:T(8,128)S(1)}, u32[]{:S(2)}, u32[]{:S(2)}) %collective-permute-start.34) | collective-permute-done | bytes 294944 | tf_op jit(solution)/shard_map/ppermute | solution.py:547
  434.4 8.6 %collective-permute-done.38 = f32[96,768]{1,0:T(8,128)S(1)} collective-permute-done((f32[96,768]{1,0:T(8,128)S(1)}, f32[96,768]{1,0:T(8,128)S(1)}, u32[]{:S(2)}, u32[]{:S(2)}) %collective-permute-start.38) | collective-permute-done | bytes 294944 | tf_op jit(solution)/shard_map/ppermute | solution.py:547
  448.4 5.0 %collective-permute-done.41 = f32[96,768]{1,0:T(8,128)S(1)} collective-permute-done((f32[96,768]{1,0:T(8,128)S(1)}, f32[96,768]{1,0:T(8,128)S(1)}, u32[]{:S(2)}, u32[]{:S(2)}) %collective-permute-start.41) | collective-permute-done | bytes 294944 | tf_op jit(solution)/shard_map/ppermute | solution.py:547
  (240 shorter events, 177.8 us)
Async XLA Ops:
  10.6 22.3 %collective-permute-start = (f32[4,392,128]{2,1,0:T(8,128)}, f32[4,392,128]{2,1,0:T(8,128)S(1)}, u32[]{:S(2)}, u32[]{:S(2)}) collective-permute-start(f32[4,392,128]{2,1,0:T(8,128)} %get-tuple-element.116), channel_id=1, source_target_pairs={{0,8},{8,0},{16,24},{24,16},{1,9},{9,1},{17,25},{25,17},{2,10},{10... | collective-permute-start | bytes 2408456 | tf_op jit(solution)/shard_map/ppermute | solution.py:547
  12.7 20.2 %collective-permute-start.1 = (f32[4,392,128]{2,1,0:T(8,128)}, f32[4,392,128]{2,1,0:T(8,128)S(1)}, u32[]{:S(2)}, u32[]{:S(2)}) collective-permute-start(f32[4,392,128]{2,1,0:T(8,128)} %get-tuple-element.117), channel_id=1, source_target_pairs={{0,16},{8,24},{16,0},{24,8},{1,17},{9,25},{17,1},{25,9},{2,18},{10... | collective-permute-start | bytes 2408456 | tf_op jit(solution)/shard_map/ppermute | solution.py:547
  142.7 107.1 %collective-permute-start.11 = (f32[4,192,1536]{2,1,0:T(8,128)}, f32[4,192,1536]{2,1,0:T(8,128)}, u32[]{:S(2)}, u32[]{:S(2)}) collective-permute-start(f32[4,192,1536]{2,1,0:T(8,128)} %fusion.2), channel_id=1, source_target_pairs={{0,1},{1,0},{2,3},{3,2},{4,5},{5,4},{6,7},{7,6},{8,9},{9,8},{10,11... | collective-permute-start | bytes 14155784 | tf_op jit(solution)/shard_map/ppermute | solution.py:547
  143.1 27.4 %collective-permute-start.8 = (f32[2,384,384]{2,1,0:T(8,128)S(1)}, f32[2,384,384]{2,1,0:T(8,128)S(1)}, u32[]{:S(2)}, u32[]{:S(2)}) collective-permute-start(f32[2,384,384]{2,1,0:T(8,128)S(1)} %get-tuple-element.248), channel_id=1, source_target_pairs={{0,16},{8,24},{16,0},{24,8},{1,17},{9,25},{17,1},{25,9},{2,18},{10... | collective-permute-start | bytes 3538952 | tf_op jit(solution)/shard_map/ppermute | solution.py:547
  143.1 27.4 %collective-permute-start.7 = (f32[2,384,384]{2,1,0:T(8,128)S(1)}, f32[2,384,384]{2,1,0:T(8,128)S(1)}, u32[]{:S(2)}, u32[]{:S(2)}) collective-permute-start(f32[2,384,384]{2,1,0:T(8,128)S(1)} %get-tuple-element.250), channel_id=1, source_target_pairs={{0,8},{8,0},{16,24},{24,16},{1,9},{9,1},{17,25},{25,17},{2,10},{10... | collective-permute-start | bytes 3538952 | tf_op jit(solution)/shard_map/ppermute | solution.py:547
  174.8 28.0 %collective-permute-start.5 = (f32[4,392,128]{2,1,0:T(8,128)}, f32[4,392,128]{2,1,0:T(8,128)}, u32[]{:S(2)}, u32[]{:S(2)}) collective-permute-start(f32[4,392,128]{2,1,0:T(8,128)} %get-tuple-element.154), channel_id=1, source_target_pairs={{0,8},{8,0},{16,24},{24,16},{1,9},{9,1},{17,25},{25,17},{2,10},{10... | collective-permute-start | bytes 2408456 | tf_op jit(solution)/shard_map/ppermute | solution.py:547
  175.1 29.4 %collective-permute-start.6 = (f32[4,392,128]{2,1,0:T(8,128)}, f32[4,392,128]{2,1,0:T(8,128)S(1)}, u32[]{:S(2)}, u32[]{:S(2)}) collective-permute-start(f32[4,392,128]{2,1,0:T(8,128)} %get-tuple-element.155), channel_id=1, source_target_pairs={{0,16},{8,24},{16,0},{24,8},{1,17},{9,25},{17,1},{25,9},{2,18},{10... | collective-permute-start | bytes 2408456 | tf_op jit(solution)/shard_map/ppermute | solution.py:547
  206.9 51.1 %collective-permute-start.10 = (f32[4,392,128]{2,1,0:T(8,128)}, f32[4,392,128]{2,1,0:T(8,128)S(1)}, u32[]{:S(2)}, u32[]{:S(2)}) collective-permute-start(f32[4,392,128]{2,1,0:T(8,128)} %multiply_add_fusion.2), channel_id=1, source_target_pairs={{0,8},{8,0},{16,24},{24,16},{1,9},{9,1},{17,25},{25,17},{2,10},{10... | collective-permute-start | bytes 2408456 | tf_op jit(solution)/shard_map/ppermute | solution.py:547
  209.8 48.1 %collective-permute-start.9 = (f32[4,392,128]{2,1,0:T(8,128)}, f32[4,392,128]{2,1,0:T(8,128)}, u32[]{:S(2)}, u32[]{:S(2)}) collective-permute-start(f32[4,392,128]{2,1,0:T(8,128)} %multiply_add_fusion.3), channel_id=1, source_target_pairs={{0,16},{8,24},{16,0},{24,8},{1,17},{9,25},{17,1},{25,9},{2,18},{10... | collective-permute-start | bytes 2408456 | tf_op jit(solution)/shard_map/ppermute | solution.py:547
  244.6 50.0 %collective-permute-start.17 = (f32[4,208,768]{2,1,0:T(8,128)}, f32[4,208,768]{2,1,0:T(8,128)}, u32[]{:S(2)}, u32[]{:S(2)}) collective-permute-start(f32[4,208,768]{2,1,0:T(8,128)} %select_maximum_fusion.1), channel_id=1, source_target_pairs={{0,1},{1,0},{2,3},{3,2},{4,5},{5,4},{6,7},{7,6},{8,9},{9,8},{10,11... | collective-permute-start | bytes 7667720 | tf_op jit(solution)/shard_map/ppermute | solution.py:547
  275.5 37.7 %collective-permute-start.14 = (f32[4,192,768]{2,1,0:T(8,128)}, f32[4,192,768]{2,1,0:T(8,128)}, u32[]{:S(2)}, u32[]{:S(2)}) collective-permute-start(f32[4,192,768]{2,1,0:T(8,128)} %fusion.54), channel_id=1, source_target_pairs={{0,1},{1,0},{2,3},{3,2},{4,5},{5,4},{6,7},{7,6},{8,9},{9,8},{10,11... | collective-permute-start | bytes 7077896 | tf_op jit(solution)/shard_map/ppermute | solution.py:547
  281.5 26.9 %collective-permute-start.16 = (f32[2,96,1536]{2,1,0:T(8,128)}, f32[2,96,1536]{2,1,0:T(8,128)S(1)}, u32[]{:S(2)}, u32[]{:S(2)}) collective-permute-start(f32[2,96,1536]{2,1,0:T(8,128)} %get-tuple-element.244), channel_id=1, source_target_pairs={{0,16},{8,24},{16,0},{24,8},{1,17},{9,25},{17,1},{25,9},{2,18},{10... | collective-permute-start | bytes 3538952 | tf_op jit(solution)/shard_map/ppermute | solution.py:547
  281.8 27.8 %collective-permute-start.15 = (f32[2,96,1536]{2,1,0:T(8,128)}, f32[2,96,1536]{2,1,0:T(8,128)S(1)}, u32[]{:S(2)}, u32[]{:S(2)}) collective-permute-start(f32[2,96,1536]{2,1,0:T(8,128)} %get-tuple-element.246), channel_id=1, source_target_pairs={{0,8},{8,0},{16,24},{24,16},{1,9},{9,1},{17,25},{25,17},{2,10},{10... | collective-permute-start | bytes 3538952 | tf_op jit(solution)/shard_map/ppermute | solution.py:547
  292.2 44.8 %collective-permute-start.25 = (f32[384,384]{1,0:T(8,128)S(1)}, f32[384,384]{1,0:T(8,128)}, u32[]{:S(2)}, u32[]{:S(2)}) collective-permute-start(f32[384,384]{1,0:T(8,128)S(1)} %add.219), channel_id=1, source_target_pairs={{0,4},{1,5},{2,6},{3,7},{4,0},{5,1},{6,2},{7,3},{8,12},{9,13},{10,... | collective-permute-start | bytes 1769480 | tf_op jit(solution)/shard_map/ppermute | solution.py:547
  297.0 30.6 %collective-permute-start.20 = (f32[2,104,768]{2,1,0:T(8,128)S(1)}, f32[2,104,768]{2,1,0:T(8,128)S(1)}, u32[]{:S(2)}, u32[]{:S(2)}) collective-permute-start(f32[2,104,768]{2,1,0:T(8,128)S(1)} %get-tuple-element.256), channel_id=1, source_target_pairs={{0,16},{8,24},{16,0},{24,8},{1,17},{9,25},{17,1},{25,9},{2,18},{10... | collective-permute-start | bytes 1916936 | tf_op jit(solution)/shard_map/ppermute | solution.py:547
  312.0 22.1 %collective-permute-start.27 = (f32[96,1536]{1,0:T(8,128)}, f32[96,1536]{1,0:T(8,128)}, u32[]{:S(2)}, u32[]{:S(2)}) collective-permute-start(f32[96,1536]{1,0:T(8,128)} %get-tuple-element.272), channel_id=1, source_target_pairs={{0,8},{8,0},{16,24},{24,16},{1,9},{9,1},{17,25},{25,17},{2,10},{10... | collective-permute-start | bytes 1769480 | tf_op jit(solution)/shard_map/ppermute | solution.py:547
  313.2 22.2 %collective-permute-start.26 = (f32[96,1536]{1,0:T(8,128)}, f32[96,1536]{1,0:T(8,128)}, u32[]{:S(2)}, u32[]{:S(2)}) collective-permute-start(f32[96,1536]{1,0:T(8,128)} %get-tuple-element.274), channel_id=1, source_target_pairs={{0,16},{8,24},{16,0},{24,8},{1,17},{9,25},{17,1},{25,9},{2,18},{10... | collective-permute-start | bytes 1769480 | tf_op jit(solution)/shard_map/ppermute | solution.py:547
  328.2 21.0 %collective-permute-start.23 = (f32[2,96,768]{2,1,0:T(8,128)}, f32[2,96,768]{2,1,0:T(8,128)S(1)}, u32[]{:S(2)}, u32[]{:S(2)}) collective-permute-start(f32[2,96,768]{2,1,0:T(8,128)} %get-tuple-element.270), channel_id=1, source_target_pairs={{0,8},{8,0},{16,24},{24,16},{1,9},{9,1},{17,25},{25,17},{2,10},{10... | collective-permute-start | bytes 1769480 | tf_op jit(solution)/shard_map/ppermute | solution.py:547
  364.4 37.2 %collective-permute-start.35 = (f32[768,384]{1,0:T(8,128)}, f32[768,384]{1,0:T(8,128)S(1)}, u32[]{:S(2)}, u32[]{:S(2)}) collective-permute-start(f32[768,384]{1,0:T(8,128)} %pad_maximum_fusion.4), channel_id=1, source_target_pairs={{0,1},{1,0},{2,3},{3,2},{4,5},{5,4},{6,7},{7,6},{8,9},{9,8},{10,11... | collective-permute-start | bytes 3538952 | tf_op jit(solution)/shard_map/ppermute | solution.py:547
  368.8 28.7 %collective-permute-start.36 = (f32[96,1536]{1,0:T(8,128)S(1)}, f32[96,1536]{1,0:T(8,128)S(1)}, u32[]{:S(2)}, u32[]{:S(2)}) collective-permute-start(f32[96,1536]{1,0:T(8,128)S(1)} %add.233), channel_id=1, source_target_pairs={{0,4},{1,5},{2,6},{3,7},{4,0},{5,1},{6,2},{7,3},{8,12},{9,13},{10,... | collective-permute-start | bytes 1769480 | tf_op jit(solution)/shard_map/ppermute | solution.py:547
  397.6 28.5 %collective-permute-start.39 = (f32[96,1536]{1,0:T(8,128)S(1)}, f32[96,1536]{1,0:T(8,128)}, u32[]{:S(2)}, u32[]{:S(2)}) collective-permute-start(f32[96,1536]{1,0:T(8,128)S(1)} %add.237), channel_id=1, source_target_pairs={{0,2},{1,3},{2,0},{3,1},{4,6},{5,7},{6,4},{7,5},{8,10},{9,11},{10,... | collective-permute-start | bytes 1769480 | tf_op jit(solution)/shard_map/ppermute | solution.py:547
  398.4 26.7 %collective-permute-start.33 = (f32[104,768]{1,0:T(8,128)S(1)}, f32[104,768]{1,0:T(8,128)}, u32[]{:S(2)}, u32[]{:S(2)}) collective-permute-start(f32[104,768]{1,0:T(8,128)S(1)} %add.236), channel_id=1, source_target_pairs={{0,4},{1,5},{2,6},{3,7},{4,0},{5,1},{6,2},{7,3},{8,12},{9,13},{10,... | collective-permute-start | bytes 958472 | tf_op jit(solution)/shard_map/ppermute | solution.py:547
  401.5 23.5 %collective-permute-start.34 = (f32[96,768]{1,0:T(8,128)}, f32[96,768]{1,0:T(8,128)S(1)}, u32[]{:S(2)}, u32[]{:S(2)}) collective-permute-start(f32[96,768]{1,0:T(8,128)} %get-tuple-element.264), channel_id=1, source_target_pairs={{0,2},{1,3},{2,0},{3,1},{4,6},{5,7},{6,4},{7,5},{8,10},{9,11},{10,... | collective-permute-start | bytes 884744 | tf_op jit(solution)/shard_map/ppermute | solution.py:547
  427.3 20.9 %collective-permute-start.42 = (f32[192,1536]{1,0:T(8,128)S(1)}, f32[192,1536]{1,0:T(8,128)S(1)}, u32[]{:S(2)}, u32[]{:S(2)}) collective-permute-start(f32[192,1536]{1,0:T(8,128)S(1)} %pad_maximum_fusion.5), channel_id=1, source_target_pairs={{0,1},{1,0},{2,3},{3,2},{4,5},{5,4},{6,7},{7,6},{8,9},{9,8},{10,11... | collective-permute-start | bytes 3538952 | tf_op jit(solution)/shard_map/ppermute | solution.py:547
  (46 other events, 470.3 us)

commit v3 on v2

--- a/solution.py
+++ b/solution.py
@@ -15,7 +15,8 @@
 bf16 = jnp.bfloat16
 half_pi = 1.5707963267948966
 norm_eps = 1e-05
-VMEM_LIMIT = 58 * 1024 * 1024
+VMEM_LIMIT = 60 * 1024 * 1024
+LIGHT_LIMIT = 32 * 1024 * 1024
 
 NN = (((1,), (0,)), ((), ()))
 NT = (((1,), (1,)), ((), ()))
@@ -252,7 +253,11 @@
     return inv_scale * (grad_norm - mean_rows(grad_norm) - normed * mean_rows(grad_norm * normed))
 
 
-def forward_kernel(
+def lane_total(ref):
+    return jnp.sum(ref[...], axis=1, keepdims=True)
+
+
+def layer_kernel(
     tab_ref,
     q_t_ref,
     numer_ref,
@@ -264,129 +269,112 @@
     w_out_t,
     w_in_t,
     w_back_t,
+    w_out_ref,
+    w_in_ref,
+    w_back_ref,
     gain_one_ref,
     shift_one_ref,
     gain_two_ref,
     shift_two_ref,
     layer_ref,
-    denom_ref,
     att_t_ref,
-    att_low_ref,
     first_t_ref,
-    normed_t_ref,
-    scale_ref,
     active_t_ref,
-    slope_t_ref,
-    grad_mid_ref,
     grad_second_ref,
-    grad_gain_ref,
-    grad_shift_ref,
-    second,
-):
-    table = tab_ref[0]
-    cos, sin = table[COS_READ : COS_READ + 1], table[SIN_READ : SIN_READ + 1]
-    states = (state_a, state_b)
-    denom_ref[...] = denom_loc_ref[...]
-    for h in range(HEADS):
-        reads = trig_rows(q_t_ref[head_slice(h), :], cos, sin)
-        more = mm(take_state(states, h), reads)
-        numer = numer_ref[head_slice(h), :] + more[:HEAD_DIM]
-        denom = denom_loc_ref[h : h + 1, :] + more[HEAD_DIM : HEAD_DIM + 1]
-        denom_ref[h : h + 1, :] = denom
-        high, low = two_parts(numer * (1.0 / denom))
-        att_t_ref[head_slice(h), :] = high
-        att_low_ref[head_slice(h), :] = low
-    summed = tok_t_ref[...].astype(f32) + mm(w_out_t[...], att_t_ref[...])
-    centered = summed - mean_rows(summed)
-    inv_scale = lax.rsqrt(mean_rows(centered * centered) + norm_eps)
-    scale_ref[...] = jnp.broadcast_to(inv_scale, scale_ref.shape)
-    normed = centered * inv_scale
-    normed_t_ref[...] = normed
-    first_out = normed * gain_one_ref[...] + shift_one_ref[...]
-    first_low = first_out.astype(bf16)
-    first_t_ref[...] = first_low
-    for at in range(0, w_in_t.shape[0], 768):
-        hidden = mm(w_in_t[at : at + 768, :], first_low)
-        half = 0.5 * (1.0 + lax.erf(hidden * 0.7071067811865476))
-        bell = jnp.exp(hidden * hidden * -0.5) * 0.3989422804014327
-        active = (hidden * half).astype(bf16)
-        active_t_ref[at : at + 768, :] = active
-        slope_t_ref[at : at + 768, :] = (half + hidden * bell).astype(bf16)
-        part = mm(w_back_t[:, at : at + 768], active)
-        if at == 0:
-            second[...] = part
-        else:
-            second[...] += part
-    summed = normed_t_ref[...] * gain_one_ref[...] + shift_one_ref[...] + second[...]
-    centered = summed - mean_rows(summed)
-    inv_scale = lax.rsqrt(mean_rows(centered * centered) + norm_eps)
-    normed = centered * inv_scale
-    layer_ref[0] = (normed * gain_two_ref[...] + shift_two_ref[...]).T.astype(bf16)
-    grad_top = cot_ref[0].T.astype(f32)
-    add_to(grad_gain_ref, fold_lanes(grad_top * normed))
-    add_to(grad_shift_ref, fold_lanes(grad_top))
-    grad_mid = norm_back(grad_top * gain_two_ref[...], normed, inv_scale)
-    grad_mid_ref[...] = grad_mid
-    grad_second_ref[...] = grad_mid.astype(bf16)
-
-
-def backward_kernel(
-    tab_ref,
-    q_t_ref,
-    denom_ref,
-    att_t_ref,
-    att_low_ref,
-    normed_t_ref,
-    scale_ref,
-    slope_t_ref,
-    grad_mid_ref,
-    grad_second_ref,
-    w_out_ref,
-    w_in_ref,
-    w_back_ref,
-    gain_one_ref,
     grad_hidden_ref,
     grad_base_ref,
     grad_branch_ref,
     grad_numer_ref,
     grad_denom_ref,
-    grad_gain_ref,
-    grad_shift_ref,
-    state_a,
-    state_b,
+    small_ref,
+    out_a,
+    out_b,
+    slope,
+    normed_one,
+    attended,
+    inverse_denom,
     total,
+    fold_gain_one,
+    fold_shift_one,
+    fold_gain_two,
+    fold_shift_two,
 ):
-    total[...] = grad_mid_ref[...]
-    grad_second = grad_second_ref[...]
-    for at in range(0, w_in_ref.shape[1], 768):
-        grad_active = mm(w_back_ref[at : at + 768, :], grad_second)
-        low = (grad_active * slope_t_ref[at : at + 768, :].astype(f32)).astype(bf16)
-        grad_hidden_ref[at : at + 768, :] = low
-        total[...] += mm(w_in_ref[:, at : at + 768], low)
+    ff = w_in_ref.shape[1]
+    step = 768
+    table = tab_ref[0]
+    cos, sin = table[COS_READ : COS_READ + 1], table[SIN_READ : SIN_READ + 1]
+    states = (state_a, state_b)
+    for h in range(HEADS):
+        reads = trig_rows(q_t_ref[head_slice(h), :], cos, sin)
+        more = mm(take_state(states, h), reads)
+        numer = numer_ref[head_slice(h), :] + more[:HEAD_DIM]
+        inverse = 1.0 / (denom_loc_ref[h : h + 1, :] + more[HEAD_DIM : HEAD_DIM + 1])
+        inverse_denom[h : h + 1, :] = inverse
+        value = numer * inverse
+        attended[head_slice(h), :] = value
+        att_t_ref[head_slice(h), :] = value.astype(bf16)
+    summed = tok_t_ref[...].astype(f32) + mm(w_out_t[...], att_t_ref[...])
+    centered = summed - mean_rows(summed)
+    scale_one = lax.rsqrt(mean_rows(centered * centered) + norm_eps)
+    normed = centered * scale_one
+    normed_one[...] = normed
+    first_out = normed * gain_one_ref[...] + shift_one_ref[...]
+    total[...] = first_out
+    first_low = first_out.astype(bf16)
+    first_t_ref[...] = first_low
+    for at in range(0, ff, step):
+        hidden = mm(w_in_t[at : at + step, :], first_low)
+        half = 0.5 * (1.0 + lax.erf(hidden * 0.7071067811865476))
+        bell = jnp.exp(hidden * hidden * -0.5) * 0.3989422804014327
+        active = (hidden * half).astype(bf16)
+        active_t_ref[at : at + step, :] = active
+        slope[at : at + step, :] = (half + hidden * bell).astype(bf16)
+        total[...] += mm(w_back_t[:, at : at + step], active)
+    summed = total[...]
+    centered = summed - mean_rows(summed)
+    scale_two = lax.rsqrt(mean_rows(centered * centered) + norm_eps)
+    normed = centered * scale_two
+    layer_ref[0] = (normed * gain_two_ref[...] + shift_two_ref[...]).T.astype(bf16)
+    grad_top = cot_ref[0].T.astype(f32)
+    add_to(fold_gain_two, fold_lanes(grad_top * normed))
+    add_to(fold_shift_two, fold_lanes(grad_top))
+    grad_mid = norm_back(grad_top * gain_two_ref[...], normed, scale_two)
+    total[...] = grad_mid
+    grad_second = grad_mid.astype(bf16)
+    grad_second_ref[...] = grad_second
+    for at in range(0, ff, step):
+        grad_active = mm(w_back_ref[at : at + step, :], grad_second)
+        low = (grad_active * slope[at : at + step, :].astype(f32)).astype(bf16)
+        grad_hidden_ref[at : at + step, :] = low
+        total[...] += mm(w_in_ref[:, at : at + step], low)
     grad_first = total[...]
-    normed = normed_t_ref[...]
-    add_to(grad_gain_ref, fold_lanes(grad_first * normed))
-    add_to(grad_shift_ref, fold_lanes(grad_first))
-    grad_base = norm_back(grad_first * gain_one_ref[...], normed, scale_ref[0:1, :])
+    normed = normed_one[...]
+    add_to(fold_gain_one, fold_lanes(grad_first * normed))
+    add_to(fold_shift_one, fold_lanes(grad_first))
+    grad_base = norm_back(grad_first * gain_one_ref[...], normed, scale_one)
     grad_base_ref[...] = grad_base
     grad_branch = grad_base.astype(bf16)
     grad_branch_ref[...] = grad_branch
     total[...] = mm(w_out_ref[...], grad_branch)
-    table = tab_ref[0]
-    cos, sin = table[COS_READ : COS_READ + 1], table[SIN_READ : SIN_READ + 1]
-    states = (state_a, state_b)
-    clear_pad(states)
+    outs = (out_a, out_b)
+    clear_pad(outs)
     grad_denom_ref[...] = jnp.zeros_like(grad_denom_ref)
     for h in range(HEADS):
-        inverse = 1.0 / denom_ref[h : h + 1, :]
-        grad_att = total[head_slice(h), :]
-        grad_numer = (grad_att * inverse).astype(bf16)
-        attended = att_t_ref[head_slice(h), :].astype(f32) + att_low_ref[head_slice(h), :].astype(f32)
-        grad_denom = -jnp.sum(grad_numer.astype(f32) * attended, axis=0, keepdims=True)
+        rows = head_slice(h)
+        grad_numer = (total[rows, :] * inverse_denom[h : h + 1, :]).astype(bf16)
+        grad_denom = -jnp.sum(grad_numer.astype(f32) * attended[rows, :], axis=0, keepdims=True)
         grad_denom_ref[h : h + 1, :] = grad_denom
-        grad_numer_ref[head_slice(h), :] = grad_numer
-        reads = trig_rows(q_t_ref[head_slice(h), :], cos, sin)
-        put_state(states, h, mm(with_row(grad_numer, grad_denom), reads, NT))
+        grad_numer_ref[rows, :] = grad_numer
+        reads = trig_rows(q_t_ref[rows, :], cos, sin)
+        put_state(outs, h, mm(with_row(grad_numer, grad_denom), reads, NT))
+
+    @pl.when(pl.program_id(0) == pl.num_programs(0) - 1)
+    def _():
+        lane = lax.broadcasted_iota(jnp.int32, small_ref.shape, 1)
+        value = jnp.zeros(small_ref.shape, f32)
+        for i, ref in enumerate((fold_gain_one, fold_shift_one, fold_gain_two, fold_shift_two)):
+            value = jnp.where(lane == i, lane_total(ref), value)
+        small_ref[...] = value
 
 
 def local_back_kernel(
@@ -464,6 +452,250 @@
     out_ref[0] = total.T
 
 
+def spec(block, index):
+    return pl.BlockSpec(block, index)
+
+
+def light(kernel, grid, ins, outs, scalars, *args):
+    return pl.pallas_call(
+        kernel,
+        grid_spec=pltpu.PrefetchScalarGridSpec(
+            num_scalar_prefetch=1,
+            grid=grid,
+            in_specs=ins,
+            out_specs=[o for o, _ in outs],
+        ),
+        out_shape=[jax.ShapeDtypeStruct(shape, f32) for _, shape in outs],
+        compiler_params=pltpu.CompilerParams(
+            dimension_semantics=("arbitrary",) * len(grid), vmem_limit_bytes=LIGHT_LIMIT
+        ),
+        cost_estimate=pl.CostEstimate(flops=1, bytes_accessed=1, transcendentals=0),
+    )(scalars, *args)
+
+
+def pick_halves(core, value):
+    cut = value.shape[1] // 2
+    low, high = value[:, :cut], value[:, cut:]
+    return jnp.where(core == 0, high, low), jnp.where(core == 0, low, high)
+
+
+def tall_kernel(s_ref, a_ref, b_ref, away_ref, keep_ref):
+    away_ref[0], keep_ref[0] = pick_halves(s_ref[0], mm(a_ref[...], b_ref[...], NT))
+
+
+def tall_product(core, shards, a, b):
+    count, flat = a.shape
+    rows, cut = count // shards, b.shape[0] // 2
+    out = (spec((1, rows, cut), lambda i, s: (i, 0, 0)), (shards, rows, cut))
+    return light(
+        tall_kernel,
+        (shards,),
+        [spec((rows, flat), lambda i, s: (i, 0)), spec(b.shape, lambda i, s: (0, 0))],
+        [out, out],
+        core[None],
+        a,
+        b,
+    )
+
+
+def wide_kernel(s_ref, a_ref, b_ref, away_ref, keep_ref):
+    value = mm(a_ref[...], b_ref[...], NT)
+    first = pl.program_id(0) < pl.num_programs(0) // 2
+
+    @pl.when(first)
+    def _():
+        away_ref[...] = value
+
+    @pl.when(jnp.logical_not(first))
+    def _():
+        keep_ref[...] = value
+
+
+def wide_product(core, shards, a, b):
+    count, flat = a.shape
+    cut = b.shape[0] // 2
+    tile = 512
+    half = cut // tile
+
+    def source(i, s):
+        return jnp.where(i < half, (1 - s[0]) * half + i, s[0] * half + i - half), 0
+
+    outs = [
+        (spec((count, tile), lambda i, s: (0, jnp.minimum(i, half - 1))), (count, cut)),
+        (spec((count, tile), lambda i, s: (0, jnp.maximum(i - half, 0))), (count, cut)),
+    ]
+    return [
+        v.reshape(shards, count // shards, cut)
+        for v in light(
+            wide_kernel,
+            (2 * half,),
+            [spec(a.shape, lambda i, s: (0, 0)), spec((tile, flat), source)],
+            outs,
+            core[None],
+            a,
+            b,
+        )
+    ]
+
+
+def twin_kernel(s_ref, a_ref, b_ref, c_ref, d_ref, *refs):
+    away_ref, keep_ref = refs[-2:]
+    core = s_ref[0]
+    at = 0
+    for left, right in ((a_ref, b_ref), (c_ref, d_ref)):
+        away, keep = pick_halves(core, mm(left[...], right[...].reshape(right.shape[-2:]), NT))
+        away_ref[:, at : at + away.shape[1]] = away
+        keep_ref[:, at : at + keep.shape[1]] = keep
+        at += away.shape[1]
+    if len(refs) == 3:
+        value = refs[0][...]
+        away_ref[:, at:] = jnp.where(core == 0, 0.0, value)
+        keep_ref[:, at:] = jnp.where(core == 0, value, 0.0)
+
+
+def twin_product(core, shards, a, b, c, d, small=None):
+    count, flat = a.shape
+    tile = count // 2
+
+    def full(v):
+        if isinstance(v, tuple):
+            return spec((1,) + v[0].shape[1:], lambda i, s, g=v[1]: (g, 0, 0)), v[0]
+        return spec(v.shape, lambda i, s: (0, 0)), v
+
+    rows = spec((tile, flat), lambda i, s: (i, 0))
+    (b_spec, b), (d_spec, d) = full(b), full(d)
+    ins, args = [rows, b_spec, rows, d_spec], [a, b, c, d]
+    columns = (b.shape[-2] + d.shape[-2]) // 2
+    if small is not None:
+        ins.append(spec((tile, small.shape[1]), lambda i, s: (i, 0)))
+        args.append(small)
+        columns += small.shape[1]
+    out = (spec((tile, columns), lambda i, s: (i, 0)), (count, columns))
+    return [
+        v.reshape(shards, count // shards, columns)
+        for v in light(twin_kernel, (2,), ins, [out, out], core[None], *args)
+    ]
+
+
+def route_kernel(s_ref, *refs):
+    for i in range(4):
+        refs[8 + i][...] = refs[2 * i][...] + refs[2 * i + 1][...]
+
+
+def route(left, right, low_bit, high_bit):
+    (a, b), (c, d) = left, right
+    shards, rows, columns = a.shape
+    same = a is c
+    if same:
+        rows //= 2
+    lower = 1 if same else 0
+    half = shards // 2
+
+    def by_low(flip):
+        def index(i, s):
+            mine = s[0]
+            return 2 * i + ((1 - mine) if flip else mine), 0, 0
+
+        return index
+
+    def by_high(flip):
+        def index(i, s):
+            mine = s[1]
+            return i + ((1 - mine) if flip else mine) * half, lower, 0
+
+        return index
+
+    block = (1, rows, columns)
+    maps = [by_low(True), by_low(False), by_high(True), by_high(False)]
+    ins = [spec(block, m) for m in maps for _ in range(2)]
+    out = (spec(block, lambda i, s: (i, 0, 0)), (half, rows, columns))
+    return light(
+        route_kernel,
+        (half,),
+        ins,
+        [out] * 4,
+        jnp.stack([low_bit, high_bit]),
+        a,
+        b,
+        a,
+        b,
+        c,
+        d,
+        c,
+        d,
+    )
+
+
+def choose_kernel(s_ref, a_ref, b_ref, c_ref, d_ref, away_ref, keep_ref):
+    upper, lower = a_ref[...] + b_ref[...], c_ref[...] + d_ref[...]
+    odd = s_ref[0] == 1
+    away_ref[...] = jnp.where(odd, upper, lower)
+    keep_ref[...] = jnp.where(odd, lower, upper)
+
+
+def choose(left, right, odd):
+    shape = left[0].shape
+    whole = spec(shape, lambda i, s: (0, 0, 0))
+    return light(choose_kernel, (1,), [whole] * 4, [(whole, shape)] * 2, odd[None], *left, *right)
+
+
+def add_kernel(s_ref, a_ref, b_ref, out_ref):
+    out_ref[...] = a_ref[...] + b_ref[...]
+
+
+def add(a, b):
+    whole = spec(a.shape, lambda i, s: (0,) * a.ndim)
+    return light(add_kernel, (1,), [whole] * 2, [(whole, a.shape)], jnp.zeros((1,), jnp.int32), a, b)[0]
+
+
+def join_kernel(s_ref, part_ref, got_ref, other_part_ref, other_got_ref, *outs):
+    odd, first = s_ref[0] == 1, s_ref[1] == 0
+    rows = part_ref.shape[1]
+    for upper in (True, False):
+        swapped = odd if upper else jnp.logical_not(odd)
+        mine = jnp.where(swapped, got_ref[0], part_ref[0])
+        other = jnp.where(swapped, other_got_ref[0], other_part_ref[0])
+        low, high = jnp.where(first, mine, other), jnp.where(first, other, mine)
+        lines = slice(0, rows) if upper else slice(rows, 2 * rows)
+        at = 0
+        for out in outs:
+            cut = out.shape[1] // 2
+            if cut < 128:
+                out[lines, :] = low[:, at:]
+            else:
+                out[lines, :cut] = low[:, at : at + cut]
+                out[lines, cut:] = high[:, at : at + cut]
+            at += cut
+
+
+def join(odd, core, part, got, other_part, other_got, widths):
+    rows = 2 * part.shape[1]
+    whole = spec(part.shape, lambda i, s: (0, 0, 0))
+    outs = [(spec((rows, w), lambda i, s: (0, 0)), (rows, w)) for w in widths]
+    return light(
+        join_kernel,
+        (1,),
+        [whole] * 4,
+        outs,
+        jnp.stack([odd, core]),
+        part,
+        got,
+        other_part,
+        other_got,
+    )
+
+
+def mix_kernel(s_ref, *refs):
+    row = pl.program_id(0)
+    for i in range(2):
+        refs[4 + i][...] = s_ref[2 * i, row] * refs[2 * i][...] + s_ref[2 * i + 1, row] * refs[2 * i + 1][...]
+
+
+def mix(weights, a, b, c, d):
+    block = spec((1,) + a.shape[1:], lambda r, s: (r, 0, 0))
+    return light(mix_kernel, (a.shape[0],), [block] * 4, [(block, a.shape)] * 2, weights, a, b, c, d)
+
+
 def first_begins(lengths, count, tok_count):
     slots = lengths.shape[1]
     order = jnp.arange(slots)
@@ -478,7 +710,7 @@
     out = values[0]
     for i in range(1, len(values)):
         out = jnp.where(index == i, values[i], out)
-    return out[:, None, None]
+    return out
 
 
 class Order:
@@ -519,27 +751,32 @@
     zero = jnp.zeros_like(begin_first[:, 0], f32)
     one = zero + 1.0
     m02, m03, m13 = covers(0, 2), covers(0, 3), covers(1, 3)
-    own_a, first_a = pick(index, [m02, m13, zero, zero]), pick(index, [one, m03, zero, zero])
-    own_b, first_b = pick(index, [one, zero, one, zero]), pick(index, [zero, zero, m03, one])
-    end_a, then_a = pick(index, [zero, one, zero, one]), pick(index, [zero, zero, one, one])
-    end_b, then_b = pick(index, [zero, zero, m02, m13]), pick(index, [zero, one, one, one])
+    onward = jnp.stack(
+        [
+            pick(index, [m02, m13, zero, zero]),
+            pick(index, [one, m03, zero, zero]),
+            pick(index, [one, zero, one, zero]),
+            pick(index, [zero, zero, m03, one]),
+        ]
+    )
+    final = jnp.stack(
+        [
+            pick(index, [zero, one, zero, one]),
+            pick(index, [zero, zero, one, one]),
+            pick(index, [zero, zero, m02, m13]),
+            pick(index, [zero, one, one, one]),
+        ]
+    )
     got_a = swap(part_a, "seq", 1)
     got_b = swap(part_b, "seq", 2)
     yield
     got_a, got_b = order.tie((got_a, got_b))
-    next_a = own_a * part_a + first_a * got_a
-    next_b = own_b * part_b + first_b * got_b
-    order.done((next_a, next_b))
+    next_a, next_b = order.done(mix(onward, part_a, got_a, part_b, got_b))
     last_a = swap(next_a, "seq", 2)
     last_b = swap(next_b, "seq", 1)
     yield
     last_a, last_b = order.tie((last_a, last_b))
-    full = (end_a * got_a + then_a * last_a, end_b * got_b + then_b * last_b)
-    yield order.done(full)
-
-
-def take(value, index, dim):
-    return lax.dynamic_index_in_dim(value, index, dim, False)
+    yield order.done(mix(final, got_a, last_a, got_b, last_b))
 
 
 def swap(value, axis, distance):
@@ -547,59 +784,43 @@
     return lax.ppermute(value, axis, [(i, i ^ distance) for i in range(count)])
 
 
-def reduced(order, away, keep):
-    shards, rows, columns = keep.shape
-    place = lax.axis_index("seq")
-    batch_place = lax.axis_index("batch")
+def reduced(order, core, away, keep, widths):
+    place = lax.axis_index("seq").astype(jnp.int32)
+    odd = ((lax.axis_index("batch") >> 1) & 1).astype(jnp.int32)
     count = lax.axis_size("batch")
-    bits = shards.bit_length() - 1
+    bits = keep.shape[0].bit_length() - 1
     got = swap(away, "batch", 1)
     yield
-    summed = keep + order.tie(got)
-    shape = (2,) * bits + (rows // 2, columns)
-    parts = [summed[:, : rows // 2].reshape(shape), summed[:, rows // 2 :].reshape(shape)]
-    left = [list(range(bits - 1, -1, -1)) for _ in parts]
-    orders = [list(range(bits)), list(range(bits - 1, -1, -1))]
+    left = right = (keep, order.tie(got))
     for step in range(bits):
-        aways, keeps = [], []
-        for side, part in enumerate(parts):
-            bit = orders[side][step]
-            dim = left[side].index(bit)
-            left[side].pop(dim)
-            mine = (place >> bit) & 1
-            aways.append(take(part, 1 - mine, dim))
-            keeps.append(take(part, mine, dim))
-        aways, keeps = order.done((aways, keeps))
-        gots = [swap(a, "seq", 1 << orders[side][step]) for side, a in enumerate(aways)]
+        high = bits - 1 - step
+        away_l, keep_l, away_r, keep_r = order.done(
+            route(left, right, (place >> step) & 1, (place >> high) & 1)
+        )
+        got_l, got_r = swap(away_l, "seq", 1 << step), swap(away_r, "seq", 1 << high)
         yield
-        parts = [k + g for k, g in zip(keeps, order.tie(gots))]
-    odd = (batch_place >> 1) & 1 == 1
-    away = jnp.where(odd, parts[0], parts[1])
-    part = jnp.where(odd, parts[1], parts[0])
-    away, part = order.done((away, part))
+        got_l, got_r = order.tie((got_l, got_r))
+        left, right = (keep_l, got_l), (keep_r, got_r)
+    away, part = order.done(choose(left, right, odd))
     got = swap(away, "batch", 2)
+    distance = 4
     yield
-    part = order.done(part + order.tie(got))
-    distance = 4
+    part = order.done(add(part, order.tie(got)))
     while distance < count:
         got = swap(part, "batch", distance)
         yield
-        part = order.done(part + order.tie(got))
+        part = order.done(add(part, order.tie(got)))
         distance *= 2
     got = swap(part, "batch", 2)
+    other_part = swap(part, "batch", 1)
     yield
-    got = order.tie(got)
-    mine = order.done(
-        jnp.concatenate([jnp.where(odd, got, part), jnp.where(odd, part, got)], axis=0)
-    )
-    other = swap(mine, "batch", 1)
+    got = order.done(order.tie(got))
+    other_got = swap(got, "batch", 1)
     yield
-    other = order.tie(other)
-    first = batch_place & 1 == 0
-    yield order.done((jnp.where(first, mine, other), jnp.where(first, other, mine)))
-
-
-def call(kernel, grid, ins, outs, scratch, flops, moved, *args):
+    yield order.done(join(odd, core, part, got, order.tie(other_part), other_got, widths))
+
+
+def call(kernel, grid, ins, outs, scratch, *args):
     return pl.pallas_call(
         kernel,
         grid=grid,
@@ -610,7 +831,7 @@
         compiler_params=pltpu.CompilerParams(
             dimension_semantics=("arbitrary",) * len(grid), vmem_limit_bytes=VMEM_LIMIT
         ),
-        cost_estimate=pl.CostEstimate(flops=flops, bytes_accessed=moved, transcendentals=0),
+        cost_estimate=pl.CostEstimate(flops=1, bytes_accessed=1, transcendentals=0),
     )(*args)
 
 
@@ -640,7 +861,6 @@
     token_major = pl.BlockSpec((1, toks, width), lambda r: (r, 0, 0))
     table_spec = pl.BlockSpec((1, 8, toks), lambda r: (r, 0, 0))
     state_spec = pl.BlockSpec((1, STATE_ROWS, 2 * HEAD_DIM), lambda r: (r, 0, 0))
-    fold_spec = pl.BlockSpec((width, 128), lambda r: (0, 0))
 
     def feature(count):
         return pl.BlockSpec((count, toks), lambda r: (0, r))
@@ -650,30 +870,15 @@
     wide_full = (feature(width), ((width, flat), f32))
     ff_low = (feature(ff), ((ff, flat), bf16))
     head_rows = (feature(16), ((16, flat), f32))
-    one_row = (feature(8), ((8, flat), f32))
-    fold = (fold_spec, ((width, 128), f32))
+    fold = (pl.BlockSpec((width, 128), lambda r: (0, 0)), ((width, 128), f32))
     state = (state_spec, ((rows, STATE_ROWS, 2 * HEAD_DIM), f32))
-    cell = 2 * flat * toks * 256
     grid = (rows,)
 
     order = Order()
     core = (lax.axis_index("batch") % 2).astype(jnp.int32)
 
-    def run(kernel, ins, outs, scratch, flops, first, *args):
-        return order.done(call(kernel, grid, ins, outs, scratch, flops // 4, 1_000_000, order.tie(first), *args))
-
-    def halves(b):
-        split = b.reshape(b.shape[0], 2, b.shape[1] // 2, flat)
-        return [take(split, c, 1).reshape(-1, flat) for c in (1 - core, core)]
-
-    def product(a, b):
-        grad = lax.dot_general(order.tie(a), b, NT, preferred_element_type=f32)
-        return order.done(grad.reshape(shards, a.shape[0] // shards, b.shape[0]))
-
-    def reduction(a, b):
-        away, keep = halves(b)
-        away = product(a, away)
-        return reduced(order, away, product(a, keep))
+    def run(kernel, ins, outs, scratch, first, *args):
+        return order.done(call(kernel, grid, ins, outs, scratch, order.tie(first), *args))
 
     def column(v):
         return v[:, None]
@@ -687,7 +892,6 @@
         + [wide_low]
         + [state] * 2,
         [pltpu.VMEM((2, width, width), bf16)],
-        4 * flat * width * width,
         place[None],
         doc_lengths,
         tokens,
@@ -719,7 +923,6 @@
             (pl.BlockSpec((width, part), lambda r: (0, r)), ((width, ff), bf16)),
         ],
         [pltpu.VMEM((width, width), bf16)],
-        2 * cell * HEADS,
         table,
         tok_t,
         key,
@@ -733,20 +936,20 @@
     in_a, in_b = next(states)
     (
         layer_out,
-        denom,
         att_t,
-        att_low,
         first_t,
-        normed_t,
-        scale_one,
         active_t,
-        slope_t,
-        grad_mid,
         grad_second,
-        fold_gain_two,
-        fold_shift_two,
+        grad_hidden,
+        grad_base,
+        grad_branch,
+        grad_numer,
+        grad_denom,
+        small,
+        out_a,
+        out_b,
     ) = run(
-        forward_kernel,
+        layer_kernel,
         [
             table_spec,
             feature(width),
@@ -757,24 +960,30 @@
             feature(width),
             token_major,
         ]
-        + [whole] * 7,
+        + [whole] * 10,
         [
             tok_low,
-            head_rows,
             wide_low,
             wide_low,
+            ff_low,
             wide_low,
-            wide_full,
-            one_row,
-            ff_low,
             ff_low,
             wide_full,
             wide_low,
+            wide_low,
+            head_rows,
             fold,
-            fold,
+            state,
+            state,
         ],
-        [pltpu.VMEM((width, toks), f32)],
-        2 * flat * width * (width + 2 * ff),
+        [
+            pltpu.VMEM((ff, toks), bf16),
+            pltpu.VMEM((width, toks), f32),
+            pltpu.VMEM((width, toks), f32),
+            pltpu.VMEM((16, toks), f32),
+            pltpu.VMEM((width, toks), f32),
+        ]
+        + [pltpu.VMEM((width, 128), f32)] * 4,
         table,
         q_t,
         numer,
@@ -786,64 +995,27 @@
         w_out_t,
         w_in_t,
         w_back_t,
+        w_out,
+        w_in,
+        w_back,
         column(gain_one),
         column(shift_one),
         column(gain_two),
         column(shift_two),
     )
 
-    back = reduction(active_t, grad_second[None])
-    next(back)
-    next(back)
-    (
-        grad_hidden,
-        grad_base,
-        grad_branch,
-        grad_numer,
-        grad_denom,
-        fold_gain_one,
-        fold_shift_one,
-        out_a,
-        out_b,
-    ) = run(
-        backward_kernel,
-        [
-            table_spec,
-            feature(width),
-            feature(16),
-            feature(width),
-            feature(width),
-            feature(width),
-            feature(8),
-            feature(ff),
-            feature(width),
-            feature(width),
-        ]
-        + [whole] * 4,
-        [ff_low, wide_full, wide_low, wide_low, head_rows, fold, fold, state, state],
-        [pltpu.VMEM((width, toks), f32)],
-        2 * flat * width * (width + 2 * ff),
-        table,
-        q_t,
-        denom,
-        att_t,
-        att_low,
-        normed_t,
-        scale_one,
-        slope_t,
-        grad_mid,
-        grad_second,
-        w_out,
-        w_in,
-        w_back,
-        column(gain_one),
-    )
+    def reduction(product, widths, first, *rest):
+        away, keep = order.done(product(core, shards, order.tie(first), *rest))
+        steps = reduced(order, core, away, keep, widths)
+        next(steps)
+        return steps
+
     back_states = entering(order, (out_a, out_b), begin_first, toks, True)
     next(back_states)
-    into = reduction(first_t, grad_hidden[None])
-    next(into)
+    back = reduction(tall_product, (width,), active_t, grad_second)
+    into = reduction(wide_product, (ff,), first_t, grad_hidden)
+    next(back_states)
     next(back)
-    next(back_states)
     grad_qpre, grad_k_loc, grad_v_loc = run(
         local_back_kernel,
         [
@@ -860,7 +1032,6 @@
         ],
         [wide_low, wide_full, wide_full],
         [],
-        5 * cell * HEADS,
         table,
         q_t,
         k_t,
@@ -872,36 +1043,9 @@
         in_a,
         in_b,
     )
-    share = width // shards
-    small = jnp.stack(
-        [
-            jnp.sum(v, axis=1)
-            for v in order.tie((fold_gain_one, fold_shift_one, fold_gain_two, fold_shift_two))
-        ]
-    )
-    small = small.reshape(4, shards, share).transpose(1, 0, 2).reshape(shards, 1, 4 * share)
-    small = order.done(jnp.pad(small, ((0, 0), (0, 15), (0, width - 4 * share))))
-
-    def mixed_part(half, out_rows, query_rows):
-        columns = jnp.concatenate(
-            [
-                lax.dot_general(a, b, NT, preferred_element_type=f32)
-                for a, b in ((order.tie(att_t), out_rows), (tok_t, query_rows))
-            ],
-            axis=1,
-        )
-        cut = width // 2
-        extra = lax.dynamic_slice_in_dim(small, half * cut, cut, 2)
-        extra = jnp.pad(extra, ((0, 0), (0, 0), (0, cut)))
-        return order.done(
-            jnp.concatenate([columns.reshape(shards, share, width), extra], axis=1)
-        )
-
-    out_halves, query_halves = halves(grad_branch[None]), halves(grad_qpre[None])
-    away = mixed_part(1 - core, out_halves[0], query_halves[0])
-    mixed = reduced(order, away, mixed_part(core, out_halves[1], query_halves[1]))
-    next(mixed)
-    next(back)
+    mixed = reduction(
+        twin_product, (width, width, 128), att_t, grad_branch, tok_t, grad_qpre, small
+    )
     next(into)
     back_a, back_b = next(back_states)
     (grad_kv,) = run(
@@ -912,7 +1056,6 @@
         + [feature(width)] * 2,
         [(pl.BlockSpec((2, width, toks), lambda r: (0, 0, r)), ((2, width, flat), bf16))],
         [],
-        2 * cell * HEADS,
         table,
         k_t,
         v_t,
@@ -922,10 +1065,10 @@
         grad_k_loc,
         grad_v_loc,
     )
-    last = reduction(tok_t, grad_kv)
-    next(last)
     next(back)
+    last = reduction(twin_product, (width, width), tok_t, (grad_kv, 0), tok_t, (grad_kv, 1))
     next(mixed)
+    next(back)
     next(into)
     next(last)
     (grad_tokens,) = run(
@@ -938,7 +1081,6 @@
         + [whole] * 3,
         [(token_major, ((rows, toks, width), f32))],
         [],
-        6 * flat * width * width,
         grad_qpre,
         grad_kv,
         grad_base,
@@ -946,7 +1088,7 @@
         w_key,
         w_value,
     )
-    pending = [mixed, into, back, last]
+    pending = [back, mixed, into, last]
     ends = {}
     while pending:
         for steps in list(pending):
@@ -954,32 +1096,22 @@
             if value is not None:
                 ends[id(steps)] = value
                 pending.remove(steps)
-
-    def joined(steps, groups):
-        low, high = ends[id(steps)]
-        size = low.shape[1] // groups
-        return [
-            jnp.concatenate([v[:, g * size : (g + 1) * size] for v in (low, high)], axis=1)
-            for g in range(groups)
-        ]
-
-    (total_back,), (total_in,) = joined(back, 1), joined(into, 1)
-    total_out, total_query = joined(mixed, 2)
-    total_key, total_value = joined(last, 2)
-    vectors = total_out[share, : 4 * share].reshape(4, share)
+    (total_back,), (total_in,) = ends[id(back)], ends[id(into)]
+    total_out, total_query, vectors = ends[id(mixed)]
+    total_key, total_value = ends[id(last)]
     return (
         layer_out,
         grad_tokens,
-        total_query[:share],
+        total_query,
         total_key,
         total_value,
-        total_out[:share],
+        total_out,
         total_in,
         total_back,
-        vectors[0],
-        vectors[1],
-        vectors[2],
-        vectors[3],
+        vectors[:, 0],
+        vectors[:, 1],
+        vectors[:, 2],
+        vectors[:, 3],
     )
 
 

time: 471 us -> 463 us (0.983); the launches traced: 462 us -> 462 us
  Pallas kernels: 117 us -> 178 us
  other arithmetic: 57.7 us -> 1.2 us
  matrix products: 39.6 us -> 0 us
  waiting for transfers between devices: 158 us -> 173 us
  local copies, waits for them, and re-layouts: 30.8 us -> 44.3 us
  starting transfers between devices: 57.9 us -> 65 us
    pallas_call x0 -> x32, Pallas kernels: none -> 65.3 us  [light(): pl.pallas_call(kernel, grid_spec=pltpu.PrefetchScalarGridSpec(num_scalar_...]
    dot_general x10 -> x0, matrix products: 39.6 us -> none  [the longest x6 32.5 us: product(): grad = lax.dot_general(order.tie(a), b, NT, preferred_element_type=f32)]
    unnamed x54 -> x122, local copies, waits for them, and re-layouts: 2.27 us -> 39.5 us
    add x27 -> x0, other arithmetic: 29.4 us -> none  [the longest x4 11.8 us: reduced(): summed = keep + order.tie(got)]
    ppermute x44 -> x48, waiting for transfers between devices: 158 us -> 173 us  [swap(): return lax.ppermute(value, axis, [(i, i ^ distance) for i in range(count)])]
    concatenate x13 -> x0, other arithmetic: 11.2 us -> none  [the longest x6 6.56 us: joined(): jnp.concatenate([v[:, g * size:(g + 1) * size] for v in (low, high)], axi...]
    squeeze x16 -> x0, local copies, waits for them, and re-layouts: 9.05 us -> none  [take(): return lax.dynamic_index_in_dim(value, index, dim, False)]
    select_n x13 -> x0, other arithmetic: 9.01 us -> none  [the longest x3 4.82 us: reduced(): part = jnp.where(odd, parts[1], parts[0])]
  transfers between devices with their start and end apart: 44 -> 48, of which waited for: 20 -> 17; matrix products, arithmetic and copies ran while one was open for 21% -> 1% of each run, Pallas kernels for 11% -> 22%
where the time goes in v3:
time: 463 us; the launch traced here: 462 us
  Pallas kernels  178 us (38%)
  waiting for transfers between devices  173 us (37%)
  starting transfers between devices  65 us (14%)
  local copies, waits for them, and re-layouts  44.3 us (10%)
    ppermute x48, waiting for transfers between devices, swap(): return lax.ppermute(value, axis, [(i, i ^ distance) for i in range(count)])  173 us
    pallas_call x6, Pallas kernels, call(): pl.pallas_call(kernel, grid=grid, in_specs=[s for s in ins], out_specs=[s...  113 us
    pallas_call x32, Pallas kernels, light(): pl.pallas_call(kernel, grid_spec=pltpu.PrefetchScalarGridSpec(num_scalar_...  65.3 us
    ppermute x48, starting transfers between devices, swap(): return lax.ppermute(value, axis, [(i, i ^ distance) for i in range(count)])  65 us
    unnamed x122, local copies, waits for them, and re-layouts  39.5 us
  transfers between devices with their start and end apart: 48, of which 17 were waited for; matrix products, arithmetic and copies ran while one was open for 1% of the time, Pallas kernels for 22%

profile of v3, /device:TPU:1, one launch (start us, length us, event | category | flops | bytes accessed | tf_op | source)
XLA Modules:
  0.0 462.4 jit_solution(11044851797572380899)
XLA Ops:
  0.6 9.9 %shard_map.220 = (f32[4,8,256]{2,1,0:T(8,128)}, bf16[768,1024]{1,0:T(8,128)(2,1)}, bf16[768,1024]{1,0:T(8,128)(2,1)}, bf16[768,1024]{1,0:T(8,128)(2,1)}, bf16[4,...) custom-call(s32[1]{0:T(128)} %bitcast.place_ref, ...), custom_call_target="tpu_custom_call" | custom-call | flops 1 | bytes 1 | tf_op jit(solution)/shard_map/pallas_call | solution.py:824
  14.0 17.7 %shard_map.221 = (bf16[768,1024]{1,0:T(8,128)(2,1)}, bf16[768,1024]{1,0:T(8,128)(2,1)}, f32[768,1024]{1,0:T(8,128)}, f32[16,1024]{1,0:T(8,128)}, bf16[768,768]{1...) custom-call(f32[4,8,256]{2,1,0:T(8,128)} %get-tuple-element.228.tab_ref, ...), custom_call_target="tpu_custom_call" | custom-call | flops 1 | bytes 1 | tf_op jit(solution)/shard_map/pallas_call | solution.py:824
  39.1 14.0 %collective-permute-done.2.refs_1_ = f32[4,392,128]{2,1,0:T(8,128)S(1)} collective-permute-done((f32[4,392,128]{2,1,0:T(8,128)}, f32[4,392,128]{2,1,0:T(8,128)S(1)}, u32[]{:S(2)}, u32[]{:S(2)}) %collective-permute-start.2) | collective-permute-done | bytes 802848 | tf_op jit(solution)/shard_map/ppermute | solution.py:784
  55.8 53.8 %shard_map.224 = (bf16[4,256,768]{2,1,0:T(8,128)(2,1)}, bf16[768,1024]{1,0:T(8,128)(2,1)}, bf16[768,1024]{1,0:T(8,128)(2,1)}, bf16[3072,1024]{1,0:T(8,128)(2,1)}...) custom-call(f32[4,8,256]{2,1,0:T(8,128)} %get-tuple-element.228.tab_, ...), custom_call_target="tpu_custom_call" | custom-call | flops 1 | bytes 1 | tf_op jit(solution)/shard_map/pallas_call | solution.py:824
  113.8 6.8 %shard_map.225 = (f32[4,768,384]{2,1,0:T(8,128)}, f32[4,768,384]{2,1,0:T(8,128)S(1)}) custom-call(s32[1]{0:T(128)} %bitcast.3.s_ref, bf16[3072,1024]{1,0:T(8,128)(2,1)S(1)} %copy-done.13, bf16[768,1024]{1,0:T(8,128)(2,1)S(1)} %copy-done.37), custom_call_target="tpu_custom_call" | custom-call | flops 1 | bytes 1 | tf_op jit(solution)/shard_map/pallas_call | solution.py:460
  125.1 8.3 %shard_map.226 = (f32[768,1536]{1,0:T(8,128)}, f32[768,1536]{1,0:T(8,128)S(1)}) custom-call(s32[1]{0:T(128)} %bitcast.3.s_ref, bf16[768,1024]{1,0:T(8,128)(2,1)S(1)} %copy-done.36, bf16[3072,1024]{1,0:T(8,128)(2,1)S(1)} %copy-done.12), custom_call_target="tpu_custom_call" | custom-call | flops 1 | bytes 1 | tf_op jit(solution)/shard_map/pallas_call | solution.py:460
  137.4 17.3 %collective-permute-done.5.refs_1_.refs_0_ = f32[4,392,128]{2,1,0:T(8,128)S(1)} collective-permute-done((f32[4,392,128]{2,1,0:T(8,128)S(1)}, f32[4,392,128]{2,1,0:T(8,128)S(1)}, u32[]{:S(2)}, u32[]{:S(2)}) %collective-permute-start.5) | collective-permute-done | bytes 802848 | tf_op jit(solution)/shard_map/ppermute | solution.py:784
  154.8 4.0 shard_map.227
  161.2 4.2 shard_map.228
  167.5 14.4 %shard_map.229 = (bf16[768,1024]{1,0:T(8,128)(2,1)}, f32[768,1024]{1,0:T(8,128)}, f32[768,1024]{1,0:T(8,128)}) custom-call(f32[4,8,256]{2,1,0:T(8,128)} %get-tuple-element.228.tab_ref, bf16[768,1024]{1,0:T(8,128)(2,1)} %get-tuple-element.168.q_t_ref, bf16[768,1024]{1,0:T(8,128)(2,1)} %get-tuple-element.162.k_t_ref, ...), custom_call_target="tpu_custom_call" | custom-call | flops 1 | bytes 1 | tf_op jit(solution)/shard_map/pallas_call | solution.py:824
  198.8 4.1 shard_map.231
  203.0 35.5 %collective-permute-done.10.refs_3_ = f32[4,392,128]{2,1,0:T(8,128)} collective-permute-done((f32[4,392,128]{2,1,0:T(8,128)}, f32[4,392,128]{2,1,0:T(8,128)}, u32[]{:S(2)}, u32[]{:S(2)}) %collective-permute-start.10) | collective-permute-done | bytes 802848 | tf_op jit(solution)/shard_map/ppermute | solution.py:784
  244.2 7.4 %shard_map.233.b_ref.d_ref.gkv_ref = bf16[2,768,1024]{2,1,0:T(8,128)(2,1)} custom-call(f32[4,8,256]{2,1,0:T(8,128)} %get-tuple-element.228.tab_ref, bf16[768,1024]{1,0:T(8,128)(2,1)} %get-tuple-element.162.k_t_ref, bf16[768,1024]{1,0:T(8,128)(2,1)} %get-tuple-element.163.v_t_ref, bf16[768,1024]{1,0:T(8,128)(2,1)} %get-tuple-element.166.sig_k_ref, ...), custom_call_target="tpu_custom_call" | custom-call | flops 1 | bytes 1 | tf_op jit(solution)/shard_map/pallas_call | solution.py:824
  276.6 32.4 %collective-permute-done.15.b_ref = f32[1,384,384]{2,1,0:T(8,128)} collective-permute-done((f32[1,384,384]{2,1,0:T(8,128)}, f32[1,384,384]{2,1,0:T(8,128)}, u32[]{:S(2)}, u32[]{:S(2)}) %collective-permute-start.15) | collective-permute-done | bytes 589856 | tf_op jit(solution)/shard_map/ppermute | solution.py:784
  320.6 4.7 %collective-permute-done.20.b_ref = f32[1,384,384]{2,1,0:T(8,128)S(1)} collective-permute-done((f32[1,384,384]{2,1,0:T(8,128)S(1)}, f32[1,384,384]{2,1,0:T(8,128)S(1)}, u32[]{:S(2)}, u32[]{:S(2)}) %collective-permute-start.20) | collective-permute-done | bytes 589856 | tf_op jit(solution)/shard_map/ppermute | solution.py:784
  327.2 9.2 %shard_map.240 = f32[4,256,768]{2,1,0:T(8,128)} custom-call(bf16[768,1024]{1,0:T(8,128)(2,1)} %get-tuple-element.258.d_ref.gq_ref, bf16[2,768,1024]{2,1,0:T(8,128)(2,1)} %shard_map.233.b_ref.d_ref.gkv_ref, f32[768,1024]{1,0:T(8,128)} %get-tuple-element.190.base_ref, bf16[768,768]{1,0:T(8,128)(2,1)} %wq_ref.3, bf16[768,768]{1,0:T(8,128)(2,1)} %wk_ref.3, ...), custom_call_target="tpu_custom_call" | custom-call | flops 1 | bytes 1 | tf_op jit(solution)/shard_map/pallas_call | solution.py:824
  346.5 7.4 %collective-permute-done.24.refs_1_.refs_3_ = f32[2,96,768]{2,1,0:T(8,128)S(1)} collective-permute-done((f32[2,96,768]{2,1,0:T(8,128)}, f32[2,96,768]{2,1,0:T(8,128)S(1)}, u32[]{:S(2)}, u32[]{:S(2)}) %collective-permute-start.24) | collective-permute-done | bytes 589856 | tf_op jit(solution)/shard_map/ppermute | solution.py:784
  355.6 11.2 %collective-permute-done.23.b_ref = f32[1,384,384]{2,1,0:T(8,128)S(1)} collective-permute-done((f32[1,384,384]{2,1,0:T(8,128)S(1)}, f32[1,384,384]{2,1,0:T(8,128)S(1)}, u32[]{:S(2)}, u32[]{:S(2)}) %collective-permute-start.23) | collective-permute-done | bytes 589856 | tf_op jit(solution)/shard_map/ppermute | solution.py:784
  372.5 5.2 %collective-permute-done.30.b_ref = f32[1,96,768]{2,1,0:T(8,128)S(1)} collective-permute-done((f32[1,96,768]{2,1,0:T(8,128)S(1)}, f32[1,96,768]{2,1,0:T(8,128)S(1)}, u32[]{:S(2)}, u32[]{:S(2)}) %collective-permute-start.30) | collective-permute-done | bytes 294944 | tf_op jit(solution)/shard_map/ppermute | solution.py:784
  377.7 9.8 %collective-permute-start.34 = (f32[1,384,384]{2,1,0:T(8,128)S(1)}, f32[1,384,384]{2,1,0:T(8,128)S(1)}, u32[]{:S(2)}, u32[]{:S(2)}) collective-permute-start(f32[1,384,384]{2,1,0:T(8,128)S(1)} %shard_map.245.part_ref), channel_id=1, source_target_pairs={{0,1},{1,0},{2,3},{3,2},{4,5},{5,4},{6,7},{7,6},{8,9},{9,8},{10,11... | collective-permute-start | bytes 1769480 | tf_op jit(solution)/shard_map/ppermute | solution.py:784
  389.4 4.4 collective-permute-start.37
  393.8 6.9 %collective-permute-done.28.b_ref = f32[1,96,896]{2,1,0:T(8,128)S(1)} collective-permute-done((f32[1,96,896]{2,1,0:T(8,128)S(1)}, f32[1,96,896]{2,1,0:T(8,128)S(1)}, u32[]{:S(2)}, u32[]{:S(2)}) %collective-permute-start.28) | collective-permute-done | bytes 344096 | tf_op jit(solution)/shard_map/ppermute | solution.py:784
  406.4 20.9 %collective-permute-done.35.b_ref = f32[1,96,768]{2,1,0:T(8,128)S(1)} collective-permute-done((f32[1,96,768]{2,1,0:T(8,128)S(1)}, f32[1,96,768]{2,1,0:T(8,128)S(1)}, u32[]{:S(2)}, u32[]{:S(2)}) %collective-permute-start.35) | collective-permute-done | bytes 294944 | tf_op jit(solution)/shard_map/ppermute | solution.py:784
  438.3 8.9 %collective-permute-done.39.b_ref = f32[1,96,768]{2,1,0:T(8,128)S(1)} collective-permute-done((f32[1,96,768]{2,1,0:T(8,128)S(1)}, f32[1,96,768]{2,1,0:T(8,128)S(1)}, u32[]{:S(2)}, u32[]{:S(2)}) %collective-permute-start.39) | collective-permute-done | bytes 294944 | tf_op jit(solution)/shard_map/ppermute | solution.py:784
  (255 shorter events, 142.7 us)
Async XLA Ops:
  122.8 36.1 %collective-permute-start.4 = (f32[4,768,384]{2,1,0:T(8,128)}, f32[4,768,384]{2,1,0:T(8,128)}, u32[]{:S(2)}, u32[]{:S(2)}) collective-permute-start(f32[4,768,384]{2,1,0:T(8,128)} %get-tuple-element.199), channel_id=1, source_target_pairs={{0,1},{1,0},{2,3},{3,2},{4,5},{5,4},{6,7},{7,6},{8,9},{9,8},{10,11... | collective-permute-start | bytes 14155784 | tf_op jit(solution)/shard_map/ppermute | solution.py:784
  135.7 60.4 %collective-permute-start.11 = (f32[4,192,1536]{2,1,0:T(8,128)}, f32[4,192,1536]{2,1,0:T(8,128)}, u32[]{:S(2)}, u32[]{:S(2)}) collective-permute-start(f32[4,192,1536]{2,1,0:T(8,128)} %bitcast.4), channel_id=1, source_target_pairs={{0,1},{1,0},{2,3},{3,2},{4,5},{5,4},{6,7},{7,6},{8,9},{9,8},{10,11... | collective-permute-start | bytes 14155784 | tf_op jit(solution)/shard_map/ppermute | solution.py:784
  191.7 78.6 %collective-permute-start.17 = (f32[4,192,896]{2,1,0:T(8,128)}, f32[4,192,896]{2,1,0:T(8,128)}, u32[]{:S(2)}, u32[]{:S(2)}) collective-permute-start(f32[4,192,896]{2,1,0:T(8,128)} %bitcast.6), channel_id=1, source_target_pairs={{0,1},{1,0},{2,3},{3,2},{4,5},{5,4},{6,7},{7,6},{8,9},{9,8},{10,11... | collective-permute-start | bytes 8257544 | tf_op jit(solution)/shard_map/ppermute | solution.py:784
  193.3 58.3 %collective-permute-start.7 = (f32[2,384,384]{2,1,0:T(8,128)}, f32[2,384,384]{2,1,0:T(8,128)S(1)}, u32[]{:S(2)}, u32[]{:S(2)}) collective-permute-start(f32[2,384,384]{2,1,0:T(8,128)} %get-tuple-element.208), channel_id=1, source_target_pairs={{0,8},{8,0},{16,24},{24,16},{1,9},{9,1},{17,25},{25,17},{2,10},{10... | collective-permute-start | bytes 3538952 | tf_op jit(solution)/shard_map/ppermute | solution.py:784
  194.6 58.1 %collective-permute-start.8 = (f32[2,384,384]{2,1,0:T(8,128)}, f32[2,384,384]{2,1,0:T(8,128)S(1)}, u32[]{:S(2)}, u32[]{:S(2)}) collective-permute-start(f32[2,384,384]{2,1,0:T(8,128)} %get-tuple-element.210), channel_id=1, source_target_pairs={{0,16},{8,24},{16,0},{24,8},{1,17},{9,25},{17,1},{25,9},{2,18},{10... | collective-permute-start | bytes 3538952 | tf_op jit(solution)/shard_map/ppermute | solution.py:784
  195.8 42.6 %collective-permute-start.10 = (f32[4,392,128]{2,1,0:T(8,128)}, f32[4,392,128]{2,1,0:T(8,128)}, u32[]{:S(2)}, u32[]{:S(2)}) collective-permute-start(f32[4,392,128]{2,1,0:T(8,128)} %get-tuple-element.206), channel_id=1, source_target_pairs={{0,8},{8,0},{16,24},{24,16},{1,9},{9,1},{17,25},{25,17},{2,10},{10... | collective-permute-start | bytes 2408456 | tf_op jit(solution)/shard_map/ppermute | solution.py:784
  196.1 43.3 %collective-permute-start.9 = (f32[4,392,128]{2,1,0:T(8,128)}, f32[4,392,128]{2,1,0:T(8,128)}, u32[]{:S(2)}, u32[]{:S(2)}) collective-permute-start(f32[4,392,128]{2,1,0:T(8,128)} %get-tuple-element.205), channel_id=1, source_target_pairs={{0,16},{8,24},{16,0},{24,8},{1,17},{9,25},{17,1},{25,9},{2,18},{10... | collective-permute-start | bytes 2408456 | tf_op jit(solution)/shard_map/ppermute | solution.py:784
  267.5 51.1 %collective-permute-start.12 = (f32[4,192,768]{2,1,0:T(8,128)}, f32[4,192,768]{2,1,0:T(8,128)S(1)}, u32[]{:S(2)}, u32[]{:S(2)}) collective-permute-start(f32[4,192,768]{2,1,0:T(8,128)} %bitcast.9), channel_id=1, source_target_pairs={{0,1},{1,0},{2,3},{3,2},{4,5},{5,4},{6,7},{7,6},{8,9},{9,8},{10,11... | collective-permute-start | bytes 7077896 | tf_op jit(solution)/shard_map/ppermute | solution.py:784
  268.6 45.3 %collective-permute-start.13 = (f32[2,96,1536]{2,1,0:T(8,128)}, f32[2,96,1536]{2,1,0:T(8,128)S(1)}, u32[]{:S(2)}, u32[]{:S(2)}) collective-permute-start(f32[2,96,1536]{2,1,0:T(8,128)} %get-tuple-element.220), channel_id=1, source_target_pairs={{0,8},{8,0},{16,24},{24,16},{1,9},{9,1},{17,25},{25,17},{2,10},{10... | collective-permute-start | bytes 3538952 | tf_op jit(solution)/shard_map/ppermute | solution.py:784
  268.8 46.3 %collective-permute-start.14 = (f32[2,96,1536]{2,1,0:T(8,128)}, f32[2,96,1536]{2,1,0:T(8,128)}, u32[]{:S(2)}, u32[]{:S(2)}) collective-permute-start(f32[2,96,1536]{2,1,0:T(8,128)} %get-tuple-element.222), channel_id=1, source_target_pairs={{0,16},{8,24},{16,0},{24,8},{1,17},{9,25},{17,1},{25,9},{2,18},{10... | collective-permute-start | bytes 3538952 | tf_op jit(solution)/shard_map/ppermute | solution.py:784
  270.1 39.0 %collective-permute-start.15 = (f32[1,384,384]{2,1,0:T(8,128)}, f32[1,384,384]{2,1,0:T(8,128)}, u32[]{:S(2)}, u32[]{:S(2)}) collective-permute-start(f32[1,384,384]{2,1,0:T(8,128)} %get-tuple-element.231), channel_id=1, source_target_pairs={{0,16},{8,24},{16,0},{24,8},{1,17},{9,25},{17,1},{25,9},{2,18},{10... | collective-permute-start | bytes 1769480 | tf_op jit(solution)/shard_map/ppermute | solution.py:784
  270.3 38.8 %collective-permute-start.16 = (f32[1,384,384]{2,1,0:T(8,128)}, f32[1,384,384]{2,1,0:T(8,128)}, u32[]{:S(2)}, u32[]{:S(2)}) collective-permute-start(f32[1,384,384]{2,1,0:T(8,128)} %get-tuple-element.233), channel_id=1, source_target_pairs={{0,8},{8,0},{16,24},{24,16},{1,9},{9,1},{17,25},{25,17},{2,10},{10... | collective-permute-start | bytes 1769480 | tf_op jit(solution)/shard_map/ppermute | solution.py:784
  313.9 25.1 %collective-permute-start.19 = (f32[2,96,896]{2,1,0:T(8,128)}, f32[2,96,896]{2,1,0:T(8,128)}, u32[]{:S(2)}, u32[]{:S(2)}) collective-permute-start(f32[2,96,896]{2,1,0:T(8,128)} %get-tuple-element.241), channel_id=1, source_target_pairs={{0,16},{8,24},{16,0},{24,8},{1,17},{9,25},{17,1},{25,9},{2,18},{10... | collective-permute-start | bytes 2064392 | tf_op jit(solution)/shard_map/ppermute | solution.py:784
  318.4 25.0 %collective-permute-start.26 = (f32[1,96,1536]{2,1,0:T(8,128)}, f32[1,96,1536]{2,1,0:T(8,128)}, u32[]{:S(2)}, u32[]{:S(2)}) collective-permute-start(f32[1,96,1536]{2,1,0:T(8,128)} %get-tuple-element.249), channel_id=1, source_target_pairs={{0,16},{8,24},{16,0},{24,8},{1,17},{9,25},{17,1},{25,9},{2,18},{10... | collective-permute-start | bytes 1769480 | tf_op jit(solution)/shard_map/ppermute | solution.py:784
  318.6 24.7 %collective-permute-start.27 = (f32[1,96,1536]{2,1,0:T(8,128)}, f32[1,96,1536]{2,1,0:T(8,128)}, u32[]{:S(2)}, u32[]{:S(2)}) collective-permute-start(f32[1,96,1536]{2,1,0:T(8,128)} %get-tuple-element.251), channel_id=1, source_target_pairs={{0,8},{8,0},{16,24},{24,16},{1,9},{9,1},{17,25},{25,17},{2,10},{10... | collective-permute-start | bytes 1769480 | tf_op jit(solution)/shard_map/ppermute | solution.py:784
  326.2 27.7 %collective-permute-start.24 = (f32[2,96,768]{2,1,0:T(8,128)}, f32[2,96,768]{2,1,0:T(8,128)S(1)}, u32[]{:S(2)}, u32[]{:S(2)}) collective-permute-start(f32[2,96,768]{2,1,0:T(8,128)} %get-tuple-element.254), channel_id=1, source_target_pairs={{0,8},{8,0},{16,24},{24,16},{1,9},{9,1},{17,25},{25,17},{2,10},{10... | collective-permute-start | bytes 1769480 | tf_op jit(solution)/shard_map/ppermute | solution.py:784
  339.0 27.9 %collective-permute-start.23 = (f32[1,384,384]{2,1,0:T(8,128)S(1)}, f32[1,384,384]{2,1,0:T(8,128)S(1)}, u32[]{:S(2)}, u32[]{:S(2)}) collective-permute-start(f32[1,384,384]{2,1,0:T(8,128)S(1)} %shard_map.241.a_ref), channel_id=1, source_target_pairs={{0,4},{1,5},{2,6},{3,7},{4,0},{5,1},{6,2},{7,3},{8,12},{9,13},{10,... | collective-permute-start | bytes 1769480 | tf_op jit(solution)/shard_map/ppermute | solution.py:784
  368.6 32.1 %collective-permute-start.36 = (f32[1,96,1536]{2,1,0:T(8,128)S(1)}, f32[1,96,1536]{2,1,0:T(8,128)S(1)}, u32[]{:S(2)}, u32[]{:S(2)}) collective-permute-start(f32[1,96,1536]{2,1,0:T(8,128)S(1)} %shard_map.247.a_ref), channel_id=1, source_target_pairs={{0,4},{1,5},{2,6},{3,7},{4,0},{5,1},{6,2},{7,3},{8,12},{9,13},{10,... | collective-permute-start | bytes 1769480 | tf_op jit(solution)/shard_map/ppermute | solution.py:784
  371.8 28.9 %collective-permute-start.28 = (f32[1,96,896]{2,1,0:T(8,128)S(1)}, f32[1,96,896]{2,1,0:T(8,128)S(1)}, u32[]{:S(2)}, u32[]{:S(2)}) collective-permute-start(f32[1,96,896]{2,1,0:T(8,128)S(1)} %get-tuple-element.280), channel_id=1, source_target_pairs={{0,2},{1,3},{2,0},{3,1},{4,6},{5,7},{6,4},{7,5},{8,10},{9,11},{10,... | collective-permute-start | bytes 1032200 | tf_op jit(solution)/shard_map/ppermute | solution.py:784
  377.7 53.6 %collective-permute-start.34 = (f32[1,384,384]{2,1,0:T(8,128)S(1)}, f32[1,384,384]{2,1,0:T(8,128)S(1)}, u32[]{:S(2)}, u32[]{:S(2)}) collective-permute-start(f32[1,384,384]{2,1,0:T(8,128)S(1)} %shard_map.245.part_ref), channel_id=1, source_target_pairs={{0,1},{1,0},{2,3},{3,2},{4,5},{5,4},{6,7},{7,6},{8,9},{9,8},{10,11... | collective-permute-start | bytes 1769480 | tf_op jit(solution)/shard_map/ppermute | solution.py:784
  389.4 44.1 %collective-permute-start.37 = (f32[1,384,384]{2,1,0:T(8,128)S(1)}, f32[1,384,384]{2,1,0:T(8,128)S(1)}, u32[]{:S(2)}, u32[]{:S(2)}) collective-permute-start(f32[1,384,384]{2,1,0:T(8,128)S(1)} %collective-permute-done.29.got_ref), channel_id=1, source_target_pairs={{0,1},{1,0},{2,3},{3,2},{4,5},{5,4},{6,7},{7,6},{8,9},{9,8},{10,11... | collective-permute-start | bytes 1769480 | tf_op jit(solution)/shard_map/ppermute | solution.py:784
  400.8 34.9 %collective-permute-start.40 = (f32[1,96,1536]{2,1,0:T(8,128)S(1)}, f32[1,96,1536]{2,1,0:T(8,128)S(1)}, u32[]{:S(2)}, u32[]{:S(2)}) collective-permute-start(f32[1,96,1536]{2,1,0:T(8,128)S(1)} %shard_map.250.part_ref), channel_id=1, source_target_pairs={{0,2},{1,3},{2,0},{3,1},{4,6},{5,7},{6,4},{7,5},{8,10},{9,11},{10,... | collective-permute-start | bytes 1769480 | tf_op jit(solution)/shard_map/ppermute | solution.py:784
  403.1 32.6 %collective-permute-start.33 = (f32[1,96,896]{2,1,0:T(8,128)S(1)}, f32[1,96,896]{2,1,0:T(8,128)S(1)}, u32[]{:S(2)}, u32[]{:S(2)}) collective-permute-start(f32[1,96,896]{2,1,0:T(8,128)S(1)} %shard_map.249.a_ref), channel_id=1, source_target_pairs={{0,4},{1,5},{2,6},{3,7},{4,0},{5,1},{6,2},{7,3},{8,12},{9,13},{10,... | collective-permute-start | bytes 1032200 | tf_op jit(solution)/shard_map/ppermute | solution.py:784
  427.3 24.8 %collective-permute-start.43 = (f32[1,96,1536]{2,1,0:T(8,128)S(1)}, f32[1,96,1536]{2,1,0:T(8,128)S(1)}, u32[]{:S(2)}, u32[]{:S(2)}) collective-permute-start(f32[1,96,1536]{2,1,0:T(8,128)S(1)} %shard_map.250.part_ref), channel_id=1, source_target_pairs={{0,1},{1,0},{2,3},{3,2},{4,5},{5,4},{6,7},{7,6},{8,9},{9,8},{10,11... | collective-permute-start | bytes 1769480 | tf_op jit(solution)/shard_map/ppermute | solution.py:784
  (85 other events, 953.2 us)

commit v4 on v3

--- a/solution.py
+++ b/solution.py
@@ -1,3 +1,5 @@
+from functools import partial
+
 import jax
 import jax.numpy as jnp
 from jax import lax
@@ -16,7 +18,7 @@
 half_pi = 1.5707963267948966
 norm_eps = 1e-05
 VMEM_LIMIT = 60 * 1024 * 1024
-LIGHT_LIMIT = 32 * 1024 * 1024
+SMALL_LIMIT = 20 * 1024 * 1024
 
 NN = (((1,), (0,)), ((), ()))
 NT = (((1,), (1,)), ((), ()))
@@ -120,7 +122,7 @@
 
 
 def project_kernel(
-    place_ref,
+    s_ref,
     lens_ref,
     tok_ref,
     wk_ref,
@@ -145,7 +147,7 @@
 
     tok_t = tok_ref[0].T
     tok_t_ref[...] = tok_t
-    table = make_table(place_ref[0], lens_ref, row, tok_t.shape[1])
+    table = make_table(s_ref[PLACE] * tok_t.shape[1], lens_ref, row, tok_t.shape[1])
     tab_ref[0] = table
     soft, sig = softplus_sigmoid(mm(w_t[0], tok_t))
     key_t = soft.astype(bf16)
@@ -183,6 +185,7 @@
 
 
 def local_kernel(
+    s_ref,
     tab_ref,
     tok_t_ref,
     k_ref,
@@ -258,6 +261,7 @@
 
 
 def layer_kernel(
+    s_ref,
     tab_ref,
     q_t_ref,
     numer_ref,
@@ -378,6 +382,7 @@
 
 
 def local_back_kernel(
+    s_ref,
     tab_ref,
     q_t_ref,
     k_t_ref,
@@ -422,6 +427,7 @@
 
 
 def tail_kernel(
+    s_ref,
     tab_ref,
     k_t_ref,
     v_t_ref,
@@ -445,32 +451,56 @@
         grad_kv_ref[1, rows, :] = (grad_v_in[rows, :] + mm(state[:HEAD_DIM], keys)).astype(bf16)
 
 
-def token_kernel(gq_ref, gkv_ref, base_ref, wq_ref, wk_ref, wv_ref, out_ref):
+def token_kernel(s_ref, gq_ref, gkv_ref, base_ref, wq_ref, wk_ref, wv_ref, out_ref):
     total = base_ref[...] + mm(wq_ref[...], gq_ref[...])
     total = total + mm(wk_ref[...], gkv_ref[0])
     total = total + mm(wv_ref[...], gkv_ref[1])
     out_ref[0] = total.T
 
 
+def in_hbm(v):
+    return pltpu.with_memory_space_constraint(v, pltpu.HBM)
+
+
 def spec(block, index):
     return pl.BlockSpec(block, index)
 
 
-def light(kernel, grid, ins, outs, scalars, *args):
-    return pl.pallas_call(
-        kernel,
-        grid_spec=pltpu.PrefetchScalarGridSpec(
-            num_scalar_prefetch=1,
-            grid=grid,
-            in_specs=ins,
-            out_specs=[o for o, _ in outs],
-        ),
-        out_shape=[jax.ShapeDtypeStruct(shape, f32) for _, shape in outs],
-        compiler_params=pltpu.CompilerParams(
-            dimension_semantics=("arbitrary",) * len(grid), vmem_limit_bytes=LIGHT_LIMIT
-        ),
-        cost_estimate=pl.CostEstimate(flops=1, bytes_accessed=1, transcendentals=0),
-    )(scalars, *args)
+CORE, ODD, PLACE = range(3)
+
+
+class Order:
+    def __init__(self, scalars):
+        self.scalars = scalars
+
+    def call(self, kernel, grid, ins, outs, scratch, args, extra=(), free=(), limit=VMEM_LIMIT):
+        count = 1 + len(extra)
+        placed = len(scratch)
+
+        def stepped(*refs):
+            s_ref, handed = refs[0], refs[len(refs) - placed - 1]
+            rest = refs[: len(refs) - placed - 1] + refs[len(refs) - placed :]
+            kernel(*rest)
+            for i in range(s_ref.shape[0]):
+                handed[i] = s_ref[i]
+
+        *values, self.scalars = pl.pallas_call(
+            stepped,
+            grid_spec=pltpu.PrefetchScalarGridSpec(
+                num_scalar_prefetch=count,
+                grid=grid,
+                in_specs=ins,
+                out_specs=[o for o, _ in outs] + [pl.BlockSpec(memory_space=pltpu.SMEM)],
+                scratch_shapes=scratch,
+            ),
+            out_shape=[pltpu.HBM(shape, kind) for _, (shape, kind) in outs]
+            + [jax.ShapeDtypeStruct(self.scalars.shape, jnp.int32)],
+            compiler_params=pltpu.CompilerParams(
+                dimension_semantics=("arbitrary",) * len(grid), vmem_limit_bytes=limit
+            ),
+            cost_estimate=pl.CostEstimate(flops=1000000000000, bytes_accessed=1, transcendentals=0),
+        )(self.scalars, *extra, *[v if i in free else in_hbm(v) for i, v in enumerate(args)])
+        return values
 
 
 def pick_halves(core, value):
@@ -480,22 +510,15 @@
 
 
 def tall_kernel(s_ref, a_ref, b_ref, away_ref, keep_ref):
-    away_ref[0], keep_ref[0] = pick_halves(s_ref[0], mm(a_ref[...], b_ref[...], NT))
-
-
-def tall_product(core, shards, a, b):
+    away_ref[...], keep_ref[...] = pick_halves(s_ref[CORE], mm(a_ref[...], b_ref[...], NT))
+
+
+def tall_product(order, a, b):
     count, flat = a.shape
-    rows, cut = count // shards, b.shape[0] // 2
-    out = (spec((1, rows, cut), lambda i, s: (i, 0, 0)), (shards, rows, cut))
-    return light(
-        tall_kernel,
-        (shards,),
-        [spec((rows, flat), lambda i, s: (i, 0)), spec(b.shape, lambda i, s: (0, 0))],
-        [out, out],
-        core[None],
-        a,
-        b,
-    )
+    tile, cut = count // 4, b.shape[0] // 2
+    out = (spec((tile, cut), lambda i, *s: (i, 0)), ((count, cut), f32))
+    ins = [spec((tile, flat), lambda i, *s: (i, 0)), spec(b.shape, lambda i, *s: (0, 0))]
+    return order.call(tall_kernel, (4,), ins, [out, out], [], (a, b))
 
 
 def wide_kernel(s_ref, a_ref, b_ref, away_ref, keep_ref):
@@ -511,39 +534,29 @@
         keep_ref[...] = value
 
 
-def wide_product(core, shards, a, b):
+def wide_product(order, a, b):
     count, flat = a.shape
     cut = b.shape[0] // 2
     tile = 512
     half = cut // tile
 
     def source(i, s):
-        return jnp.where(i < half, (1 - s[0]) * half + i, s[0] * half + i - half), 0
+        return jnp.where(i < half, (1 - s[CORE]) * half + i, s[CORE] * half + i - half), 0
 
     outs = [
-        (spec((count, tile), lambda i, s: (0, jnp.minimum(i, half - 1))), (count, cut)),
-        (spec((count, tile), lambda i, s: (0, jnp.maximum(i - half, 0))), (count, cut)),
+        (spec((count, tile), lambda i, s: (0, jnp.minimum(i, half - 1))), ((count, cut), f32)),
+        (spec((count, tile), lambda i, s: (0, jnp.maximum(i - half, 0))), ((count, cut), f32)),
     ]
-    return [
-        v.reshape(shards, count // shards, cut)
-        for v in light(
-            wide_kernel,
-            (2 * half,),
-            [spec(a.shape, lambda i, s: (0, 0)), spec((tile, flat), source)],
-            outs,
-            core[None],
-            a,
-            b,
-        )
-    ]
+    ins = [spec(a.shape, lambda i, s: (0, 0)), spec((tile, flat), source)]
+    return order.call(wide_kernel, (2 * half,), ins, outs, [], (a, b))
 
 
 def twin_kernel(s_ref, a_ref, b_ref, c_ref, d_ref, *refs):
+    core = s_ref[CORE]
     away_ref, keep_ref = refs[-2:]
-    core = s_ref[0]
     at = 0
-    for left, right in ((a_ref, b_ref), (c_ref, d_ref)):
-        away, keep = pick_halves(core, mm(left[...], right[...].reshape(right.shape[-2:]), NT))
+    for left, right in ((a_ref, b_ref[0]), (c_ref, d_ref[0])):
+        away, keep = pick_halves(core, mm(left[...], right, NT))
         away_ref[:, at : at + away.shape[1]] = away
         keep_ref[:, at : at + keep.shape[1]] = keep
         at += away.shape[1]
@@ -553,28 +566,20 @@
         keep_ref[:, at:] = jnp.where(core == 0, value, 0.0)
 
 
-def twin_product(core, shards, a, b, c, d, small=None):
+def twin_product(order, a, b, c, d, small=None):
     count, flat = a.shape
     tile = count // 2
-
-    def full(v):
-        if isinstance(v, tuple):
-            return spec((1,) + v[0].shape[1:], lambda i, s, g=v[1]: (g, 0, 0)), v[0]
-        return spec(v.shape, lambda i, s: (0, 0)), v
-
+    columns = count + (0 if small is None else small.shape[1])
     rows = spec((tile, flat), lambda i, s: (i, 0))
-    (b_spec, b), (d_spec, d) = full(b), full(d)
-    ins, args = [rows, b_spec, rows, d_spec], [a, b, c, d]
-    columns = (b.shape[-2] + d.shape[-2]) // 2
+    ins, args = [], []
+    for left, (right, group) in ((a, b), (c, d)):
+        ins += [rows, spec((1, count, flat), lambda i, s, g=group: (g, 0, 0))]
+        args += [left, right]
     if small is not None:
         ins.append(spec((tile, small.shape[1]), lambda i, s: (i, 0)))
         args.append(small)
-        columns += small.shape[1]
-    out = (spec((tile, columns), lambda i, s: (i, 0)), (count, columns))
-    return [
-        v.reshape(shards, count // shards, columns)
-        for v in light(twin_kernel, (2,), ins, [out, out], core[None], *args)
-    ]
+    out = (spec((tile, columns), lambda i, s: (i, 0)), ((count, columns), f32))
+    return order.call(twin_kernel, (2,), ins, [out, out], [], args)
 
 
 def route_kernel(s_ref, *refs):
@@ -582,7 +587,7 @@
         refs[8 + i][...] = refs[2 * i][...] + refs[2 * i + 1][...]
 
 
-def route(left, right, low_bit, high_bit):
+def route(order, left, right, low_bit, high_bit):
     (a, b), (c, d) = left, right
     shards, rows, columns = a.shape
     same = a is c
@@ -593,14 +598,14 @@
 
     def by_low(flip):
         def index(i, s):
-            mine = s[0]
+            mine = (s[PLACE] >> low_bit) & 1
             return 2 * i + ((1 - mine) if flip else mine), 0, 0
 
         return index
 
     def by_high(flip):
         def index(i, s):
-            mine = s[1]
+            mine = (s[PLACE] >> high_bit) & 1
             return i + ((1 - mine) if flip else mine) * half, lower, 0
 
         return index
@@ -608,92 +613,104 @@
     block = (1, rows, columns)
     maps = [by_low(True), by_low(False), by_high(True), by_high(False)]
     ins = [spec(block, m) for m in maps for _ in range(2)]
-    out = (spec(block, lambda i, s: (i, 0, 0)), (half, rows, columns))
-    return light(
-        route_kernel,
-        (half,),
-        ins,
-        [out] * 4,
-        jnp.stack([low_bit, high_bit]),
-        a,
-        b,
-        a,
-        b,
-        c,
-        d,
-        c,
-        d,
+    out = (spec(block, lambda i, s: (i, 0, 0)), ((half, rows, columns), f32))
+    return order.call(route_kernel, (half,), ins, [out] * 4, [], (a, b, a, b, c, d, c, d))
+
+
+def choose_kernel(s_ref, a_ref, b_ref, c_ref, d_ref, away_ref, kept_ref):
+    upper, lower = a_ref[0] + b_ref[0], c_ref[0] + d_ref[0]
+    odd = s_ref[ODD] == 1
+    away_ref[...] = jnp.where(odd, upper, lower)
+    kept_ref[...] = jnp.where(odd, lower, upper)
+
+
+def choose(order, left, right):
+    shape = left[0].shape[1:]
+    whole = spec((1,) + shape, lambda i, s: (0, 0, 0))
+    out = (spec(shape, lambda i, s: (0, 0)), (shape, f32))
+    return order.call(
+        choose_kernel,
+        (1,),
+        [whole] * 4,
+        [out] * 2,
+        [],
+        (*left, *right),
+        free=(1, 3),
+        limit=SMALL_LIMIT,
     )
-
-
-def choose_kernel(s_ref, a_ref, b_ref, c_ref, d_ref, away_ref, keep_ref):
-    upper, lower = a_ref[...] + b_ref[...], c_ref[...] + d_ref[...]
-    odd = s_ref[0] == 1
-    away_ref[...] = jnp.where(odd, upper, lower)
-    keep_ref[...] = jnp.where(odd, lower, upper)
-
-
-def choose(left, right, odd):
-    shape = left[0].shape
-    whole = spec(shape, lambda i, s: (0, 0, 0))
-    return light(choose_kernel, (1,), [whole] * 4, [(whole, shape)] * 2, odd[None], *left, *right)
 
 
 def add_kernel(s_ref, a_ref, b_ref, out_ref):
     out_ref[...] = a_ref[...] + b_ref[...]
 
 
-def add(a, b):
-    whole = spec(a.shape, lambda i, s: (0,) * a.ndim)
-    return light(add_kernel, (1,), [whole] * 2, [(whole, a.shape)], jnp.zeros((1,), jnp.int32), a, b)[0]
-
-
-def join_kernel(s_ref, part_ref, got_ref, other_part_ref, other_got_ref, *outs):
-    odd, first = s_ref[0] == 1, s_ref[1] == 0
-    rows = part_ref.shape[1]
-    for upper in (True, False):
-        swapped = odd if upper else jnp.logical_not(odd)
-        mine = jnp.where(swapped, got_ref[0], part_ref[0])
-        other = jnp.where(swapped, other_got_ref[0], other_part_ref[0])
-        low, high = jnp.where(first, mine, other), jnp.where(first, other, mine)
-        lines = slice(0, rows) if upper else slice(rows, 2 * rows)
-        at = 0
-        for out in outs:
-            cut = out.shape[1] // 2
-            if cut < 128:
-                out[lines, :] = low[:, at:]
-            else:
-                out[lines, :cut] = low[:, at : at + cut]
-                out[lines, cut:] = high[:, at : at + cut]
-            at += cut
-
-
-def join(odd, core, part, got, other_part, other_got, widths):
-    rows = 2 * part.shape[1]
-    whole = spec(part.shape, lambda i, s: (0, 0, 0))
-    outs = [(spec((rows, w), lambda i, s: (0, 0)), (rows, w)) for w in widths]
-    return light(
-        join_kernel,
-        (1,),
-        [whole] * 4,
-        outs,
-        jnp.stack([odd, core]),
-        part,
-        got,
-        other_part,
-        other_got,
+def add(order, a, b):
+    whole = spec(a.shape, lambda i, s: (0, 0))
+    return order.call(
+        add_kernel, (1,), [whole] * 2, [(whole, (a.shape, f32))], [], (a, b), free=(1,), limit=SMALL_LIMIT
+    )[0]
+
+
+def merge_kernel(s_ref, kept_ref, got_ref, out_ref):
+    odd = s_ref[ODD] == 1
+    rows = kept_ref.shape[0]
+    kept, got = kept_ref[...], got_ref[...]
+    out_ref[:rows, :] = jnp.where(odd, got, kept)
+    out_ref[rows:, :] = jnp.where(odd, kept, got)
+
+
+def merge(order, kept, got):
+    rows, columns = kept.shape
+    whole = spec((rows, columns), lambda i, s: (0, 0))
+    out = (spec((2 * rows, columns), lambda i, s: (0, 0)), ((2 * rows, columns), f32))
+    return order.call(
+        merge_kernel, (1,), [whole] * 2, [out], [], (kept, got), free=(1,), limit=SMALL_LIMIT
+    )[0]
+
+
+def side_kernel(s_ref, mine_ref, other_ref, *outs):
+    first = s_ref[CORE] == 0
+    at = 0
+    for out in outs:
+        cut = out.shape[1] // 2
+        if cut < 128:
+            out[...] = jnp.where(first, mine_ref[:, at:], other_ref[:, at:])
+            break
+        mine, other = mine_ref[:, at : at + cut], other_ref[:, at : at + cut]
+        out[:, :cut] = jnp.where(first, mine, other)
+        out[:, cut:] = jnp.where(first, other, mine)
+        at += cut
+
+
+def side(order, mine, other, widths):
+    whole = spec(mine.shape, lambda i, s: (0, 0))
+    outs = [(spec((mine.shape[0], w), lambda i, s: (0, 0)), ((mine.shape[0], w), f32)) for w in widths]
+    return order.call(
+        side_kernel, (1,), [whole] * 2, outs, [], (mine, other), free=(1,), limit=SMALL_LIMIT
     )
 
 
-def mix_kernel(s_ref, *refs):
+def mix_kernel(first, s_ref, w_ref, *refs):
     row = pl.program_id(0)
     for i in range(2):
-        refs[4 + i][...] = s_ref[2 * i, row] * refs[2 * i][...] + s_ref[2 * i + 1, row] * refs[2 * i + 1][...]
-
-
-def mix(weights, a, b, c, d):
-    block = spec((1,) + a.shape[1:], lambda r, s: (r, 0, 0))
-    return light(mix_kernel, (a.shape[0],), [block] * 4, [(block, a.shape)] * 2, weights, a, b, c, d)
+        own, other = (w_ref[first + 2 * i + j, row] for j in range(2))
+        refs[4 + i][...] = own * refs[2 * i][...] + other * refs[2 * i + 1][...]
+
+
+def mix(order, weights, first, *parts):
+    shape = parts[0].shape
+    block = spec((1,) + shape[1:], lambda r, *s: (r, 0, 0))
+    return order.call(
+        partial(mix_kernel, first),
+        (shape[0],),
+        [block] * 4,
+        [(block, (shape, f32))] * 2,
+        [],
+        parts,
+        (weights,),
+        free=range(4),
+        limit=SMALL_LIMIT,
+    )
 
 
 def first_begins(lengths, count, tok_count):
@@ -713,24 +730,9 @@
     return out
 
 
-class Order:
-    def __init__(self):
-        self.last = None
-
-    def tie(self, value):
-        if self.last is None:
-            return value
-        return lax.optimization_barrier((value, self.last))[0]
-
-    def done(self, value):
-        self.last = value
-        return value
-
-
-def entering(order, parts, begin_first, tok_count, reverse):
+def weights_of(begin_first, tok_count, reverse):
     count = lax.axis_size("seq")
     place = lax.axis_index("seq")
-    part_a, part_b = parts
 
     def covers(i, j):
         low, high = (count - 1 - j, count - 1 - i) if reverse else (i, j)
@@ -741,42 +743,39 @@
         mine = begin_first.T if reverse else begin_first[:, place][None]
         reach = (place if reverse else spots[:, None]) + 1
         ahead = (spots > place) if reverse else (spots < place)
-        weight = ((mine < reach * tok_count) & ahead[:, None]).astype(f32)
+        return ((mine < reach * tok_count) & ahead[:, None]).astype(f32)
+    index = count - 1 - place if reverse else place
+    zero = jnp.zeros_like(begin_first[:, 0], f32)
+    one = zero + 1.0
+    m02, m03, m13 = covers(0, 2), covers(0, 3), covers(1, 3)
+    onward = [
+        pick(index, [m02, m13, zero, zero]),
+        pick(index, [one, m03, zero, zero]),
+        pick(index, [one, zero, one, zero]),
+        pick(index, [zero, zero, m03, one]),
+    ]
+    final = [
+        pick(index, [zero, one, zero, one]),
+        pick(index, [zero, zero, one, one]),
+        pick(index, [zero, zero, m02, m13]),
+        pick(index, [zero, one, one, one]),
+    ]
+    return onward + final
+
+
+def entering(order, parts, weights, first):
+    if lax.axis_size("seq") != 4:
         gathered = [lax.all_gather(p, "seq") for p in parts]
         yield
         yield
-        yield tuple(jnp.sum(g * weight[:, :, None, None], axis=0) for g in gathered)
-    index = count - 1 - place if reverse else place
-
-    zero = jnp.zeros_like(begin_first[:, 0], f32)
-    one = zero + 1.0
-    m02, m03, m13 = covers(0, 2), covers(0, 3), covers(1, 3)
-    onward = jnp.stack(
-        [
-            pick(index, [m02, m13, zero, zero]),
-            pick(index, [one, m03, zero, zero]),
-            pick(index, [one, zero, one, zero]),
-            pick(index, [zero, zero, m03, one]),
-        ]
-    )
-    final = jnp.stack(
-        [
-            pick(index, [zero, one, zero, one]),
-            pick(index, [zero, zero, one, one]),
-            pick(index, [zero, zero, m02, m13]),
-            pick(index, [zero, one, one, one]),
-        ]
-    )
-    got_a = swap(part_a, "seq", 1)
-    got_b = swap(part_b, "seq", 2)
+        yield tuple(jnp.sum(g * weights[first][:, :, None, None], axis=0) for g in gathered)
+    part_a, part_b = parts
+    got_a, got_b = swap(part_a, "seq", 1), swap(part_b, "seq", 2)
     yield
-    got_a, got_b = order.tie((got_a, got_b))
-    next_a, next_b = order.done(mix(onward, part_a, got_a, part_b, got_b))
-    last_a = swap(next_a, "seq", 2)
-    last_b = swap(next_b, "seq", 1)
+    next_a, next_b = mix(order, weights, first, part_a, got_a, part_b, got_b)
+    last_a, last_b = swap(next_a, "seq", 2), swap(next_b, "seq", 1)
     yield
-    last_a, last_b = order.tie((last_a, last_b))
-    yield order.done(mix(final, got_a, last_a, got_b, last_b))
+    yield mix(order, weights, first + 4, got_a, last_a, got_b, last_b)
 
 
 def swap(value, axis, distance):
@@ -784,55 +783,47 @@
     return lax.ppermute(value, axis, [(i, i ^ distance) for i in range(count)])
 
 
-def reduced(order, core, away, keep, widths):
-    place = lax.axis_index("seq").astype(jnp.int32)
-    odd = ((lax.axis_index("batch") >> 1) & 1).astype(jnp.int32)
+def reduced(order, away, keep, widths):
     count = lax.axis_size("batch")
-    bits = keep.shape[0].bit_length() - 1
-    got = swap(away, "batch", 1)
+    shards = lax.axis_size("seq")
+    bits = shards.bit_length() - 1
+    shape = (shards, keep.shape[0] // shards, keep.shape[1])
+    got = swap(away, "batch", 1).reshape(shape)
     yield
-    left = right = (keep, order.tie(got))
+    left = right = (keep.reshape(shape), got)
     for step in range(bits):
         high = bits - 1 - step
-        away_l, keep_l, away_r, keep_r = order.done(
-            route(left, right, (place >> step) & 1, (place >> high) & 1)
-        )
-        got_l, got_r = swap(away_l, "seq", 1 << step), swap(away_r, "seq", 1 << high)
+        away_l, keep_l, away_r, keep_r = route(order, left, right, step, high)
+        left = keep_l, swap(away_l, "seq", 1 << step)
+        right = keep_r, swap(away_r, "seq", 1 << high)
         yield
-        got_l, got_r = order.tie((got_l, got_r))
-        left, right = (keep_l, got_l), (keep_r, got_r)
-    away, part = order.done(choose(left, right, odd))
+    away, kept = choose(order, left, right)
     got = swap(away, "batch", 2)
     distance = 4
+    while distance < count:
+        yield
+        kept = add(order, kept, got)
+        got = swap(kept, "batch", distance)
+        distance *= 2
     yield
-    part = order.done(add(part, order.tie(got)))
-    while distance < count:
-        got = swap(part, "batch", distance)
-        yield
-        part = order.done(add(part, order.tie(got)))
-        distance *= 2
-    got = swap(part, "batch", 2)
-    other_part = swap(part, "batch", 1)
+    kept = add(order, kept, got)
+    got = swap(kept, "batch", 2)
     yield
-    got = order.done(order.tie(got))
-    other_got = swap(got, "batch", 1)
+    merged = merge(order, kept, got)
+    other = swap(merged, "batch", 1)
     yield
-    yield order.done(join(odd, core, part, got, order.tie(other_part), other_got, widths))
-
-
-def call(kernel, grid, ins, outs, scratch, *args):
-    return pl.pallas_call(
-        kernel,
-        grid=grid,
-        in_specs=[s for s in ins],
-        out_specs=[s for s, _ in outs],
-        out_shape=[jax.ShapeDtypeStruct(shape, kind) for _, (shape, kind) in outs],
-        scratch_shapes=scratch,
-        compiler_params=pltpu.CompilerParams(
-            dimension_semantics=("arbitrary",) * len(grid), vmem_limit_bytes=VMEM_LIMIT
-        ),
-        cost_estimate=pl.CostEstimate(flops=1, bytes_accessed=1, transcendentals=0),
-    )(*args)
+    yield side(order, merged, other, widths)
+
+
+SCHEDULE = (
+    "in_product", "states", "back_product", "in", "states", "back",
+    "local", "mixed_product", "tail", "in", "back", "in",
+    "mixed", "back", "mixed", "back", "last_product", "mixed",
+    "last", "in", "back", "last", "mixed", "last",
+    "in", "back", "last", "tokens", "mixed", "back",
+    "last", "in", "mixed", "last", "in", "mixed",
+    "last",
+)
 
 
 def body(
@@ -854,51 +845,57 @@
     ff = w_in.shape[1]
     flat = rows * toks
     shards = lax.axis_size("seq")
-    place = (lax.axis_index("seq") * toks).astype(jnp.int32)
-    begin_first = first_begins(doc_lengths, shards, toks)
-    smem = pl.BlockSpec(memory_space=pltpu.SMEM)
     whole = pl.BlockSpec(memory_space=pltpu.VMEM)
-    token_major = pl.BlockSpec((1, toks, width), lambda r: (r, 0, 0))
-    table_spec = pl.BlockSpec((1, 8, toks), lambda r: (r, 0, 0))
-    state_spec = pl.BlockSpec((1, STATE_ROWS, 2 * HEAD_DIM), lambda r: (r, 0, 0))
+    token_major = pl.BlockSpec((1, toks, width), lambda r, *s: (r, 0, 0))
+    table_spec = pl.BlockSpec((1, 8, toks), lambda r, *s: (r, 0, 0))
+    state_spec = pl.BlockSpec((1, STATE_ROWS, 2 * HEAD_DIM), lambda r, *s: (r, 0, 0))
 
     def feature(count):
-        return pl.BlockSpec((count, toks), lambda r: (0, r))
+        return pl.BlockSpec((count, toks), lambda r, *s: (0, r))
 
     tok_low = (token_major, ((rows, toks, width), bf16))
     wide_low = (feature(width), ((width, flat), bf16))
     wide_full = (feature(width), ((width, flat), f32))
     ff_low = (feature(ff), ((ff, flat), bf16))
     head_rows = (feature(16), ((16, flat), f32))
-    fold = (pl.BlockSpec((width, 128), lambda r: (0, 0)), ((width, 128), f32))
+    fold = (pl.BlockSpec((width, 128), lambda r, *s: (0, 0)), ((width, 128), f32))
     state = (state_spec, ((rows, STATE_ROWS, 2 * HEAD_DIM), f32))
     grid = (rows,)
 
-    order = Order()
-    core = (lax.axis_index("batch") % 2).astype(jnp.int32)
-
-    def run(kernel, ins, outs, scratch, first, *args):
-        return order.done(call(kernel, grid, ins, outs, scratch, order.tie(first), *args))
+    batch_place = lax.axis_index("batch").astype(jnp.int32)
+    scalars = jnp.stack(
+        [batch_place & 1, (batch_place >> 1) & 1, lax.axis_index("seq").astype(jnp.int32)]
+    )
+    order = Order(scalars)
+
+    def run(kernel, ins, outs, scratch, *args, extra=()):
+        return order.call(kernel, grid, ins, outs, scratch, args, extra)
 
     def column(v):
         return v[:, None]
 
     table, tok_t, k_t, v_t, key, value, sig_k, state_a, state_b = run(
         project_kernel,
-        [smem, smem, token_major, whole, whole],
+        [token_major, whole, whole],
         [(table_spec, ((rows, 8, toks), f32))]
         + [wide_low] * 3
         + [tok_low] * 2
         + [wide_low]
         + [state] * 2,
         [pltpu.VMEM((2, width, width), bf16)],
-        place[None],
-        doc_lengths,
         tokens,
         w_key,
         w_value,
+        extra=(doc_lengths,),
     )
-    states = entering(order, (state_a, state_b), begin_first, toks, False)
+    begins = first_begins(doc_lengths, shards, toks)
+    if shards == 4:
+        weights = jnp.stack(weights_of(begins, toks, False) + weights_of(begins, toks, True))
+        later = 8
+    else:
+        weights = [weights_of(begins, toks, False), weights_of(begins, toks, True)]
+        later = 1
+    states = entering(order, (state_a, state_b), weights, 0)
     next(states)
     part = ff // rows
     q_t, sig_q, numer, denom_loc, w_out_t, w_in_t, w_back_t = run(
@@ -910,17 +907,17 @@
             feature(width),
             whole,
             whole,
-            pl.BlockSpec((width, part), lambda r: (0, r)),
-            pl.BlockSpec((part, width), lambda r: (r, 0)),
+            pl.BlockSpec((width, part), lambda r, *s: (0, r)),
+            pl.BlockSpec((part, width), lambda r, *s: (r, 0)),
         ],
         [
             wide_low,
             wide_low,
             wide_full,
             head_rows,
-            (pl.BlockSpec((width, width), lambda r: (0, 0)), ((width, width), bf16)),
-            (pl.BlockSpec((part, width), lambda r: (r, 0)), ((ff, width), bf16)),
-            (pl.BlockSpec((width, part), lambda r: (0, r)), ((width, ff), bf16)),
+            (pl.BlockSpec((width, width), lambda r, *s: (0, 0)), ((width, width), bf16)),
+            (pl.BlockSpec((part, width), lambda r, *s: (r, 0)), ((ff, width), bf16)),
+            (pl.BlockSpec((width, part), lambda r, *s: (0, r)), ((width, ff), bf16)),
         ],
         [pltpu.VMEM((width, width), bf16)],
         table,
@@ -1004,101 +1001,123 @@
         column(shift_two),
     )
 
-    def reduction(product, widths, first, *rest):
-        away, keep = order.done(product(core, shards, order.tie(first), *rest))
-        steps = reduced(order, core, away, keep, widths)
-        next(steps)
-        return steps
-
-    back_states = entering(order, (out_a, out_b), begin_first, toks, True)
+    back_states = entering(order, (out_a, out_b), weights, later)
     next(back_states)
-    back = reduction(tall_product, (width,), active_t, grad_second)
-    into = reduction(wide_product, (ff,), first_t, grad_hidden)
-    next(back_states)
-    next(back)
-    grad_qpre, grad_k_loc, grad_v_loc = run(
-        local_back_kernel,
-        [
-            table_spec,
-            feature(width),
-            feature(width),
-            token_major,
-            token_major,
-            feature(width),
-            feature(width),
-            feature(16),
-            state_spec,
-            state_spec,
-        ],
-        [wide_low, wide_full, wide_full],
-        [],
-        table,
-        q_t,
-        k_t,
-        key,
-        value,
-        sig_q,
-        grad_numer,
-        grad_denom,
-        in_a,
-        in_b,
-    )
-    mixed = reduction(
-        twin_product, (width, width, 128), att_t, grad_branch, tok_t, grad_qpre, small
-    )
-    next(into)
-    back_a, back_b = next(back_states)
-    (grad_kv,) = run(
-        tail_kernel,
-        [table_spec]
-        + [feature(width)] * 3
-        + [state_spec] * 2
-        + [feature(width)] * 2,
-        [(pl.BlockSpec((2, width, toks), lambda r: (0, 0, r)), ((2, width, flat), bf16))],
-        [],
-        table,
-        k_t,
-        v_t,
-        sig_k,
-        back_a,
-        back_b,
-        grad_k_loc,
-        grad_v_loc,
-    )
-    next(back)
-    last = reduction(twin_product, (width, width), tok_t, (grad_kv, 0), tok_t, (grad_kv, 1))
-    next(mixed)
-    next(back)
-    next(into)
-    next(last)
-    (grad_tokens,) = run(
-        token_kernel,
-        [
-            feature(width),
-            pl.BlockSpec((2, width, toks), lambda r: (0, 0, r)),
-            feature(width),
-        ]
-        + [whole] * 3,
-        [(token_major, ((rows, toks, width), f32))],
-        [],
-        grad_qpre,
-        grad_kv,
-        grad_base,
-        w_query,
-        w_key,
-        w_value,
-    )
-    pending = [back, mixed, into, last]
+    pieces, made = {}, {}
+
+    def begin(name, product, widths):
+        pieces[name] = reduced(order, *product, widths)
+        next(pieces[name])
+
+    def local_back():
+        made["query"], made["key"], made["value"] = run(
+            local_back_kernel,
+            [
+                table_spec,
+                feature(width),
+                feature(width),
+                token_major,
+                token_major,
+                feature(width),
+                feature(width),
+                feature(16),
+                state_spec,
+                state_spec,
+            ],
+            [wide_low, wide_full, wide_full],
+            [],
+            table,
+            q_t,
+            k_t,
+            key,
+            value,
+            sig_q,
+            grad_numer,
+            grad_denom,
+            in_a,
+            in_b,
+        )
+
+    def tail():
+        back_a, back_b = made["states"]
+        (made["kv"],) = run(
+            tail_kernel,
+            [table_spec]
+            + [feature(width)] * 3
+            + [state_spec] * 2
+            + [feature(width)] * 2,
+            [(pl.BlockSpec((2, width, toks), lambda r, *s: (0, 0, r)), ((2, width, flat), bf16))],
+            [],
+            table,
+            k_t,
+            v_t,
+            sig_k,
+            back_a,
+            back_b,
+            made["key"],
+            made["value"],
+        )
+
+    def token_grads():
+        (made["tokens"],) = run(
+            token_kernel,
+            [
+                feature(width),
+                pl.BlockSpec((2, width, toks), lambda r, *s: (0, 0, r)),
+                feature(width),
+            ]
+            + [whole] * 3,
+            [(token_major, ((rows, toks, width), f32))],
+            [],
+            made["query"],
+            made["kv"],
+            grad_base,
+            w_query,
+            w_key,
+            w_value,
+        )
+
+    def states_on():
+        made["states"] = next(back_states)
+
+    steps = {
+        "back_product": lambda: begin("back", tall_product(order, active_t, grad_second), (width,)),
+        "in_product": lambda: begin("in", wide_product(order, first_t, grad_hidden), (ff,)),
+        "mixed_product": lambda: begin(
+            "mixed",
+            twin_product(order, att_t, (grad_branch[None], 0), tok_t, (made["query"][None], 0), small),
+            (width, width, 128),
+        ),
+        "last_product": lambda: begin(
+            "last",
+            twin_product(order, tok_t, (made["kv"], 0), tok_t, (made["kv"], 1)),
+            (width, width),
+        ),
+        "states": states_on,
+        "local": local_back,
+        "tail": tail,
+        "tokens": token_grads,
+    }
     ends = {}
-    while pending:
-        for steps in list(pending):
-            value = next(steps)
-            if value is not None:
-                ends[id(steps)] = value
-                pending.remove(steps)
-    (total_back,), (total_in,) = ends[id(back)], ends[id(into)]
-    total_out, total_query, vectors = ends[id(mixed)]
-    total_key, total_value = ends[id(last)]
+
+    def step(name):
+        value = next(pieces[name])
+        if value is not None:
+            ends[name] = value
+
+    for name in SCHEDULE:
+        if name in steps:
+            steps[name]()
+        elif name not in ends:
+            step(name)
+    while len(ends) < len(pieces):
+        for name in pieces:
+            if name not in ends:
+                step(name)
+    (total_back,), (total_in,) = ends["back"], ends["in"]
+    total_out, total_query, vectors = ends["mixed"]
+    total_key, total_value = ends["last"]
+    grad_tokens = made["tokens"]
     return (
         layer_out,
         grad_tokens,

time: 463 us -> 395 us (0.85)
  waiting for transfers between devices: 173 us -> 42.3 us
  Pallas kernels: 178 us -> 266 us
  local copies, waits for them, and re-layouts: 44.3 us -> 16.9 us
    ppermute x48 -> x44, waiting for transfers between devices: 173 us -> 42.3 us  [swap(): return lax.ppermute(value, axis, [(i, i ^ distance) for i in range(count)])]
    pallas_call x38 -> x42, Pallas kernels: 178 us -> 266 us  [call(): pl.pallas_call(stepped, grid_spec=pltpu.PrefetchScalarGridSpec(num_scalar...]
    unnamed x122 -> x56, local copies, waits for them, and re-layouts: 39.5 us -> 11.1 us
    ppermute x48 -> x44, starting transfers between devices: 65 us -> 65.5 us  [swap(): return lax.ppermute(value, axis, [(i, i ^ distance) for i in range(count)])]
  transfers between devices with their start and end apart: 48 -> 44, of which waited for: 17 -> 14; matrix products, arithmetic and copies ran while one was open for 1% -> 2% of each run, Pallas kernels for 22% -> 48%
where the time goes in v4:
time: 395 us; the launch traced here: 394 us
  Pallas kernels  266 us (67%)
  starting transfers between devices  65.5 us (17%)
  waiting for transfers between devices  42.3 us (11%)
  local copies, waits for them, and re-layouts  16.9 us (4%)
    pallas_call x42, Pallas kernels, call(): pl.pallas_call(stepped, grid_spec=pltpu.PrefetchScalarGridSpec(num_scalar...  266 us
    ppermute x44, starting transfers between devices, swap(): return lax.ppermute(value, axis, [(i, i ^ distance) for i in range(count)])  65.5 us
    ppermute x44, waiting for transfers between devices, swap(): return lax.ppermute(value, axis, [(i, i ^ distance) for i in range(count)])  42.3 us
    unnamed x56, local copies, waits for them, and re-layouts  11.1 us
  transfers between devices with their start and end apart: 44, of which 14 were waited for; matrix products, arithmetic and copies ran while one was open for 2% of the time, Pallas kernels for 48%

profile of v4, /device:TPU:1, one launch (start us, length us, event | category | flops | bytes accessed | tf_op | source)
XLA Modules:
  0.0 393.5 jit_solution(4380326465027438889)
XLA Ops:
  1.2 10.6 %shard_map.220 = (f32[4,8,256]{2,1,0:T(8,128)}, bf16[768,1024]{1,0:T(8,128)(2,1)}, bf16[768,1024]{1,0:T(8,128)(2,1)}, bf16[768,1024]{1,0:T(8,128)(2,1)}, bf16[4,...) custom-call(s32[3]{0:T(128)} %pad_add_fusion.refs_0_, ...), custom_call_target="tpu_custom_call" | custom-call | flops 999999995904 | bytes 1 | tf_op jit(solution)/shard_map/pallas_call | solution.py:487
  15.2 18.4 %shard_map.221 = (bf16[768,1024]{1,0:T(8,128)(2,1)}, bf16[768,1024]{1,0:T(8,128)(2,1)}, f32[768,1024]{1,0:T(8,128)}, f32[16,1024]{1,0:T(8,128)}, bf16[768,768]{1...) custom-call(s32[3]{0:T(128)} %get-tuple-element.162.refs_0_, ...), custom_call_target="tpu_custom_call" | custom-call | flops 999999995904 | bytes 1 | tf_op jit(solution)/shard_map/pallas_call | solution.py:487
  35.2 4.4 %shard_map.222 = (f32[4,392,128]{2,1,0:T(8,128)}, f32[4,392,128]{2,1,0:T(8,128)}, s32[3]{0:T(128)S(1)}) custom-call(s32[3]{0:T(128)S(1)} %copy-done.11, f32[16,4]{1,0:T(8,128)S(1)} %stack.59.refs_1_, f32[4,392,128]{2,1,0:T(8,128)S(1)} %copy-done, f32[4,392,128]{2,1,0:T(8,128)} %collective-permute-done.refs_3_.refs_2_, f32[4,392,128]{2,1,0:T(8,128)S(1)} %copy-done.1, ...), custom_call_target="tpu_custom_call" | custom-call | flops 999999995904 | bytes 1 | tf_op jit(solution)/shard_map/pallas_call | solution.py:487
  43.5 14.4 %collective-permute-done.2.refs_3_ = f32[4,392,128]{2,1,0:T(8,128)S(1)} collective-permute-done((f32[4,392,128]{2,1,0:T(8,128)}, f32[4,392,128]{2,1,0:T(8,128)S(1)}, u32[]{:S(2)}, u32[]{:S(2)}) %collective-permute-start.2) | collective-permute-done | bytes 802848 | tf_op jit(solution)/shard_map/ppermute | solution.py:783
  57.9 4.4 %shard_map.223 = (f32[4,392,128]{2,1,0:T(8,128)}, f32[4,392,128]{2,1,0:T(8,128)}, s32[3]{0:T(128)S(1)}) custom-call(s32[3]{0:T(128)S(1)} %get-tuple-element.170.refs_0_, f32[16,4]{1,0:T(8,128)S(1)} %stack.59.refs_1_, f32[4,392,128]{2,1,0:T(8,128)} %collective-permute-done.refs_3_.refs_2_, f32[4,392,128]{2,1,0:T(8,128)S(1)} %collective-permute-done.2.refs_3_, ...), custom_call_target="tpu_custom_call" | custom-call | flops 999999995904 | bytes 1 | tf_op jit(solution)/shard_map/pallas_call | solution.py:487
  62.8 54.5 %shard_map.224 = (bf16[4,256,768]{2,1,0:T(8,128)(2,1)}, bf16[768,1024]{1,0:T(8,128)(2,1)}, bf16[768,1024]{1,0:T(8,128)(2,1)}, bf16[3072,1024]{1,0:T(8,128)(2,1)}...) custom-call(s32[3]{0:T(128)} %copy-done.6, ...), custom_call_target="tpu_custom_call" | custom-call | flops 999999995904 | bytes 1 | tf_op jit(solution)/shard_map/pallas_call | solution.py:487
  118.8 12.4 %shard_map.225 = (f32[768,1536]{1,0:T(8,128)}, f32[768,1536]{1,0:T(8,128)}, s32[3]{0:T(128)}) custom-call(s32[3]{0:T(128)} %get-tuple-element.183.refs_0_, bf16[768,1024]{1,0:T(8,128)(2,1)} %get-tuple-element.184.refs_1_, bf16[3072,1024]{1,0:T(8,128)(2,1)} %get-tuple-element.185.refs_2_), custom_call_target="tpu_custom_call" | custom-call | flops 999999995904 | bytes 1 | tf_op jit(solution)/shard_map/pallas_call | solution.py:487
  135.5 4.4 %shard_map.226 = (f32[4,392,128]{2,1,0:T(8,128)}, f32[4,392,128]{2,1,0:T(8,128)}, s32[3]{0:T(128)S(1)}) custom-call(s32[3]{0:T(128)S(1)} %copy-done.17, f32[16,4]{1,0:T(8,128)S(1)} %stack.59.refs_1_, f32[4,392,128]{2,1,0:T(8,128)S(1)} %copy-done.2, f32[4,392,128]{2,1,0:T(8,128)} %collective-permute-done.4.refs_3_.refs_2_, f32[4,392,128]{2,1,0:T(8,128)S(1)} %copy-done.3, ...), custom_call_target="tpu_custom_call" | custom-call | flops 999999995904 | bytes 1 | tf_op jit(solution)/shard_map/pallas_call | solution.py:487
  142.5 10.7 %shard_map.227 = (f32[3072,384]{1,0:T(8,128)}, f32[3072,384]{1,0:T(8,128)}, s32[3]{0:T(128)}) custom-call(s32[3]{0:T(128)} %copy-done.18, bf16[3072,1024]{1,0:T(8,128)(2,1)} %get-tuple-element.190.refs_1_, bf16[768,1024]{1,0:T(8,128)(2,1)} %get-tuple-element.191.refs_2_), custom_call_target="tpu_custom_call" | custom-call | flops 999999995904 | bytes 1 | tf_op jit(solution)/shard_map/pallas_call | solution.py:487
  157.4 6.6 %shard_map.228 = (f32[2,96,1536]{2,1,0:T(8,128)}, f32[2,96,1536]{2,1,0:T(8,128)}, f32[2,96,1536]{2,1,0:T(8,128)}, f32[2,96,1536]{2,1,0:T(8,128)}, s32[3]{0:T(128)}) custom-call(s32[3]{0:T(128)} %get-tuple-element.192.refs_0_, f32[4,192,1536]{2,1,0:T(8,128)} %bitcast.35, f32[4,192,1536]{2,1,0:T(8,128)} %bitcast.4.refs_2_.refs_4_.refs_6_.refs_8_, ...), custom_call_target="tpu_custom_call" | custom-call | flops 999999995904 | bytes 1 | tf_op jit(solution)/shard_map/pallas_call | solution.py:487
  165.3 4.7 %shard_map.229 = (f32[4,392,128]{2,1,0:T(8,128)}, f32[4,392,128]{2,1,0:T(8,128)}, s32[3]{0:T(128)S(1)}) custom-call(s32[3]{0:T(128)S(1)} %copy-done.4, f32[16,4]{1,0:T(8,128)S(1)} %stack.59.refs_1_, f32[4,392,128]{2,1,0:T(8,128)} %collective-permute-done.4.refs_3_.refs_2_, f32[4,392,128]{2,1,0:T(8,128)} %collective-permute-done.7.refs_3_, ...), custom_call_target="tpu_custom_call" | custom-call | flops 999999995904 | bytes 1 | tf_op jit(solution)/shard_map/pallas_call | solution.py:487
  170.4 6.5 %shard_map.230 = (f32[2,384,384]{2,1,0:T(8,128)}, f32[2,384,384]{2,1,0:T(8,128)}, f32[2,384,384]{2,1,0:T(8,128)}, f32[2,384,384]{2,1,0:T(8,128)}, s32[3]{0:T(128)}) custom-call(s32[3]{0:T(128)} %copy-done.5, f32[4,768,384]{2,1,0:T(8,128)} %bitcast.31, f32[4,768,384]{2,1,0:T(8,128)} %bitcast.6.refs_2_.refs_4_.refs_6_.refs_8_, f32[4,768,384]{2,1,0:T(8,128)} %bitcast.32, ...), custom_call_target="tpu_custom_call" | custom-call | flops 999999995904 | bytes 1 | tf_op jit(solution)/shard_map/pallas_call | solution.py:487
  179.4 14.8 %shard_map.231 = (bf16[768,1024]{1,0:T(8,128)(2,1)}, f32[768,1024]{1,0:T(8,128)}, f32[768,1024]{1,0:T(8,128)}, s32[3]{0:T(128)}) custom-call(s32[3]{0:T(128)} %get-tuple-element.201.refs_0_, f32[4,8,256]{2,1,0:T(8,128)} %get-tuple-element.163.refs_1_, bf16[768,1024]{1,0:T(8,128)(2,1)} %get-tuple-element.174.refs_2_, ...), custom_call_target="tpu_custom_call" | custom-call | flops 999999995904 | bytes 1 | tf_op jit(solution)/shard_map/pallas_call | solution.py:487
  194.2 7.8 %shard_map.232 = (f32[768,896]{1,0:T(8,128)}, f32[768,896]{1,0:T(8,128)}, s32[3]{0:T(128)}) custom-call(s32[3]{0:T(128)} %get-tuple-element.207.refs_0_, bf16[768,1024]{1,0:T(8,128)(2,1)} %get-tuple-element.208.refs_1_, bf16[1,768,1024]{2,1,0:T(8,128)(2,1)} %bitcast.48, bf16[768,1024]{1,0:T(8,128)(2,1)} %get-tuple-element.164.refs_2_.refs_7_.refs_3_.refs_1_, ...), custom_call_target="tpu_custom_call" | custom-call | flops 999999995904 | bytes 1 | tf_op jit(solution)/shard_map/pallas_call | solution.py:487
  203.2 8.1 %shard_map.233 = (bf16[2,768,1024]{2,1,0:T(8,128)(2,1)}, s32[3]{0:T(128)}) custom-call(s32[3]{0:T(128)} %get-tuple-element.212.refs_0_, f32[4,8,256]{2,1,0:T(8,128)} %get-tuple-element.163.refs_1_, bf16[768,1024]{1,0:T(8,128)(2,1)} %get-tuple-element.202.refs_3_.refs_2_, bf16[768,1024]{1,0:T(8,128)(2,1)} %get-tuple-element.166.refs_4_.refs_3_, ...), custom_call_target="tpu_custom_call" | custom-call | flops 999999995904 | bytes 1 | tf_op jit(solution)/shard_map/pallas_call | solution.py:487
  211.3 4.5 %shard_map.234 = (f32[1,96,1536]{2,1,0:T(8,128)}, f32[1,96,1536]{2,1,0:T(8,128)}, f32[1,96,1536]{2,1,0:T(8,128)}, f32[1,96,1536]{2,1,0:T(8,128)}, s32[3]{0:T(128)}) custom-call(s32[3]{0:T(128)} %get-tuple-element.218.refs_0_, f32[2,96,1536]{2,1,0:T(8,128)} %get-tuple-element.219.refs_1_.refs_3_, f32[2,96,1536]{2,1,0:T(8,128)} %collective-permute-done.10.refs_2_.refs_4_, ...), custom_call_target="tpu_custom_call" | custom-call | flops 999999995904 | bytes 1 | tf_op jit(solution)/shard_map/pallas_call | solution.py:487
  217.2 4.5 %shard_map.235 = (f32[1,384,384]{2,1,0:T(8,128)}, f32[1,384,384]{2,1,0:T(8,128)}, f32[1,384,384]{2,1,0:T(8,128)}, f32[1,384,384]{2,1,0:T(8,128)}, s32[3]{0:T(128)}) custom-call(s32[3]{0:T(128)} %get-tuple-element.223.refs_0_, f32[2,384,384]{2,1,0:T(8,128)} %get-tuple-element.224.refs_1_.refs_3_, f32[2,384,384]{2,1,0:T(8,128)} %collective-permute-done.12.refs_2_.refs_4_, ...), custom_call_target="tpu_custom_call" | custom-call | flops 999999995904 | bytes 1 | tf_op jit(solution)/shard_map/pallas_call | solution.py:487
  223.3 7.8 %collective-permute-done.14.refs_2_ = f32[1,96,1536]{2,1,0:T(8,128)} collective-permute-done((f32[1,96,1536]{2,1,0:T(8,128)}, f32[1,96,1536]{2,1,0:T(8,128)}, u32[]{:S(2)}, u32[]{:S(2)}) %collective-permute-start.14) | collective-permute-done | bytes 589856 | tf_op jit(solution)/shard_map/ppermute | solution.py:783
  236.9 4.5 %shard_map.237 = (f32[2,96,896]{2,1,0:T(8,128)}, f32[2,96,896]{2,1,0:T(8,128)}, f32[2,96,896]{2,1,0:T(8,128)}, f32[2,96,896]{2,1,0:T(8,128)}, s32[3]{0:T(128)}) custom-call(s32[3]{0:T(128)} %copy-done.8, f32[4,192,896]{2,1,0:T(8,128)} %bitcast.39, f32[4,192,896]{2,1,0:T(8,128)} %bitcast.10.refs_2_.refs_4_.refs_6_.refs_8_, f32[4,192,896]{2,1,0:T(8,128)} %bitcast.40, ...), custom_call_target="tpu_custom_call" | custom-call | flops 999999995904 | bytes 1 | tf_op jit(solution)/shard_map/pallas_call | solution.py:487
  249.5 7.1 %collective-permute-done.19.refs_2_.refs_4_ = f32[2,96,896]{2,1,0:T(8,128)} collective-permute-done((f32[2,96,896]{2,1,0:T(8,128)}, f32[2,96,896]{2,1,0:T(8,128)}, u32[]{:S(2)}, u32[]{:S(2)}) %collective-permute-start.19) | collective-permute-done | bytes 688160 | tf_op jit(solution)/shard_map/ppermute | solution.py:783
  268.6 7.3 %shard_map.241 = (f32[768,768]{1,0:T(8,128)}, f32[768,768]{1,0:T(8,128)}, s32[3]{0:T(128)}) custom-call(s32[3]{0:T(128)} %copy-done.16, bf16[768,1024]{1,0:T(8,128)(2,1)} %get-tuple-element.164.refs_2_.refs_7_.refs_3_.refs_1_, bf16[2,768,1024]{2,1,0:T(8,128)(2,1)} %get-tuple-element.250.refs_2_.refs_4_, ...), custom_call_target="tpu_custom_call" | custom-call | flops 999999995904 | bytes 1 | tf_op jit(solution)/shard_map/pallas_call | solution.py:487
  317.7 4.4 %collective-permute-start.34 = (f32[96,768]{1,0:T(8,128)}, f32[96,768]{1,0:T(8,128)}, u32[]{:S(2)}, u32[]{:S(2)}) collective-permute-start(f32[96,768]{1,0:T(8,128)} %get-tuple-element.283), channel_id=1, source_target_pairs={{0,2},{1,3},{2,0},{3,1},{4,6},{5,7},{6,4},{7,5},{8,10},{9,11},{10,... | collective-permute-start | bytes 884744 | tf_op jit(solution)/shard_map/ppermute | solution.py:783
  326.9 10.0 %collective-permute-start.38 = (f32[96,1536]{1,0:T(8,128)}, f32[96,1536]{1,0:T(8,128)}, u32[]{:S(2)}, u32[]{:S(2)}) collective-permute-start(f32[96,1536]{1,0:T(8,128)} %get-tuple-element.294.refs_1_), channel_id=1, source_target_pairs={{0,2},{1,3},{2,0},{3,1},{4,6},{5,7},{6,4},{7,5},{8,10},{9,11},{10,... | collective-permute-start | bytes 1769480 | tf_op jit(solution)/shard_map/ppermute | solution.py:783
  349.0 9.9 %shard_map.252 = (f32[4,256,768]{2,1,0:T(8,128)}, s32[3]{0:T(128)}) custom-call(s32[3]{0:T(128)} %copy-done.12, bf16[768,1024]{1,0:T(8,128)(2,1)} %get-tuple-element.210.refs_1_, bf16[2,768,1024]{2,1,0:T(8,128)(2,1)} %get-tuple-element.250.refs_2_.refs_4_, f32[768,1024]{1,0:T(8,128)} %get-tuple-element.285.refs_3_, bf16[768,768]{1,0:T(8,128)(2,1)} %refs_4_.3, ...), custom_call_target="tpu_custom_call" | custom-call | flops 999999995904 | bytes 1 | tf_op jit(solution)/shard_map/pallas_call | solution.py:487
  (183 shorter events, 149.6 us)
Async XLA Ops:
  11.9 22.6 %collective-permute-start = (f32[4,392,128]{2,1,0:T(8,128)}, f32[4,392,128]{2,1,0:T(8,128)}, u32[]{:S(2)}, u32[]{:S(2)}) collective-permute-start(f32[4,392,128]{2,1,0:T(8,128)} %get-tuple-element.168.refs_2_), channel_id=1, source_target_pairs={{0,8},{8,0},{16,24},{24,16},{1,9},{9,1},{17,25},{25,17},{2,10},{10... | collective-permute-start | bytes 2408456 | tf_op jit(solution)/shard_map/ppermute | solution.py:783
  14.0 20.5 %collective-permute-start.1 = (f32[4,392,128]{2,1,0:T(8,128)}, f32[4,392,128]{2,1,0:T(8,128)}, u32[]{:S(2)}, u32[]{:S(2)}) collective-permute-start(f32[4,392,128]{2,1,0:T(8,128)} %get-tuple-element.169.refs_4_), channel_id=1, source_target_pairs={{0,16},{8,24},{16,0},{24,8},{1,17},{9,25},{17,1},{25,9},{2,18},{10... | collective-permute-start | bytes 2408456 | tf_op jit(solution)/shard_map/ppermute | solution.py:783
  131.2 26.2 %collective-permute-start.6 = (f32[768,1536]{1,0:T(8,128)}, f32[768,1536]{1,0:T(8,128)}, u32[]{:S(2)}, u32[]{:S(2)}) collective-permute-start(f32[768,1536]{1,0:T(8,128)} %get-tuple-element.194), channel_id=1, source_target_pairs={{0,1},{1,0},{2,3},{3,2},{4,5},{5,4},{6,7},{7,6},{8,9},{9,8},{10,11... | collective-permute-start | bytes 14155784 | tf_op jit(solution)/shard_map/ppermute | solution.py:783
  140.4 24.2 %collective-permute-start.7 = (f32[4,392,128]{2,1,0:T(8,128)}, f32[4,392,128]{2,1,0:T(8,128)}, u32[]{:S(2)}, u32[]{:S(2)}) collective-permute-start(f32[4,392,128]{2,1,0:T(8,128)} %get-tuple-element.196), channel_id=1, source_target_pairs={{0,16},{8,24},{16,0},{24,8},{1,17},{9,25},{17,1},{25,9},{2,18},{10... | collective-permute-start | bytes 2408456 | tf_op jit(solution)/shard_map/ppermute | solution.py:783
  141.4 23.2 %collective-permute-start.8 = (f32[4,392,128]{2,1,0:T(8,128)}, f32[4,392,128]{2,1,0:T(8,128)}, u32[]{:S(2)}, u32[]{:S(2)}) collective-permute-start(f32[4,392,128]{2,1,0:T(8,128)} %get-tuple-element.197), channel_id=1, source_target_pairs={{0,8},{8,0},{16,24},{24,16},{1,9},{9,1},{17,25},{25,17},{2,10},{10... | collective-permute-start | bytes 2408456 | tf_op jit(solution)/shard_map/ppermute | solution.py:783
  164.0 47.3 %collective-permute-start.10 = (f32[2,96,1536]{2,1,0:T(8,128)}, f32[2,96,1536]{2,1,0:T(8,128)}, u32[]{:S(2)}, u32[]{:S(2)}) collective-permute-start(f32[2,96,1536]{2,1,0:T(8,128)} %get-tuple-element.220), channel_id=1, source_target_pairs={{0,8},{8,0},{16,24},{24,16},{1,9},{9,1},{17,25},{25,17},{2,10},{10... | collective-permute-start | bytes 3538952 | tf_op jit(solution)/shard_map/ppermute | solution.py:783
  164.3 47.0 %collective-permute-start.11 = (f32[2,96,1536]{2,1,0:T(8,128)}, f32[2,96,1536]{2,1,0:T(8,128)}, u32[]{:S(2)}, u32[]{:S(2)}) collective-permute-start(f32[2,96,1536]{2,1,0:T(8,128)} %get-tuple-element.222), channel_id=1, source_target_pairs={{0,16},{8,24},{16,0},{24,8},{1,17},{9,25},{17,1},{25,9},{2,18},{10... | collective-permute-start | bytes 3538952 | tf_op jit(solution)/shard_map/ppermute | solution.py:783
  176.9 40.3 %collective-permute-start.12 = (f32[2,384,384]{2,1,0:T(8,128)}, f32[2,384,384]{2,1,0:T(8,128)}, u32[]{:S(2)}, u32[]{:S(2)}) collective-permute-start(f32[2,384,384]{2,1,0:T(8,128)} %get-tuple-element.225), channel_id=1, source_target_pairs={{0,8},{8,0},{16,24},{24,16},{1,9},{9,1},{17,25},{25,17},{2,10},{10... | collective-permute-start | bytes 3538952 | tf_op jit(solution)/shard_map/ppermute | solution.py:783
  178.2 39.0 %collective-permute-start.13 = (f32[2,384,384]{2,1,0:T(8,128)}, f32[2,384,384]{2,1,0:T(8,128)}, u32[]{:S(2)}, u32[]{:S(2)}) collective-permute-start(f32[2,384,384]{2,1,0:T(8,128)} %get-tuple-element.227), channel_id=1, source_target_pairs={{0,16},{8,24},{16,0},{24,8},{1,17},{9,25},{17,1},{25,9},{2,18},{10... | collective-permute-start | bytes 3538952 | tf_op jit(solution)/shard_map/ppermute | solution.py:783
  202.0 34.8 %collective-permute-start.16 = (f32[768,896]{1,0:T(8,128)}, f32[768,896]{1,0:T(8,128)}, u32[]{:S(2)}, u32[]{:S(2)}) collective-permute-start(f32[768,896]{1,0:T(8,128)} %get-tuple-element.235), channel_id=1, source_target_pairs={{0,1},{1,0},{2,3},{3,2},{4,5},{5,4},{6,7},{7,6},{8,9},{9,8},{10,11... | collective-permute-start | bytes 8257544 | tf_op jit(solution)/shard_map/ppermute | solution.py:783
  221.7 22.1 %collective-permute-start.17 = (f32[1,384,384]{2,1,0:T(8,128)}, f32[1,384,384]{2,1,0:T(8,128)}, u32[]{:S(2)}, u32[]{:S(2)}) collective-permute-start(f32[1,384,384]{2,1,0:T(8,128)} %get-tuple-element.238), channel_id=1, source_target_pairs={{0,16},{8,24},{16,0},{24,8},{1,17},{9,25},{17,1},{25,9},{2,18},{10... | collective-permute-start | bytes 1769480 | tf_op jit(solution)/shard_map/ppermute | solution.py:783
  222.1 21.6 %collective-permute-start.18 = (f32[1,384,384]{2,1,0:T(8,128)}, f32[1,384,384]{2,1,0:T(8,128)}, u32[]{:S(2)}, u32[]{:S(2)}) collective-permute-start(f32[1,384,384]{2,1,0:T(8,128)} %get-tuple-element.240), channel_id=1, source_target_pairs={{0,8},{8,0},{16,24},{24,16},{1,9},{9,1},{17,25},{25,17},{2,10},{10... | collective-permute-start | bytes 1769480 | tf_op jit(solution)/shard_map/ppermute | solution.py:783
  235.6 54.4 %collective-permute-start.25 = (f32[96,1536]{1,0:T(8,128)}, f32[96,1536]{1,0:T(8,128)}, u32[]{:S(2)}, u32[]{:S(2)}) collective-permute-start(f32[96,1536]{1,0:T(8,128)} %get-tuple-element.261), channel_id=1, source_target_pairs={{0,2},{1,3},{2,0},{3,1},{4,6},{5,7},{6,4},{7,5},{8,10},{9,11},{10,... | collective-permute-start | bytes 1769480 | tf_op jit(solution)/shard_map/ppermute | solution.py:783
  260.1 20.0 %collective-permute-start.22 = (f32[1,96,896]{2,1,0:T(8,128)}, f32[1,96,896]{2,1,0:T(8,128)}, u32[]{:S(2)}, u32[]{:S(2)}) collective-permute-start(f32[1,96,896]{2,1,0:T(8,128)} %get-tuple-element.253), channel_id=1, source_target_pairs={{0,16},{8,24},{16,0},{24,8},{1,17},{9,25},{17,1},{25,9},{2,18},{10... | collective-permute-start | bytes 1032200 | tf_op jit(solution)/shard_map/ppermute | solution.py:783
  261.3 18.8 %collective-permute-start.23 = (f32[1,96,896]{2,1,0:T(8,128)}, f32[1,96,896]{2,1,0:T(8,128)}, u32[]{:S(2)}, u32[]{:S(2)}) collective-permute-start(f32[1,96,896]{2,1,0:T(8,128)} %get-tuple-element.255), channel_id=1, source_target_pairs={{0,8},{8,0},{16,24},{24,16},{1,9},{9,1},{17,25},{25,17},{2,10},{10... | collective-permute-start | bytes 1032200 | tf_op jit(solution)/shard_map/ppermute | solution.py:783
  266.3 27.9 %collective-permute-start.26 = (f32[384,384]{1,0:T(8,128)}, f32[384,384]{1,0:T(8,128)}, u32[]{:S(2)}, u32[]{:S(2)}) collective-permute-start(f32[384,384]{1,0:T(8,128)} %get-tuple-element.263.refs_1_), channel_id=1, source_target_pairs={{0,4},{1,5},{2,6},{3,7},{4,0},{5,1},{6,2},{7,3},{8,12},{9,13},{10,... | collective-permute-start | bytes 1769480 | tf_op jit(solution)/shard_map/ppermute | solution.py:783
  284.1 24.4 %collective-permute-start.29 = (f32[96,896]{1,0:T(8,128)}, f32[96,896]{1,0:T(8,128)}, u32[]{:S(2)}, u32[]{:S(2)}) collective-permute-start(f32[96,896]{1,0:T(8,128)} %get-tuple-element.271), channel_id=1, source_target_pairs={{0,2},{1,3},{2,0},{3,1},{4,6},{5,7},{6,4},{7,5},{8,10},{9,11},{10,... | collective-permute-start | bytes 1032200 | tf_op jit(solution)/shard_map/ppermute | solution.py:783
  297.4 39.6 %collective-permute-start.33 = (f32[384,384]{1,0:T(8,128)}, f32[384,384]{1,0:T(8,128)}, u32[]{:S(2)}, u32[]{:S(2)}) collective-permute-start(f32[384,384]{1,0:T(8,128)} %get-tuple-element.280.refs_1_), channel_id=1, source_target_pairs={{0,2},{1,3},{2,0},{3,1},{4,6},{5,7},{6,4},{7,5},{8,10},{9,11},{10,... | collective-permute-start | bytes 1769480 | tf_op jit(solution)/shard_map/ppermute | solution.py:783
  299.0 25.2 %collective-permute-start.32 = (f32[96,1536]{1,0:T(8,128)}, f32[96,1536]{1,0:T(8,128)}, u32[]{:S(2)}, u32[]{:S(2)}) collective-permute-start(f32[96,1536]{1,0:T(8,128)} %get-tuple-element.278.refs_1_), channel_id=1, source_target_pairs={{0,4},{1,5},{2,6},{3,7},{4,0},{5,1},{6,2},{7,3},{8,12},{9,13},{10,... | collective-permute-start | bytes 1769480 | tf_op jit(solution)/shard_map/ppermute | solution.py:783
  311.6 47.2 %collective-permute-start.35 = (f32[96,896]{1,0:T(8,128)}, f32[96,896]{1,0:T(8,128)}, u32[]{:S(2)}, u32[]{:S(2)}) collective-permute-start(f32[96,896]{1,0:T(8,128)} %get-tuple-element.288.refs_1_), channel_id=1, source_target_pairs={{0,4},{1,5},{2,6},{3,7},{4,0},{5,1},{6,2},{7,3},{8,12},{9,13},{10,... | collective-permute-start | bytes 1032200 | tf_op jit(solution)/shard_map/ppermute | solution.py:783
  317.7 25.6 %collective-permute-start.34 = (f32[96,768]{1,0:T(8,128)}, f32[96,768]{1,0:T(8,128)}, u32[]{:S(2)}, u32[]{:S(2)}) collective-permute-start(f32[96,768]{1,0:T(8,128)} %get-tuple-element.283), channel_id=1, source_target_pairs={{0,2},{1,3},{2,0},{3,1},{4,6},{5,7},{6,4},{7,5},{8,10},{9,11},{10,... | collective-permute-start | bytes 884744 | tf_op jit(solution)/shard_map/ppermute | solution.py:783
  326.9 42.8 %collective-permute-start.38 = (f32[96,1536]{1,0:T(8,128)}, f32[96,1536]{1,0:T(8,128)}, u32[]{:S(2)}, u32[]{:S(2)}) collective-permute-start(f32[96,1536]{1,0:T(8,128)} %get-tuple-element.294.refs_1_), channel_id=1, source_target_pairs={{0,2},{1,3},{2,0},{3,1},{4,6},{5,7},{6,4},{7,5},{8,10},{9,11},{10,... | collective-permute-start | bytes 1769480 | tf_op jit(solution)/shard_map/ppermute | solution.py:783
  339.8 22.2 %collective-permute-start.36 = (f32[768,384]{1,0:T(8,128)}, f32[768,384]{1,0:T(8,128)}, u32[]{:S(2)}, u32[]{:S(2)}) collective-permute-start(f32[768,384]{1,0:T(8,128)} %get-tuple-element.290.refs_1_), channel_id=1, source_target_pairs={{0,1},{1,0},{2,3},{3,2},{4,5},{5,4},{6,7},{7,6},{8,9},{9,8},{10,11... | collective-permute-start | bytes 3538952 | tf_op jit(solution)/shard_map/ppermute | solution.py:783
  346.2 19.6 %collective-permute-start.37 = (f32[96,768]{1,0:T(8,128)}, f32[96,768]{1,0:T(8,128)}, u32[]{:S(2)}, u32[]{:S(2)}) collective-permute-start(f32[96,768]{1,0:T(8,128)} %get-tuple-element.292.refs_1_), channel_id=1, source_target_pairs={{0,4},{1,5},{2,6},{3,7},{4,0},{5,1},{6,2},{7,3},{8,12},{9,13},{10,... | collective-permute-start | bytes 884744 | tf_op jit(solution)/shard_map/ppermute | solution.py:783
  (48 other events, 386.7 us)

commit v5 on v4

--- a/solution.py
+++ b/solution.py
@@ -17,8 +17,9 @@
 bf16 = jnp.bfloat16
 half_pi = 1.5707963267948966
 norm_eps = 1e-05
-VMEM_LIMIT = 60 * 1024 * 1024
-SMALL_LIMIT = 20 * 1024 * 1024
+VMEM_LIMIT = 30 * 1024 * 1024
+SMALL_LIMIT = 16 * 1024 * 1024
+LAYER_LIMIT = 38 * 1024 * 1024
 
 NN = (((1,), (0,)), ((), ()))
 NT = (((1,), (1,)), ((), ()))
@@ -458,13 +459,11 @@
     out_ref[0] = total.T
 
 
-def in_hbm(v):
-    return pltpu.with_memory_space_constraint(v, pltpu.HBM)
-
-
 def spec(block, index):
     return pl.BlockSpec(block, index)
 
+
+NEAR = pl.BlockSpec(memory_space=pltpu.VMEM)
 
 CORE, ODD, PLACE = range(3)
 
@@ -473,7 +472,9 @@
     def __init__(self, scalars):
         self.scalars = scalars
 
-    def call(self, kernel, grid, ins, outs, scratch, args, extra=(), free=(), limit=VMEM_LIMIT):
+    def call(
+        self, kernel, grid, ins, outs, scratch, args, extra=(), free=(), near=(), near_out=(), limit=VMEM_LIMIT
+    ):
         count = 1 + len(extra)
         placed = len(scratch)
 
@@ -493,13 +494,25 @@
                 out_specs=[o for o, _ in outs] + [pl.BlockSpec(memory_space=pltpu.SMEM)],
                 scratch_shapes=scratch,
             ),
-            out_shape=[pltpu.HBM(shape, kind) for _, (shape, kind) in outs]
+            out_shape=[
+                (pltpu.VMEM if i in near_out else pltpu.HBM)(shape, kind)
+                for i, (_, (shape, kind)) in enumerate(outs)
+            ]
             + [jax.ShapeDtypeStruct(self.scalars.shape, jnp.int32)],
             compiler_params=pltpu.CompilerParams(
                 dimension_semantics=("arbitrary",) * len(grid), vmem_limit_bytes=limit
             ),
             cost_estimate=pl.CostEstimate(flops=1000000000000, bytes_accessed=1, transcendentals=0),
-        )(self.scalars, *extra, *[v if i in free else in_hbm(v) for i, v in enumerate(args)])
+        )(
+            self.scalars,
+            *extra,
+            *[
+                v
+                if i in free
+                else pltpu.with_memory_space_constraint(v, pltpu.VMEM if i in near else pltpu.HBM)
+                for i, v in enumerate(args)
+            ],
+        )
         return values
 
 
@@ -626,16 +639,15 @@
 
 def choose(order, left, right):
     shape = left[0].shape[1:]
-    whole = spec((1,) + shape, lambda i, s: (0, 0, 0))
-    out = (spec(shape, lambda i, s: (0, 0)), (shape, f32))
     return order.call(
         choose_kernel,
         (1,),
-        [whole] * 4,
-        [out] * 2,
+        [NEAR] * 4,
+        [(NEAR, (shape, f32))] * 2,
         [],
         (*left, *right),
-        free=(1, 3),
+        free=range(4),
+        near_out=range(2),
         limit=SMALL_LIMIT,
     )
 
@@ -645,9 +657,9 @@
 
 
 def add(order, a, b):
-    whole = spec(a.shape, lambda i, s: (0, 0))
+    outs = [(NEAR, (a.shape, f32))]
     return order.call(
-        add_kernel, (1,), [whole] * 2, [(whole, (a.shape, f32))], [], (a, b), free=(1,), limit=SMALL_LIMIT
+        add_kernel, (1,), [NEAR] * 2, outs, [], (a, b), near=range(2), near_out=range(1), limit=SMALL_LIMIT
     )[0]
 
 
@@ -661,10 +673,17 @@
 
 def merge(order, kept, got):
     rows, columns = kept.shape
-    whole = spec((rows, columns), lambda i, s: (0, 0))
-    out = (spec((2 * rows, columns), lambda i, s: (0, 0)), ((2 * rows, columns), f32))
+    outs = [(NEAR, ((2 * rows, columns), f32))]
     return order.call(
-        merge_kernel, (1,), [whole] * 2, [out], [], (kept, got), free=(1,), limit=SMALL_LIMIT
+        merge_kernel,
+        (1,),
+        [NEAR] * 2,
+        outs,
+        [],
+        (kept, got),
+        near=range(2),
+        near_out=range(1),
+        limit=SMALL_LIMIT,
     )[0]
 
 
@@ -683,10 +702,10 @@
 
 
 def side(order, mine, other, widths):
-    whole = spec(mine.shape, lambda i, s: (0, 0))
-    outs = [(spec((mine.shape[0], w), lambda i, s: (0, 0)), ((mine.shape[0], w), f32)) for w in widths]
+    rows = mine.shape[0]
+    outs = [(spec((rows, w), lambda i, s: (0, 0)), ((rows, w), f32)) for w in widths]
     return order.call(
-        side_kernel, (1,), [whole] * 2, outs, [], (mine, other), free=(1,), limit=SMALL_LIMIT
+        side_kernel, (1,), [NEAR] * 2, outs, [], (mine, other), near=range(2), limit=SMALL_LIMIT
     )
 
 
@@ -868,8 +887,8 @@
     )
     order = Order(scalars)
 
-    def run(kernel, ins, outs, scratch, *args, extra=()):
-        return order.call(kernel, grid, ins, outs, scratch, args, extra)
+    def run(kernel, ins, outs, scratch, *args, **more):
+        return order.call(kernel, grid, ins, outs, scratch, args, **more)
 
     def column(v):
         return v[:, None]
@@ -999,6 +1018,8 @@
         column(shift_one),
         column(gain_two),
         column(shift_two),
+        near=range(8, 14),
+        limit=LAYER_LIMIT,
     )
 
     back_states = entering(order, (out_a, out_b), weights, later)

time: 395 us -> 386 us (0.977)
  waiting for transfers between devices: 42.3 us -> 51.7 us
  Pallas kernels: 266 us -> 257 us
  local copies, waits for them, and re-layouts: 16.9 us -> 10 us
    ppermute x44, waiting for transfers between devices: 42.3 us -> 51.7 us  [swap(): return lax.ppermute(value, axis, [(i, i ^ distance) for i in range(count)])]
    pallas_call x42, Pallas kernels: 266 us -> 257 us  [call(): pl.pallas_call(stepped, grid_spec=pltpu.PrefetchScalarGridSpec(num_scalar...]
    unnamed x56 -> x52, local copies, waits for them, and re-layouts: 11.1 us -> 4.19 us
  transfers between devices with their start and end apart: 44 -> 44, of which waited for: 14 -> 15; matrix products, arithmetic and copies ran while one was open for 2% -> 2% of each run, Pallas kernels for 48% -> 48%
where the time goes in v5:
time: 386 us; the launch traced here: 384 us
  Pallas kernels  257 us (67%)
  starting transfers between devices  63.7 us (17%)
  waiting for transfers between devices  51.7 us (13%)
  local copies, waits for them, and re-layouts  10 us (3%)
    pallas_call x42, Pallas kernels, call(): pl.pallas_call(stepped, grid_spec=pltpu.PrefetchScalarGridSpec(num_scalar...  257 us
    ppermute x44, starting transfers between devices, swap(): return lax.ppermute(value, axis, [(i, i ^ distance) for i in range(count)])  63.7 us
    ppermute x44, waiting for transfers between devices, swap(): return lax.ppermute(value, axis, [(i, i ^ distance) for i in range(count)])  51.7 us
  transfers between devices with their start and end apart: 44, of which 15 were waited for; matrix products, arithmetic and copies ran while one was open for 2% of the time, Pallas kernels for 48%

profile of v5, /device:TPU:1, one launch (start us, length us, event | category | flops | bytes accessed | tf_op | source)
XLA Modules:
  0.0 384.4 jit_solution(9980001948415009515)
XLA Ops:
  1.4 10.5 %shard_map.220 = (f32[4,8,256]{2,1,0:T(8,128)}, bf16[768,1024]{1,0:T(8,128)(2,1)}, bf16[768,1024]{1,0:T(8,128)(2,1)}, bf16[768,1024]{1,0:T(8,128)(2,1)}, bf16[4,...) custom-call(s32[3]{0:T(128)S(1)} %pad_add_fusion.refs_0_, ...), custom_call_target="tpu_custom_call" | custom-call | flops 999999995904 | bytes 1 | tf_op jit(solution)/shard_map/pallas_call | solution.py:488
  15.2 18.2 %shard_map.221 = (bf16[768,1024]{1,0:T(8,128)(2,1)}, bf16[768,1024]{1,0:T(8,128)(2,1)}, f32[768,1024]{1,0:T(8,128)}, f32[16,1024]{1,0:T(8,128)}, bf16[768,768]{1...) custom-call(s32[3]{0:T(128)S(1)} %get-tuple-element.162.refs_0_, ...), custom_call_target="tpu_custom_call" | custom-call | flops 999999995904 | bytes 1 | tf_op jit(solution)/shard_map/pallas_call | solution.py:488
  34.4 4.4 %shard_map.222 = (f32[4,392,128]{2,1,0:T(8,128)}, f32[4,392,128]{2,1,0:T(8,128)}, s32[3]{0:T(128)S(1)}) custom-call(s32[3]{0:T(128)S(1)} %get-tuple-element.167.refs_0_, f32[16,4]{1,0:T(8,128)S(1)} %stack.59.refs_1_, f32[4,392,128]{2,1,0:T(8,128)S(1)} %copy-done.5, f32[4,392,128]{2,1,0:T(8,128)} %collective-permute-done.refs_3_.refs_2_, ...), custom_call_target="tpu_custom_call" | custom-call | flops 999999995904 | bytes 1 | tf_op jit(solution)/shard_map/pallas_call | solution.py:488
  42.7 14.4 %collective-permute-done.2.refs_3_ = f32[4,392,128]{2,1,0:T(8,128)S(1)} collective-permute-done((f32[4,392,128]{2,1,0:T(8,128)}, f32[4,392,128]{2,1,0:T(8,128)S(1)}, u32[]{:S(2)}, u32[]{:S(2)}) %collective-permute-start.2) | collective-permute-done | bytes 802848 | tf_op jit(solution)/shard_map/ppermute | solution.py:802
  57.2 5.5 %shard_map.223 = (f32[4,392,128]{2,1,0:T(8,128)}, f32[4,392,128]{2,1,0:T(8,128)}, s32[3]{0:T(128)S(1)}) custom-call(s32[3]{0:T(128)S(1)} %get-tuple-element.170.refs_0_, f32[16,4]{1,0:T(8,128)S(1)} %stack.59.refs_1_, f32[4,392,128]{2,1,0:T(8,128)} %collective-permute-done.refs_3_.refs_2_, f32[4,392,128]{2,1,0:T(8,128)S(1)} %collective-permute-done.2.refs_3_, ...), custom_call_target="tpu_custom_call" | custom-call | flops 999999995904 | bytes 1 | tf_op jit(solution)/shard_map/pallas_call | solution.py:488
  65.4 48.3 %shard_map.224 = (bf16[4,256,768]{2,1,0:T(8,128)(2,1)}, bf16[768,1024]{1,0:T(8,128)(2,1)}, bf16[768,1024]{1,0:T(8,128)(2,1)}, bf16[3072,1024]{1,0:T(8,128)(2,1)}...) custom-call(s32[3]{0:T(128)} %copy-done.21, ...), custom_call_target="tpu_custom_call" | custom-call | flops 999999995904 | bytes 1 | tf_op jit(solution)/shard_map/pallas_call | solution.py:488
  115.9 12.2 %shard_map.225 = (f32[768,1536]{1,0:T(8,128)}, f32[768,1536]{1,0:T(8,128)}, s32[3]{0:T(128)S(1)}) custom-call(s32[3]{0:T(128)S(1)} %copy-done.20, bf16[768,1024]{1,0:T(8,128)(2,1)} %get-tuple-element.184.refs_1_, bf16[3072,1024]{1,0:T(8,128)(2,1)} %get-tuple-element.185.refs_2_), custom_call_target="tpu_custom_call" | custom-call | flops 999999995904 | bytes 1 | tf_op jit(solution)/shard_map/pallas_call | solution.py:488
  131.3 4.4 %shard_map.226 = (f32[4,392,128]{2,1,0:T(8,128)}, f32[4,392,128]{2,1,0:T(8,128)}, s32[3]{0:T(128)S(1)}) custom-call(s32[3]{0:T(128)S(1)} %get-tuple-element.186.refs_0_, f32[16,4]{1,0:T(8,128)S(1)} %stack.59.refs_1_, f32[4,392,128]{2,1,0:T(8,128)S(1)} %copy-done.7, f32[4,392,128]{2,1,0:T(8,128)} %collective-permute-done.4.refs_3_.refs_2_, ...), custom_call_target="tpu_custom_call" | custom-call | flops 999999995904 | bytes 1 | tf_op jit(solution)/shard_map/pallas_call | solution.py:488
  137.8 10.6 %shard_map.227 = (f32[3072,384]{1,0:T(8,128)}, f32[3072,384]{1,0:T(8,128)}, s32[3]{0:T(128)S(1)}) custom-call(s32[3]{0:T(128)S(1)} %get-tuple-element.189.refs_0_, bf16[3072,1024]{1,0:T(8,128)(2,1)} %get-tuple-element.190.refs_1_, bf16[768,1024]{1,0:T(8,128)(2,1)} %get-tuple-element.191.refs_2_), custom_call_target="tpu_custom_call" | custom-call | flops 999999995904 | bytes 1 | tf_op jit(solution)/shard_map/pallas_call | solution.py:488
  152.6 6.4 %shard_map.228 = (f32[2,96,1536]{2,1,0:T(8,128)}, f32[2,96,1536]{2,1,0:T(8,128)}, f32[2,96,1536]{2,1,0:T(8,128)}, f32[2,96,1536]{2,1,0:T(8,128)}, s32[3]{0:T(128)S(1)}) custom-call(s32[3]{0:T(128)S(1)} %get-tuple-element.192.refs_0_, f32[4,192,1536]{2,1,0:T(8,128)} %bitcast.35, f32[4,192,1536]{2,1,0:T(8,128)} %bitcast.4.refs_2_.refs_4_.refs_6_.refs_8_, ...), custom_call_target="tpu_custom_call" | custom-call | flops 999999995904 | bytes 1 | tf_op jit(solution)/shard_map/pallas_call | solution.py:488
  159.7 4.7 %shard_map.229 = (f32[4,392,128]{2,1,0:T(8,128)}, f32[4,392,128]{2,1,0:T(8,128)}, s32[3]{0:T(128)S(1)}) custom-call(s32[3]{0:T(128)S(1)} %get-tuple-element.195.refs_0_, f32[16,4]{1,0:T(8,128)S(1)} %stack.59.refs_1_, f32[4,392,128]{2,1,0:T(8,128)} %collective-permute-done.4.refs_3_.refs_2_, f32[4,392,128]{2,1,0:T(8,128)} %collective-permute-done.7.refs_3_, ...), custom_call_target="tpu_custom_call" | custom-call | flops 999999995904 | bytes 1 | tf_op jit(solution)/shard_map/pallas_call | solution.py:488
  164.3 6.4 %shard_map.230 = (f32[2,384,384]{2,1,0:T(8,128)}, f32[2,384,384]{2,1,0:T(8,128)}, f32[2,384,384]{2,1,0:T(8,128)}, f32[2,384,384]{2,1,0:T(8,128)}, s32[3]{0:T(128)S(1)}) custom-call(s32[3]{0:T(128)S(1)} %get-tuple-element.198.refs_0_, f32[4,768,384]{2,1,0:T(8,128)} %bitcast.31, f32[4,768,384]{2,1,0:T(8,128)} %bitcast.6.refs_2_.refs_4_.refs_6_.refs_8_, ...), custom_call_target="tpu_custom_call" | custom-call | flops 999999995904 | bytes 1 | tf_op jit(solution)/shard_map/pallas_call | solution.py:488
  173.2 14.7 %shard_map.231 = (bf16[768,1024]{1,0:T(8,128)(2,1)}, f32[768,1024]{1,0:T(8,128)}, f32[768,1024]{1,0:T(8,128)}, s32[3]{0:T(128)S(1)}) custom-call(s32[3]{0:T(128)S(1)} %get-tuple-element.201.refs_0_, f32[4,8,256]{2,1,0:T(8,128)} %get-tuple-element.163.refs_1_, bf16[768,1024]{1,0:T(8,128)(2,1)} %get-tuple-element.174.refs_2_, ...), custom_call_target="tpu_custom_call" | custom-call | flops 999999995904 | bytes 1 | tf_op jit(solution)/shard_map/pallas_call | solution.py:488
  187.9 7.7 %shard_map.232 = (f32[768,896]{1,0:T(8,128)}, f32[768,896]{1,0:T(8,128)}, s32[3]{0:T(128)S(1)}) custom-call(s32[3]{0:T(128)S(1)} %get-tuple-element.207.refs_0_, bf16[768,1024]{1,0:T(8,128)(2,1)} %get-tuple-element.208.refs_1_, bf16[1,768,1024]{2,1,0:T(8,128)(2,1)} %bitcast.48, bf16[768,1024]{1,0:T(8,128)(2,1)} %get-tuple-element.164.refs_2_.refs_7_.refs_3_.refs_1_, ...), custom_call_target="tpu_custom_call" | custom-call | flops 999999995904 | bytes 1 | tf_op jit(solution)/shard_map/pallas_call | solution.py:488
  196.8 8.0 %shard_map.233 = (bf16[2,768,1024]{2,1,0:T(8,128)(2,1)}, s32[3]{0:T(128)S(1)}) custom-call(s32[3]{0:T(128)S(1)} %get-tuple-element.212.refs_0_, f32[4,8,256]{2,1,0:T(8,128)} %get-tuple-element.163.refs_1_, bf16[768,1024]{1,0:T(8,128)(2,1)} %get-tuple-element.202.refs_3_.refs_2_, bf16[768,1024]{1,0:T(8,128)(2,1)} %get-tuple-element.166.refs_4_.refs_3_, ...), custom_call_target="tpu_custom_call" | custom-call | flops 999999995904 | bytes 1 | tf_op jit(solution)/shard_map/pallas_call | solution.py:488
  204.8 4.3 %shard_map.234 = (f32[1,96,1536]{2,1,0:T(8,128)}, f32[1,96,1536]{2,1,0:T(8,128)}, f32[1,96,1536]{2,1,0:T(8,128)}, f32[1,96,1536]{2,1,0:T(8,128)}, s32[3]{0:T(128)S(1)}) custom-call(s32[3]{0:T(128)S(1)} %get-tuple-element.218.refs_0_, f32[2,96,1536]{2,1,0:T(8,128)} %get-tuple-element.219.refs_1_.refs_3_, ...), custom_call_target="tpu_custom_call" | custom-call | flops 999999995904 | bytes 1 | tf_op jit(solution)/shard_map/pallas_call | solution.py:488
  212.3 4.3 %shard_map.235 = (f32[1,384,384]{2,1,0:T(8,128)}, f32[1,384,384]{2,1,0:T(8,128)}, f32[1,384,384]{2,1,0:T(8,128)}, f32[1,384,384]{2,1,0:T(8,128)}, s32[3]{0:T(128)S(1)}) custom-call(s32[3]{0:T(128)S(1)} %get-tuple-element.223.refs_0_, f32[2,384,384]{2,1,0:T(8,128)} %get-tuple-element.224.refs_1_.refs_3_, ...), custom_call_target="tpu_custom_call" | custom-call | flops 999999995904 | bytes 1 | tf_op jit(solution)/shard_map/pallas_call | solution.py:488
  218.1 6.7 %collective-permute-done.14.refs_2_ = f32[1,96,1536]{2,1,0:T(8,128)} collective-permute-done((f32[1,96,1536]{2,1,0:T(8,128)}, f32[1,96,1536]{2,1,0:T(8,128)}, u32[]{:S(2)}, u32[]{:S(2)}) %collective-permute-start.14) | collective-permute-done | bytes 589856 | tf_op jit(solution)/shard_map/ppermute | solution.py:802
  229.0 4.4 %shard_map.237 = (f32[2,96,896]{2,1,0:T(8,128)}, f32[2,96,896]{2,1,0:T(8,128)}, f32[2,96,896]{2,1,0:T(8,128)}, f32[2,96,896]{2,1,0:T(8,128)}, s32[3]{0:T(128)S(1)}) custom-call(s32[3]{0:T(128)S(1)} %get-tuple-element.233.refs_0_, f32[4,192,896]{2,1,0:T(8,128)} %bitcast.39, f32[4,192,896]{2,1,0:T(8,128)} %bitcast.10.refs_2_.refs_4_.refs_6_.refs_8_, ...), custom_call_target="tpu_custom_call" | custom-call | flops 999999995904 | bytes 1 | tf_op jit(solution)/shard_map/pallas_call | solution.py:488
  241.7 9.9 %collective-permute-done.19.refs_2_.refs_4_ = f32[2,96,896]{2,1,0:T(8,128)} collective-permute-done((f32[2,96,896]{2,1,0:T(8,128)}, f32[2,96,896]{2,1,0:T(8,128)}, u32[]{:S(2)}, u32[]{:S(2)}) %collective-permute-start.19) | collective-permute-done | bytes 688160 | tf_op jit(solution)/shard_map/ppermute | solution.py:802
  261.2 7.2 %shard_map.241 = (f32[768,768]{1,0:T(8,128)}, f32[768,768]{1,0:T(8,128)}, s32[3]{0:T(128)S(1)}) custom-call(s32[3]{0:T(128)S(1)} %get-tuple-element.249.refs_0_, bf16[768,1024]{1,0:T(8,128)(2,1)} %get-tuple-element.164.refs_2_.refs_7_.refs_3_.refs_1_, bf16[2,768,1024]{2,1,0:T(8,128)(2,1)} %get-tuple-element.250.refs_2_.refs_4_, ...), custom_call_target="tpu_custom_call" | custom-call | flops 999999995904 | bytes 1 | tf_op jit(solution)/shard_map/pallas_call | solution.py:488
  310.0 6.3 %collective-permute-done.32.refs_2_ = f32[96,1536]{1,0:T(8,128)} collective-permute-done((f32[96,1536]{1,0:T(8,128)}, f32[96,1536]{1,0:T(8,128)}, u32[]{:S(2)}, u32[]{:S(2)}) %collective-permute-start.32) | collective-permute-done | bytes 589856 | tf_op jit(solution)/shard_map/ppermute | solution.py:802
  319.0 10.2 %collective-permute-start.38 = (f32[96,1536]{1,0:T(8,128)}, f32[96,1536]{1,0:T(8,128)}, u32[]{:S(2)}, u32[]{:S(2)}) collective-permute-start(f32[96,1536]{1,0:T(8,128)} %get-tuple-element.294.refs_1_), channel_id=1, source_target_pairs={{0,2},{1,3},{2,0},{3,1},{4,6},{5,7},{6,4},{7,5},{8,10},{9,11},{10,... | collective-permute-start | bytes 1769480 | tf_op jit(solution)/shard_map/ppermute | solution.py:802
  340.6 9.8 %shard_map.252 = (f32[4,256,768]{2,1,0:T(8,128)}, s32[3]{0:T(128)S(1)}) custom-call(s32[3]{0:T(128)S(1)} %get-tuple-element.284.refs_0_, bf16[768,1024]{1,0:T(8,128)(2,1)} %get-tuple-element.210.refs_1_, bf16[2,768,1024]{2,1,0:T(8,128)(2,1)} %get-tuple-element.250.refs_2_.refs_4_, f32[768,1024]{1,0:T(8,128)} %get-tuple-element.285.refs_3_, ...), custom_call_target="tpu_custom_call" | custom-call | flops 999999995904 | bytes 1 | tf_op jit(solution)/shard_map/pallas_call | solution.py:488
  (179 shorter events, 143.5 us)
Async XLA Ops:
  11.9 22.4 %collective-permute-start = (f32[4,392,128]{2,1,0:T(8,128)}, f32[4,392,128]{2,1,0:T(8,128)}, u32[]{:S(2)}, u32[]{:S(2)}) collective-permute-start(f32[4,392,128]{2,1,0:T(8,128)} %get-tuple-element.168.refs_2_), channel_id=1, source_target_pairs={{0,8},{8,0},{16,24},{24,16},{1,9},{9,1},{17,25},{25,17},{2,10},{10... | collective-permute-start | bytes 2408456 | tf_op jit(solution)/shard_map/ppermute | solution.py:802
  14.0 20.3 %collective-permute-start.1 = (f32[4,392,128]{2,1,0:T(8,128)}, f32[4,392,128]{2,1,0:T(8,128)}, u32[]{:S(2)}, u32[]{:S(2)}) collective-permute-start(f32[4,392,128]{2,1,0:T(8,128)} %get-tuple-element.169.refs_4_), channel_id=1, source_target_pairs={{0,16},{8,24},{16,0},{24,8},{1,17},{9,25},{17,1},{25,9},{2,18},{10... | collective-permute-start | bytes 2408456 | tf_op jit(solution)/shard_map/ppermute | solution.py:802
  38.8 18.4 %collective-permute-start.2 = (f32[4,392,128]{2,1,0:T(8,128)}, f32[4,392,128]{2,1,0:T(8,128)S(1)}, u32[]{:S(2)}, u32[]{:S(2)}) collective-permute-start(f32[4,392,128]{2,1,0:T(8,128)} %get-tuple-element.171), channel_id=1, source_target_pairs={{0,16},{8,24},{16,0},{24,8},{1,17},{9,25},{17,1},{25,9},{2,18},{10... | collective-permute-start | bytes 2408456 | tf_op jit(solution)/shard_map/ppermute | solution.py:802
  39.0 18.2 %collective-permute-start.3 = (f32[4,392,128]{2,1,0:T(8,128)}, f32[4,392,128]{2,1,0:T(8,128)S(1)}, u32[]{:S(2)}, u32[]{:S(2)}) collective-permute-start(f32[4,392,128]{2,1,0:T(8,128)} %get-tuple-element.172), channel_id=1, source_target_pairs={{0,8},{8,0},{16,24},{24,16},{1,9},{9,1},{17,25},{25,17},{2,10},{10... | collective-permute-start | bytes 2408456 | tf_op jit(solution)/shard_map/ppermute | solution.py:802
  128.1 24.5 %collective-permute-start.6 = (f32[768,1536]{1,0:T(8,128)}, f32[768,1536]{1,0:T(8,128)}, u32[]{:S(2)}, u32[]{:S(2)}) collective-permute-start(f32[768,1536]{1,0:T(8,128)} %get-tuple-element.194), channel_id=1, source_target_pairs={{0,1},{1,0},{2,3},{3,2},{4,5},{5,4},{6,7},{7,6},{8,9},{9,8},{10,11... | collective-permute-start | bytes 14155784 | tf_op jit(solution)/shard_map/ppermute | solution.py:802
  135.7 24.0 %collective-permute-start.7 = (f32[4,392,128]{2,1,0:T(8,128)}, f32[4,392,128]{2,1,0:T(8,128)}, u32[]{:S(2)}, u32[]{:S(2)}) collective-permute-start(f32[4,392,128]{2,1,0:T(8,128)} %get-tuple-element.196), channel_id=1, source_target_pairs={{0,16},{8,24},{16,0},{24,8},{1,17},{9,25},{17,1},{25,9},{2,18},{10... | collective-permute-start | bytes 2408456 | tf_op jit(solution)/shard_map/ppermute | solution.py:802
  136.7 23.0 %collective-permute-start.8 = (f32[4,392,128]{2,1,0:T(8,128)}, f32[4,392,128]{2,1,0:T(8,128)}, u32[]{:S(2)}, u32[]{:S(2)}) collective-permute-start(f32[4,392,128]{2,1,0:T(8,128)} %get-tuple-element.197), channel_id=1, source_target_pairs={{0,8},{8,0},{16,24},{24,16},{1,9},{9,1},{17,25},{25,17},{2,10},{10... | collective-permute-start | bytes 2408456 | tf_op jit(solution)/shard_map/ppermute | solution.py:802
  159.1 45.7 %collective-permute-start.10 = (f32[2,96,1536]{2,1,0:T(8,128)}, f32[2,96,1536]{2,1,0:T(8,128)}, u32[]{:S(2)}, u32[]{:S(2)}) collective-permute-start(f32[2,96,1536]{2,1,0:T(8,128)} %get-tuple-element.220), channel_id=1, source_target_pairs={{0,8},{8,0},{16,24},{24,16},{1,9},{9,1},{17,25},{25,17},{2,10},{10... | collective-permute-start | bytes 3538952 | tf_op jit(solution)/shard_map/ppermute | solution.py:802
  159.4 45.4 %collective-permute-start.11 = (f32[2,96,1536]{2,1,0:T(8,128)}, f32[2,96,1536]{2,1,0:T(8,128)}, u32[]{:S(2)}, u32[]{:S(2)}) collective-permute-start(f32[2,96,1536]{2,1,0:T(8,128)} %get-tuple-element.222), channel_id=1, source_target_pairs={{0,16},{8,24},{16,0},{24,8},{1,17},{9,25},{17,1},{25,9},{2,18},{10... | collective-permute-start | bytes 3538952 | tf_op jit(solution)/shard_map/ppermute | solution.py:802
  170.8 41.5 %collective-permute-start.12 = (f32[2,384,384]{2,1,0:T(8,128)}, f32[2,384,384]{2,1,0:T(8,128)}, u32[]{:S(2)}, u32[]{:S(2)}) collective-permute-start(f32[2,384,384]{2,1,0:T(8,128)} %get-tuple-element.225), channel_id=1, source_target_pairs={{0,8},{8,0},{16,24},{24,16},{1,9},{9,1},{17,25},{25,17},{2,10},{10... | collective-permute-start | bytes 3538952 | tf_op jit(solution)/shard_map/ppermute | solution.py:802
  172.0 40.3 %collective-permute-start.13 = (f32[2,384,384]{2,1,0:T(8,128)}, f32[2,384,384]{2,1,0:T(8,128)}, u32[]{:S(2)}, u32[]{:S(2)}) collective-permute-start(f32[2,384,384]{2,1,0:T(8,128)} %get-tuple-element.227), channel_id=1, source_target_pairs={{0,16},{8,24},{16,0},{24,8},{1,17},{9,25},{17,1},{25,9},{2,18},{10... | collective-permute-start | bytes 3538952 | tf_op jit(solution)/shard_map/ppermute | solution.py:802
  195.6 33.4 %collective-permute-start.16 = (f32[768,896]{1,0:T(8,128)}, f32[768,896]{1,0:T(8,128)}, u32[]{:S(2)}, u32[]{:S(2)}) collective-permute-start(f32[768,896]{1,0:T(8,128)} %get-tuple-element.235), channel_id=1, source_target_pairs={{0,1},{1,0},{2,3},{3,2},{4,5},{5,4},{6,7},{7,6},{8,9},{9,8},{10,11... | collective-permute-start | bytes 8257544 | tf_op jit(solution)/shard_map/ppermute | solution.py:802
  216.6 20.9 %collective-permute-start.17 = (f32[1,384,384]{2,1,0:T(8,128)}, f32[1,384,384]{2,1,0:T(8,128)}, u32[]{:S(2)}, u32[]{:S(2)}) collective-permute-start(f32[1,384,384]{2,1,0:T(8,128)} %get-tuple-element.238), channel_id=1, source_target_pairs={{0,16},{8,24},{16,0},{24,8},{1,17},{9,25},{17,1},{25,9},{2,18},{10... | collective-permute-start | bytes 1769480 | tf_op jit(solution)/shard_map/ppermute | solution.py:802
  217.0 20.5 %collective-permute-start.18 = (f32[1,384,384]{2,1,0:T(8,128)}, f32[1,384,384]{2,1,0:T(8,128)}, u32[]{:S(2)}, u32[]{:S(2)}) collective-permute-start(f32[1,384,384]{2,1,0:T(8,128)} %get-tuple-element.240), channel_id=1, source_target_pairs={{0,8},{8,0},{16,24},{24,16},{1,9},{9,1},{17,25},{25,17},{2,10},{10... | collective-permute-start | bytes 1769480 | tf_op jit(solution)/shard_map/ppermute | solution.py:802
  227.7 53.6 %collective-permute-start.25 = (f32[96,1536]{1,0:T(8,128)}, f32[96,1536]{1,0:T(8,128)}, u32[]{:S(2)}, u32[]{:S(2)}) collective-permute-start(f32[96,1536]{1,0:T(8,128)} %get-tuple-element.261), channel_id=1, source_target_pairs={{0,2},{1,3},{2,0},{3,1},{4,6},{5,7},{6,4},{7,5},{8,10},{9,11},{10,... | collective-permute-start | bytes 1769480 | tf_op jit(solution)/shard_map/ppermute | solution.py:802
  258.8 27.2 %collective-permute-start.26 = (f32[384,384]{1,0:T(8,128)}, f32[384,384]{1,0:T(8,128)}, u32[]{:S(2)}, u32[]{:S(2)}) collective-permute-start(f32[384,384]{1,0:T(8,128)} %get-tuple-element.263.refs_1_), channel_id=1, source_target_pairs={{0,4},{1,5},{2,6},{3,7},{4,0},{5,1},{6,2},{7,3},{8,12},{9,13},{10,... | collective-permute-start | bytes 1769480 | tf_op jit(solution)/shard_map/ppermute | solution.py:802
  273.8 26.5 %collective-permute-start.29 = (f32[96,896]{1,0:T(8,128)}, f32[96,896]{1,0:T(8,128)}, u32[]{:S(2)}, u32[]{:S(2)}) collective-permute-start(f32[96,896]{1,0:T(8,128)} %get-tuple-element.271), channel_id=1, source_target_pairs={{0,2},{1,3},{2,0},{3,1},{4,6},{5,7},{6,4},{7,5},{8,10},{9,11},{10,... | collective-permute-start | bytes 1032200 | tf_op jit(solution)/shard_map/ppermute | solution.py:802
  288.7 40.5 %collective-permute-start.33 = (f32[384,384]{1,0:T(8,128)}, f32[384,384]{1,0:T(8,128)}, u32[]{:S(2)}, u32[]{:S(2)}) collective-permute-start(f32[384,384]{1,0:T(8,128)} %get-tuple-element.280.refs_1_), channel_id=1, source_target_pairs={{0,2},{1,3},{2,0},{3,1},{4,6},{5,7},{6,4},{7,5},{8,10},{9,11},{10,... | collective-permute-start | bytes 1769480 | tf_op jit(solution)/shard_map/ppermute | solution.py:802
  291.1 25.2 %collective-permute-start.32 = (f32[96,1536]{1,0:T(8,128)}, f32[96,1536]{1,0:T(8,128)}, u32[]{:S(2)}, u32[]{:S(2)}) collective-permute-start(f32[96,1536]{1,0:T(8,128)} %get-tuple-element.278.refs_1_), channel_id=1, source_target_pairs={{0,4},{1,5},{2,6},{3,7},{4,0},{5,1},{6,2},{7,3},{8,12},{9,13},{10,... | collective-permute-start | bytes 1769480 | tf_op jit(solution)/shard_map/ppermute | solution.py:802
  302.7 47.7 %collective-permute-start.35 = (f32[96,896]{1,0:T(8,128)}, f32[96,896]{1,0:T(8,128)}, u32[]{:S(2)}, u32[]{:S(2)}) collective-permute-start(f32[96,896]{1,0:T(8,128)} %get-tuple-element.288.refs_1_), channel_id=1, source_target_pairs={{0,4},{1,5},{2,6},{3,7},{4,0},{5,1},{6,2},{7,3},{8,12},{9,13},{10,... | collective-permute-start | bytes 1032200 | tf_op jit(solution)/shard_map/ppermute | solution.py:802
  308.7 26.9 %collective-permute-start.34 = (f32[96,768]{1,0:T(8,128)}, f32[96,768]{1,0:T(8,128)}, u32[]{:S(2)}, u32[]{:S(2)}) collective-permute-start(f32[96,768]{1,0:T(8,128)} %get-tuple-element.283), channel_id=1, source_target_pairs={{0,2},{1,3},{2,0},{3,1},{4,6},{5,7},{6,4},{7,5},{8,10},{9,11},{10,... | collective-permute-start | bytes 884744 | tf_op jit(solution)/shard_map/ppermute | solution.py:802
  319.0 41.5 %collective-permute-start.38 = (f32[96,1536]{1,0:T(8,128)}, f32[96,1536]{1,0:T(8,128)}, u32[]{:S(2)}, u32[]{:S(2)}) collective-permute-start(f32[96,1536]{1,0:T(8,128)} %get-tuple-element.294.refs_1_), channel_id=1, source_target_pairs={{0,2},{1,3},{2,0},{3,1},{4,6},{5,7},{6,4},{7,5},{8,10},{9,11},{10,... | collective-permute-start | bytes 1769480 | tf_op jit(solution)/shard_map/ppermute | solution.py:802
  332.1 20.8 %collective-permute-start.36 = (f32[768,384]{1,0:T(8,128)}, f32[768,384]{1,0:T(8,128)}, u32[]{:S(2)}, u32[]{:S(2)}) collective-permute-start(f32[768,384]{1,0:T(8,128)} %get-tuple-element.290.refs_1_), channel_id=1, source_target_pairs={{0,1},{1,0},{2,3},{3,2},{4,5},{5,4},{6,7},{7,6},{8,9},{9,8},{10,11... | collective-permute-start | bytes 3538952 | tf_op jit(solution)/shard_map/ppermute | solution.py:802
  337.9 18.8 %collective-permute-start.37 = (f32[96,768]{1,0:T(8,128)}, f32[96,768]{1,0:T(8,128)}, u32[]{:S(2)}, u32[]{:S(2)}) collective-permute-start(f32[96,768]{1,0:T(8,128)} %get-tuple-element.292.refs_1_), channel_id=1, source_target_pairs={{0,4},{1,5},{2,6},{3,7},{4,0},{5,1},{6,2},{7,3},{8,12},{9,13},{10,... | collective-permute-start | bytes 884744 | tf_op jit(solution)/shard_map/ppermute | solution.py:802
  (46 other events, 490.6 us)

commit v6 on v5

--- a/solution.py
+++ b/solution.py
@@ -471,38 +471,35 @@
 class Order:
     def __init__(self, scalars):
         self.scalars = scalars
+        self.last = None
 
     def call(
         self, kernel, grid, ins, outs, scratch, args, extra=(), free=(), near=(), near_out=(), limit=VMEM_LIMIT
     ):
         count = 1 + len(extra)
-        placed = len(scratch)
+        before = () if self.last is None else (pltpu.with_memory_space_constraint(*self.last),)
+        at = count + len(ins)
 
         def stepped(*refs):
-            s_ref, handed = refs[0], refs[len(refs) - placed - 1]
-            rest = refs[: len(refs) - placed - 1] + refs[len(refs) - placed :]
-            kernel(*rest)
-            for i in range(s_ref.shape[0]):
-                handed[i] = s_ref[i]
-
-        *values, self.scalars = pl.pallas_call(
+            kernel(*refs[:at], *refs[at + len(before) :])
+
+        values = pl.pallas_call(
             stepped,
             grid_spec=pltpu.PrefetchScalarGridSpec(
                 num_scalar_prefetch=count,
                 grid=grid,
-                in_specs=ins,
-                out_specs=[o for o, _ in outs] + [pl.BlockSpec(memory_space=pltpu.SMEM)],
+                in_specs=list(ins) + [pl.BlockSpec(memory_space=pl.ANY) for _ in before],
+                out_specs=[o for o, _ in outs],
                 scratch_shapes=scratch,
             ),
             out_shape=[
                 (pltpu.VMEM if i in near_out else pltpu.HBM)(shape, kind)
                 for i, (_, (shape, kind)) in enumerate(outs)
-            ]
-            + [jax.ShapeDtypeStruct(self.scalars.shape, jnp.int32)],
+            ],
             compiler_params=pltpu.CompilerParams(
                 dimension_semantics=("arbitrary",) * len(grid), vmem_limit_bytes=limit
             ),
-            cost_estimate=pl.CostEstimate(flops=1000000000000, bytes_accessed=1, transcendentals=0),
+            cost_estimate=pl.CostEstimate(flops=10**12, bytes_accessed=1, transcendentals=0),
         )(
             self.scalars,
             *extra,
@@ -512,7 +509,10 @@
                 else pltpu.with_memory_space_constraint(v, pltpu.VMEM if i in near else pltpu.HBM)
                 for i, v in enumerate(args)
             ],
+            *before,
         )
+        at, value = min(reversed(list(enumerate(values))), key=lambda v: v[1].size * v[1].dtype.itemsize)
+        self.last = value, pltpu.VMEM if at in near_out else pltpu.HBM
         return values
 
 

time: 386 us -> 395 us (1.023)
  waiting for transfers between devices: 51.7 us -> 83.3 us
  starting transfers between devices: 63.7 us -> 42.7 us
    ppermute x44, waiting for transfers between devices: 51.7 us -> 83.3 us  [swap(): return lax.ppermute(value, axis, [(i, i ^ distance) for i in range(count)])]
    ppermute x44, starting transfers between devices: 63.7 us -> 42.7 us  [swap(): return lax.ppermute(value, axis, [(i, i ^ distance) for i in range(count)])]
  transfers between devices with their start and end apart: 44 -> 44, of which waited for: 15 -> 15; matrix products, arithmetic and copies ran while one was open for 2% -> 2% of each run, Pallas kernels for 48% -> 47%
where the time goes in v6:
time: 395 us; the launch traced here: 393 us
  Pallas kernels  256 us (65%)
  waiting for transfers between devices  83.3 us (21%)
  starting transfers between devices  42.7 us (11%)
  local copies, waits for them, and re-layouts  9.22 us (2%)
    pallas_call x42, Pallas kernels, call(): pl.pallas_call(stepped, grid_spec=pltpu.PrefetchScalarGridSpec(num_scalar...  256 us
    ppermute x44, waiting for transfers between devices, swap(): return lax.ppermute(value, axis, [(i, i ^ distance) for i in range(count)])  83.3 us
    ppermute x44, starting transfers between devices, swap(): return lax.ppermute(value, axis, [(i, i ^ distance) for i in range(count)])  42.7 us
  transfers between devices with their start and end apart: 44, of which 15 were waited for; matrix products, arithmetic and copies ran while one was open for 2% of the time, Pallas kernels for 47%

profile of v6, /device:TPU:1, one launch (start us, length us, event | category | flops | bytes accessed | tf_op | source)
XLA Modules:
  0.0 393.3 jit_solution(415755799110927345)
XLA Ops:
  1.4 10.4 %shard_map.220 = (f32[4,8,256]{2,1,0:T(8,128)}, bf16[768,1024]{1,0:T(8,128)(2,1)}, bf16[768,1024]{1,0:T(8,128)(2,1)}, bf16[768,1024]{1,0:T(8,128)(2,1)}, bf16[4,...) custom-call(s32[3]{0:T(128)S(1)} %pad_add_fusion.refs_0_, ...), custom_call_target="tpu_custom_call" | custom-call | flops 999999995904 | bytes 1 | tf_op jit(solution)/shard_map/pallas_call | solution.py:486
  15.1 18.1 %shard_map.221 = (bf16[768,1024]{1,0:T(8,128)(2,1)}, bf16[768,1024]{1,0:T(8,128)(2,1)}, f32[768,1024]{1,0:T(8,128)}, f32[16,1024]{1,0:T(8,128)}, bf16[768,768]{1...) custom-call(s32[3]{0:T(128)S(1)} %pad_add_fusion.refs_0_, ...), custom_call_target="tpu_custom_call" | custom-call | flops 999999995904 | bytes 1 | tf_op jit(solution)/shard_map/pallas_call | solution.py:486
  34.2 4.4 %shard_map.222 = (f32[4,392,128]{2,1,0:T(8,128)}, f32[4,392,128]{2,1,0:T(8,128)}) custom-call(s32[3]{0:T(128)S(1)} %pad_add_fusion.refs_0_, f32[16,4]{1,0:T(8,128)S(1)} %stack.59.refs_1_, f32[4,392,128]{2,1,0:T(8,128)S(1)} %copy-done.7, f32[4,392,128]{2,1,0:T(8,128)} %collective-permute-done.refs_3_.refs_2_, f32[4,392,128]{2,1,0:T(8,128)S(1)} %copy-done.8, ...), custom_call_target="tpu_custom_call" | custom-call | flops 999999995904 | bytes 1 | tf_op jit(solution)/shard_map/pallas_call | solution.py:486
  42.6 14.3 %collective-permute-done.2.refs_3_ = f32[4,392,128]{2,1,0:T(8,128)S(1)} collective-permute-done((f32[4,392,128]{2,1,0:T(8,128)}, f32[4,392,128]{2,1,0:T(8,128)S(1)}, u32[]{:S(2)}, u32[]{:S(2)}) %collective-permute-start.2) | collective-permute-done | bytes 802848 | tf_op jit(solution)/shard_map/ppermute | solution.py:802
  56.9 5.5 %shard_map.223 = (f32[4,392,128]{2,1,0:T(8,128)}, f32[4,392,128]{2,1,0:T(8,128)}) custom-call(s32[3]{0:T(128)S(1)} %pad_add_fusion.refs_0_, f32[16,4]{1,0:T(8,128)S(1)} %stack.59.refs_1_, f32[4,392,128]{2,1,0:T(8,128)} %collective-permute-done.refs_3_.refs_2_, f32[4,392,128]{2,1,0:T(8,128)S(1)} %collective-permute-done.2.refs_3_, ...), custom_call_target="tpu_custom_call" | custom-call | flops 999999995904 | bytes 1 | tf_op jit(solution)/shard_map/pallas_call | solution.py:486
  65.2 48.5 %shard_map.224 = (bf16[4,256,768]{2,1,0:T(8,128)(2,1)}, bf16[768,1024]{1,0:T(8,128)(2,1)}, bf16[768,1024]{1,0:T(8,128)(2,1)}, bf16[3072,1024]{1,0:T(8,128)(2,1)}...) custom-call(s32[3]{0:T(128)} %copy-done.2, ...), custom_call_target="tpu_custom_call" | custom-call | flops 999999995904 | bytes 1 | tf_op jit(solution)/shard_map/pallas_call | solution.py:486
  115.3 12.2 %shard_map.225 = (f32[768,1536]{1,0:T(8,128)}, f32[768,1536]{1,0:T(8,128)}) custom-call(s32[3]{0:T(128)S(1)} %copy-done.3, bf16[768,1024]{1,0:T(8,128)(2,1)} %get-tuple-element.131.refs_1_, bf16[3072,1024]{1,0:T(8,128)(2,1)} %get-tuple-element.132.refs_2_, f32[16,1024]{1,0:T(8,128)} %get-tuple-element.126.refs_3_.refs_8_), custom_call_target="tpu_custom_call" | custom-call | flops 999999995904 | bytes 1 | tf_op jit(solution)/shard_map/pallas_call | solution.py:486
  131.4 4.3 %shard_map.226 = (f32[4,392,128]{2,1,0:T(8,128)}, f32[4,392,128]{2,1,0:T(8,128)}) custom-call(s32[3]{0:T(128)S(1)} %copy-done.3, f32[16,4]{1,0:T(8,128)S(1)} %stack.59.refs_1_, f32[4,392,128]{2,1,0:T(8,128)S(1)} %copy-done.9, f32[4,392,128]{2,1,0:T(8,128)} %collective-permute-done.4.refs_3_.refs_2_, f32[4,392,128]{2,1,0:T(8,128)S(1)} %copy-done.10, ...), custom_call_target="tpu_custom_call" | custom-call | flops 999999995904 | bytes 1 | tf_op jit(solution)/shard_map/pallas_call | solution.py:486
  137.7 10.5 %shard_map.227 = (f32[3072,384]{1,0:T(8,128)}, f32[3072,384]{1,0:T(8,128)}) custom-call(s32[3]{0:T(128)S(1)} %copy-done.3, bf16[3072,1024]{1,0:T(8,128)(2,1)} %get-tuple-element.127.refs_1_, bf16[768,1024]{1,0:T(8,128)(2,1)} %get-tuple-element.128.refs_2_, f32[4,392,128]{2,1,0:T(8,128)} %get-tuple-element.134.refs_3_), custom_call_target="tpu_custom_call" | custom-call | flops 999999995904 | bytes 1 | tf_op jit(solution)/shard_map/pallas_call | solution.py:486
  152.4 6.4 %shard_map.228 = (f32[2,96,1536]{2,1,0:T(8,128)}, f32[2,96,1536]{2,1,0:T(8,128)}, f32[2,96,1536]{2,1,0:T(8,128)}, f32[2,96,1536]{2,1,0:T(8,128)}) custom-call(s32[3]{0:T(128)S(1)} %copy-done.3, f32[4,192,1536]{2,1,0:T(8,128)} %bitcast.35, f32[4,192,1536]{2,1,0:T(8,128)} %bitcast.6.refs_2_.refs_4_.refs_6_.refs_8_, f32[4,192,1536]{2,1,0:T(8,128)} %bitcast.36, ...), custom_call_target="tpu_custom_call" | custom-call | flops 999999995904 | bytes 1 | tf_op jit(solution)/shard_map/pallas_call | solution.py:486
  159.6 4.7 %shard_map.229 = (f32[4,392,128]{2,1,0:T(8,128)}, f32[4,392,128]{2,1,0:T(8,128)}) custom-call(s32[3]{0:T(128)S(1)} %copy-done.3, f32[16,4]{1,0:T(8,128)S(1)} %stack.59.refs_1_, f32[4,392,128]{2,1,0:T(8,128)} %collective-permute-done.4.refs_3_.refs_2_, f32[4,392,128]{2,1,0:T(8,128)} %collective-permute-done.7.refs_3_, ...), custom_call_target="tpu_custom_call" | custom-call | flops 999999995904 | bytes 1 | tf_op jit(solution)/shard_map/pallas_call | solution.py:486
  164.3 6.5 %shard_map.230 = (f32[2,384,384]{2,1,0:T(8,128)}, f32[2,384,384]{2,1,0:T(8,128)}, f32[2,384,384]{2,1,0:T(8,128)}, f32[2,384,384]{2,1,0:T(8,128)}) custom-call(s32[3]{0:T(128)S(1)} %copy-done.3, f32[4,768,384]{2,1,0:T(8,128)} %bitcast.31, f32[4,768,384]{2,1,0:T(8,128)} %bitcast.4.refs_2_.refs_4_.refs_6_.refs_8_, f32[4,768,384]{2,1,0:T(8,128)} %bitcast.32, ...), custom_call_target="tpu_custom_call" | custom-call | flops 999999995904 | bytes 1 | tf_op jit(solution)/shard_map/pallas_call | solution.py:486
  173.1 14.7 %shard_map.231 = (bf16[768,1024]{1,0:T(8,128)(2,1)}, f32[768,1024]{1,0:T(8,128)}, f32[768,1024]{1,0:T(8,128)}) custom-call(s32[3]{0:T(128)S(1)} %copy-done.3, f32[4,8,256]{2,1,0:T(8,128)} %get-tuple-element.105.refs_1_.refs_9_, bf16[768,1024]{1,0:T(8,128)(2,1)} %get-tuple-element.109.refs_2_, bf16[768,1024]{1,0:T(8,128)(2,1)} %get-tuple-element.122.refs_3_.refs_2_, ...), custom_call_target="tpu_custom_call" | custom-call | flops 999999995904 | bytes 1 | tf_op jit(solution)/shard_map/pallas_call | solution.py:486
  187.7 7.7 %shard_map.232 = (f32[768,896]{1,0:T(8,128)}, f32[768,896]{1,0:T(8,128)}) custom-call(s32[3]{0:T(128)S(1)} %copy-done.3, bf16[768,1024]{1,0:T(8,128)(2,1)} %get-tuple-element.147.refs_1_, bf16[1,768,1024]{2,1,0:T(8,128)(2,1)} %bitcast.48, bf16[768,1024]{1,0:T(8,128)(2,1)} %get-tuple-element.106.refs_2_.refs_7_.refs_3_.refs_1_, ...), custom_call_target="tpu_custom_call" | custom-call | flops 999999995904 | bytes 1 | tf_op jit(solution)/shard_map/pallas_call | solution.py:486
  196.6 8.0 %shard_map.233.refs_9_.refs_2_.refs_4_ = bf16[2,768,1024]{2,1,0:T(8,128)(2,1)} custom-call(s32[3]{0:T(128)S(1)} %copy-done.3, f32[4,8,256]{2,1,0:T(8,128)} %get-tuple-element.105.refs_1_.refs_9_, bf16[768,1024]{1,0:T(8,128)(2,1)} %get-tuple-element.122.refs_3_.refs_2_, bf16[768,1024]{1,0:T(8,128)(2,1)} %get-tuple-element.108.refs_4_.refs_3_, ...), custom_call_target="tpu_custom_call" | custom-call | flops 999999995904 | bytes 1 | tf_op jit(solution)/shard_map/pallas_call | solution.py:486
  212.2 4.4 %shard_map.235 = (f32[1,384,384]{2,1,0:T(8,128)}, f32[1,384,384]{2,1,0:T(8,128)}, f32[1,384,384]{2,1,0:T(8,128)}, f32[1,384,384]{2,1,0:T(8,128)}) custom-call(s32[3]{0:T(128)S(1)} %copy-done.3, f32[2,384,384]{2,1,0:T(8,128)} %get-tuple-element.152.refs_1_.refs_3_, f32[2,384,384]{2,1,0:T(8,128)} %collective-permute-done.10.refs_2_.refs_4_, ...), custom_call_target="tpu_custom_call" | custom-call | flops 999999995904 | bytes 1 | tf_op jit(solution)/shard_map/pallas_call | solution.py:486
  216.6 8.2 %collective-permute-done.17.refs_2_ = f32[1,96,1536]{2,1,0:T(8,128)} collective-permute-done((f32[1,96,1536]{2,1,0:T(8,128)}, f32[1,96,1536]{2,1,0:T(8,128)}, u32[]{:S(2)}, u32[]{:S(2)}) %collective-permute-start.17) | collective-permute-done | bytes 589856 | tf_op jit(solution)/shard_map/ppermute | solution.py:802
  230.4 4.4 %shard_map.237 = (f32[2,96,896]{2,1,0:T(8,128)}, f32[2,96,896]{2,1,0:T(8,128)}, f32[2,96,896]{2,1,0:T(8,128)}, f32[2,96,896]{2,1,0:T(8,128)}) custom-call(s32[3]{0:T(128)S(1)} %copy-done.3, f32[4,192,896]{2,1,0:T(8,128)} %bitcast.39, f32[4,192,896]{2,1,0:T(8,128)} %bitcast.10.refs_2_.refs_4_.refs_6_.refs_8_, f32[4,192,896]{2,1,0:T(8,128)} %bitcast.40, ...), custom_call_target="tpu_custom_call" | custom-call | flops 999999995904 | bytes 1 | tf_op jit(solution)/shard_map/pallas_call | solution.py:486
  236.3 6.5 %collective-permute-done.14.refs_2_ = f32[1,384,384]{2,1,0:T(8,128)} collective-permute-done((f32[1,384,384]{2,1,0:T(8,128)}, f32[1,384,384]{2,1,0:T(8,128)}, u32[]{:S(2)}, u32[]{:S(2)}) %collective-permute-start.14) | collective-permute-done | bytes 589856 | tf_op jit(solution)/shard_map/ppermute | solution.py:802
  245.7 12.0 %collective-permute-done.20.refs_2_.refs_4_ = f32[2,96,896]{2,1,0:T(8,128)} collective-permute-done((f32[2,96,896]{2,1,0:T(8,128)}, f32[2,96,896]{2,1,0:T(8,128)}, u32[]{:S(2)}, u32[]{:S(2)}) %collective-permute-start.20) | collective-permute-done | bytes 688160 | tf_op jit(solution)/shard_map/ppermute | solution.py:802
  267.8 7.2 %shard_map.241 = (f32[768,768]{1,0:T(8,128)}, f32[768,768]{1,0:T(8,128)}) custom-call(s32[3]{0:T(128)S(1)} %copy-done.3, bf16[768,1024]{1,0:T(8,128)(2,1)} %get-tuple-element.106.refs_2_.refs_7_.refs_3_.refs_1_, bf16[2,768,1024]{2,1,0:T(8,128)(2,1)} %shard_map.233.refs_9_.refs_2_.refs_4_, ...), custom_call_target="tpu_custom_call" | custom-call | flops 999999995904 | bytes 1 | tf_op jit(solution)/shard_map/pallas_call | solution.py:486
  290.6 16.7 %collective-permute-done.27.refs_2_ = f32[384,384]{1,0:T(8,128)} collective-permute-done((f32[384,384]{1,0:T(8,128)}, f32[384,384]{1,0:T(8,128)}, u32[]{:S(2)}, u32[]{:S(2)}) %collective-permute-start.27) | collective-permute-done | bytes 589856 | tf_op jit(solution)/shard_map/ppermute | solution.py:802
  327.6 12.3 %collective-permute-done.33.refs_2_ = f32[384,384]{1,0:T(8,128)} collective-permute-done((f32[384,384]{1,0:T(8,128)}, f32[384,384]{1,0:T(8,128)}, u32[]{:S(2)}, u32[]{:S(2)}) %collective-permute-start.33) | collective-permute-done | bytes 589856 | tf_op jit(solution)/shard_map/ppermute | solution.py:802
  348.9 9.7 %shard_map.252.refs_3_ = f32[4,256,768]{2,1,0:T(8,128)} custom-call(s32[3]{0:T(128)S(1)} %copy-done.3, bf16[768,1024]{1,0:T(8,128)(2,1)} %get-tuple-element.142.refs_6_.refs_1_, bf16[2,768,1024]{2,1,0:T(8,128)(2,1)} %shard_map.233.refs_9_.refs_2_.refs_4_, f32[768,1024]{1,0:T(8,128)} %get-tuple-element.151.refs_3_, bf16[768,768]{1,0:T(8,128)(2,1)} %refs_4_.3, ...), custom_call_target="tpu_custom_call" | custom-call | flops 999999995904 | bytes 1 | tf_op jit(solution)/shard_map/pallas_call | solution.py:486
  (191 shorter events, 134.7 us)
Async XLA Ops:
  11.9 22.3 %collective-permute-start = (f32[4,392,128]{2,1,0:T(8,128)}, f32[4,392,128]{2,1,0:T(8,128)}, u32[]{:S(2)}, u32[]{:S(2)}) collective-permute-start(f32[4,392,128]{2,1,0:T(8,128)} %get-tuple-element.112.refs_2_), channel_id=1, source_target_pairs={{0,8},{8,0},{16,24},{24,16},{1,9},{9,1},{17,25},{25,17},{2,10},{10... | collective-permute-start | bytes 2408456 | tf_op jit(solution)/shard_map/ppermute | solution.py:802
  13.9 20.2 %collective-permute-start.1 = (f32[4,392,128]{2,1,0:T(8,128)}, f32[4,392,128]{2,1,0:T(8,128)}, u32[]{:S(2)}, u32[]{:S(2)}) collective-permute-start(f32[4,392,128]{2,1,0:T(8,128)} %get-tuple-element.113.refs_4_), channel_id=1, source_target_pairs={{0,16},{8,24},{16,0},{24,8},{1,17},{9,25},{17,1},{25,9},{2,18},{10... | collective-permute-start | bytes 2408456 | tf_op jit(solution)/shard_map/ppermute | solution.py:802
  127.5 25.0 %collective-permute-start.9 = (f32[768,1536]{1,0:T(8,128)}, f32[768,1536]{1,0:T(8,128)}, u32[]{:S(2)}, u32[]{:S(2)}) collective-permute-start(f32[768,1536]{1,0:T(8,128)} %get-tuple-element.138), channel_id=1, source_target_pairs={{0,1},{1,0},{2,3},{3,2},{4,5},{5,4},{6,7},{7,6},{8,9},{9,8},{10,11... | collective-permute-start | bytes 14155784 | tf_op jit(solution)/shard_map/ppermute | solution.py:802
  135.7 23.9 %collective-permute-start.7 = (f32[4,392,128]{2,1,0:T(8,128)}, f32[4,392,128]{2,1,0:T(8,128)}, u32[]{:S(2)}, u32[]{:S(2)}) collective-permute-start(f32[4,392,128]{2,1,0:T(8,128)} %get-tuple-element.137), channel_id=1, source_target_pairs={{0,16},{8,24},{16,0},{24,8},{1,17},{9,25},{17,1},{25,9},{2,18},{10... | collective-permute-start | bytes 2408456 | tf_op jit(solution)/shard_map/ppermute | solution.py:802
  136.7 22.9 %collective-permute-start.8 = (f32[4,392,128]{2,1,0:T(8,128)}, f32[4,392,128]{2,1,0:T(8,128)}, u32[]{:S(2)}, u32[]{:S(2)}) collective-permute-start(f32[4,392,128]{2,1,0:T(8,128)} %get-tuple-element.134.refs_3_), channel_id=1, source_target_pairs={{0,8},{8,0},{16,24},{24,16},{1,9},{9,1},{17,25},{25,17},{2,10},{10... | collective-permute-start | bytes 2408456 | tf_op jit(solution)/shard_map/ppermute | solution.py:802
  158.9 45.7 %collective-permute-start.12 = (f32[2,96,1536]{2,1,0:T(8,128)}, f32[2,96,1536]{2,1,0:T(8,128)}, u32[]{:S(2)}, u32[]{:S(2)}) collective-permute-start(f32[2,96,1536]{2,1,0:T(8,128)} %get-tuple-element.156), channel_id=1, source_target_pairs={{0,8},{8,0},{16,24},{24,16},{1,9},{9,1},{17,25},{25,17},{2,10},{10... | collective-permute-start | bytes 3538952 | tf_op jit(solution)/shard_map/ppermute | solution.py:802
  159.3 45.2 %collective-permute-start.13 = (f32[2,96,1536]{2,1,0:T(8,128)}, f32[2,96,1536]{2,1,0:T(8,128)}, u32[]{:S(2)}, u32[]{:S(2)}) collective-permute-start(f32[2,96,1536]{2,1,0:T(8,128)} %get-tuple-element.157), channel_id=1, source_target_pairs={{0,16},{8,24},{16,0},{24,8},{1,17},{9,25},{17,1},{25,9},{2,18},{10... | collective-permute-start | bytes 3538952 | tf_op jit(solution)/shard_map/ppermute | solution.py:802
  170.7 41.3 %collective-permute-start.10 = (f32[2,384,384]{2,1,0:T(8,128)}, f32[2,384,384]{2,1,0:T(8,128)}, u32[]{:S(2)}, u32[]{:S(2)}) collective-permute-start(f32[2,384,384]{2,1,0:T(8,128)} %get-tuple-element.153), channel_id=1, source_target_pairs={{0,8},{8,0},{16,24},{24,16},{1,9},{9,1},{17,25},{25,17},{2,10},{10... | collective-permute-start | bytes 3538952 | tf_op jit(solution)/shard_map/ppermute | solution.py:802
  171.9 40.3 %collective-permute-start.11 = (f32[2,384,384]{2,1,0:T(8,128)}, f32[2,384,384]{2,1,0:T(8,128)}, u32[]{:S(2)}, u32[]{:S(2)}) collective-permute-start(f32[2,384,384]{2,1,0:T(8,128)} %get-tuple-element.154), channel_id=1, source_target_pairs={{0,16},{8,24},{16,0},{24,8},{1,17},{9,25},{17,1},{25,9},{2,18},{10... | collective-permute-start | bytes 3538952 | tf_op jit(solution)/shard_map/ppermute | solution.py:802
  195.4 34.9 %collective-permute-start.16 = (f32[768,896]{1,0:T(8,128)}, f32[768,896]{1,0:T(8,128)}, u32[]{:S(2)}, u32[]{:S(2)}) collective-permute-start(f32[768,896]{1,0:T(8,128)} %get-tuple-element.163), channel_id=1, source_target_pairs={{0,1},{1,0},{2,3},{3,2},{4,5},{5,4},{6,7},{7,6},{8,9},{9,8},{10,11... | collective-permute-start | bytes 8257544 | tf_op jit(solution)/shard_map/ppermute | solution.py:802
  227.6 60.3 %collective-permute-start.28 = (f32[96,1536]{1,0:T(8,128)}, f32[96,1536]{1,0:T(8,128)}, u32[]{:S(2)}, u32[]{:S(2)}) collective-permute-start(f32[96,1536]{1,0:T(8,128)} %get-tuple-element.185), channel_id=1, source_target_pairs={{0,2},{1,3},{2,0},{3,1},{4,6},{5,7},{6,4},{7,5},{8,10},{9,11},{10,... | collective-permute-start | bytes 1769480 | tf_op jit(solution)/shard_map/ppermute | solution.py:802
  234.7 22.9 %collective-permute-start.20 = (f32[2,96,896]{2,1,0:T(8,128)}, f32[2,96,896]{2,1,0:T(8,128)}, u32[]{:S(2)}, u32[]{:S(2)}) collective-permute-start(f32[2,96,896]{2,1,0:T(8,128)} %get-tuple-element.172), channel_id=1, source_target_pairs={{0,8},{8,0},{16,24},{24,16},{1,9},{9,1},{17,25},{25,17},{2,10},{10... | collective-permute-start | bytes 2064392 | tf_op jit(solution)/shard_map/ppermute | solution.py:802
  235.4 22.3 %collective-permute-start.21 = (f32[2,96,896]{2,1,0:T(8,128)}, f32[2,96,896]{2,1,0:T(8,128)}, u32[]{:S(2)}, u32[]{:S(2)}) collective-permute-start(f32[2,96,896]{2,1,0:T(8,128)} %get-tuple-element.173), channel_id=1, source_target_pairs={{0,16},{8,24},{16,0},{24,8},{1,17},{9,25},{17,1},{25,9},{2,18},{10... | collective-permute-start | bytes 2064392 | tf_op jit(solution)/shard_map/ppermute | solution.py:802
  265.6 41.6 %collective-permute-start.27 = (f32[384,384]{1,0:T(8,128)}, f32[384,384]{1,0:T(8,128)}, u32[]{:S(2)}, u32[]{:S(2)}) collective-permute-start(f32[384,384]{1,0:T(8,128)} %shard_map.240.refs_5_.refs_1_), channel_id=1, source_target_pairs={{0,4},{1,5},{2,6},{3,7},{4,0},{5,1},{6,2},{7,3},{8,12},{9,13},{10,... | collective-permute-start | bytes 1769480 | tf_op jit(solution)/shard_map/ppermute | solution.py:802
  280.9 32.2 %collective-permute-start.31 = (f32[96,896]{1,0:T(8,128)}, f32[96,896]{1,0:T(8,128)}, u32[]{:S(2)}, u32[]{:S(2)}) collective-permute-start(f32[96,896]{1,0:T(8,128)} %get-tuple-element.190), channel_id=1, source_target_pairs={{0,2},{1,3},{2,0},{3,1},{4,6},{5,7},{6,4},{7,5},{8,10},{9,11},{10,... | collective-permute-start | bytes 1032200 | tf_op jit(solution)/shard_map/ppermute | solution.py:802
  286.9 22.9 %collective-permute-start.25 = (f32[2,96,768]{2,1,0:T(8,128)}, f32[2,96,768]{2,1,0:T(8,128)}, u32[]{:S(2)}, u32[]{:S(2)}) collective-permute-start(f32[2,96,768]{2,1,0:T(8,128)} %get-tuple-element.182), channel_id=1, source_target_pairs={{0,8},{8,0},{16,24},{24,16},{1,9},{9,1},{17,25},{25,17},{2,10},{10... | collective-permute-start | bytes 1769480 | tf_op jit(solution)/shard_map/ppermute | solution.py:802
  287.4 22.5 %collective-permute-start.26 = (f32[2,96,768]{2,1,0:T(8,128)}, f32[2,96,768]{2,1,0:T(8,128)}, u32[]{:S(2)}, u32[]{:S(2)}) collective-permute-start(f32[2,96,768]{2,1,0:T(8,128)} %get-tuple-element.184), channel_id=1, source_target_pairs={{0,16},{8,24},{16,0},{24,8},{1,17},{9,25},{17,1},{25,9},{2,18},{10... | collective-permute-start | bytes 1769480 | tf_op jit(solution)/shard_map/ppermute | solution.py:802
  290.4 34.6 %collective-permute-start.34 = (f32[96,1536]{1,0:T(8,128)}, f32[96,1536]{1,0:T(8,128)}, u32[]{:S(2)}, u32[]{:S(2)}) collective-permute-start(f32[96,1536]{1,0:T(8,128)} %shard_map.244.refs_3_.refs_1_), channel_id=1, source_target_pairs={{0,4},{1,5},{2,6},{3,7},{4,0},{5,1},{6,2},{7,3},{8,12},{9,13},{10,... | collective-permute-start | bytes 1769480 | tf_op jit(solution)/shard_map/ppermute | solution.py:802
  309.9 30.0 %collective-permute-start.33 = (f32[384,384]{1,0:T(8,128)}, f32[384,384]{1,0:T(8,128)}, u32[]{:S(2)}, u32[]{:S(2)}) collective-permute-start(f32[384,384]{1,0:T(8,128)} %shard_map.245.refs_9_.refs_1_), channel_id=1, source_target_pairs={{0,2},{1,3},{2,0},{3,1},{4,6},{5,7},{6,4},{7,5},{8,10},{9,11},{10,... | collective-permute-start | bytes 1769480 | tf_op jit(solution)/shard_map/ppermute | solution.py:802
  315.4 43.2 %collective-permute-start.35 = (f32[96,896]{1,0:T(8,128)}, f32[96,896]{1,0:T(8,128)}, u32[]{:S(2)}, u32[]{:S(2)}) collective-permute-start(f32[96,896]{1,0:T(8,128)} %shard_map.247.refs_5_.refs_1_), channel_id=1, source_target_pairs={{0,4},{1,5},{2,6},{3,7},{4,0},{5,1},{6,2},{7,3},{8,12},{9,13},{10,... | collective-permute-start | bytes 1032200 | tf_op jit(solution)/shard_map/ppermute | solution.py:802
  323.0 23.2 %collective-permute-start.32 = (f32[96,768]{1,0:T(8,128)}, f32[96,768]{1,0:T(8,128)}, u32[]{:S(2)}, u32[]{:S(2)}) collective-permute-start(f32[96,768]{1,0:T(8,128)} %get-tuple-element.192), channel_id=1, source_target_pairs={{0,2},{1,3},{2,0},{3,1},{4,6},{5,7},{6,4},{7,5},{8,10},{9,11},{10,... | collective-permute-start | bytes 884744 | tf_op jit(solution)/shard_map/ppermute | solution.py:802
  327.6 41.8 %collective-permute-start.37 = (f32[96,1536]{1,0:T(8,128)}, f32[96,1536]{1,0:T(8,128)}, u32[]{:S(2)}, u32[]{:S(2)}) collective-permute-start(f32[96,1536]{1,0:T(8,128)} %shard_map.249.refs_3_.refs_1_), channel_id=1, source_target_pairs={{0,2},{1,3},{2,0},{3,1},{4,6},{5,7},{6,4},{7,5},{8,10},{9,11},{10,... | collective-permute-start | bytes 1769480 | tf_op jit(solution)/shard_map/ppermute | solution.py:802
  342.7 20.5 %collective-permute-start.39 = (f32[768,384]{1,0:T(8,128)}, f32[768,384]{1,0:T(8,128)}, u32[]{:S(2)}, u32[]{:S(2)}) collective-permute-start(f32[768,384]{1,0:T(8,128)} %shard_map.250.refs_3_.refs_1_), channel_id=1, source_target_pairs={{0,1},{1,0},{2,3},{3,2},{4,5},{5,4},{6,7},{7,6},{8,9},{9,8},{10,11... | collective-permute-start | bytes 3538952 | tf_op jit(solution)/shard_map/ppermute | solution.py:802
  348.4 18.6 %collective-permute-start.38 = (f32[96,768]{1,0:T(8,128)}, f32[96,768]{1,0:T(8,128)}, u32[]{:S(2)}, u32[]{:S(2)}) collective-permute-start(f32[96,768]{1,0:T(8,128)} %shard_map.251.refs_7_.refs_1_), channel_id=1, source_target_pairs={{0,4},{1,5},{2,6},{3,7},{4,0},{5,1},{6,2},{7,3},{8,12},{9,13},{10,... | collective-permute-start | bytes 884744 | tf_op jit(solution)/shard_map/ppermute | solution.py:802
  (52 other events, 648.1 us)

commit v7 on v5

--- a/solution.py
+++ b/solution.py
@@ -522,16 +522,30 @@
     return jnp.where(core == 0, high, low), jnp.where(core == 0, low, high)
 
 
-def tall_kernel(s_ref, a_ref, b_ref, away_ref, keep_ref):
-    away_ref[...], keep_ref[...] = pick_halves(s_ref[CORE], mm(a_ref[...], b_ref[...], NT))
-
-
-def tall_product(order, a, b):
-    count, flat = a.shape
-    tile, cut = count // 4, b.shape[0] // 2
-    out = (spec((tile, cut), lambda i, *s: (i, 0)), ((count, cut), f32))
-    ins = [spec((tile, flat), lambda i, *s: (i, 0)), spec(b.shape, lambda i, *s: (0, 0))]
-    return order.call(tall_kernel, (4,), ins, [out, out], [], (a, b))
+def tall_kernel(s_ref, a_ref, b_ref, c_ref, d_ref, away_ref, keep_ref):
+    count = a_ref.shape[0]
+    for left, right, lines in (
+        (a_ref, b_ref, slice(0, count)),
+        (c_ref, d_ref, slice(count, away_ref.shape[0])),
+    ):
+        away_ref[lines, :], keep_ref[lines, :] = pick_halves(
+            s_ref[CORE], mm(left[...], right[...], NT)
+        )
+
+
+def tall_product(order, a, b, c, d):
+    shards = lax.axis_size("seq")
+    flat = a.shape[1]
+    tall, low, cut = a.shape[0] // shards, c.shape[0] // shards, b.shape[0] // 2
+    rows = tall + low
+    out = (spec((rows, cut), lambda i, *s: (i, 0)), ((shards * rows, cut), f32))
+    ins = [
+        spec((tall, flat), lambda i, *s: (i, 0)),
+        spec(b.shape, lambda i, *s: (0, 0)),
+        spec((low, flat), lambda i, *s: (i, 0)),
+        spec(d.shape, lambda i, *s: (0, 0)),
+    ]
+    return order.call(tall_kernel, (shards,), ins, [out, out], [], (a, b, c, d))
 
 
 def wide_kernel(s_ref, a_ref, b_ref, away_ref, keep_ref):
@@ -564,35 +578,31 @@
     return order.call(wide_kernel, (2 * half,), ins, outs, [], (a, b))
 
 
-def twin_kernel(s_ref, a_ref, b_ref, c_ref, d_ref, *refs):
+def side_product_kernel(s_ref, a_ref, query_ref, kv_ref, small_ref, away_ref, keep_ref):
     core = s_ref[CORE]
-    away_ref, keep_ref = refs[-2:]
     at = 0
-    for left, right in ((a_ref, b_ref[0]), (c_ref, d_ref[0])):
-        away, keep = pick_halves(core, mm(left[...], right, NT))
+    for right in (query_ref[...], kv_ref[0], kv_ref[1]):
+        away, keep = pick_halves(core, mm(a_ref[...], right, NT))
         away_ref[:, at : at + away.shape[1]] = away
         keep_ref[:, at : at + keep.shape[1]] = keep
         at += away.shape[1]
-    if len(refs) == 3:
-        value = refs[0][...]
-        away_ref[:, at:] = jnp.where(core == 0, 0.0, value)
-        keep_ref[:, at:] = jnp.where(core == 0, value, 0.0)
-
-
-def twin_product(order, a, b, c, d, small=None):
+    value = small_ref[...]
+    away_ref[:, at:] = jnp.where(core == 0, 0.0, value)
+    keep_ref[:, at:] = jnp.where(core == 0, value, 0.0)
+
+
+def side_product(order, a, query, kv, small):
     count, flat = a.shape
     tile = count // 2
-    columns = count + (0 if small is None else small.shape[1])
-    rows = spec((tile, flat), lambda i, s: (i, 0))
-    ins, args = [], []
-    for left, (right, group) in ((a, b), (c, d)):
-        ins += [rows, spec((1, count, flat), lambda i, s, g=group: (g, 0, 0))]
-        args += [left, right]
-    if small is not None:
-        ins.append(spec((tile, small.shape[1]), lambda i, s: (i, 0)))
-        args.append(small)
+    columns = 3 * (count // 2) + small.shape[1]
+    ins = [
+        spec((tile, flat), lambda i, s: (i, 0)),
+        spec(query.shape, lambda i, s: (0, 0)),
+        spec(kv.shape, lambda i, s: (0, 0, 0)),
+        spec((tile, small.shape[1]), lambda i, s: (i, 0)),
+    ]
     out = (spec((tile, columns), lambda i, s: (i, 0)), ((count, columns), f32))
-    return order.call(twin_kernel, (2,), ins, [out, out], [], args)
+    return order.call(side_product_kernel, (2,), ins, [out, out], [], (a, query, kv, small))
 
 
 def route_kernel(s_ref, *refs):
@@ -835,13 +845,11 @@
 
 
 SCHEDULE = (
-    "in_product", "states", "back_product", "in", "states", "back",
-    "local", "mixed_product", "tail", "in", "back", "in",
-    "mixed", "back", "mixed", "back", "last_product", "mixed",
-    "last", "in", "back", "last", "mixed", "last",
-    "in", "back", "last", "tokens", "mixed", "back",
-    "last", "in", "mixed", "last", "in", "mixed",
-    "last",
+    "back_product", "in_product", "states", "back", "local", "states",
+    "in", "back", "tail", "last_product", "in", "back",
+    "last", "in", "back", "last", "in", "last",
+    "back", "last", "tokens", "in", "last", "back",
+    "in", "last", "back", "in", "last",
 )
 
 
@@ -1102,17 +1110,14 @@
         made["states"] = next(back_states)
 
     steps = {
-        "back_product": lambda: begin("back", tall_product(order, active_t, grad_second), (width,)),
+        "back_product": lambda: begin(
+            "back", tall_product(order, active_t, grad_second, att_t, grad_branch), (width,)
+        ),
         "in_product": lambda: begin("in", wide_product(order, first_t, grad_hidden), (ff,)),
-        "mixed_product": lambda: begin(
-            "mixed",
-            twin_product(order, att_t, (grad_branch[None], 0), tok_t, (made["query"][None], 0), small),
-            (width, width, 128),
-        ),
         "last_product": lambda: begin(
             "last",
-            twin_product(order, tok_t, (made["kv"], 0), tok_t, (made["kv"], 1)),
-            (width, width),
+            side_product(order, tok_t, made["query"], made["kv"], small),
+            (width, width, width, 128),
         ),
         "states": states_on,
         "local": local_back,
@@ -1135,9 +1140,9 @@
         for name in pieces:
             if name not in ends:
                 step(name)
-    (total_back,), (total_in,) = ends["back"], ends["in"]
-    total_out, total_query, vectors = ends["mixed"]
-    total_key, total_value = ends["last"]
+    (above,), (total_in,) = ends["back"], ends["in"]
+    total_back, total_out = above[: ff // shards], above[ff // shards :]
+    total_query, total_key, total_value, vectors = ends["last"]
     grad_tokens = made["tokens"]
     return (
         layer_out,

time: 386 us -> 401 us (1.039)
  waiting for transfers between devices: 51.7 us -> 80.1 us
  Pallas kernels: 257 us -> 240 us
    ppermute x44 -> x35, waiting for transfers between devices: 51.7 us -> 80.1 us  [swap(): return lax.ppermute(value, axis, [(i, i ^ distance) for i in range(count)])]
    pallas_call x42 -> x34, Pallas kernels: 257 us -> 240 us  [call(): pl.pallas_call(stepped, grid_spec=pltpu.PrefetchScalarGridSpec(num_scalar...]
    ppermute x44 -> x35, starting transfers between devices: 63.7 us -> 64.7 us  [swap(): return lax.ppermute(value, axis, [(i, i ^ distance) for i in range(count)])]
  transfers between devices with their start and end apart: 44 -> 35, of which waited for: 15 -> 16; matrix products, arithmetic and copies ran while one was open for 2% -> 2% of each run, Pallas kernels for 48% -> 42%
where the time goes in v7:
time: 401 us; the launch traced here: 399 us
  Pallas kernels  240 us (60%)
  waiting for transfers between devices  80.1 us (20%)
  starting transfers between devices  64.7 us (16%)
  local copies, waits for them, and re-layouts  12.3 us (3%)
    pallas_call x34, Pallas kernels, call(): pl.pallas_call(stepped, grid_spec=pltpu.PrefetchScalarGridSpec(num_scalar...  240 us
    ppermute x35, waiting for transfers between devices, swap(): return lax.ppermute(value, axis, [(i, i ^ distance) for i in range(count)])  80.1 us
    ppermute x35, starting transfers between devices, swap(): return lax.ppermute(value, axis, [(i, i ^ distance) for i in range(count)])  64.7 us
  transfers between devices with their start and end apart: 35, of which 16 were waited for; matrix products, arithmetic and copies ran while one was open for 2% of the time, Pallas kernels for 42%

profile of v7, /device:TPU:1, one launch (start us, length us, event | category | flops | bytes accessed | tf_op | source)
XLA Modules:
  0.0 399.3 jit_solution(581394465025815053)
XLA Ops:
  1.4 10.5 %shard_map.220 = (f32[4,8,256]{2,1,0:T(8,128)}, bf16[768,1024]{1,0:T(8,128)(2,1)}, bf16[768,1024]{1,0:T(8,128)(2,1)}, bf16[768,1024]{1,0:T(8,128)(2,1)}, bf16[4,...) custom-call(s32[3]{0:T(128)S(1)} %pad_add_fusion.refs_0_, ...), custom_call_target="tpu_custom_call" | custom-call | flops 999999995904 | bytes 1 | tf_op jit(solution)/shard_map/pallas_call | solution.py:488
  15.2 18.2 %shard_map.221 = (bf16[768,1024]{1,0:T(8,128)(2,1)}, bf16[768,1024]{1,0:T(8,128)(2,1)}, f32[768,1024]{1,0:T(8,128)}, f32[16,1024]{1,0:T(8,128)}, bf16[768,768]{1...) custom-call(s32[3]{0:T(128)S(1)} %get-tuple-element.138.refs_0_, ...), custom_call_target="tpu_custom_call" | custom-call | flops 999999995904 | bytes 1 | tf_op jit(solution)/shard_map/pallas_call | solution.py:488
  42.8 14.4 %collective-permute-done.2.refs_3_ = f32[4,392,128]{2,1,0:T(8,128)S(1)} collective-permute-done((f32[4,392,128]{2,1,0:T(8,128)}, f32[4,392,128]{2,1,0:T(8,128)S(1)}, u32[]{:S(2)}, u32[]{:S(2)}) %collective-permute-start.2) | collective-permute-done | bytes 802848 | tf_op jit(solution)/shard_map/ppermute | solution.py:812
  57.2 5.5 %shard_map.223 = (f32[4,392,128]{2,1,0:T(8,128)}, f32[4,392,128]{2,1,0:T(8,128)}, s32[3]{0:T(128)S(1)}) custom-call(s32[3]{0:T(128)S(1)} %get-tuple-element.146.refs_0_, f32[16,4]{1,0:T(8,128)S(1)} %stack.59.refs_1_, f32[4,392,128]{2,1,0:T(8,128)} %collective-permute-done.refs_3_.refs_2_, f32[4,392,128]{2,1,0:T(8,128)S(1)} %collective-permute-done.2.refs_3_, ...), custom_call_target="tpu_custom_call" | custom-call | flops 999999995904 | bytes 1 | tf_op jit(solution)/shard_map/pallas_call | solution.py:488
  65.5 48.4 %shard_map.224 = (bf16[4,256,768]{2,1,0:T(8,128)(2,1)}, bf16[768,1024]{1,0:T(8,128)(2,1)}, bf16[768,1024]{1,0:T(8,128)(2,1)}, bf16[3072,1024]{1,0:T(8,128)(2,1)}...) custom-call(s32[3]{0:T(128)} %copy-done.19, ...), custom_call_target="tpu_custom_call" | custom-call | flops 999999995904 | bytes 1 | tf_op jit(solution)/shard_map/pallas_call | solution.py:488
  116.0 13.0 %shard_map.225 = (f32[3840,384]{1,0:T(8,128)}, f32[3840,384]{1,0:T(8,128)}, s32[3]{0:T(128)S(1)}) custom-call(s32[3]{0:T(128)S(1)} %copy-done.18, bf16[3072,1024]{1,0:T(8,128)(2,1)} %get-tuple-element.160.refs_1_, bf16[768,1024]{1,0:T(8,128)(2,1)} %get-tuple-element.161.refs_2_, bf16[768,1024]{1,0:T(8,128)(2,1)} %get-tuple-element.162.refs_3_, ...), custom_call_target="tpu_custom_call" | custom-call | flops 999999995904 | bytes 1 | tf_op jit(solution)/shard_map/pallas_call | solution.py:488
  129.0 12.2 %shard_map.226 = (f32[768,1536]{1,0:T(8,128)}, f32[768,1536]{1,0:T(8,128)}, s32[3]{0:T(128)S(1)}) custom-call(s32[3]{0:T(128)S(1)} %get-tuple-element.164.refs_0_, bf16[768,1024]{1,0:T(8,128)(2,1)} %get-tuple-element.165.refs_1_, bf16[3072,1024]{1,0:T(8,128)(2,1)} %get-tuple-element.166.refs_2_), custom_call_target="tpu_custom_call" | custom-call | flops 999999995904 | bytes 1 | tf_op jit(solution)/shard_map/pallas_call | solution.py:488
  150.0 10.5 %collective-permute-done.6 = f32[3840,384]{1,0:T(8,128)} collective-permute-done((f32[3840,384]{1,0:T(8,128)}, f32[3840,384]{1,0:T(8,128)}, u32[]{:S(2)}, u32[]{:S(2)}) %collective-permute-start.6) | collective-permute-done | bytes 5898272 | tf_op jit(solution)/shard_map/ppermute | solution.py:812
  160.4 8.0 %shard_map.228 = (f32[2,480,384]{2,1,0:T(8,128)}, f32[2,480,384]{2,1,0:T(8,128)}, f32[2,480,384]{2,1,0:T(8,128)}, f32[2,480,384]{2,1,0:T(8,128)}, s32[3]{0:T(128)S(1)}) custom-call(s32[3]{0:T(128)S(1)} %get-tuple-element.170.refs_0_, f32[4,960,384]{2,1,0:T(8,128)} %bitcast.27, f32[4,960,384]{2,1,0:T(8,128)} %bitcast.4.refs_2_.refs_4_.refs_6_.refs_8_, ...), custom_call_target="tpu_custom_call" | custom-call | flops 999999995904 | bytes 1 | tf_op jit(solution)/shard_map/pallas_call | solution.py:488
  169.9 14.7 %shard_map.229 = (bf16[768,1024]{1,0:T(8,128)(2,1)}, f32[768,1024]{1,0:T(8,128)}, f32[768,1024]{1,0:T(8,128)}, s32[3]{0:T(128)S(1)}) custom-call(s32[3]{0:T(128)S(1)} %get-tuple-element.173.refs_0_, f32[4,8,256]{2,1,0:T(8,128)} %get-tuple-element.139.refs_1_, bf16[768,1024]{1,0:T(8,128)(2,1)} %get-tuple-element.150.refs_2_, ...), custom_call_target="tpu_custom_call" | custom-call | flops 999999995904 | bytes 1 | tf_op jit(solution)/shard_map/pallas_call | solution.py:488
  184.6 4.7 %shard_map.230 = (f32[4,392,128]{2,1,0:T(8,128)}, f32[4,392,128]{2,1,0:T(8,128)}, s32[3]{0:T(128)S(1)}) custom-call(s32[3]{0:T(128)S(1)} %get-tuple-element.179.refs_0_, f32[16,4]{1,0:T(8,128)S(1)} %stack.59.refs_1_, f32[4,392,128]{2,1,0:T(8,128)} %collective-permute-done.4.refs_3_.refs_2_, f32[4,392,128]{2,1,0:T(8,128)} %collective-permute-done.7.refs_3_, ...), custom_call_target="tpu_custom_call" | custom-call | flops 999999995904 | bytes 1 | tf_op jit(solution)/shard_map/pallas_call | solution.py:488
  189.3 6.4 %shard_map.231 = (f32[2,96,1536]{2,1,0:T(8,128)}, f32[2,96,1536]{2,1,0:T(8,128)}, f32[2,96,1536]{2,1,0:T(8,128)}, f32[2,96,1536]{2,1,0:T(8,128)}, s32[3]{0:T(128)S(1)}) custom-call(s32[3]{0:T(128)S(1)} %get-tuple-element.182.refs_0_, f32[4,192,1536]{2,1,0:T(8,128)} %bitcast.31, f32[4,192,1536]{2,1,0:T(8,128)} %bitcast.6.refs_2_.refs_4_.refs_6_.refs_8_, ...), custom_call_target="tpu_custom_call" | custom-call | flops 999999995904 | bytes 1 | tf_op jit(solution)/shard_map/pallas_call | solution.py:488
  197.3 5.0 %collective-permute-done.10.refs_2_.refs_4_ = f32[2,480,384]{2,1,0:T(8,128)} collective-permute-done((f32[2,480,384]{2,1,0:T(8,128)}, f32[2,480,384]{2,1,0:T(8,128)}, u32[]{:S(2)}, u32[]{:S(2)}) %collective-permute-start.10) | collective-permute-done | bytes 1474592 | tf_op jit(solution)/shard_map/ppermute | solution.py:812
  203.2 4.9 %shard_map.232 = (f32[1,480,384]{2,1,0:T(8,128)}, f32[1,480,384]{2,1,0:T(8,128)}, f32[1,480,384]{2,1,0:T(8,128)}, f32[1,480,384]{2,1,0:T(8,128)}, s32[3]{0:T(128)S(1)}) custom-call(s32[3]{0:T(128)S(1)} %get-tuple-element.185.refs_0_, f32[2,480,384]{2,1,0:T(8,128)} %get-tuple-element.186.refs_1_.refs_3_, ...), custom_call_target="tpu_custom_call" | custom-call | flops 999999995904 | bytes 1 | tf_op jit(solution)/shard_map/pallas_call | solution.py:488
  208.7 8.0 %shard_map.233 = (bf16[2,768,1024]{2,1,0:T(8,128)(2,1)}, s32[3]{0:T(128)S(1)}) custom-call(s32[3]{0:T(128)S(1)} %get-tuple-element.190.refs_0_, f32[4,8,256]{2,1,0:T(8,128)} %get-tuple-element.139.refs_1_, bf16[768,1024]{1,0:T(8,128)(2,1)} %get-tuple-element.174.refs_3_.refs_2_, bf16[768,1024]{1,0:T(8,128)(2,1)} %get-tuple-element.142.refs_4_.refs_3_, ...), custom_call_target="tpu_custom_call" | custom-call | flops 999999995904 | bytes 1 | tf_op jit(solution)/shard_map/pallas_call | solution.py:488
  216.7 9.3 %shard_map.234 = (f32[768,1280]{1,0:T(8,128)}, f32[768,1280]{1,0:T(8,128)}, s32[3]{0:T(128)S(1)}) custom-call(s32[3]{0:T(128)S(1)} %get-tuple-element.196.refs_0_, bf16[768,1024]{1,0:T(8,128)(2,1)} %get-tuple-element.140.refs_2_.refs_7_.refs_1_, bf16[768,1024]{1,0:T(8,128)(2,1)} %get-tuple-element.197.refs_2_.refs_1_, ...), custom_call_target="tpu_custom_call" | custom-call | flops 999999995904 | bytes 1 | tf_op jit(solution)/shard_map/pallas_call | solution.py:488
  236.6 7.6 %collective-permute-done.14.refs_2_ = f32[1,480,384]{2,1,0:T(8,128)} collective-permute-done((f32[1,480,384]{2,1,0:T(8,128)}, f32[1,480,384]{2,1,0:T(8,128)}, u32[]{:S(2)}, u32[]{:S(2)}) %collective-permute-start.14) | collective-permute-done | bytes 737312 | tf_op jit(solution)/shard_map/ppermute | solution.py:812
  248.6 5.4 %shard_map.237 = (f32[2,96,1280]{2,1,0:T(8,128)}, f32[2,96,1280]{2,1,0:T(8,128)}, f32[2,96,1280]{2,1,0:T(8,128)}, f32[2,96,1280]{2,1,0:T(8,128)}, s32[3]{0:T(128)S(1)}) custom-call(s32[3]{0:T(128)S(1)} %get-tuple-element.210.refs_0_, f32[4,192,1280]{2,1,0:T(8,128)} %bitcast.35, f32[4,192,1280]{2,1,0:T(8,128)} %bitcast.8.refs_2_.refs_4_.refs_6_.refs_8_, ...), custom_call_target="tpu_custom_call" | custom-call | flops 999999995904 | bytes 1 | tf_op jit(solution)/shard_map/pallas_call | solution.py:488
  268.0 14.8 %collective-permute-done.20.refs_2_.refs_4_ = f32[2,96,1280]{2,1,0:T(8,128)} collective-permute-done((f32[2,96,1280]{2,1,0:T(8,128)}, f32[2,96,1280]{2,1,0:T(8,128)}, u32[]{:S(2)}, u32[]{:S(2)}) %collective-permute-start.20) | collective-permute-done | bytes 983072 | tf_op jit(solution)/shard_map/ppermute | solution.py:812
  304.1 9.0 %collective-permute-done.26.refs_2_ = f32[96,1280]{1,0:T(8,128)} collective-permute-done((f32[96,1280]{1,0:T(8,128)}, f32[96,1280]{1,0:T(8,128)}, u32[]{:S(2)}, u32[]{:S(2)}) %collective-permute-start.26) | collective-permute-done | bytes 491552 | tf_op jit(solution)/shard_map/ppermute | solution.py:812
  315.4 16.7 %collective-permute-start.28 = (f32[96,1280]{1,0:T(8,128)}, f32[96,1280]{1,0:T(8,128)}, u32[]{:S(2)}, u32[]{:S(2)}) collective-permute-start(f32[96,1280]{1,0:T(8,128)} %get-tuple-element.245.refs_1_), channel_id=1, source_target_pairs={{0,4},{1,5},{2,6},{3,7},{4,0},{5,1},{6,2},{7,3},{8,12},{9,13},{10,... | collective-permute-start | bytes 1474568 | tf_op jit(solution)/shard_map/ppermute | solution.py:812
  332.2 9.8 %shard_map.245 = (f32[4,256,768]{2,1,0:T(8,128)}, s32[3]{0:T(128)S(1)}) custom-call(s32[3]{0:T(128)S(1)} %get-tuple-element.239.refs_0_, bf16[768,1024]{1,0:T(8,128)(2,1)} %get-tuple-element.197.refs_2_.refs_1_, bf16[2,768,1024]{2,1,0:T(8,128)(2,1)} %get-tuple-element.198.refs_3_.refs_2_, f32[768,1024]{1,0:T(8,128)} %get-tuple-element.240.refs_3_, ...), custom_call_target="tpu_custom_call" | custom-call | flops 999999995904 | bytes 1 | tf_op jit(solution)/shard_map/pallas_call | solution.py:488
  358.7 4.4 %collective-permute-start.32 = (f32[960,384]{1,0:T(8,128)}, f32[960,384]{1,0:T(8,128)}, u32[]{:S(2)}, u32[]{:S(2)}) collective-permute-start(f32[960,384]{1,0:T(8,128)} %get-tuple-element.253.refs_1_), channel_id=1, source_target_pairs={{0,1},{1,0},{2,3},{3,2},{4,5},{5,4},{6,7},{7,6},{8,9},{9,8},{10,11... | collective-permute-start | bytes 4423688 | tf_op jit(solution)/shard_map/ppermute | solution.py:812
  369.5 6.1 %collective-permute-start.33 = (f32[192,1536]{1,0:T(8,128)}, f32[192,1536]{1,0:T(8,128)}, u32[]{:S(2)}, u32[]{:S(2)}) collective-permute-start(f32[192,1536]{1,0:T(8,128)} %get-tuple-element.255.refs_1_), channel_id=1, source_target_pairs={{0,1},{1,0},{2,3},{3,2},{4,5},{5,4},{6,7},{7,6},{8,9},{9,8},{10,11... | collective-permute-start | bytes 3538952 | tf_op jit(solution)/shard_map/ppermute | solution.py:812
  (153 shorter events, 130.8 us)
Async XLA Ops:
  11.9 22.4 %collective-permute-start = (f32[4,392,128]{2,1,0:T(8,128)}, f32[4,392,128]{2,1,0:T(8,128)}, u32[]{:S(2)}, u32[]{:S(2)}) collective-permute-start(f32[4,392,128]{2,1,0:T(8,128)} %get-tuple-element.144.refs_2_), channel_id=1, source_target_pairs={{0,8},{8,0},{16,24},{24,16},{1,9},{9,1},{17,25},{25,17},{2,10},{10... | collective-permute-start | bytes 2408456 | tf_op jit(solution)/shard_map/ppermute | solution.py:812
  113.8 30.3 %collective-permute-start.4 = (f32[4,392,128]{2,1,0:T(8,128)}, f32[4,392,128]{2,1,0:T(8,128)}, u32[]{:S(2)}, u32[]{:S(2)}) collective-permute-start(f32[4,392,128]{2,1,0:T(8,128)} %get-tuple-element.168.refs_2_), channel_id=1, source_target_pairs={{0,8},{8,0},{16,24},{24,16},{1,9},{9,1},{17,25},{25,17},{2,10},{10... | collective-permute-start | bytes 2408456 | tf_op jit(solution)/shard_map/ppermute | solution.py:812
  114.1 30.0 %collective-permute-start.5 = (f32[4,392,128]{2,1,0:T(8,128)}, f32[4,392,128]{2,1,0:T(8,128)}, u32[]{:S(2)}, u32[]{:S(2)}) collective-permute-start(f32[4,392,128]{2,1,0:T(8,128)} %get-tuple-element.169.refs_4_), channel_id=1, source_target_pairs={{0,16},{8,24},{16,0},{24,8},{1,17},{9,25},{17,1},{25,9},{2,18},{10... | collective-permute-start | bytes 2408456 | tf_op jit(solution)/shard_map/ppermute | solution.py:812
  141.1 48.2 %collective-permute-start.9 = (f32[768,1536]{1,0:T(8,128)}, f32[768,1536]{1,0:T(8,128)}, u32[]{:S(2)}, u32[]{:S(2)}) collective-permute-start(f32[768,1536]{1,0:T(8,128)} %get-tuple-element.184), channel_id=1, source_target_pairs={{0,1},{1,0},{2,3},{3,2},{4,5},{5,4},{6,7},{7,6},{8,9},{9,8},{10,11... | collective-permute-start | bytes 14155784 | tf_op jit(solution)/shard_map/ppermute | solution.py:812
  148.5 36.0 %collective-permute-start.7 = (f32[4,392,128]{2,1,0:T(8,128)}, f32[4,392,128]{2,1,0:T(8,128)}, u32[]{:S(2)}, u32[]{:S(2)}) collective-permute-start(f32[4,392,128]{2,1,0:T(8,128)} %get-tuple-element.180), channel_id=1, source_target_pairs={{0,16},{8,24},{16,0},{24,8},{1,17},{9,25},{17,1},{25,9},{2,18},{10... | collective-permute-start | bytes 2408456 | tf_op jit(solution)/shard_map/ppermute | solution.py:812
  148.6 36.0 %collective-permute-start.8 = (f32[4,392,128]{2,1,0:T(8,128)}, f32[4,392,128]{2,1,0:T(8,128)}, u32[]{:S(2)}, u32[]{:S(2)}) collective-permute-start(f32[4,392,128]{2,1,0:T(8,128)} %get-tuple-element.181), channel_id=1, source_target_pairs={{0,8},{8,0},{16,24},{24,16},{1,9},{9,1},{17,25},{25,17},{2,10},{10... | collective-permute-start | bytes 2408456 | tf_op jit(solution)/shard_map/ppermute | solution.py:812
  168.4 33.9 %collective-permute-start.10 = (f32[2,480,384]{2,1,0:T(8,128)}, f32[2,480,384]{2,1,0:T(8,128)}, u32[]{:S(2)}, u32[]{:S(2)}) collective-permute-start(f32[2,480,384]{2,1,0:T(8,128)} %get-tuple-element.187), channel_id=1, source_target_pairs={{0,8},{8,0},{16,24},{24,16},{1,9},{9,1},{17,25},{25,17},{2,10},{10... | collective-permute-start | bytes 4423688 | tf_op jit(solution)/shard_map/ppermute | solution.py:812
  169.7 33.5 %collective-permute-start.11 = (f32[2,480,384]{2,1,0:T(8,128)}, f32[2,480,384]{2,1,0:T(8,128)}, u32[]{:S(2)}, u32[]{:S(2)}) collective-permute-start(f32[2,480,384]{2,1,0:T(8,128)} %get-tuple-element.189), channel_id=1, source_target_pairs={{0,16},{8,24},{16,0},{24,8},{1,17},{9,25},{17,1},{25,9},{2,18},{10... | collective-permute-start | bytes 4423688 | tf_op jit(solution)/shard_map/ppermute | solution.py:812
  195.7 31.8 %collective-permute-start.12 = (f32[2,96,1536]{2,1,0:T(8,128)}, f32[2,96,1536]{2,1,0:T(8,128)}, u32[]{:S(2)}, u32[]{:S(2)}) collective-permute-start(f32[2,96,1536]{2,1,0:T(8,128)} %get-tuple-element.202), channel_id=1, source_target_pairs={{0,8},{8,0},{16,24},{24,16},{1,9},{9,1},{17,25},{25,17},{2,10},{10... | collective-permute-start | bytes 3538952 | tf_op jit(solution)/shard_map/ppermute | solution.py:812
  195.9 32.6 %collective-permute-start.13 = (f32[2,96,1536]{2,1,0:T(8,128)}, f32[2,96,1536]{2,1,0:T(8,128)}, u32[]{:S(2)}, u32[]{:S(2)}) collective-permute-start(f32[2,96,1536]{2,1,0:T(8,128)} %get-tuple-element.204), channel_id=1, source_target_pairs={{0,16},{8,24},{16,0},{24,8},{1,17},{9,25},{17,1},{25,9},{2,18},{10... | collective-permute-start | bytes 3538952 | tf_op jit(solution)/shard_map/ppermute | solution.py:812
  208.1 36.2 %collective-permute-start.14 = (f32[1,480,384]{2,1,0:T(8,128)}, f32[1,480,384]{2,1,0:T(8,128)}, u32[]{:S(2)}, u32[]{:S(2)}) collective-permute-start(f32[1,480,384]{2,1,0:T(8,128)} %get-tuple-element.207), channel_id=1, source_target_pairs={{0,16},{8,24},{16,0},{24,8},{1,17},{9,25},{17,1},{25,9},{2,18},{10... | collective-permute-start | bytes 2211848 | tf_op jit(solution)/shard_map/ppermute | solution.py:812
  208.3 35.9 %collective-permute-start.15 = (f32[1,480,384]{2,1,0:T(8,128)}, f32[1,480,384]{2,1,0:T(8,128)}, u32[]{:S(2)}, u32[]{:S(2)}) collective-permute-start(f32[1,480,384]{2,1,0:T(8,128)} %get-tuple-element.209), channel_id=1, source_target_pairs={{0,8},{8,0},{16,24},{24,16},{1,9},{9,1},{17,25},{25,17},{2,10},{10... | collective-permute-start | bytes 2211848 | tf_op jit(solution)/shard_map/ppermute | solution.py:812
  232.8 24.1 %collective-permute-start.17 = (f32[1,96,1536]{2,1,0:T(8,128)}, f32[1,96,1536]{2,1,0:T(8,128)}, u32[]{:S(2)}, u32[]{:S(2)}) collective-permute-start(f32[1,96,1536]{2,1,0:T(8,128)} %get-tuple-element.215), channel_id=1, source_target_pairs={{0,16},{8,24},{16,0},{24,8},{1,17},{9,25},{17,1},{25,9},{2,18},{10... | collective-permute-start | bytes 1769480 | tf_op jit(solution)/shard_map/ppermute | solution.py:812
  233.1 23.8 %collective-permute-start.18 = (f32[1,96,1536]{2,1,0:T(8,128)}, f32[1,96,1536]{2,1,0:T(8,128)}, u32[]{:S(2)}, u32[]{:S(2)}) collective-permute-start(f32[1,96,1536]{2,1,0:T(8,128)} %get-tuple-element.217), channel_id=1, source_target_pairs={{0,8},{8,0},{16,24},{24,16},{1,9},{9,1},{17,25},{25,17},{2,10},{10... | collective-permute-start | bytes 1769480 | tf_op jit(solution)/shard_map/ppermute | solution.py:812
  259.7 28.6 %collective-permute-start.22 = (f32[96,1536]{1,0:T(8,128)}, f32[96,1536]{1,0:T(8,128)}, u32[]{:S(2)}, u32[]{:S(2)}) collective-permute-start(f32[96,1536]{1,0:T(8,128)} %get-tuple-element.228), channel_id=1, source_target_pairs={{0,2},{1,3},{2,0},{3,1},{4,6},{5,7},{6,4},{7,5},{8,10},{9,11},{10,... | collective-permute-start | bytes 1769480 | tf_op jit(solution)/shard_map/ppermute | solution.py:812
  261.1 21.8 %collective-permute-start.20 = (f32[2,96,1280]{2,1,0:T(8,128)}, f32[2,96,1280]{2,1,0:T(8,128)}, u32[]{:S(2)}, u32[]{:S(2)}) collective-permute-start(f32[2,96,1280]{2,1,0:T(8,128)} %get-tuple-element.223), channel_id=1, source_target_pairs={{0,8},{8,0},{16,24},{24,16},{1,9},{9,1},{17,25},{25,17},{2,10},{10... | collective-permute-start | bytes 2949128 | tf_op jit(solution)/shard_map/ppermute | solution.py:812
  261.4 21.5 %collective-permute-start.21 = (f32[2,96,1280]{2,1,0:T(8,128)}, f32[2,96,1280]{2,1,0:T(8,128)}, u32[]{:S(2)}, u32[]{:S(2)}) collective-permute-start(f32[2,96,1280]{2,1,0:T(8,128)} %get-tuple-element.225), channel_id=1, source_target_pairs={{0,16},{8,24},{16,0},{24,8},{1,17},{9,25},{17,1},{25,9},{2,18},{10... | collective-permute-start | bytes 2949128 | tf_op jit(solution)/shard_map/ppermute | solution.py:812
  265.6 34.6 %collective-permute-start.25 = (f32[480,384]{1,0:T(8,128)}, f32[480,384]{1,0:T(8,128)}, u32[]{:S(2)}, u32[]{:S(2)}) collective-permute-start(f32[480,384]{1,0:T(8,128)} %get-tuple-element.235.refs_1_), channel_id=1, source_target_pairs={{0,4},{1,5},{2,6},{3,7},{4,0},{5,1},{6,2},{7,3},{8,12},{9,13},{10,... | collective-permute-start | bytes 2211848 | tf_op jit(solution)/shard_map/ppermute | solution.py:812
  290.8 51.2 %collective-permute-start.27 = (f32[96,1536]{1,0:T(8,128)}, f32[96,1536]{1,0:T(8,128)}, u32[]{:S(2)}, u32[]{:S(2)}) collective-permute-start(f32[96,1536]{1,0:T(8,128)} %get-tuple-element.243.refs_1_), channel_id=1, source_target_pairs={{0,4},{1,5},{2,6},{3,7},{4,0},{5,1},{6,2},{7,3},{8,12},{9,13},{10,... | collective-permute-start | bytes 1769480 | tf_op jit(solution)/shard_map/ppermute | solution.py:812
  303.0 52.6 %collective-permute-start.29 = (f32[480,384]{1,0:T(8,128)}, f32[480,384]{1,0:T(8,128)}, u32[]{:S(2)}, u32[]{:S(2)}) collective-permute-start(f32[480,384]{1,0:T(8,128)} %get-tuple-element.247.refs_1_), channel_id=1, source_target_pairs={{0,2},{1,3},{2,0},{3,1},{4,6},{5,7},{6,4},{7,5},{8,10},{9,11},{10,... | collective-permute-start | bytes 2211848 | tf_op jit(solution)/shard_map/ppermute | solution.py:812
  315.4 33.7 %collective-permute-start.28 = (f32[96,1280]{1,0:T(8,128)}, f32[96,1280]{1,0:T(8,128)}, u32[]{:S(2)}, u32[]{:S(2)}) collective-permute-start(f32[96,1280]{1,0:T(8,128)} %get-tuple-element.245.refs_1_), channel_id=1, source_target_pairs={{0,4},{1,5},{2,6},{3,7},{4,0},{5,1},{6,2},{7,3},{8,12},{9,13},{10,... | collective-permute-start | bytes 1474568 | tf_op jit(solution)/shard_map/ppermute | solution.py:812
  344.6 22.0 %collective-permute-start.30 = (f32[96,1536]{1,0:T(8,128)}, f32[96,1536]{1,0:T(8,128)}, u32[]{:S(2)}, u32[]{:S(2)}) collective-permute-start(f32[96,1536]{1,0:T(8,128)} %get-tuple-element.249.refs_1_), channel_id=1, source_target_pairs={{0,2},{1,3},{2,0},{3,1},{4,6},{5,7},{6,4},{7,5},{8,10},{9,11},{10,... | collective-permute-start | bytes 1769480 | tf_op jit(solution)/shard_map/ppermute | solution.py:812
  351.7 25.4 %collective-permute-start.31 = (f32[96,1280]{1,0:T(8,128)}, f32[96,1280]{1,0:T(8,128)}, u32[]{:S(2)}, u32[]{:S(2)}) collective-permute-start(f32[96,1280]{1,0:T(8,128)} %get-tuple-element.251.refs_1_), channel_id=1, source_target_pairs={{0,2},{1,3},{2,0},{3,1},{4,6},{5,7},{6,4},{7,5},{8,10},{9,11},{10,... | collective-permute-start | bytes 1474568 | tf_op jit(solution)/shard_map/ppermute | solution.py:812
  358.7 24.5 %collective-permute-start.32 = (f32[960,384]{1,0:T(8,128)}, f32[960,384]{1,0:T(8,128)}, u32[]{:S(2)}, u32[]{:S(2)}) collective-permute-start(f32[960,384]{1,0:T(8,128)} %get-tuple-element.253.refs_1_), channel_id=1, source_target_pairs={{0,1},{1,0},{2,3},{3,2},{4,5},{5,4},{6,7},{7,6},{8,9},{9,8},{10,11... | collective-permute-start | bytes 4423688 | tf_op jit(solution)/shard_map/ppermute | solution.py:812
  (36 other events, 393.6 us)

commit v8 on v5

--- a/solution.py
+++ b/solution.py
@@ -230,10 +230,6 @@
             denom_ref[h : h + 1, :] = out[HEAD_DIM : HEAD_DIM + 1]
 
 
-def mean_rows(v):
-    return jnp.sum(v, axis=0, keepdims=True) * (1.0 / v.shape[0])
-
-
 def fold_lanes(v):
     total = v[:, :128]
     for at in range(128, v.shape[1], 128):
@@ -241,20 +237,34 @@
     return total
 
 
-def add_to(ref, value):
-    first = pl.program_id(0) == 0
-
-    @pl.when(first)
-    def _():
-        ref[...] = value
-
-    @pl.when(jnp.logical_not(first))
-    def _():
-        ref[...] += value
-
-
-def norm_back(grad_norm, normed, inv_scale):
-    return inv_scale * (grad_norm - mean_rows(grad_norm) - normed * mean_rows(grad_norm * normed))
+def chunks_of(ref):
+    return [slice(at, at + 128) for at in range(0, ref.shape[0], 128)]
+
+
+def fold_rows(v):
+    return jnp.sum(v.reshape(v.shape[0] // 8, 8, v.shape[1]), axis=0)
+
+
+def mean_of(fold, count):
+    return jnp.sum(fold, axis=0, keepdims=True) * (1.0 / count)
+
+
+def center(ref, more=None):
+    width, lanes = ref.shape
+    fold = jnp.zeros((8, lanes), f32)
+    for c in chunks_of(ref):
+        value = ref[c, :]
+        if more is not None:
+            value = value + more[c, :].astype(f32)
+            ref[c, :] = value
+        fold = fold + fold_rows(value)
+    mean = mean_of(fold, width)
+    fold = jnp.zeros((8, lanes), f32)
+    for c in chunks_of(ref):
+        value = ref[c, :] - mean
+        ref[c, :] = value
+        fold = fold + fold_rows(value * value)
+    return lax.rsqrt(mean_of(fold, width) + norm_eps)
 
 
 def lane_total(ref):
@@ -303,9 +313,16 @@
     fold_shift_one,
     fold_gain_two,
     fold_shift_two,
+    work,
 ):
     ff = w_in_ref.shape[1]
     step = 768
+
+    @pl.when(pl.program_id(0) == 0)
+    def _():
+        for ref in (fold_gain_one, fold_shift_one, fold_gain_two, fold_shift_two):
+            ref[...] = jnp.zeros_like(ref)
+
     table = tab_ref[0]
     cos, sin = table[COS_READ : COS_READ + 1], table[SIN_READ : SIN_READ + 1]
     states = (state_a, state_b)
@@ -318,15 +335,15 @@
         value = numer * inverse
         attended[head_slice(h), :] = value
         att_t_ref[head_slice(h), :] = value.astype(bf16)
-    summed = tok_t_ref[...].astype(f32) + mm(w_out_t[...], att_t_ref[...])
-    centered = summed - mean_rows(summed)
-    scale_one = lax.rsqrt(mean_rows(centered * centered) + norm_eps)
-    normed = centered * scale_one
-    normed_one[...] = normed
-    first_out = normed * gain_one_ref[...] + shift_one_ref[...]
-    total[...] = first_out
-    first_low = first_out.astype(bf16)
-    first_t_ref[...] = first_low
+    total[...] = mm(w_out_t[...], att_t_ref[...])
+    scale_one = center(total, tok_t_ref)
+    for c in chunks_of(total):
+        normed = total[c, :] * scale_one
+        normed_one[c, :] = normed
+        first_out = normed * gain_one_ref[c, :] + shift_one_ref[c, :]
+        total[c, :] = first_out
+        first_t_ref[c, :] = first_out.astype(bf16)
+    first_low = first_t_ref[...]
     for at in range(0, ff, step):
         hidden = mm(w_in_t[at : at + step, :], first_low)
         half = 0.5 * (1.0 + lax.erf(hidden * 0.7071067811865476))
@@ -335,31 +352,45 @@
         active_t_ref[at : at + step, :] = active
         slope[at : at + step, :] = (half + hidden * bell).astype(bf16)
         total[...] += mm(w_back_t[:, at : at + step], active)
-    summed = total[...]
-    centered = summed - mean_rows(summed)
-    scale_two = lax.rsqrt(mean_rows(centered * centered) + norm_eps)
-    normed = centered * scale_two
-    layer_ref[0] = (normed * gain_two_ref[...] + shift_two_ref[...]).T.astype(bf16)
-    grad_top = cot_ref[0].T.astype(f32)
-    add_to(fold_gain_two, fold_lanes(grad_top * normed))
-    add_to(fold_shift_two, fold_lanes(grad_top))
-    grad_mid = norm_back(grad_top * gain_two_ref[...], normed, scale_two)
-    total[...] = grad_mid
-    grad_second = grad_mid.astype(bf16)
-    grad_second_ref[...] = grad_second
+    scale_two = center(total)
+    fold_one = fold_two = jnp.zeros((8, total.shape[1]), f32)
+    for c in chunks_of(total):
+        normed = total[c, :] * scale_two
+        total[c, :] = normed
+        layer_ref[0, :, c] = (normed * gain_two_ref[c, :] + shift_two_ref[c, :]).T.astype(bf16)
+        grad_top = cot_ref[0, :, c].T.astype(f32)
+        fold_gain_two[c, :] += fold_lanes(grad_top * normed)
+        fold_shift_two[c, :] += fold_lanes(grad_top)
+        grad_norm = grad_top * gain_two_ref[c, :]
+        work[c, :] = grad_norm
+        fold_one = fold_one + fold_rows(grad_norm)
+        fold_two = fold_two + fold_rows(grad_norm * normed)
+    mean_one, mean_two = mean_of(fold_one, total.shape[0]), mean_of(fold_two, total.shape[0])
+    for c in chunks_of(total):
+        grad_mid = scale_two * (work[c, :] - mean_one - total[c, :] * mean_two)
+        total[c, :] = grad_mid
+        grad_second_ref[c, :] = grad_mid.astype(bf16)
+    grad_second = grad_second_ref[...]
     for at in range(0, ff, step):
         grad_active = mm(w_back_ref[at : at + step, :], grad_second)
         low = (grad_active * slope[at : at + step, :].astype(f32)).astype(bf16)
         grad_hidden_ref[at : at + step, :] = low
         total[...] += mm(w_in_ref[:, at : at + step], low)
-    grad_first = total[...]
-    normed = normed_one[...]
-    add_to(fold_gain_one, fold_lanes(grad_first * normed))
-    add_to(fold_shift_one, fold_lanes(grad_first))
-    grad_base = norm_back(grad_first * gain_one_ref[...], normed, scale_one)
-    grad_base_ref[...] = grad_base
-    grad_branch = grad_base.astype(bf16)
-    grad_branch_ref[...] = grad_branch
+    fold_one = fold_two = jnp.zeros((8, total.shape[1]), f32)
+    for c in chunks_of(total):
+        grad_first, normed = total[c, :], normed_one[c, :]
+        fold_gain_one[c, :] += fold_lanes(grad_first * normed)
+        fold_shift_one[c, :] += fold_lanes(grad_first)
+        grad_norm = grad_first * gain_one_ref[c, :]
+        work[c, :] = grad_norm
+        fold_one = fold_one + fold_rows(grad_norm)
+        fold_two = fold_two + fold_rows(grad_norm * normed)
+    mean_one, mean_two = mean_of(fold_one, total.shape[0]), mean_of(fold_two, total.shape[0])
+    for c in chunks_of(total):
+        grad_base = scale_one * (work[c, :] - mean_one - normed_one[c, :] * mean_two)
+        grad_base_ref[c, :] = grad_base
+        grad_branch_ref[c, :] = grad_base.astype(bf16)
+    grad_branch = grad_branch_ref[...]
     total[...] = mm(w_out_ref[...], grad_branch)
     outs = (out_a, out_b)
     clear_pad(outs)
@@ -710,24 +741,25 @@
 
 
 def mix_kernel(first, s_ref, w_ref, *refs):
-    row = pl.program_id(0)
-    for i in range(2):
-        own, other = (w_ref[first + 2 * i + j, row] for j in range(2))
-        refs[4 + i][...] = own * refs[2 * i][...] + other * refs[2 * i + 1][...]
-
-
-def mix(order, weights, first, *parts):
+    for row in range(refs[0].shape[0]):
+        for i in range(2):
+            own, other = (w_ref[first + 2 * i + j, row] for j in range(2))
+            refs[4 + i][row] = own * refs[2 * i][row] + other * refs[2 * i + 1][row]
+
+
+def mix(order, weights, first, last, *parts):
     shape = parts[0].shape
-    block = spec((1,) + shape[1:], lambda r, *s: (r, 0, 0))
+    out = spec(shape, lambda i, *s: (0, 0, 0)) if last else NEAR
     return order.call(
         partial(mix_kernel, first),
-        (shape[0],),
-        [block] * 4,
-        [(block, (shape, f32))] * 2,
+        (1,),
+        [NEAR] * 4,
+        [(out, (shape, f32))] * 2,
         [],
         parts,
         (weights,),
-        free=range(4),
+        near=range(4),
+        near_out=() if last else range(2),
         limit=SMALL_LIMIT,
     )
 
@@ -791,10 +823,10 @@
     part_a, part_b = parts
     got_a, got_b = swap(part_a, "seq", 1), swap(part_b, "seq", 2)
     yield
-    next_a, next_b = mix(order, weights, first, part_a, got_a, part_b, got_b)
+    next_a, next_b = mix(order, weights, first, False, part_a, got_a, part_b, got_b)
     last_a, last_b = swap(next_a, "seq", 2), swap(next_b, "seq", 1)
     yield
-    yield mix(order, weights, first + 4, got_a, last_a, got_b, last_b)
+    yield mix(order, weights, first + 4, True, got_a, last_a, got_b, last_b)
 
 
 def swap(value, axis, distance):
@@ -999,7 +1031,8 @@
             pltpu.VMEM((16, toks), f32),
             pltpu.VMEM((width, toks), f32),
         ]
-        + [pltpu.VMEM((width, 128), f32)] * 4,
+        + [pltpu.VMEM((width, 128), f32)] * 4
+        + [pltpu.VMEM((width, toks), f32)],
         table,
         q_t,
         numer,

time: 386 us -> 380 us (0.984)
  Pallas kernels: 257 us -> 249 us
    pallas_call x42, Pallas kernels: 257 us -> 249 us  [call(): pl.pallas_call(stepped, grid_spec=pltpu.PrefetchScalarGridSpec(num_scalar...]
  transfers between devices with their start and end apart: 44 -> 44, of which waited for: 15 -> 16; matrix products, arithmetic and copies ran while one was open for 2% -> 2% of each run, Pallas kernels for 48% -> 48%
where the time goes in v8:
time: 380 us; the launch traced here: 379 us
  Pallas kernels  249 us (66%)
  starting transfers between devices  64 us (17%)
  waiting for transfers between devices  52.4 us (14%)
  local copies, waits for them, and re-layouts  11.6 us (3%)
    pallas_call x42, Pallas kernels, call(): pl.pallas_call(stepped, grid_spec=pltpu.PrefetchScalarGridSpec(num_scalar...  249 us
    ppermute x44, starting transfers between devices, swap(): return lax.ppermute(value, axis, [(i, i ^ distance) for i in range(count)])  64 us
    ppermute x44, waiting for transfers between devices, swap(): return lax.ppermute(value, axis, [(i, i ^ distance) for i in range(count)])  52.4 us
  transfers between devices with their start and end apart: 44, of which 16 were waited for; matrix products, arithmetic and copies ran while one was open for 2% of the time, Pallas kernels for 48%

profile of v8, /device:TPU:1, one launch (start us, length us, event | category | flops | bytes accessed | tf_op | source)
XLA Modules:
  0.0 378.8 jit_solution(15361209133684106708)
XLA Ops:
  1.4 10.5 %shard_map.220 = (f32[4,8,256]{2,1,0:T(8,128)}, bf16[768,1024]{1,0:T(8,128)(2,1)}, bf16[768,1024]{1,0:T(8,128)(2,1)}, bf16[768,1024]{1,0:T(8,128)(2,1)}, bf16[4,...) custom-call(s32[3]{0:T(128)S(1)} %pad_add_fusion.refs_0_, ...), custom_call_target="tpu_custom_call" | custom-call | flops 999999995904 | bytes 1 | tf_op jit(solution)/shard_map/pallas_call | solution.py:519
  15.2 18.2 %shard_map.221 = (bf16[768,1024]{1,0:T(8,128)(2,1)}, bf16[768,1024]{1,0:T(8,128)(2,1)}, f32[768,1024]{1,0:T(8,128)}, f32[16,1024]{1,0:T(8,128)}, bf16[768,768]{1...) custom-call(s32[3]{0:T(128)S(1)} %get-tuple-element.162.refs_0_, ...), custom_call_target="tpu_custom_call" | custom-call | flops 999999995904 | bytes 1 | tf_op jit(solution)/shard_map/pallas_call | solution.py:519
  41.2 14.2 %collective-permute-done.2.refs_3_ = f32[4,392,128]{2,1,0:T(8,128)S(1)} collective-permute-done((f32[4,392,128]{2,1,0:T(8,128)S(1)}, f32[4,392,128]{2,1,0:T(8,128)S(1)}, u32[]{:S(2)}, u32[]{:S(2)}) %collective-permute-start.2) | collective-permute-done | bytes 802848 | tf_op jit(solution)/shard_map/ppermute | solution.py:834
  63.5 45.3 %shard_map.224 = (bf16[4,256,768]{2,1,0:T(8,128)(2,1)}, bf16[768,1024]{1,0:T(8,128)(2,1)}, bf16[768,1024]{1,0:T(8,128)(2,1)}, bf16[3072,1024]{1,0:T(8,128)(2,1)}...) custom-call(s32[3]{0:T(128)} %copy-done.21, ...), custom_call_target="tpu_custom_call" | custom-call | flops 999999995904 | bytes 1 | tf_op jit(solution)/shard_map/pallas_call | solution.py:519
  111.0 12.2 %shard_map.225 = (f32[768,1536]{1,0:T(8,128)}, f32[768,1536]{1,0:T(8,128)}, s32[3]{0:T(128)S(1)}) custom-call(s32[3]{0:T(128)S(1)} %copy-done.20, bf16[768,1024]{1,0:T(8,128)(2,1)} %get-tuple-element.184.refs_1_, bf16[3072,1024]{1,0:T(8,128)(2,1)} %get-tuple-element.185.refs_2_), custom_call_target="tpu_custom_call" | custom-call | flops 999999995904 | bytes 1 | tf_op jit(solution)/shard_map/pallas_call | solution.py:519
  132.1 10.6 %shard_map.227 = (f32[3072,384]{1,0:T(8,128)}, f32[3072,384]{1,0:T(8,128)}, s32[3]{0:T(128)S(1)}) custom-call(s32[3]{0:T(128)S(1)} %get-tuple-element.189.refs_0_, bf16[3072,1024]{1,0:T(8,128)(2,1)} %get-tuple-element.190.refs_1_, bf16[768,1024]{1,0:T(8,128)(2,1)} %get-tuple-element.191.refs_2_), custom_call_target="tpu_custom_call" | custom-call | flops 999999995904 | bytes 1 | tf_op jit(solution)/shard_map/pallas_call | solution.py:519
  142.6 4.2 %collective-permute-start.9 = (f32[3072,384]{1,0:T(8,128)}, f32[3072,384]{1,0:T(8,128)}, u32[]{:S(2)}, u32[]{:S(2)}) collective-permute-start(f32[3072,384]{1,0:T(8,128)} %get-tuple-element.200), channel_id=1, source_target_pairs={{0,1},{1,0},{2,3},{3,2},{4,5},{5,4},{6,7},{7,6},{8,9},{9,8},{10,11... | collective-permute-start | bytes 14155784 | tf_op jit(solution)/shard_map/ppermute | solution.py:834
  146.8 6.4 %shard_map.228 = (f32[2,96,1536]{2,1,0:T(8,128)}, f32[2,96,1536]{2,1,0:T(8,128)}, f32[2,96,1536]{2,1,0:T(8,128)}, f32[2,96,1536]{2,1,0:T(8,128)}, s32[3]{0:T(128)S(1)}) custom-call(s32[3]{0:T(128)S(1)} %get-tuple-element.192.refs_0_, f32[4,192,1536]{2,1,0:T(8,128)} %bitcast.35, f32[4,192,1536]{2,1,0:T(8,128)} %bitcast.4.refs_2_.refs_4_.refs_6_.refs_8_, ...), custom_call_target="tpu_custom_call" | custom-call | flops 999999995904 | bytes 1 | tf_op jit(solution)/shard_map/pallas_call | solution.py:519
  153.9 3.9 %shard_map.229 = (f32[4,392,128]{2,1,0:T(8,128)}, f32[4,392,128]{2,1,0:T(8,128)}, s32[3]{0:T(128)S(1)}) custom-call(s32[3]{0:T(128)S(1)} %get-tuple-element.195.refs_0_, f32[16,4]{1,0:T(8,128)S(1)} %stack.59.refs_1_, f32[4,392,128]{2,1,0:T(8,128)} %collective-permute-done.4.refs_3_.refs_2_, f32[4,392,128]{2,1,0:T(8,128)} %collective-permute-done.7.refs_3_, ...), custom_call_target="tpu_custom_call" | custom-call | flops 999999995904 | bytes 1 | tf_op jit(solution)/shard_map/pallas_call | solution.py:519
  157.8 6.4 %shard_map.230 = (f32[2,384,384]{2,1,0:T(8,128)}, f32[2,384,384]{2,1,0:T(8,128)}, f32[2,384,384]{2,1,0:T(8,128)}, f32[2,384,384]{2,1,0:T(8,128)}, s32[3]{0:T(128)S(1)}) custom-call(s32[3]{0:T(128)S(1)} %get-tuple-element.198.refs_0_, f32[4,768,384]{2,1,0:T(8,128)} %bitcast.31, f32[4,768,384]{2,1,0:T(8,128)} %bitcast.6.refs_2_.refs_4_.refs_6_.refs_8_, ...), custom_call_target="tpu_custom_call" | custom-call | flops 999999995904 | bytes 1 | tf_op jit(solution)/shard_map/pallas_call | solution.py:519
  166.7 14.7 %shard_map.231 = (bf16[768,1024]{1,0:T(8,128)(2,1)}, f32[768,1024]{1,0:T(8,128)}, f32[768,1024]{1,0:T(8,128)}, s32[3]{0:T(128)S(1)}) custom-call(s32[3]{0:T(128)S(1)} %get-tuple-element.201.refs_0_, f32[4,8,256]{2,1,0:T(8,128)} %get-tuple-element.163.refs_1_, bf16[768,1024]{1,0:T(8,128)(2,1)} %get-tuple-element.174.refs_2_, ...), custom_call_target="tpu_custom_call" | custom-call | flops 999999995904 | bytes 1 | tf_op jit(solution)/shard_map/pallas_call | solution.py:519
  181.4 7.7 %shard_map.232 = (f32[768,896]{1,0:T(8,128)}, f32[768,896]{1,0:T(8,128)}, s32[3]{0:T(128)S(1)}) custom-call(s32[3]{0:T(128)S(1)} %get-tuple-element.207.refs_0_, bf16[768,1024]{1,0:T(8,128)(2,1)} %get-tuple-element.208.refs_1_, bf16[1,768,1024]{2,1,0:T(8,128)(2,1)} %bitcast.48, bf16[768,1024]{1,0:T(8,128)(2,1)} %get-tuple-element.164.refs_2_.refs_7_.refs_3_.refs_1_, ...), custom_call_target="tpu_custom_call" | custom-call | flops 999999995904 | bytes 1 | tf_op jit(solution)/shard_map/pallas_call | solution.py:519
  190.2 8.0 %shard_map.233 = (bf16[2,768,1024]{2,1,0:T(8,128)(2,1)}, s32[3]{0:T(128)S(1)}) custom-call(s32[3]{0:T(128)S(1)} %get-tuple-element.212.refs_0_, f32[4,8,256]{2,1,0:T(8,128)} %get-tuple-element.163.refs_1_, bf16[768,1024]{1,0:T(8,128)(2,1)} %get-tuple-element.202.refs_3_.refs_2_, bf16[768,1024]{1,0:T(8,128)(2,1)} %get-tuple-element.166.refs_4_.refs_3_, ...), custom_call_target="tpu_custom_call" | custom-call | flops 999999995904 | bytes 1 | tf_op jit(solution)/shard_map/pallas_call | solution.py:519
  198.2 4.3 %shard_map.234 = (f32[1,96,1536]{2,1,0:T(8,128)}, f32[1,96,1536]{2,1,0:T(8,128)}, f32[1,96,1536]{2,1,0:T(8,128)}, f32[1,96,1536]{2,1,0:T(8,128)}, s32[3]{0:T(128)S(1)}) custom-call(s32[3]{0:T(128)S(1)} %get-tuple-element.218.refs_0_, f32[2,96,1536]{2,1,0:T(8,128)} %get-tuple-element.219.refs_1_.refs_3_, ...), custom_call_target="tpu_custom_call" | custom-call | flops 999999995904 | bytes 1 | tf_op jit(solution)/shard_map/pallas_call | solution.py:519
  206.6 4.3 %shard_map.235 = (f32[1,384,384]{2,1,0:T(8,128)}, f32[1,384,384]{2,1,0:T(8,128)}, f32[1,384,384]{2,1,0:T(8,128)}, f32[1,384,384]{2,1,0:T(8,128)}, s32[3]{0:T(128)S(1)}) custom-call(s32[3]{0:T(128)S(1)} %get-tuple-element.223.refs_0_, f32[2,384,384]{2,1,0:T(8,128)} %get-tuple-element.224.refs_1_.refs_3_, ...), custom_call_target="tpu_custom_call" | custom-call | flops 999999995904 | bytes 1 | tf_op jit(solution)/shard_map/pallas_call | solution.py:519
  212.4 6.7 %collective-permute-done.14.refs_2_ = f32[1,96,1536]{2,1,0:T(8,128)} collective-permute-done((f32[1,96,1536]{2,1,0:T(8,128)}, f32[1,96,1536]{2,1,0:T(8,128)}, u32[]{:S(2)}, u32[]{:S(2)}) %collective-permute-start.14) | collective-permute-done | bytes 589856 | tf_op jit(solution)/shard_map/ppermute | solution.py:834
  223.3 4.4 %shard_map.237 = (f32[2,96,896]{2,1,0:T(8,128)}, f32[2,96,896]{2,1,0:T(8,128)}, f32[2,96,896]{2,1,0:T(8,128)}, f32[2,96,896]{2,1,0:T(8,128)}, s32[3]{0:T(128)S(1)}) custom-call(s32[3]{0:T(128)S(1)} %get-tuple-element.233.refs_0_, f32[4,192,896]{2,1,0:T(8,128)} %bitcast.39, f32[4,192,896]{2,1,0:T(8,128)} %bitcast.10.refs_2_.refs_4_.refs_6_.refs_8_, ...), custom_call_target="tpu_custom_call" | custom-call | flops 999999995904 | bytes 1 | tf_op jit(solution)/shard_map/pallas_call | solution.py:519
  236.0 9.8 %collective-permute-done.19.refs_2_.refs_4_ = f32[2,96,896]{2,1,0:T(8,128)} collective-permute-done((f32[2,96,896]{2,1,0:T(8,128)}, f32[2,96,896]{2,1,0:T(8,128)}, u32[]{:S(2)}, u32[]{:S(2)}) %collective-permute-start.19) | collective-permute-done | bytes 688160 | tf_op jit(solution)/shard_map/ppermute | solution.py:834
  255.6 7.2 %shard_map.241 = (f32[768,768]{1,0:T(8,128)}, f32[768,768]{1,0:T(8,128)}, s32[3]{0:T(128)S(1)}) custom-call(s32[3]{0:T(128)S(1)} %get-tuple-element.249.refs_0_, bf16[768,1024]{1,0:T(8,128)(2,1)} %get-tuple-element.164.refs_2_.refs_7_.refs_3_.refs_1_, bf16[2,768,1024]{2,1,0:T(8,128)(2,1)} %get-tuple-element.250.refs_2_.refs_4_, ...), custom_call_target="tpu_custom_call" | custom-call | flops 999999995904 | bytes 1 | tf_op jit(solution)/shard_map/pallas_call | solution.py:519
  270.0 4.0 %shard_map.243 = (f32[2,96,768]{2,1,0:T(8,128)}, f32[2,96,768]{2,1,0:T(8,128)}, f32[2,96,768]{2,1,0:T(8,128)}, f32[2,96,768]{2,1,0:T(8,128)}, s32[3]{0:T(128)S(1)}) custom-call(s32[3]{0:T(128)S(1)} %get-tuple-element.256.refs_0_, f32[4,192,768]{2,1,0:T(8,128)} %bitcast.43, f32[4,192,768]{2,1,0:T(8,128)} %bitcast.12.refs_2_.refs_4_.refs_6_.refs_8_, ...), custom_call_target="tpu_custom_call" | custom-call | flops 999999995904 | bytes 1 | tf_op jit(solution)/shard_map/pallas_call | solution.py:519
  304.3 6.5 %collective-permute-done.32.refs_2_ = f32[96,1536]{1,0:T(8,128)} collective-permute-done((f32[96,1536]{1,0:T(8,128)}, f32[96,1536]{1,0:T(8,128)}, u32[]{:S(2)}, u32[]{:S(2)}) %collective-permute-start.32) | collective-permute-done | bytes 589856 | tf_op jit(solution)/shard_map/ppermute | solution.py:834
  313.5 10.2 %collective-permute-start.38 = (f32[96,1536]{1,0:T(8,128)}, f32[96,1536]{1,0:T(8,128)}, u32[]{:S(2)}, u32[]{:S(2)}) collective-permute-start(f32[96,1536]{1,0:T(8,128)} %get-tuple-element.294.refs_1_), channel_id=1, source_target_pairs={{0,2},{1,3},{2,0},{3,1},{4,6},{5,7},{6,4},{7,5},{8,10},{9,11},{10,... | collective-permute-start | bytes 1769480 | tf_op jit(solution)/shard_map/ppermute | solution.py:834
  335.1 9.8 %shard_map.252 = (f32[4,256,768]{2,1,0:T(8,128)}, s32[3]{0:T(128)S(1)}) custom-call(s32[3]{0:T(128)S(1)} %get-tuple-element.284.refs_0_, bf16[768,1024]{1,0:T(8,128)(2,1)} %get-tuple-element.210.refs_1_, bf16[2,768,1024]{2,1,0:T(8,128)(2,1)} %get-tuple-element.250.refs_2_.refs_4_, f32[768,1024]{1,0:T(8,128)} %get-tuple-element.285.refs_3_, ...), custom_call_target="tpu_custom_call" | custom-call | flops 999999995904 | bytes 1 | tf_op jit(solution)/shard_map/pallas_call | solution.py:519
  347.3 3.8 %shard_map.254 = (f32[768,768]{1,0:T(8,128)}, s32[3]{0:T(128)S(1)}) custom-call(s32[3]{0:T(128)S(1)} %get-tuple-element.289.refs_0_, f32[768,384]{1,0:T(8,128)} %get-tuple-element.290.refs_1_, f32[768,384]{1,0:T(8,128)} %collective-permute-done.36.refs_2_), custom_call_target="tpu_custom_call" | custom-call | flops 999999995904 | bytes 1 | tf_op jit(solution)/shard_map/pallas_call | solution.py:519
  (179 shorter events, 144.0 us)
Async XLA Ops:
  11.9 22.4 %collective-permute-start = (f32[4,392,128]{2,1,0:T(8,128)}, f32[4,392,128]{2,1,0:T(8,128)}, u32[]{:S(2)}, u32[]{:S(2)}) collective-permute-start(f32[4,392,128]{2,1,0:T(8,128)} %get-tuple-element.168.refs_2_), channel_id=1, source_target_pairs={{0,8},{8,0},{16,24},{24,16},{1,9},{9,1},{17,25},{25,17},{2,10},{10... | collective-permute-start | bytes 2408456 | tf_op jit(solution)/shard_map/ppermute | solution.py:834
  14.0 20.3 %collective-permute-start.1 = (f32[4,392,128]{2,1,0:T(8,128)}, f32[4,392,128]{2,1,0:T(8,128)}, u32[]{:S(2)}, u32[]{:S(2)}) collective-permute-start(f32[4,392,128]{2,1,0:T(8,128)} %get-tuple-element.169.refs_4_), channel_id=1, source_target_pairs={{0,16},{8,24},{16,0},{24,8},{1,17},{9,25},{17,1},{25,9},{2,18},{10... | collective-permute-start | bytes 2408456 | tf_op jit(solution)/shard_map/ppermute | solution.py:834
  37.2 18.2 %collective-permute-start.2 = (f32[4,392,128]{2,1,0:T(8,128)S(1)}, f32[4,392,128]{2,1,0:T(8,128)S(1)}, u32[]{:S(2)}, u32[]{:S(2)}) collective-permute-start(f32[4,392,128]{2,1,0:T(8,128)S(1)} %get-tuple-element.171), channel_id=1, source_target_pairs={{0,16},{8,24},{16,0},{24,8},{1,17},{9,25},{17,1},{25,9},{2,18},{10... | collective-permute-start | bytes 2408456 | tf_op jit(solution)/shard_map/ppermute | solution.py:834
  123.2 23.6 %collective-permute-start.6 = (f32[768,1536]{1,0:T(8,128)}, f32[768,1536]{1,0:T(8,128)}, u32[]{:S(2)}, u32[]{:S(2)}) collective-permute-start(f32[768,1536]{1,0:T(8,128)} %get-tuple-element.194), channel_id=1, source_target_pairs={{0,1},{1,0},{2,3},{3,2},{4,5},{5,4},{6,7},{7,6},{8,9},{9,8},{10,11... | collective-permute-start | bytes 14155784 | tf_op jit(solution)/shard_map/ppermute | solution.py:834
  129.8 24.1 %collective-permute-start.7 = (f32[4,392,128]{2,1,0:T(8,128)}, f32[4,392,128]{2,1,0:T(8,128)}, u32[]{:S(2)}, u32[]{:S(2)}) collective-permute-start(f32[4,392,128]{2,1,0:T(8,128)} %get-tuple-element.196), channel_id=1, source_target_pairs={{0,16},{8,24},{16,0},{24,8},{1,17},{9,25},{17,1},{25,9},{2,18},{10... | collective-permute-start | bytes 2408456 | tf_op jit(solution)/shard_map/ppermute | solution.py:834
  130.9 23.0 %collective-permute-start.8 = (f32[4,392,128]{2,1,0:T(8,128)}, f32[4,392,128]{2,1,0:T(8,128)}, u32[]{:S(2)}, u32[]{:S(2)}) collective-permute-start(f32[4,392,128]{2,1,0:T(8,128)} %get-tuple-element.197), channel_id=1, source_target_pairs={{0,8},{8,0},{16,24},{24,16},{1,9},{9,1},{17,25},{25,17},{2,10},{10... | collective-permute-start | bytes 2408456 | tf_op jit(solution)/shard_map/ppermute | solution.py:834
  153.3 44.9 %collective-permute-start.10 = (f32[2,96,1536]{2,1,0:T(8,128)}, f32[2,96,1536]{2,1,0:T(8,128)}, u32[]{:S(2)}, u32[]{:S(2)}) collective-permute-start(f32[2,96,1536]{2,1,0:T(8,128)} %get-tuple-element.220), channel_id=1, source_target_pairs={{0,8},{8,0},{16,24},{24,16},{1,9},{9,1},{17,25},{25,17},{2,10},{10... | collective-permute-start | bytes 3538952 | tf_op jit(solution)/shard_map/ppermute | solution.py:834
  153.6 44.6 %collective-permute-start.11 = (f32[2,96,1536]{2,1,0:T(8,128)}, f32[2,96,1536]{2,1,0:T(8,128)}, u32[]{:S(2)}, u32[]{:S(2)}) collective-permute-start(f32[2,96,1536]{2,1,0:T(8,128)} %get-tuple-element.222), channel_id=1, source_target_pairs={{0,16},{8,24},{16,0},{24,8},{1,17},{9,25},{17,1},{25,9},{2,18},{10... | collective-permute-start | bytes 3538952 | tf_op jit(solution)/shard_map/ppermute | solution.py:834
  164.2 42.3 %collective-permute-start.12 = (f32[2,384,384]{2,1,0:T(8,128)}, f32[2,384,384]{2,1,0:T(8,128)}, u32[]{:S(2)}, u32[]{:S(2)}) collective-permute-start(f32[2,384,384]{2,1,0:T(8,128)} %get-tuple-element.225), channel_id=1, source_target_pairs={{0,8},{8,0},{16,24},{24,16},{1,9},{9,1},{17,25},{25,17},{2,10},{10... | collective-permute-start | bytes 3538952 | tf_op jit(solution)/shard_map/ppermute | solution.py:834
  165.5 41.0 %collective-permute-start.13 = (f32[2,384,384]{2,1,0:T(8,128)}, f32[2,384,384]{2,1,0:T(8,128)}, u32[]{:S(2)}, u32[]{:S(2)}) collective-permute-start(f32[2,384,384]{2,1,0:T(8,128)} %get-tuple-element.227), channel_id=1, source_target_pairs={{0,16},{8,24},{16,0},{24,8},{1,17},{9,25},{17,1},{25,9},{2,18},{10... | collective-permute-start | bytes 3538952 | tf_op jit(solution)/shard_map/ppermute | solution.py:834
  189.1 34.3 %collective-permute-start.16 = (f32[768,896]{1,0:T(8,128)}, f32[768,896]{1,0:T(8,128)}, u32[]{:S(2)}, u32[]{:S(2)}) collective-permute-start(f32[768,896]{1,0:T(8,128)} %get-tuple-element.235), channel_id=1, source_target_pairs={{0,1},{1,0},{2,3},{3,2},{4,5},{5,4},{6,7},{7,6},{8,9},{9,8},{10,11... | collective-permute-start | bytes 8257544 | tf_op jit(solution)/shard_map/ppermute | solution.py:834
  210.9 20.9 %collective-permute-start.17 = (f32[1,384,384]{2,1,0:T(8,128)}, f32[1,384,384]{2,1,0:T(8,128)}, u32[]{:S(2)}, u32[]{:S(2)}) collective-permute-start(f32[1,384,384]{2,1,0:T(8,128)} %get-tuple-element.238), channel_id=1, source_target_pairs={{0,16},{8,24},{16,0},{24,8},{1,17},{9,25},{17,1},{25,9},{2,18},{10... | collective-permute-start | bytes 1769480 | tf_op jit(solution)/shard_map/ppermute | solution.py:834
  211.2 20.6 %collective-permute-start.18 = (f32[1,384,384]{2,1,0:T(8,128)}, f32[1,384,384]{2,1,0:T(8,128)}, u32[]{:S(2)}, u32[]{:S(2)}) collective-permute-start(f32[1,384,384]{2,1,0:T(8,128)} %get-tuple-element.240), channel_id=1, source_target_pairs={{0,8},{8,0},{16,24},{24,16},{1,9},{9,1},{17,25},{25,17},{2,10},{10... | collective-permute-start | bytes 1769480 | tf_op jit(solution)/shard_map/ppermute | solution.py:834
  222.0 53.5 %collective-permute-start.25 = (f32[96,1536]{1,0:T(8,128)}, f32[96,1536]{1,0:T(8,128)}, u32[]{:S(2)}, u32[]{:S(2)}) collective-permute-start(f32[96,1536]{1,0:T(8,128)} %get-tuple-element.261), channel_id=1, source_target_pairs={{0,2},{1,3},{2,0},{3,1},{4,6},{5,7},{6,4},{7,5},{8,10},{9,11},{10,... | collective-permute-start | bytes 1769480 | tf_op jit(solution)/shard_map/ppermute | solution.py:834
  227.7 18.1 %collective-permute-start.19 = (f32[2,96,896]{2,1,0:T(8,128)}, f32[2,96,896]{2,1,0:T(8,128)}, u32[]{:S(2)}, u32[]{:S(2)}) collective-permute-start(f32[2,96,896]{2,1,0:T(8,128)} %get-tuple-element.243), channel_id=1, source_target_pairs={{0,8},{8,0},{16,24},{24,16},{1,9},{9,1},{17,25},{25,17},{2,10},{10... | collective-permute-start | bytes 2064392 | tf_op jit(solution)/shard_map/ppermute | solution.py:834
  253.3 27.4 %collective-permute-start.26 = (f32[384,384]{1,0:T(8,128)}, f32[384,384]{1,0:T(8,128)}, u32[]{:S(2)}, u32[]{:S(2)}) collective-permute-start(f32[384,384]{1,0:T(8,128)} %get-tuple-element.263.refs_1_), channel_id=1, source_target_pairs={{0,4},{1,5},{2,6},{3,7},{4,0},{5,1},{6,2},{7,3},{8,12},{9,13},{10,... | collective-permute-start | bytes 1769480 | tf_op jit(solution)/shard_map/ppermute | solution.py:834
  268.0 26.5 %collective-permute-start.29 = (f32[96,896]{1,0:T(8,128)}, f32[96,896]{1,0:T(8,128)}, u32[]{:S(2)}, u32[]{:S(2)}) collective-permute-start(f32[96,896]{1,0:T(8,128)} %get-tuple-element.271), channel_id=1, source_target_pairs={{0,2},{1,3},{2,0},{3,1},{4,6},{5,7},{6,4},{7,5},{8,10},{9,11},{10,... | collective-permute-start | bytes 1032200 | tf_op jit(solution)/shard_map/ppermute | solution.py:834
  283.4 40.3 %collective-permute-start.33 = (f32[384,384]{1,0:T(8,128)}, f32[384,384]{1,0:T(8,128)}, u32[]{:S(2)}, u32[]{:S(2)}) collective-permute-start(f32[384,384]{1,0:T(8,128)} %get-tuple-element.280.refs_1_), channel_id=1, source_target_pairs={{0,2},{1,3},{2,0},{3,1},{4,6},{5,7},{6,4},{7,5},{8,10},{9,11},{10,... | collective-permute-start | bytes 1769480 | tf_op jit(solution)/shard_map/ppermute | solution.py:834
  285.6 25.2 %collective-permute-start.32 = (f32[96,1536]{1,0:T(8,128)}, f32[96,1536]{1,0:T(8,128)}, u32[]{:S(2)}, u32[]{:S(2)}) collective-permute-start(f32[96,1536]{1,0:T(8,128)} %get-tuple-element.278.refs_1_), channel_id=1, source_target_pairs={{0,4},{1,5},{2,6},{3,7},{4,0},{5,1},{6,2},{7,3},{8,12},{9,13},{10,... | collective-permute-start | bytes 1769480 | tf_op jit(solution)/shard_map/ppermute | solution.py:834
  296.9 47.9 %collective-permute-start.35 = (f32[96,896]{1,0:T(8,128)}, f32[96,896]{1,0:T(8,128)}, u32[]{:S(2)}, u32[]{:S(2)}) collective-permute-start(f32[96,896]{1,0:T(8,128)} %get-tuple-element.288.refs_1_), channel_id=1, source_target_pairs={{0,4},{1,5},{2,6},{3,7},{4,0},{5,1},{6,2},{7,3},{8,12},{9,13},{10,... | collective-permute-start | bytes 1032200 | tf_op jit(solution)/shard_map/ppermute | solution.py:834
  302.9 27.1 %collective-permute-start.34 = (f32[96,768]{1,0:T(8,128)}, f32[96,768]{1,0:T(8,128)}, u32[]{:S(2)}, u32[]{:S(2)}) collective-permute-start(f32[96,768]{1,0:T(8,128)} %get-tuple-element.283), channel_id=1, source_target_pairs={{0,2},{1,3},{2,0},{3,1},{4,6},{5,7},{6,4},{7,5},{8,10},{9,11},{10,... | collective-permute-start | bytes 884744 | tf_op jit(solution)/shard_map/ppermute | solution.py:834
  313.5 41.5 %collective-permute-start.38 = (f32[96,1536]{1,0:T(8,128)}, f32[96,1536]{1,0:T(8,128)}, u32[]{:S(2)}, u32[]{:S(2)}) collective-permute-start(f32[96,1536]{1,0:T(8,128)} %get-tuple-element.294.refs_1_), channel_id=1, source_target_pairs={{0,2},{1,3},{2,0},{3,1},{4,6},{5,7},{6,4},{7,5},{8,10},{9,11},{10,... | collective-permute-start | bytes 1769480 | tf_op jit(solution)/shard_map/ppermute | solution.py:834
  326.5 20.8 %collective-permute-start.36 = (f32[768,384]{1,0:T(8,128)}, f32[768,384]{1,0:T(8,128)}, u32[]{:S(2)}, u32[]{:S(2)}) collective-permute-start(f32[768,384]{1,0:T(8,128)} %get-tuple-element.290.refs_1_), channel_id=1, source_target_pairs={{0,1},{1,0},{2,3},{3,2},{4,5},{5,4},{6,7},{7,6},{8,9},{9,8},{10,11... | collective-permute-start | bytes 3538952 | tf_op jit(solution)/shard_map/ppermute | solution.py:834
  332.3 18.8 %collective-permute-start.37 = (f32[96,768]{1,0:T(8,128)}, f32[96,768]{1,0:T(8,128)}, u32[]{:S(2)}, u32[]{:S(2)}) collective-permute-start(f32[96,768]{1,0:T(8,128)} %get-tuple-element.292.refs_1_), channel_id=1, source_target_pairs={{0,4},{1,5},{2,6},{3,7},{4,0},{5,1},{6,2},{7,3},{8,12},{9,13},{10,... | collective-permute-start | bytes 884744 | tf_op jit(solution)/shard_map/ppermute | solution.py:834
  (46 other events, 481.4 us)

commit v9 on v8

--- a/solution.py
+++ b/solution.py
@@ -867,12 +867,12 @@
 
 
 SCHEDULE = (
-    "in_product", "states", "back_product", "in", "states", "back",
-    "local", "mixed_product", "tail", "in", "back", "in",
-    "mixed", "back", "mixed", "back", "last_product", "mixed",
-    "last", "in", "back", "last", "mixed", "last",
-    "in", "back", "last", "tokens", "mixed", "back",
-    "last", "in", "mixed", "last", "in", "mixed",
+    "back_product", "states", "back", "local", "in_product", "states",
+    "back", "in", "mixed_product", "back", "mixed", "tail",
+    "back", "mixed", "in", "mixed", "last_product", "in",
+    "last", "mixed", "back", "in", "last", "tokens",
+    "last", "back", "mixed", "last", "in", "mixed",
+    "last", "in", "mixed", "last", "in", "back",
     "last",
 )
 

time: 380 us -> 374 us (0.984)
  starting transfers between devices: 64 us -> 55 us
    ppermute x44, starting transfers between devices: 64 us -> 55 us  [swap(): return lax.ppermute(value, axis, [(i, i ^ distance) for i in range(count)])]
  transfers between devices with their start and end apart: 44 -> 44, of which waited for: 16 -> 14; matrix products, arithmetic and copies ran while one was open for 2% -> 1% of each run, Pallas kernels for 48% -> 50%
where the time goes in v9:
time: 374 us; the launch traced here: 372 us
  Pallas kernels  249 us (67%)
  starting transfers between devices  55 us (15%)
  waiting for transfers between devices  54.7 us (15%)
  local copies, waits for them, and re-layouts  10.4 us (3%)
    pallas_call x42, Pallas kernels, call(): pl.pallas_call(stepped, grid_spec=pltpu.PrefetchScalarGridSpec(num_scalar...  249 us
    ppermute x44, starting transfers between devices, swap(): return lax.ppermute(value, axis, [(i, i ^ distance) for i in range(count)])  55 us
    ppermute x44, waiting for transfers between devices, swap(): return lax.ppermute(value, axis, [(i, i ^ distance) for i in range(count)])  54.7 us
  transfers between devices with their start and end apart: 44, of which 14 were waited for; matrix products, arithmetic and copies ran while one was open for 1% of the time, Pallas kernels for 50%

profile of v9, /device:TPU:1, one launch (start us, length us, event | category | flops | bytes accessed | tf_op | source)
XLA Modules:
  0.0 371.6 jit_solution(15682133846554630069)
XLA Ops:
  1.4 10.5 %shard_map.220 = (f32[4,8,256]{2,1,0:T(8,128)}, bf16[768,1024]{1,0:T(8,128)(2,1)}, bf16[768,1024]{1,0:T(8,128)(2,1)}, bf16[768,1024]{1,0:T(8,128)(2,1)}, bf16[4,...) custom-call(s32[3]{0:T(128)S(1)} %pad_add_fusion.refs_0_, ...), custom_call_target="tpu_custom_call" | custom-call | flops 999999995904 | bytes 1 | tf_op jit(solution)/shard_map/pallas_call | solution.py:519
  15.2 18.2 %shard_map.221 = (bf16[768,1024]{1,0:T(8,128)(2,1)}, bf16[768,1024]{1,0:T(8,128)(2,1)}, f32[768,1024]{1,0:T(8,128)}, f32[16,1024]{1,0:T(8,128)}, bf16[768,768]{1...) custom-call(s32[3]{0:T(128)S(1)} %get-tuple-element.162.refs_0_, ...), custom_call_target="tpu_custom_call" | custom-call | flops 999999995904 | bytes 1 | tf_op jit(solution)/shard_map/pallas_call | solution.py:519
  41.2 14.2 %collective-permute-done.2.refs_3_ = f32[4,392,128]{2,1,0:T(8,128)S(1)} collective-permute-done((f32[4,392,128]{2,1,0:T(8,128)S(1)}, f32[4,392,128]{2,1,0:T(8,128)S(1)}, u32[]{:S(2)}, u32[]{:S(2)}) %collective-permute-start.2) | collective-permute-done | bytes 802848 | tf_op jit(solution)/shard_map/ppermute | solution.py:834
  63.5 45.3 %shard_map.224 = (bf16[4,256,768]{2,1,0:T(8,128)(2,1)}, bf16[768,1024]{1,0:T(8,128)(2,1)}, bf16[768,1024]{1,0:T(8,128)(2,1)}, bf16[3072,1024]{1,0:T(8,128)(2,1)}...) custom-call(s32[3]{0:T(128)} %copy-done.21, ...), custom_call_target="tpu_custom_call" | custom-call | flops 999999995904 | bytes 1 | tf_op jit(solution)/shard_map/pallas_call | solution.py:519
  111.0 10.6 %shard_map.225 = (f32[3072,384]{1,0:T(8,128)}, f32[3072,384]{1,0:T(8,128)}, s32[3]{0:T(128)S(1)}) custom-call(s32[3]{0:T(128)S(1)} %copy-done.20, bf16[3072,1024]{1,0:T(8,128)(2,1)} %get-tuple-element.184.refs_1_, bf16[768,1024]{1,0:T(8,128)(2,1)} %get-tuple-element.185.refs_2_), custom_call_target="tpu_custom_call" | custom-call | flops 999999995904 | bytes 1 | tf_op jit(solution)/shard_map/pallas_call | solution.py:519
  132.5 6.4 %shard_map.227 = (f32[2,384,384]{2,1,0:T(8,128)}, f32[2,384,384]{2,1,0:T(8,128)}, f32[2,384,384]{2,1,0:T(8,128)}, f32[2,384,384]{2,1,0:T(8,128)}, s32[3]{0:T(128)S(1)}) custom-call(s32[3]{0:T(128)S(1)} %get-tuple-element.189.refs_0_, f32[4,768,384]{2,1,0:T(8,128)} %bitcast.35, f32[4,768,384]{2,1,0:T(8,128)} %bitcast.4.refs_2_.refs_4_.refs_6_.refs_8_, ...), custom_call_target="tpu_custom_call" | custom-call | flops 999999995904 | bytes 1 | tf_op jit(solution)/shard_map/pallas_call | solution.py:519
  140.4 14.9 %shard_map.228 = (bf16[768,1024]{1,0:T(8,128)(2,1)}, f32[768,1024]{1,0:T(8,128)}, f32[768,1024]{1,0:T(8,128)}, s32[3]{0:T(128)S(1)}) custom-call(s32[3]{0:T(128)S(1)} %get-tuple-element.192.refs_0_, f32[4,8,256]{2,1,0:T(8,128)} %get-tuple-element.163.refs_1_, bf16[768,1024]{1,0:T(8,128)(2,1)} %get-tuple-element.174.refs_2_, ...), custom_call_target="tpu_custom_call" | custom-call | flops 999999995904 | bytes 1 | tf_op jit(solution)/shard_map/pallas_call | solution.py:519
  155.3 12.2 %shard_map.229 = (f32[768,1536]{1,0:T(8,128)}, f32[768,1536]{1,0:T(8,128)}, s32[3]{0:T(128)S(1)}) custom-call(s32[3]{0:T(128)S(1)} %get-tuple-element.198.refs_0_, bf16[768,1024]{1,0:T(8,128)(2,1)} %get-tuple-element.199.refs_1_, bf16[3072,1024]{1,0:T(8,128)(2,1)} %get-tuple-element.200.refs_2_), custom_call_target="tpu_custom_call" | custom-call | flops 999999995904 | bytes 1 | tf_op jit(solution)/shard_map/pallas_call | solution.py:519
  171.1 3.8 %shard_map.230 = (f32[4,392,128]{2,1,0:T(8,128)}, f32[4,392,128]{2,1,0:T(8,128)}, s32[3]{0:T(128)S(1)}) custom-call(s32[3]{0:T(128)S(1)} %get-tuple-element.201.refs_0_, f32[16,4]{1,0:T(8,128)S(1)} %stack.59.refs_1_, f32[4,392,128]{2,1,0:T(8,128)} %collective-permute-done.4.refs_3_.refs_2_, f32[4,392,128]{2,1,0:T(8,128)} %collective-permute-done.7.refs_3_, ...), custom_call_target="tpu_custom_call" | custom-call | flops 999999995904 | bytes 1 | tf_op jit(solution)/shard_map/pallas_call | solution.py:519
  174.9 4.4 %shard_map.231 = (f32[1,384,384]{2,1,0:T(8,128)}, f32[1,384,384]{2,1,0:T(8,128)}, f32[1,384,384]{2,1,0:T(8,128)}, f32[1,384,384]{2,1,0:T(8,128)}, s32[3]{0:T(128)S(1)}) custom-call(s32[3]{0:T(128)S(1)} %get-tuple-element.204.refs_0_, f32[2,384,384]{2,1,0:T(8,128)} %get-tuple-element.205.refs_1_.refs_3_, ...), custom_call_target="tpu_custom_call" | custom-call | flops 999999995904 | bytes 1 | tf_op jit(solution)/shard_map/pallas_call | solution.py:519
  181.7 6.4 %shard_map.232 = (f32[2,96,1536]{2,1,0:T(8,128)}, f32[2,96,1536]{2,1,0:T(8,128)}, f32[2,96,1536]{2,1,0:T(8,128)}, f32[2,96,1536]{2,1,0:T(8,128)}, s32[3]{0:T(128)S(1)}) custom-call(s32[3]{0:T(128)S(1)} %get-tuple-element.209.refs_0_, f32[4,192,1536]{2,1,0:T(8,128)} %bitcast.31, f32[4,192,1536]{2,1,0:T(8,128)} %bitcast.6.refs_2_.refs_4_.refs_6_.refs_8_, ...), custom_call_target="tpu_custom_call" | custom-call | flops 999999995904 | bytes 1 | tf_op jit(solution)/shard_map/pallas_call | solution.py:519
  188.8 7.7 %shard_map.233 = (f32[768,896]{1,0:T(8,128)}, f32[768,896]{1,0:T(8,128)}, s32[3]{0:T(128)S(1)}) custom-call(s32[3]{0:T(128)S(1)} %get-tuple-element.212.refs_0_, bf16[768,1024]{1,0:T(8,128)(2,1)} %get-tuple-element.213.refs_1_, bf16[1,768,1024]{2,1,0:T(8,128)(2,1)} %bitcast.48, bf16[768,1024]{1,0:T(8,128)(2,1)} %get-tuple-element.164.refs_2_.refs_7_.refs_3_.refs_1_, ...), custom_call_target="tpu_custom_call" | custom-call | flops 999999995904 | bytes 1 | tf_op jit(solution)/shard_map/pallas_call | solution.py:519
  204.6 4.3 %shard_map.235 = (f32[2,96,896]{2,1,0:T(8,128)}, f32[2,96,896]{2,1,0:T(8,128)}, f32[2,96,896]{2,1,0:T(8,128)}, f32[2,96,896]{2,1,0:T(8,128)}, s32[3]{0:T(128)S(1)}) custom-call(s32[3]{0:T(128)S(1)} %get-tuple-element.222.refs_0_, f32[4,192,896]{2,1,0:T(8,128)} %bitcast.39, f32[4,192,896]{2,1,0:T(8,128)} %bitcast.10.refs_2_.refs_4_.refs_6_.refs_8_, ...), custom_call_target="tpu_custom_call" | custom-call | flops 999999995904 | bytes 1 | tf_op jit(solution)/shard_map/pallas_call | solution.py:519
  210.5 8.0 %shard_map.236 = (bf16[2,768,1024]{2,1,0:T(8,128)(2,1)}, s32[3]{0:T(128)S(1)}) custom-call(s32[3]{0:T(128)S(1)} %get-tuple-element.225.refs_0_, f32[4,8,256]{2,1,0:T(8,128)} %get-tuple-element.163.refs_1_, bf16[768,1024]{1,0:T(8,128)(2,1)} %get-tuple-element.193.refs_3_.refs_2_, bf16[768,1024]{1,0:T(8,128)(2,1)} %get-tuple-element.166.refs_4_.refs_3_, ...), custom_call_target="tpu_custom_call" | custom-call | flops 999999995904 | bytes 1 | tf_op jit(solution)/shard_map/pallas_call | solution.py:519
  223.4 10.8 %collective-permute-done.16.refs_2_.refs_4_ = f32[2,96,896]{2,1,0:T(8,128)} collective-permute-done((f32[2,96,896]{2,1,0:T(8,128)}, f32[2,96,896]{2,1,0:T(8,128)}, u32[]{:S(2)}, u32[]{:S(2)}) %collective-permute-start.16) | collective-permute-done | bytes 688160 | tf_op jit(solution)/shard_map/ppermute | solution.py:834
  239.3 4.3 %shard_map.239 = (f32[1,96,1536]{2,1,0:T(8,128)}, f32[1,96,1536]{2,1,0:T(8,128)}, f32[1,96,1536]{2,1,0:T(8,128)}, f32[1,96,1536]{2,1,0:T(8,128)}, s32[3]{0:T(128)S(1)}) custom-call(s32[3]{0:T(128)S(1)} %get-tuple-element.239.refs_0_, f32[2,96,1536]{2,1,0:T(8,128)} %get-tuple-element.240.refs_1_.refs_3_, ...), custom_call_target="tpu_custom_call" | custom-call | flops 999999995904 | bytes 1 | tf_op jit(solution)/shard_map/pallas_call | solution.py:519
  249.3 7.2 %shard_map.241 = (f32[768,768]{1,0:T(8,128)}, f32[768,768]{1,0:T(8,128)}, s32[3]{0:T(128)S(1)}) custom-call(s32[3]{0:T(128)S(1)} %get-tuple-element.249.refs_0_, bf16[768,1024]{1,0:T(8,128)(2,1)} %get-tuple-element.164.refs_2_.refs_7_.refs_3_.refs_1_, bf16[2,768,1024]{2,1,0:T(8,128)(2,1)} %get-tuple-element.250.refs_2_.refs_4_, ...), custom_call_target="tpu_custom_call" | custom-call | flops 999999995904 | bytes 1 | tf_op jit(solution)/shard_map/pallas_call | solution.py:519
  256.5 4.9 %collective-permute-start.24 = (f32[768,768]{1,0:T(8,128)}, f32[768,768]{1,0:T(8,128)}, u32[]{:S(2)}, u32[]{:S(2)}) collective-permute-start(f32[768,768]{1,0:T(8,128)} %get-tuple-element.258), channel_id=1, source_target_pairs={{0,1},{1,0},{2,3},{3,2},{4,5},{5,4},{6,7},{7,6},{8,9},{9,8},{10,11... | collective-permute-start | bytes 7077896 | tf_op jit(solution)/shard_map/ppermute | solution.py:834
  265.9 4.0 %shard_map.243 = (f32[2,96,768]{2,1,0:T(8,128)}, f32[2,96,768]{2,1,0:T(8,128)}, f32[2,96,768]{2,1,0:T(8,128)}, f32[2,96,768]{2,1,0:T(8,128)}, s32[3]{0:T(128)S(1)}) custom-call(s32[3]{0:T(128)S(1)} %get-tuple-element.256.refs_0_, f32[4,192,768]{2,1,0:T(8,128)} %bitcast.43, f32[4,192,768]{2,1,0:T(8,128)} %bitcast.12.refs_2_.refs_4_.refs_6_.refs_8_, ...), custom_call_target="tpu_custom_call" | custom-call | flops 999999995904 | bytes 1 | tf_op jit(solution)/shard_map/pallas_call | solution.py:519
  280.9 4.2 %collective-permute-done.27.refs_2_ = f32[96,1536]{1,0:T(8,128)} collective-permute-done((f32[96,1536]{1,0:T(8,128)}, f32[96,1536]{1,0:T(8,128)}, u32[]{:S(2)}, u32[]{:S(2)}) %collective-permute-start.27) | collective-permute-done | bytes 589856 | tf_op jit(solution)/shard_map/ppermute | solution.py:834
  296.0 10.0 %shard_map.248 = (f32[4,256,768]{2,1,0:T(8,128)}, s32[3]{0:T(128)S(1)}) custom-call(s32[3]{0:T(128)S(1)} %get-tuple-element.272.refs_0_, bf16[768,1024]{1,0:T(8,128)(2,1)} %get-tuple-element.215.refs_1_, bf16[2,768,1024]{2,1,0:T(8,128)(2,1)} %get-tuple-element.250.refs_2_.refs_4_, f32[768,1024]{1,0:T(8,128)} %get-tuple-element.273.refs_3_, ...), custom_call_target="tpu_custom_call" | custom-call | flops 999999995904 | bytes 1 | tf_op jit(solution)/shard_map/pallas_call | solution.py:519
  308.8 4.1 %collective-permute-done.32.refs_2_ = f32[384,384]{1,0:T(8,128)} collective-permute-done((f32[384,384]{1,0:T(8,128)}, f32[384,384]{1,0:T(8,128)}, u32[]{:S(2)}, u32[]{:S(2)}) %collective-permute-start.32) | collective-permute-done | bytes 589856 | tf_op jit(solution)/shard_map/ppermute | solution.py:834
  333.8 7.8 %collective-permute-done.37.refs_2_ = f32[96,768]{1,0:T(8,128)} collective-permute-done((f32[96,768]{1,0:T(8,128)}, f32[96,768]{1,0:T(8,128)}, u32[]{:S(2)}, u32[]{:S(2)}) %collective-permute-start.37) | collective-permute-done | bytes 294944 | tf_op jit(solution)/shard_map/ppermute | solution.py:834
  344.0 5.6 %collective-permute-done.38.refs_2_ = f32[96,1536]{1,0:T(8,128)} collective-permute-done((f32[96,1536]{1,0:T(8,128)}, f32[96,1536]{1,0:T(8,128)}, u32[]{:S(2)}, u32[]{:S(2)}) %collective-permute-start.38) | collective-permute-done | bytes 589856 | tf_op jit(solution)/shard_map/ppermute | solution.py:834
  (181 shorter events, 140.0 us)
Async XLA Ops:
  11.9 22.4 %collective-permute-start = (f32[4,392,128]{2,1,0:T(8,128)}, f32[4,392,128]{2,1,0:T(8,128)}, u32[]{:S(2)}, u32[]{:S(2)}) collective-permute-start(f32[4,392,128]{2,1,0:T(8,128)} %get-tuple-element.168.refs_2_), channel_id=1, source_target_pairs={{0,8},{8,0},{16,24},{24,16},{1,9},{9,1},{17,25},{25,17},{2,10},{10... | collective-permute-start | bytes 2408456 | tf_op jit(solution)/shard_map/ppermute | solution.py:834
  14.0 20.3 %collective-permute-start.1 = (f32[4,392,128]{2,1,0:T(8,128)}, f32[4,392,128]{2,1,0:T(8,128)}, u32[]{:S(2)}, u32[]{:S(2)}) collective-permute-start(f32[4,392,128]{2,1,0:T(8,128)} %get-tuple-element.169.refs_4_), channel_id=1, source_target_pairs={{0,16},{8,24},{16,0},{24,8},{1,17},{9,25},{17,1},{25,9},{2,18},{10... | collective-permute-start | bytes 2408456 | tf_op jit(solution)/shard_map/ppermute | solution.py:834
  37.2 18.2 %collective-permute-start.2 = (f32[4,392,128]{2,1,0:T(8,128)S(1)}, f32[4,392,128]{2,1,0:T(8,128)S(1)}, u32[]{:S(2)}, u32[]{:S(2)}) collective-permute-start(f32[4,392,128]{2,1,0:T(8,128)S(1)} %get-tuple-element.171), channel_id=1, source_target_pairs={{0,16},{8,24},{16,0},{24,8},{1,17},{9,25},{17,1},{25,9},{2,18},{10... | collective-permute-start | bytes 2408456 | tf_op jit(solution)/shard_map/ppermute | solution.py:834
  37.5 17.9 %collective-permute-start.3 = (f32[4,392,128]{2,1,0:T(8,128)S(1)}, f32[4,392,128]{2,1,0:T(8,128)S(1)}, u32[]{:S(2)}, u32[]{:S(2)}) collective-permute-start(f32[4,392,128]{2,1,0:T(8,128)S(1)} %get-tuple-element.172), channel_id=1, source_target_pairs={{0,8},{8,0},{16,24},{24,16},{1,9},{9,1},{17,25},{25,17},{2,10},{10... | collective-permute-start | bytes 2408456 | tf_op jit(solution)/shard_map/ppermute | solution.py:834
  129.9 41.2 %collective-permute-start.7 = (f32[4,392,128]{2,1,0:T(8,128)}, f32[4,392,128]{2,1,0:T(8,128)}, u32[]{:S(2)}, u32[]{:S(2)}) collective-permute-start(f32[4,392,128]{2,1,0:T(8,128)} %get-tuple-element.202), channel_id=1, source_target_pairs={{0,16},{8,24},{16,0},{24,8},{1,17},{9,25},{17,1},{25,9},{2,18},{10... | collective-permute-start | bytes 2408456 | tf_op jit(solution)/shard_map/ppermute | solution.py:834
  131.0 40.1 %collective-permute-start.8 = (f32[4,392,128]{2,1,0:T(8,128)}, f32[4,392,128]{2,1,0:T(8,128)}, u32[]{:S(2)}, u32[]{:S(2)}) collective-permute-start(f32[4,392,128]{2,1,0:T(8,128)} %get-tuple-element.203), channel_id=1, source_target_pairs={{0,8},{8,0},{16,24},{24,16},{1,9},{9,1},{17,25},{25,17},{2,10},{10... | collective-permute-start | bytes 2408456 | tf_op jit(solution)/shard_map/ppermute | solution.py:834
  138.9 36.0 %collective-permute-start.9 = (f32[2,384,384]{2,1,0:T(8,128)}, f32[2,384,384]{2,1,0:T(8,128)}, u32[]{:S(2)}, u32[]{:S(2)}) collective-permute-start(f32[2,384,384]{2,1,0:T(8,128)} %get-tuple-element.206), channel_id=1, source_target_pairs={{0,8},{8,0},{16,24},{24,16},{1,9},{9,1},{17,25},{25,17},{2,10},{10... | collective-permute-start | bytes 3538952 | tf_op jit(solution)/shard_map/ppermute | solution.py:834
  140.1 34.8 %collective-permute-start.10 = (f32[2,384,384]{2,1,0:T(8,128)}, f32[2,384,384]{2,1,0:T(8,128)}, u32[]{:S(2)}, u32[]{:S(2)}) collective-permute-start(f32[2,384,384]{2,1,0:T(8,128)} %get-tuple-element.208), channel_id=1, source_target_pairs={{0,16},{8,24},{16,0},{24,8},{1,17},{9,25},{17,1},{25,9},{2,18},{10... | collective-permute-start | bytes 3538952 | tf_op jit(solution)/shard_map/ppermute | solution.py:834
  179.3 20.2 %collective-permute-start.12 = (f32[1,384,384]{2,1,0:T(8,128)}, f32[1,384,384]{2,1,0:T(8,128)}, u32[]{:S(2)}, u32[]{:S(2)}) collective-permute-start(f32[1,384,384]{2,1,0:T(8,128)} %get-tuple-element.219), channel_id=1, source_target_pairs={{0,16},{8,24},{16,0},{24,8},{1,17},{9,25},{17,1},{25,9},{2,18},{10... | collective-permute-start | bytes 1769480 | tf_op jit(solution)/shard_map/ppermute | solution.py:834
  180.6 19.0 %collective-permute-start.13 = (f32[1,384,384]{2,1,0:T(8,128)}, f32[1,384,384]{2,1,0:T(8,128)}, u32[]{:S(2)}, u32[]{:S(2)}) collective-permute-start(f32[1,384,384]{2,1,0:T(8,128)} %get-tuple-element.221), channel_id=1, source_target_pairs={{0,8},{8,0},{16,24},{24,16},{1,9},{9,1},{17,25},{25,17},{2,10},{10... | collective-permute-start | bytes 1769480 | tf_op jit(solution)/shard_map/ppermute | solution.py:834
  188.1 51.1 %collective-permute-start.18 = (f32[2,96,1536]{2,1,0:T(8,128)}, f32[2,96,1536]{2,1,0:T(8,128)}, u32[]{:S(2)}, u32[]{:S(2)}) collective-permute-start(f32[2,96,1536]{2,1,0:T(8,128)} %get-tuple-element.241), channel_id=1, source_target_pairs={{0,8},{8,0},{16,24},{24,16},{1,9},{9,1},{17,25},{25,17},{2,10},{10... | collective-permute-start | bytes 3538952 | tf_op jit(solution)/shard_map/ppermute | solution.py:834
  188.5 50.8 %collective-permute-start.19 = (f32[2,96,1536]{2,1,0:T(8,128)}, f32[2,96,1536]{2,1,0:T(8,128)}, u32[]{:S(2)}, u32[]{:S(2)}) collective-permute-start(f32[2,96,1536]{2,1,0:T(8,128)} %get-tuple-element.243), channel_id=1, source_target_pairs={{0,16},{8,24},{16,0},{24,8},{1,17},{9,25},{17,1},{25,9},{2,18},{10... | collective-permute-start | bytes 3538952 | tf_op jit(solution)/shard_map/ppermute | solution.py:834
  209.0 25.3 %collective-permute-start.16 = (f32[2,96,896]{2,1,0:T(8,128)}, f32[2,96,896]{2,1,0:T(8,128)}, u32[]{:S(2)}, u32[]{:S(2)}) collective-permute-start(f32[2,96,896]{2,1,0:T(8,128)} %get-tuple-element.236), channel_id=1, source_target_pairs={{0,8},{8,0},{16,24},{24,16},{1,9},{9,1},{17,25},{25,17},{2,10},{10... | collective-permute-start | bytes 2064392 | tf_op jit(solution)/shard_map/ppermute | solution.py:834
  210.2 24.1 %collective-permute-start.17 = (f32[2,96,896]{2,1,0:T(8,128)}, f32[2,96,896]{2,1,0:T(8,128)}, u32[]{:S(2)}, u32[]{:S(2)}) collective-permute-start(f32[2,96,896]{2,1,0:T(8,128)} %get-tuple-element.238), channel_id=1, source_target_pairs={{0,16},{8,24},{16,0},{24,8},{1,17},{9,25},{17,1},{25,9},{2,18},{10... | collective-permute-start | bytes 2064392 | tf_op jit(solution)/shard_map/ppermute | solution.py:834
  221.1 57.2 %collective-permute-start.26 = (f32[384,384]{1,0:T(8,128)}, f32[384,384]{1,0:T(8,128)}, u32[]{:S(2)}, u32[]{:S(2)}) collective-permute-start(f32[384,384]{1,0:T(8,128)} %get-tuple-element.263.refs_1_), channel_id=1, source_target_pairs={{0,4},{1,5},{2,6},{3,7},{4,0},{5,1},{6,2},{7,3},{8,12},{9,13},{10,... | collective-permute-start | bytes 1769480 | tf_op jit(solution)/shard_map/ppermute | solution.py:834
  243.6 17.8 %collective-permute-start.22 = (f32[1,96,1536]{2,1,0:T(8,128)}, f32[1,96,1536]{2,1,0:T(8,128)}, u32[]{:S(2)}, u32[]{:S(2)}) collective-permute-start(f32[1,96,1536]{2,1,0:T(8,128)} %get-tuple-element.253), channel_id=1, source_target_pairs={{0,16},{8,24},{16,0},{24,8},{1,17},{9,25},{17,1},{25,9},{2,18},{10... | collective-permute-start | bytes 1769480 | tf_op jit(solution)/shard_map/ppermute | solution.py:834
  247.7 22.3 %collective-permute-start.25 = (f32[96,896]{1,0:T(8,128)}, f32[96,896]{1,0:T(8,128)}, u32[]{:S(2)}, u32[]{:S(2)}) collective-permute-start(f32[96,896]{1,0:T(8,128)} %get-tuple-element.261), channel_id=1, source_target_pairs={{0,2},{1,3},{2,0},{3,1},{4,6},{5,7},{6,4},{7,5},{8,10},{9,11},{10,... | collective-permute-start | bytes 1032200 | tf_op jit(solution)/shard_map/ppermute | solution.py:834
  264.2 20.9 %collective-permute-start.27 = (f32[96,1536]{1,0:T(8,128)}, f32[96,1536]{1,0:T(8,128)}, u32[]{:S(2)}, u32[]{:S(2)}) collective-permute-start(f32[96,1536]{1,0:T(8,128)} %get-tuple-element.266), channel_id=1, source_target_pairs={{0,2},{1,3},{2,0},{3,1},{4,6},{5,7},{6,4},{7,5},{8,10},{9,11},{10,... | collective-permute-start | bytes 1769480 | tf_op jit(solution)/shard_map/ppermute | solution.py:834
  272.2 43.6 %collective-permute-start.33 = (f32[96,896]{1,0:T(8,128)}, f32[96,896]{1,0:T(8,128)}, u32[]{:S(2)}, u32[]{:S(2)}) collective-permute-start(f32[96,896]{1,0:T(8,128)} %get-tuple-element.283.refs_1_), channel_id=1, source_target_pairs={{0,4},{1,5},{2,6},{3,7},{4,0},{5,1},{6,2},{7,3},{8,12},{9,13},{10,... | collective-permute-start | bytes 1032200 | tf_op jit(solution)/shard_map/ppermute | solution.py:834
  287.6 39.5 %collective-permute-start.35 = (f32[96,1536]{1,0:T(8,128)}, f32[96,1536]{1,0:T(8,128)}, u32[]{:S(2)}, u32[]{:S(2)}) collective-permute-start(f32[96,1536]{1,0:T(8,128)} %get-tuple-element.288.refs_1_), channel_id=1, source_target_pairs={{0,4},{1,5},{2,6},{3,7},{4,0},{5,1},{6,2},{7,3},{8,12},{9,13},{10,... | collective-permute-start | bytes 1769480 | tf_op jit(solution)/shard_map/ppermute | solution.py:834
  287.7 25.2 %collective-permute-start.32 = (f32[384,384]{1,0:T(8,128)}, f32[384,384]{1,0:T(8,128)}, u32[]{:S(2)}, u32[]{:S(2)}) collective-permute-start(f32[384,384]{1,0:T(8,128)} %get-tuple-element.281.refs_1_), channel_id=1, source_target_pairs={{0,2},{1,3},{2,0},{3,1},{4,6},{5,7},{6,4},{7,5},{8,10},{9,11},{10,... | collective-permute-start | bytes 1769480 | tf_op jit(solution)/shard_map/ppermute | solution.py:834
  320.5 44.2 %collective-permute-start.42 = (f32[768,384]{1,0:T(8,128)}, f32[768,384]{1,0:T(8,128)}, u32[]{:S(2)}, u32[]{:S(2)}) collective-permute-start(f32[768,384]{1,0:T(8,128)} %get-tuple-element.303.refs_1_), channel_id=1, source_target_pairs={{0,1},{1,0},{2,3},{3,2},{4,5},{5,4},{6,7},{7,6},{8,9},{9,8},{10,11... | collective-permute-start | bytes 3538952 | tf_op jit(solution)/shard_map/ppermute | solution.py:834
  329.8 19.9 %collective-permute-start.38 = (f32[96,1536]{1,0:T(8,128)}, f32[96,1536]{1,0:T(8,128)}, u32[]{:S(2)}, u32[]{:S(2)}) collective-permute-start(f32[96,1536]{1,0:T(8,128)} %get-tuple-element.294.refs_1_), channel_id=1, source_target_pairs={{0,2},{1,3},{2,0},{3,1},{4,6},{5,7},{6,4},{7,5},{8,10},{9,11},{10,... | collective-permute-start | bytes 1769480 | tf_op jit(solution)/shard_map/ppermute | solution.py:834
  332.6 21.8 %collective-permute-start.39 = (f32[192,896]{1,0:T(8,128)}, f32[192,896]{1,0:T(8,128)}, u32[]{:S(2)}, u32[]{:S(2)}) collective-permute-start(f32[192,896]{1,0:T(8,128)} %get-tuple-element.296.refs_1_), channel_id=1, source_target_pairs={{0,1},{1,0},{2,3},{3,2},{4,5},{5,4},{6,7},{7,6},{8,9},{9,8},{10,11... | collective-permute-start | bytes 2064392 | tf_op jit(solution)/shard_map/ppermute | solution.py:834
  (47 other events, 474.2 us)

commit v10 on v9

--- a/solution.py
+++ b/solution.py
@@ -661,6 +661,30 @@
     return order.call(route_kernel, (half,), ins, [out] * 4, [], (a, b, a, b, c, d, c, d))
 
 
+def last_route_kernel(low_bit, high_bit, s_ref, a_ref, b_ref, c_ref, d_ref, *outs):
+    left, right = ((s_ref[PLACE] >> bit) & 1 for bit in (low_bit, high_bit))
+    outs[0][0] = a_ref[1 - left] + b_ref[1 - left]
+    outs[1][0] = a_ref[left] + b_ref[left]
+    outs[2][0] = c_ref[1 - right] + d_ref[1 - right]
+    outs[3][0] = c_ref[right] + d_ref[right]
+
+
+def last_route(order, left, right, low_bit, high_bit):
+    shape = (1,) + left[0].shape[1:]
+    return order.call(
+        partial(last_route_kernel, low_bit, high_bit),
+        (1,),
+        [NEAR] * 4,
+        [(NEAR, (shape, f32))] * 4,
+        [],
+        (*left, *right),
+        free=(0, 2),
+        near=(1, 3),
+        near_out=range(4),
+        limit=SMALL_LIMIT,
+    )
+
+
 def choose_kernel(s_ref, a_ref, b_ref, c_ref, d_ref, away_ref, kept_ref):
     upper, lower = a_ref[0] + b_ref[0], c_ref[0] + d_ref[0]
     odd = s_ref[ODD] == 1
@@ -844,7 +868,8 @@
     left = right = (keep.reshape(shape), got)
     for step in range(bits):
         high = bits - 1 - step
-        away_l, keep_l, away_r, keep_r = route(order, left, right, step, high)
+        part = last_route if 0 < step == bits - 1 else route
+        away_l, keep_l, away_r, keep_r = part(order, left, right, step, high)
         left = keep_l, swap(away_l, "seq", 1 << step)
         right = keep_r, swap(away_r, "seq", 1 << high)
         yield
@@ -872,7 +897,7 @@
     "back", "mixed", "in", "mixed", "last_product", "in",
     "last", "mixed", "back", "in", "last", "tokens",
     "last", "back", "mixed", "last", "in", "mixed",
-    "last", "in", "mixed", "last", "in", "back",
+    "last", "back", "in", "mixed", "last", "in",
     "last",
 )
 

time: 374 us -> 369 us (0.987)
  transfers between devices with their start and end apart: 44 -> 44, of which waited for: 14 -> 14; matrix products, arithmetic and copies ran while one was open for 1% -> 1% of each run, Pallas kernels for 50% -> 49%
where the time goes in v10:
time: 369 us; the launch traced here: 367 us
  Pallas kernels  246 us (67%)
  starting transfers between devices  55.3 us (15%)
  waiting for transfers between devices  53.1 us (14%)
  local copies, waits for them, and re-layouts  10.4 us (3%)
    pallas_call x42, Pallas kernels, call(): pl.pallas_call(stepped, grid_spec=pltpu.PrefetchScalarGridSpec(num_scalar...  246 us
    ppermute x44, starting transfers between devices, swap(): return lax.ppermute(value, axis, [(i, i ^ distance) for i in range(count)])  55.3 us
    ppermute x44, waiting for transfers between devices, swap(): return lax.ppermute(value, axis, [(i, i ^ distance) for i in range(count)])  53.1 us
  transfers between devices with their start and end apart: 44, of which 14 were waited for; matrix products, arithmetic and copies ran while one was open for 1% of the time, Pallas kernels for 49%

profile of v10, /device:TPU:1, one launch (start us, length us, event | category | flops | bytes accessed | tf_op | source)
XLA Modules:
  0.0 367.4 jit_solution(6435649180002710250)
XLA Ops:
  1.4 10.5 %shard_map.220 = (f32[4,8,256]{2,1,0:T(8,128)}, bf16[768,1024]{1,0:T(8,128)(2,1)}, bf16[768,1024]{1,0:T(8,128)(2,1)}, bf16[768,1024]{1,0:T(8,128)(2,1)}, bf16[4,...) custom-call(s32[3]{0:T(128)S(1)} %pad_add_fusion.refs_0_, ...), custom_call_target="tpu_custom_call" | custom-call | flops 999999995904 | bytes 1 | tf_op jit(solution)/shard_map/pallas_call | solution.py:519
  15.2 18.2 %shard_map.221 = (bf16[768,1024]{1,0:T(8,128)(2,1)}, bf16[768,1024]{1,0:T(8,128)(2,1)}, f32[768,1024]{1,0:T(8,128)}, f32[16,1024]{1,0:T(8,128)}, bf16[768,768]{1...) custom-call(s32[3]{0:T(128)S(1)} %get-tuple-element.162.refs_0_, ...), custom_call_target="tpu_custom_call" | custom-call | flops 999999995904 | bytes 1 | tf_op jit(solution)/shard_map/pallas_call | solution.py:519
  41.2 14.2 %collective-permute-done.2.refs_3_ = f32[4,392,128]{2,1,0:T(8,128)S(1)} collective-permute-done((f32[4,392,128]{2,1,0:T(8,128)S(1)}, f32[4,392,128]{2,1,0:T(8,128)S(1)}, u32[]{:S(2)}, u32[]{:S(2)}) %collective-permute-start.2) | collective-permute-done | bytes 802848 | tf_op jit(solution)/shard_map/ppermute | solution.py:858
  55.4 3.8 %shard_map.223 = (f32[4,392,128]{2,1,0:T(8,128)}, f32[4,392,128]{2,1,0:T(8,128)}, s32[3]{0:T(128)S(1)}) custom-call(s32[3]{0:T(128)S(1)} %get-tuple-element.170.refs_0_, f32[16,4]{1,0:T(8,128)S(1)} %stack.59.refs_1_, f32[4,392,128]{2,1,0:T(8,128)} %collective-permute-done.refs_3_.refs_2_, f32[4,392,128]{2,1,0:T(8,128)S(1)} %collective-permute-done.2.refs_3_, ...), custom_call_target="tpu_custom_call" | custom-call | flops 999999995904 | bytes 1 | tf_op jit(solution)/shard_map/pallas_call | solution.py:519
  63.5 45.3 %shard_map.224 = (bf16[4,256,768]{2,1,0:T(8,128)(2,1)}, bf16[768,1024]{1,0:T(8,128)(2,1)}, bf16[768,1024]{1,0:T(8,128)(2,1)}, bf16[3072,1024]{1,0:T(8,128)(2,1)}...) custom-call(s32[3]{0:T(128)} %copy-done.21, ...), custom_call_target="tpu_custom_call" | custom-call | flops 999999995904 | bytes 1 | tf_op jit(solution)/shard_map/pallas_call | solution.py:519
  111.0 10.6 %shard_map.225 = (f32[3072,384]{1,0:T(8,128)}, f32[3072,384]{1,0:T(8,128)}, s32[3]{0:T(128)S(1)}) custom-call(s32[3]{0:T(128)S(1)} %copy-done.20, bf16[3072,1024]{1,0:T(8,128)(2,1)} %get-tuple-element.184.refs_1_, bf16[768,1024]{1,0:T(8,128)(2,1)} %get-tuple-element.185.refs_2_), custom_call_target="tpu_custom_call" | custom-call | flops 999999995904 | bytes 1 | tf_op jit(solution)/shard_map/pallas_call | solution.py:519
  132.5 6.4 %shard_map.227 = (f32[2,384,384]{2,1,0:T(8,128)}, f32[2,384,384]{2,1,0:T(8,128)}, f32[2,384,384]{2,1,0:T(8,128)}, f32[2,384,384]{2,1,0:T(8,128)}, s32[3]{0:T(128)S(1)}) custom-call(s32[3]{0:T(128)S(1)} %get-tuple-element.189.refs_0_, f32[4,768,384]{2,1,0:T(8,128)} %bitcast.35, f32[4,768,384]{2,1,0:T(8,128)} %bitcast.4.refs_2_.refs_4_.refs_6_.refs_8_, ...), custom_call_target="tpu_custom_call" | custom-call | flops 999999995904 | bytes 1 | tf_op jit(solution)/shard_map/pallas_call | solution.py:519
  140.4 14.9 %shard_map.228 = (bf16[768,1024]{1,0:T(8,128)(2,1)}, f32[768,1024]{1,0:T(8,128)}, f32[768,1024]{1,0:T(8,128)}, s32[3]{0:T(128)S(1)}) custom-call(s32[3]{0:T(128)S(1)} %get-tuple-element.192.refs_0_, f32[4,8,256]{2,1,0:T(8,128)} %get-tuple-element.163.refs_1_, bf16[768,1024]{1,0:T(8,128)(2,1)} %get-tuple-element.174.refs_2_, ...), custom_call_target="tpu_custom_call" | custom-call | flops 999999995904 | bytes 1 | tf_op jit(solution)/shard_map/pallas_call | solution.py:519
  155.3 12.2 %shard_map.229 = (f32[768,1536]{1,0:T(8,128)}, f32[768,1536]{1,0:T(8,128)}, s32[3]{0:T(128)S(1)}) custom-call(s32[3]{0:T(128)S(1)} %get-tuple-element.198.refs_0_, bf16[768,1024]{1,0:T(8,128)(2,1)} %get-tuple-element.199.refs_1_, bf16[3072,1024]{1,0:T(8,128)(2,1)} %get-tuple-element.200.refs_2_), custom_call_target="tpu_custom_call" | custom-call | flops 999999995904 | bytes 1 | tf_op jit(solution)/shard_map/pallas_call | solution.py:519
  171.1 3.9 %shard_map.230 = (f32[4,392,128]{2,1,0:T(8,128)}, f32[4,392,128]{2,1,0:T(8,128)}, s32[3]{0:T(128)S(1)}) custom-call(s32[3]{0:T(128)S(1)} %get-tuple-element.201.refs_0_, f32[16,4]{1,0:T(8,128)S(1)} %stack.59.refs_1_, f32[4,392,128]{2,1,0:T(8,128)} %collective-permute-done.4.refs_3_.refs_2_, f32[4,392,128]{2,1,0:T(8,128)} %collective-permute-done.7.refs_3_, ...), custom_call_target="tpu_custom_call" | custom-call | flops 999999995904 | bytes 1 | tf_op jit(solution)/shard_map/pallas_call | solution.py:519
  180.9 6.4 %shard_map.232 = (f32[2,96,1536]{2,1,0:T(8,128)}, f32[2,96,1536]{2,1,0:T(8,128)}, f32[2,96,1536]{2,1,0:T(8,128)}, f32[2,96,1536]{2,1,0:T(8,128)}, s32[3]{0:T(128)S(1)}) custom-call(s32[3]{0:T(128)S(1)} %get-tuple-element.209.refs_0_, f32[4,192,1536]{2,1,0:T(8,128)} %bitcast.31, f32[4,192,1536]{2,1,0:T(8,128)} %bitcast.6.refs_2_.refs_4_.refs_6_.refs_8_, ...), custom_call_target="tpu_custom_call" | custom-call | flops 999999995904 | bytes 1 | tf_op jit(solution)/shard_map/pallas_call | solution.py:519
  188.0 7.7 %shard_map.233 = (f32[768,896]{1,0:T(8,128)}, f32[768,896]{1,0:T(8,128)}, s32[3]{0:T(128)S(1)}) custom-call(s32[3]{0:T(128)S(1)} %get-tuple-element.212.refs_0_, bf16[768,1024]{1,0:T(8,128)(2,1)} %get-tuple-element.213.refs_1_, bf16[1,768,1024]{2,1,0:T(8,128)(2,1)} %bitcast.48, bf16[768,1024]{1,0:T(8,128)(2,1)} %get-tuple-element.164.refs_2_.refs_7_.refs_3_.refs_1_, ...), custom_call_target="tpu_custom_call" | custom-call | flops 999999995904 | bytes 1 | tf_op jit(solution)/shard_map/pallas_call | solution.py:519
  203.7 4.3 %shard_map.235 = (f32[2,96,896]{2,1,0:T(8,128)}, f32[2,96,896]{2,1,0:T(8,128)}, f32[2,96,896]{2,1,0:T(8,128)}, f32[2,96,896]{2,1,0:T(8,128)}, s32[3]{0:T(128)S(1)}) custom-call(s32[3]{0:T(128)S(1)} %get-tuple-element.222.refs_0_, f32[4,192,896]{2,1,0:T(8,128)} %bitcast.39, f32[4,192,896]{2,1,0:T(8,128)} %bitcast.10.refs_2_.refs_4_.refs_6_.refs_8_, ...), custom_call_target="tpu_custom_call" | custom-call | flops 999999995904 | bytes 1 | tf_op jit(solution)/shard_map/pallas_call | solution.py:519
  209.7 8.0 %shard_map.236 = (bf16[2,768,1024]{2,1,0:T(8,128)(2,1)}, s32[3]{0:T(128)S(1)}) custom-call(s32[3]{0:T(128)S(1)} %get-tuple-element.225.refs_0_, f32[4,8,256]{2,1,0:T(8,128)} %get-tuple-element.163.refs_1_, bf16[768,1024]{1,0:T(8,128)(2,1)} %get-tuple-element.193.refs_3_.refs_2_, bf16[768,1024]{1,0:T(8,128)(2,1)} %get-tuple-element.166.refs_4_.refs_3_, ...), custom_call_target="tpu_custom_call" | custom-call | flops 999999995904 | bytes 1 | tf_op jit(solution)/shard_map/pallas_call | solution.py:519
  222.6 10.9 %collective-permute-done.16.refs_2_ = f32[2,96,896]{2,1,0:T(8,128)} collective-permute-done((f32[2,96,896]{2,1,0:T(8,128)}, f32[2,96,896]{2,1,0:T(8,128)}, u32[]{:S(2)}, u32[]{:S(2)}) %collective-permute-start.16) | collective-permute-done | bytes 688160 | tf_op jit(solution)/shard_map/ppermute | solution.py:858
  248.2 7.2 %shard_map.241 = (f32[768,768]{1,0:T(8,128)}, f32[768,768]{1,0:T(8,128)}, s32[3]{0:T(128)S(1)}) custom-call(s32[3]{0:T(128)S(1)} %get-tuple-element.249.refs_0_, bf16[768,1024]{1,0:T(8,128)(2,1)} %get-tuple-element.164.refs_2_.refs_7_.refs_3_.refs_1_, bf16[2,768,1024]{2,1,0:T(8,128)(2,1)} %get-tuple-element.250.refs_2_.refs_4_, ...), custom_call_target="tpu_custom_call" | custom-call | flops 999999995904 | bytes 1 | tf_op jit(solution)/shard_map/pallas_call | solution.py:519
  255.4 5.7 %collective-permute-start.24 = (f32[768,768]{1,0:T(8,128)}, f32[768,768]{1,0:T(8,128)}, u32[]{:S(2)}, u32[]{:S(2)}) collective-permute-start(f32[768,768]{1,0:T(8,128)} %get-tuple-element.258), channel_id=1, source_target_pairs={{0,1},{1,0},{2,3},{3,2},{4,5},{5,4},{6,7},{7,6},{8,9},{9,8},{10,11... | collective-permute-start | bytes 7077896 | tf_op jit(solution)/shard_map/ppermute | solution.py:858
  265.6 4.0 %shard_map.243 = (f32[2,96,768]{2,1,0:T(8,128)}, f32[2,96,768]{2,1,0:T(8,128)}, f32[2,96,768]{2,1,0:T(8,128)}, f32[2,96,768]{2,1,0:T(8,128)}, s32[3]{0:T(128)S(1)}) custom-call(s32[3]{0:T(128)S(1)} %get-tuple-element.256.refs_0_, f32[4,192,768]{2,1,0:T(8,128)} %bitcast.43, f32[4,192,768]{2,1,0:T(8,128)} %bitcast.12.refs_2_.refs_4_.refs_6_.refs_8_, ...), custom_call_target="tpu_custom_call" | custom-call | flops 999999995904 | bytes 1 | tf_op jit(solution)/shard_map/pallas_call | solution.py:519
  280.4 4.4 %collective-permute-done.27.refs_2_ = f32[96,1536]{1,0:T(8,128)} collective-permute-done((f32[96,1536]{1,0:T(8,128)}, f32[96,1536]{1,0:T(8,128)}, u32[]{:S(2)}, u32[]{:S(2)}) %collective-permute-start.27) | collective-permute-done | bytes 589856 | tf_op jit(solution)/shard_map/ppermute | solution.py:858
  295.1 9.8 %shard_map.248 = (f32[4,256,768]{2,1,0:T(8,128)}, s32[3]{0:T(128)S(1)}) custom-call(s32[3]{0:T(128)S(1)} %get-tuple-element.272.refs_0_, bf16[768,1024]{1,0:T(8,128)(2,1)} %get-tuple-element.215.refs_1_, bf16[2,768,1024]{2,1,0:T(8,128)(2,1)} %get-tuple-element.250.refs_2_.refs_4_, f32[768,1024]{1,0:T(8,128)} %get-tuple-element.273.refs_3_, ...), custom_call_target="tpu_custom_call" | custom-call | flops 999999995904 | bytes 1 | tf_op jit(solution)/shard_map/pallas_call | solution.py:519
  307.6 5.0 %collective-permute-done.32.refs_2_ = f32[384,384]{1,0:T(8,128)} collective-permute-done((f32[384,384]{1,0:T(8,128)}, f32[384,384]{1,0:T(8,128)}, u32[]{:S(2)}, u32[]{:S(2)}) %collective-permute-start.32) | collective-permute-done | bytes 589856 | tf_op jit(solution)/shard_map/ppermute | solution.py:858
  333.6 7.7 %collective-permute-done.37.refs_2_ = f32[96,768]{1,0:T(8,128)} collective-permute-done((f32[96,768]{1,0:T(8,128)}, f32[96,768]{1,0:T(8,128)}, u32[]{:S(2)}, u32[]{:S(2)}) %collective-permute-start.37) | collective-permute-done | bytes 294944 | tf_op jit(solution)/shard_map/ppermute | solution.py:858
  343.7 3.8 %shard_map.256 = (f32[768,768]{1,0:T(8,128)}, s32[3]{0:T(128)S(1)}) custom-call(s32[3]{0:T(128)S(1)} %get-tuple-element.293.refs_0_, f32[768,384]{1,0:T(8,128)} %get-tuple-element.294.refs_1_, f32[768,384]{1,0:T(8,128)} %collective-permute-done.38.refs_2_), custom_call_target="tpu_custom_call" | custom-call | flops 999999995904 | bytes 1 | tf_op jit(solution)/shard_map/pallas_call | solution.py:519
  360.6 3.8 %shard_map.260 = (f32[192,3072]{1,0:T(8,128)}, s32[3]{0:T(128)S(1)}) custom-call(s32[3]{0:T(128)S(1)} %get-tuple-element.302.refs_0_, f32[192,1536]{1,0:T(8,128)} %get-tuple-element.303.refs_1_, f32[192,1536]{1,0:T(8,128)} %collective-permute-done.42.refs_2_), custom_call_target="tpu_custom_call" | custom-call | flops 999999995904 | bytes 1 | tf_op jit(solution)/shard_map/pallas_call | solution.py:519
  (181 shorter events, 137.2 us)
Async XLA Ops:
  11.9 22.4 %collective-permute-start = (f32[4,392,128]{2,1,0:T(8,128)}, f32[4,392,128]{2,1,0:T(8,128)}, u32[]{:S(2)}, u32[]{:S(2)}) collective-permute-start(f32[4,392,128]{2,1,0:T(8,128)} %get-tuple-element.168.refs_2_), channel_id=1, source_target_pairs={{0,8},{8,0},{16,24},{24,16},{1,9},{9,1},{17,25},{25,17},{2,10},{10... | collective-permute-start | bytes 2408456 | tf_op jit(solution)/shard_map/ppermute | solution.py:858
  14.0 20.3 %collective-permute-start.1 = (f32[4,392,128]{2,1,0:T(8,128)}, f32[4,392,128]{2,1,0:T(8,128)}, u32[]{:S(2)}, u32[]{:S(2)}) collective-permute-start(f32[4,392,128]{2,1,0:T(8,128)} %get-tuple-element.169.refs_4_), channel_id=1, source_target_pairs={{0,16},{8,24},{16,0},{24,8},{1,17},{9,25},{17,1},{25,9},{2,18},{10... | collective-permute-start | bytes 2408456 | tf_op jit(solution)/shard_map/ppermute | solution.py:858
  37.2 18.2 %collective-permute-start.2 = (f32[4,392,128]{2,1,0:T(8,128)S(1)}, f32[4,392,128]{2,1,0:T(8,128)S(1)}, u32[]{:S(2)}, u32[]{:S(2)}) collective-permute-start(f32[4,392,128]{2,1,0:T(8,128)S(1)} %get-tuple-element.171), channel_id=1, source_target_pairs={{0,16},{8,24},{16,0},{24,8},{1,17},{9,25},{17,1},{25,9},{2,18},{10... | collective-permute-start | bytes 2408456 | tf_op jit(solution)/shard_map/ppermute | solution.py:858
  129.9 41.2 %collective-permute-start.7 = (f32[4,392,128]{2,1,0:T(8,128)}, f32[4,392,128]{2,1,0:T(8,128)}, u32[]{:S(2)}, u32[]{:S(2)}) collective-permute-start(f32[4,392,128]{2,1,0:T(8,128)} %get-tuple-element.202), channel_id=1, source_target_pairs={{0,16},{8,24},{16,0},{24,8},{1,17},{9,25},{17,1},{25,9},{2,18},{10... | collective-permute-start | bytes 2408456 | tf_op jit(solution)/shard_map/ppermute | solution.py:858
  131.0 40.1 %collective-permute-start.8 = (f32[4,392,128]{2,1,0:T(8,128)}, f32[4,392,128]{2,1,0:T(8,128)}, u32[]{:S(2)}, u32[]{:S(2)}) collective-permute-start(f32[4,392,128]{2,1,0:T(8,128)} %get-tuple-element.203), channel_id=1, source_target_pairs={{0,8},{8,0},{16,24},{24,16},{1,9},{9,1},{17,25},{25,17},{2,10},{10... | collective-permute-start | bytes 2408456 | tf_op jit(solution)/shard_map/ppermute | solution.py:858
  138.9 36.1 %collective-permute-start.9 = (f32[2,384,384]{2,1,0:T(8,128)}, f32[2,384,384]{2,1,0:T(8,128)}, u32[]{:S(2)}, u32[]{:S(2)}) collective-permute-start(f32[2,384,384]{2,1,0:T(8,128)} %get-tuple-element.206), channel_id=1, source_target_pairs={{0,8},{8,0},{16,24},{24,16},{1,9},{9,1},{17,25},{25,17},{2,10},{10... | collective-permute-start | bytes 3538952 | tf_op jit(solution)/shard_map/ppermute | solution.py:858
  140.1 34.8 %collective-permute-start.10 = (f32[2,384,384]{2,1,0:T(8,128)}, f32[2,384,384]{2,1,0:T(8,128)}, u32[]{:S(2)}, u32[]{:S(2)}) collective-permute-start(f32[2,384,384]{2,1,0:T(8,128)} %get-tuple-element.208), channel_id=1, source_target_pairs={{0,16},{8,24},{16,0},{24,8},{1,17},{9,25},{17,1},{25,9},{2,18},{10... | collective-permute-start | bytes 3538952 | tf_op jit(solution)/shard_map/ppermute | solution.py:858
  178.5 20.2 %collective-permute-start.12 = (f32[1,384,384]{2,1,0:T(8,128)}, f32[1,384,384]{2,1,0:T(8,128)}, u32[]{:S(2)}, u32[]{:S(2)}) collective-permute-start(f32[1,384,384]{2,1,0:T(8,128)} %get-tuple-element.219), channel_id=1, source_target_pairs={{0,16},{8,24},{16,0},{24,8},{1,17},{9,25},{17,1},{25,9},{2,18},{10... | collective-permute-start | bytes 1769480 | tf_op jit(solution)/shard_map/ppermute | solution.py:858
  179.7 18.9 %collective-permute-start.13 = (f32[1,384,384]{2,1,0:T(8,128)}, f32[1,384,384]{2,1,0:T(8,128)}, u32[]{:S(2)}, u32[]{:S(2)}) collective-permute-start(f32[1,384,384]{2,1,0:T(8,128)} %get-tuple-element.221), channel_id=1, source_target_pairs={{0,8},{8,0},{16,24},{24,16},{1,9},{9,1},{17,25},{25,17},{2,10},{10... | collective-permute-start | bytes 1769480 | tf_op jit(solution)/shard_map/ppermute | solution.py:858
  187.3 50.9 %collective-permute-start.18 = (f32[2,96,1536]{2,1,0:T(8,128)}, f32[2,96,1536]{2,1,0:T(8,128)}, u32[]{:S(2)}, u32[]{:S(2)}) collective-permute-start(f32[2,96,1536]{2,1,0:T(8,128)} %get-tuple-element.241), channel_id=1, source_target_pairs={{0,8},{8,0},{16,24},{24,16},{1,9},{9,1},{17,25},{25,17},{2,10},{10... | collective-permute-start | bytes 3538952 | tf_op jit(solution)/shard_map/ppermute | solution.py:858
  187.7 50.5 %collective-permute-start.19 = (f32[2,96,1536]{2,1,0:T(8,128)}, f32[2,96,1536]{2,1,0:T(8,128)}, u32[]{:S(2)}, u32[]{:S(2)}) collective-permute-start(f32[2,96,1536]{2,1,0:T(8,128)} %get-tuple-element.243), channel_id=1, source_target_pairs={{0,16},{8,24},{16,0},{24,8},{1,17},{9,25},{17,1},{25,9},{2,18},{10... | collective-permute-start | bytes 3538952 | tf_op jit(solution)/shard_map/ppermute | solution.py:858
  208.1 25.4 %collective-permute-start.16 = (f32[2,96,896]{2,1,0:T(8,128)}, f32[2,96,896]{2,1,0:T(8,128)}, u32[]{:S(2)}, u32[]{:S(2)}) collective-permute-start(f32[2,96,896]{2,1,0:T(8,128)} %get-tuple-element.236), channel_id=1, source_target_pairs={{0,8},{8,0},{16,24},{24,16},{1,9},{9,1},{17,25},{25,17},{2,10},{10... | collective-permute-start | bytes 2064392 | tf_op jit(solution)/shard_map/ppermute | solution.py:858
  209.3 24.2 %collective-permute-start.17 = (f32[2,96,896]{2,1,0:T(8,128)}, f32[2,96,896]{2,1,0:T(8,128)}, u32[]{:S(2)}, u32[]{:S(2)}) collective-permute-start(f32[2,96,896]{2,1,0:T(8,128)} %get-tuple-element.238), channel_id=1, source_target_pairs={{0,16},{8,24},{16,0},{24,8},{1,17},{9,25},{17,1},{25,9},{2,18},{10... | collective-permute-start | bytes 2064392 | tf_op jit(solution)/shard_map/ppermute | solution.py:858
  220.2 57.5 %collective-permute-start.26 = (f32[384,384]{1,0:T(8,128)}, f32[384,384]{1,0:T(8,128)}, u32[]{:S(2)}, u32[]{:S(2)}) collective-permute-start(f32[384,384]{1,0:T(8,128)} %get-tuple-element.263.refs_1_), channel_id=1, source_target_pairs={{0,4},{1,5},{2,6},{3,7},{4,0},{5,1},{6,2},{7,3},{8,12},{9,13},{10,... | collective-permute-start | bytes 1769480 | tf_op jit(solution)/shard_map/ppermute | solution.py:858
  241.7 19.4 %collective-permute-start.22 = (f32[1,96,1536]{2,1,0:T(8,128)}, f32[1,96,1536]{2,1,0:T(8,128)}, u32[]{:S(2)}, u32[]{:S(2)}) collective-permute-start(f32[1,96,1536]{2,1,0:T(8,128)} %get-tuple-element.253), channel_id=1, source_target_pairs={{0,16},{8,24},{16,0},{24,8},{1,17},{9,25},{17,1},{25,9},{2,18},{10... | collective-permute-start | bytes 1769480 | tf_op jit(solution)/shard_map/ppermute | solution.py:858
  243.0 18.1 %collective-permute-start.23 = (f32[1,96,1536]{2,1,0:T(8,128)}, f32[1,96,1536]{2,1,0:T(8,128)}, u32[]{:S(2)}, u32[]{:S(2)}) collective-permute-start(f32[1,96,1536]{2,1,0:T(8,128)} %get-tuple-element.255), channel_id=1, source_target_pairs={{0,8},{8,0},{16,24},{24,16},{1,9},{9,1},{17,25},{25,17},{2,10},{10... | collective-permute-start | bytes 1769480 | tf_op jit(solution)/shard_map/ppermute | solution.py:858
  246.6 23.0 %collective-permute-start.25 = (f32[96,896]{1,0:T(8,128)}, f32[96,896]{1,0:T(8,128)}, u32[]{:S(2)}, u32[]{:S(2)}) collective-permute-start(f32[96,896]{1,0:T(8,128)} %get-tuple-element.261), channel_id=1, source_target_pairs={{0,2},{1,3},{2,0},{3,1},{4,6},{5,7},{6,4},{7,5},{8,10},{9,11},{10,... | collective-permute-start | bytes 1032200 | tf_op jit(solution)/shard_map/ppermute | solution.py:858
  263.9 20.9 %collective-permute-start.27 = (f32[96,1536]{1,0:T(8,128)}, f32[96,1536]{1,0:T(8,128)}, u32[]{:S(2)}, u32[]{:S(2)}) collective-permute-start(f32[96,1536]{1,0:T(8,128)} %get-tuple-element.266), channel_id=1, source_target_pairs={{0,2},{1,3},{2,0},{3,1},{4,6},{5,7},{6,4},{7,5},{8,10},{9,11},{10,... | collective-permute-start | bytes 1769480 | tf_op jit(solution)/shard_map/ppermute | solution.py:858
  272.0 43.5 %collective-permute-start.33 = (f32[96,896]{1,0:T(8,128)}, f32[96,896]{1,0:T(8,128)}, u32[]{:S(2)}, u32[]{:S(2)}) collective-permute-start(f32[96,896]{1,0:T(8,128)} %get-tuple-element.283.refs_1_), channel_id=1, source_target_pairs={{0,4},{1,5},{2,6},{3,7},{4,0},{5,1},{6,2},{7,3},{8,12},{9,13},{10,... | collective-permute-start | bytes 1032200 | tf_op jit(solution)/shard_map/ppermute | solution.py:858
  287.3 39.4 %collective-permute-start.35 = (f32[96,1536]{1,0:T(8,128)}, f32[96,1536]{1,0:T(8,128)}, u32[]{:S(2)}, u32[]{:S(2)}) collective-permute-start(f32[96,1536]{1,0:T(8,128)} %get-tuple-element.288.refs_1_), channel_id=1, source_target_pairs={{0,4},{1,5},{2,6},{3,7},{4,0},{5,1},{6,2},{7,3},{8,12},{9,13},{10,... | collective-permute-start | bytes 1769480 | tf_op jit(solution)/shard_map/ppermute | solution.py:858
  287.4 25.2 %collective-permute-start.32 = (f32[384,384]{1,0:T(8,128)}, f32[384,384]{1,0:T(8,128)}, u32[]{:S(2)}, u32[]{:S(2)}) collective-permute-start(f32[384,384]{1,0:T(8,128)} %get-tuple-element.281.refs_1_), channel_id=1, source_target_pairs={{0,2},{1,3},{2,0},{3,1},{4,6},{5,7},{6,4},{7,5},{8,10},{9,11},{10,... | collective-permute-start | bytes 1769480 | tf_op jit(solution)/shard_map/ppermute | solution.py:858
  320.2 23.5 %collective-permute-start.38 = (f32[768,384]{1,0:T(8,128)}, f32[768,384]{1,0:T(8,128)}, u32[]{:S(2)}, u32[]{:S(2)}) collective-permute-start(f32[768,384]{1,0:T(8,128)} %get-tuple-element.294.refs_1_), channel_id=1, source_target_pairs={{0,1},{1,0},{2,3},{3,2},{4,5},{5,4},{6,7},{7,6},{8,9},{9,8},{10,11... | collective-permute-start | bytes 3538952 | tf_op jit(solution)/shard_map/ppermute | solution.py:858
  329.5 19.9 %collective-permute-start.39 = (f32[96,1536]{1,0:T(8,128)}, f32[96,1536]{1,0:T(8,128)}, u32[]{:S(2)}, u32[]{:S(2)}) collective-permute-start(f32[96,1536]{1,0:T(8,128)} %get-tuple-element.296.refs_1_), channel_id=1, source_target_pairs={{0,2},{1,3},{2,0},{3,1},{4,6},{5,7},{6,4},{7,5},{8,10},{9,11},{10,... | collective-permute-start | bytes 1769480 | tf_op jit(solution)/shard_map/ppermute | solution.py:858
  332.3 21.9 %collective-permute-start.40 = (f32[192,896]{1,0:T(8,128)}, f32[192,896]{1,0:T(8,128)}, u32[]{:S(2)}, u32[]{:S(2)}) collective-permute-start(f32[192,896]{1,0:T(8,128)} %get-tuple-element.298.refs_1_), channel_id=1, source_target_pairs={{0,1},{1,0},{2,3},{3,2},{4,5},{5,4},{6,7},{7,6},{8,9},{9,8},{10,11... | collective-permute-start | bytes 2064392 | tf_op jit(solution)/shard_map/ppermute | solution.py:858
  (47 other events, 455.1 us)

commit v11 on v10

--- a/solution.py
+++ b/solution.py
@@ -559,10 +559,10 @@
 
 def tall_product(order, a, b):
     count, flat = a.shape
-    tile, cut = count // 4, b.shape[0] // 2
+    tile, cut = count // 2, b.shape[0] // 2
     out = (spec((tile, cut), lambda i, *s: (i, 0)), ((count, cut), f32))
     ins = [spec((tile, flat), lambda i, *s: (i, 0)), spec(b.shape, lambda i, *s: (0, 0))]
-    return order.call(tall_kernel, (4,), ins, [out, out], [], (a, b))
+    return order.call(tall_kernel, (2,), ins, [out, out], [], (a, b))
 
 
 def wide_kernel(s_ref, a_ref, b_ref, away_ref, keep_ref):
@@ -581,7 +581,7 @@
 def wide_product(order, a, b):
     count, flat = a.shape
     cut = b.shape[0] // 2
-    tile = 512
+    tile = 768
     half = cut // tile
 
     def source(i, s):

time: 369 us -> 368 us (level)
  no operation moved by 1% of the time
where the time goes in v11:
time: 368 us; the launch traced here: 366 us
  Pallas kernels  246 us (67%)
  starting transfers between devices  57 us (15%)
  waiting for transfers between devices  50.8 us (14%)
  local copies, waits for them, and re-layouts  10.4 us (3%)
    pallas_call x42, Pallas kernels, call(): pl.pallas_call(stepped, grid_spec=pltpu.PrefetchScalarGridSpec(num_scalar...  246 us
    ppermute x44, starting transfers between devices, swap(): return lax.ppermute(value, axis, [(i, i ^ distance) for i in range(count)])  57 us
    ppermute x44, waiting for transfers between devices, swap(): return lax.ppermute(value, axis, [(i, i ^ distance) for i in range(count)])  50.8 us
  transfers between devices with their start and end apart: 44, of which 14 were waited for; matrix products, arithmetic and copies ran while one was open for 1% of the time, Pallas kernels for 49%

profile of v11, /device:TPU:1, one launch (start us, length us, event | category | flops | bytes accessed | tf_op | source)
XLA Modules:
  0.0 366.5 jit_solution(2517190534212837022)
XLA Ops:
  1.4 10.5 %shard_map.220 = (f32[4,8,256]{2,1,0:T(8,128)}, bf16[768,1024]{1,0:T(8,128)(2,1)}, bf16[768,1024]{1,0:T(8,128)(2,1)}, bf16[768,1024]{1,0:T(8,128)(2,1)}, bf16[4,...) custom-call(s32[3]{0:T(128)S(1)} %pad_add_fusion.refs_0_, ...), custom_call_target="tpu_custom_call" | custom-call | flops 999999995904 | bytes 1 | tf_op jit(solution)/shard_map/pallas_call | solution.py:519
  15.2 18.2 %shard_map.221 = (bf16[768,1024]{1,0:T(8,128)(2,1)}, bf16[768,1024]{1,0:T(8,128)(2,1)}, f32[768,1024]{1,0:T(8,128)}, f32[16,1024]{1,0:T(8,128)}, bf16[768,768]{1...) custom-call(s32[3]{0:T(128)S(1)} %get-tuple-element.162.refs_0_, ...), custom_call_target="tpu_custom_call" | custom-call | flops 999999995904 | bytes 1 | tf_op jit(solution)/shard_map/pallas_call | solution.py:519
  41.2 14.2 %collective-permute-done.2.refs_3_ = f32[4,392,128]{2,1,0:T(8,128)S(1)} collective-permute-done((f32[4,392,128]{2,1,0:T(8,128)S(1)}, f32[4,392,128]{2,1,0:T(8,128)S(1)}, u32[]{:S(2)}, u32[]{:S(2)}) %collective-permute-start.2) | collective-permute-done | bytes 802848 | tf_op jit(solution)/shard_map/ppermute | solution.py:858
  55.4 3.8 %shard_map.223 = (f32[4,392,128]{2,1,0:T(8,128)}, f32[4,392,128]{2,1,0:T(8,128)}, s32[3]{0:T(128)S(1)}) custom-call(s32[3]{0:T(128)S(1)} %get-tuple-element.170.refs_0_, f32[16,4]{1,0:T(8,128)S(1)} %stack.59.refs_1_, f32[4,392,128]{2,1,0:T(8,128)} %collective-permute-done.refs_3_.refs_2_, f32[4,392,128]{2,1,0:T(8,128)S(1)} %collective-permute-done.2.refs_3_, ...), custom_call_target="tpu_custom_call" | custom-call | flops 999999995904 | bytes 1 | tf_op jit(solution)/shard_map/pallas_call | solution.py:519
  63.5 45.3 %shard_map.224 = (bf16[4,256,768]{2,1,0:T(8,128)(2,1)}, bf16[768,1024]{1,0:T(8,128)(2,1)}, bf16[768,1024]{1,0:T(8,128)(2,1)}, bf16[3072,1024]{1,0:T(8,128)(2,1)}...) custom-call(s32[3]{0:T(128)} %copy-done.21, ...), custom_call_target="tpu_custom_call" | custom-call | flops 999999995904 | bytes 1 | tf_op jit(solution)/shard_map/pallas_call | solution.py:519
  111.0 10.4 %shard_map.225 = (f32[3072,384]{1,0:T(8,128)}, f32[3072,384]{1,0:T(8,128)}, s32[3]{0:T(128)S(1)}) custom-call(s32[3]{0:T(128)S(1)} %copy-done.20, bf16[3072,1024]{1,0:T(8,128)(2,1)} %get-tuple-element.184.refs_1_, bf16[768,1024]{1,0:T(8,128)(2,1)} %get-tuple-element.185.refs_2_), custom_call_target="tpu_custom_call" | custom-call | flops 999999995904 | bytes 1 | tf_op jit(solution)/shard_map/pallas_call | solution.py:519
  132.3 6.4 %shard_map.227 = (f32[2,384,384]{2,1,0:T(8,128)}, f32[2,384,384]{2,1,0:T(8,128)}, f32[2,384,384]{2,1,0:T(8,128)}, f32[2,384,384]{2,1,0:T(8,128)}, s32[3]{0:T(128)S(1)}) custom-call(s32[3]{0:T(128)S(1)} %get-tuple-element.189.refs_0_, f32[4,768,384]{2,1,0:T(8,128)} %bitcast.35, f32[4,768,384]{2,1,0:T(8,128)} %bitcast.4.refs_2_.refs_4_.refs_6_.refs_8_, ...), custom_call_target="tpu_custom_call" | custom-call | flops 999999995904 | bytes 1 | tf_op jit(solution)/shard_map/pallas_call | solution.py:519
  140.2 14.9 %shard_map.228 = (bf16[768,1024]{1,0:T(8,128)(2,1)}, f32[768,1024]{1,0:T(8,128)}, f32[768,1024]{1,0:T(8,128)}, s32[3]{0:T(128)S(1)}) custom-call(s32[3]{0:T(128)S(1)} %get-tuple-element.192.refs_0_, f32[4,8,256]{2,1,0:T(8,128)} %get-tuple-element.163.refs_1_, bf16[768,1024]{1,0:T(8,128)(2,1)} %get-tuple-element.174.refs_2_, ...), custom_call_target="tpu_custom_call" | custom-call | flops 999999995904 | bytes 1 | tf_op jit(solution)/shard_map/pallas_call | solution.py:519
  155.1 11.7 %shard_map.229 = (f32[768,1536]{1,0:T(8,128)}, f32[768,1536]{1,0:T(8,128)}, s32[3]{0:T(128)S(1)}) custom-call(s32[3]{0:T(128)S(1)} %get-tuple-element.198.refs_0_, bf16[768,1024]{1,0:T(8,128)(2,1)} %get-tuple-element.199.refs_1_, bf16[3072,1024]{1,0:T(8,128)(2,1)} %get-tuple-element.200.refs_2_), custom_call_target="tpu_custom_call" | custom-call | flops 999999995904 | bytes 1 | tf_op jit(solution)/shard_map/pallas_call | solution.py:519
  170.6 3.9 %shard_map.230 = (f32[4,392,128]{2,1,0:T(8,128)}, f32[4,392,128]{2,1,0:T(8,128)}, s32[3]{0:T(128)S(1)}) custom-call(s32[3]{0:T(128)S(1)} %get-tuple-element.201.refs_0_, f32[16,4]{1,0:T(8,128)S(1)} %stack.59.refs_1_, f32[4,392,128]{2,1,0:T(8,128)} %collective-permute-done.4.refs_3_.refs_2_, f32[4,392,128]{2,1,0:T(8,128)} %collective-permute-done.7.refs_3_, ...), custom_call_target="tpu_custom_call" | custom-call | flops 999999995904 | bytes 1 | tf_op jit(solution)/shard_map/pallas_call | solution.py:519
  180.4 6.4 %shard_map.232 = (f32[2,96,1536]{2,1,0:T(8,128)}, f32[2,96,1536]{2,1,0:T(8,128)}, f32[2,96,1536]{2,1,0:T(8,128)}, f32[2,96,1536]{2,1,0:T(8,128)}, s32[3]{0:T(128)S(1)}) custom-call(s32[3]{0:T(128)S(1)} %get-tuple-element.209.refs_0_, f32[4,192,1536]{2,1,0:T(8,128)} %bitcast.31, f32[4,192,1536]{2,1,0:T(8,128)} %bitcast.6.refs_2_.refs_4_.refs_6_.refs_8_, ...), custom_call_target="tpu_custom_call" | custom-call | flops 999999995904 | bytes 1 | tf_op jit(solution)/shard_map/pallas_call | solution.py:519
  187.5 7.7 %shard_map.233 = (f32[768,896]{1,0:T(8,128)}, f32[768,896]{1,0:T(8,128)}, s32[3]{0:T(128)S(1)}) custom-call(s32[3]{0:T(128)S(1)} %get-tuple-element.212.refs_0_, bf16[768,1024]{1,0:T(8,128)(2,1)} %get-tuple-element.213.refs_1_, bf16[1,768,1024]{2,1,0:T(8,128)(2,1)} %bitcast.48, bf16[768,1024]{1,0:T(8,128)(2,1)} %get-tuple-element.164.refs_2_.refs_7_.refs_3_.refs_1_, ...), custom_call_target="tpu_custom_call" | custom-call | flops 999999995904 | bytes 1 | tf_op jit(solution)/shard_map/pallas_call | solution.py:519
  203.7 4.3 %shard_map.235 = (f32[2,96,896]{2,1,0:T(8,128)}, f32[2,96,896]{2,1,0:T(8,128)}, f32[2,96,896]{2,1,0:T(8,128)}, f32[2,96,896]{2,1,0:T(8,128)}, s32[3]{0:T(128)S(1)}) custom-call(s32[3]{0:T(128)S(1)} %get-tuple-element.222.refs_0_, f32[4,192,896]{2,1,0:T(8,128)} %bitcast.39, f32[4,192,896]{2,1,0:T(8,128)} %bitcast.10.refs_2_.refs_4_.refs_6_.refs_8_, ...), custom_call_target="tpu_custom_call" | custom-call | flops 999999995904 | bytes 1 | tf_op jit(solution)/shard_map/pallas_call | solution.py:519
  209.7 8.0 %shard_map.236 = (bf16[2,768,1024]{2,1,0:T(8,128)(2,1)}, s32[3]{0:T(128)S(1)}) custom-call(s32[3]{0:T(128)S(1)} %get-tuple-element.225.refs_0_, f32[4,8,256]{2,1,0:T(8,128)} %get-tuple-element.163.refs_1_, bf16[768,1024]{1,0:T(8,128)(2,1)} %get-tuple-element.193.refs_3_.refs_2_, bf16[768,1024]{1,0:T(8,128)(2,1)} %get-tuple-element.166.refs_4_.refs_3_, ...), custom_call_target="tpu_custom_call" | custom-call | flops 999999995904 | bytes 1 | tf_op jit(solution)/shard_map/pallas_call | solution.py:519
  222.6 9.9 %collective-permute-done.16.refs_2_ = f32[2,96,896]{2,1,0:T(8,128)} collective-permute-done((f32[2,96,896]{2,1,0:T(8,128)}, f32[2,96,896]{2,1,0:T(8,128)}, u32[]{:S(2)}, u32[]{:S(2)}) %collective-permute-start.16) | collective-permute-done | bytes 688160 | tf_op jit(solution)/shard_map/ppermute | solution.py:858
  246.7 7.2 %shard_map.241 = (f32[768,768]{1,0:T(8,128)}, f32[768,768]{1,0:T(8,128)}, s32[3]{0:T(128)S(1)}) custom-call(s32[3]{0:T(128)S(1)} %get-tuple-element.249.refs_0_, bf16[768,1024]{1,0:T(8,128)(2,1)} %get-tuple-element.164.refs_2_.refs_7_.refs_3_.refs_1_, bf16[2,768,1024]{2,1,0:T(8,128)(2,1)} %get-tuple-element.250.refs_2_.refs_4_, ...), custom_call_target="tpu_custom_call" | custom-call | flops 999999995904 | bytes 1 | tf_op jit(solution)/shard_map/pallas_call | solution.py:519
  253.9 6.2 %collective-permute-start.24 = (f32[768,768]{1,0:T(8,128)}, f32[768,768]{1,0:T(8,128)}, u32[]{:S(2)}, u32[]{:S(2)}) collective-permute-start(f32[768,768]{1,0:T(8,128)} %get-tuple-element.258), channel_id=1, source_target_pairs={{0,1},{1,0},{2,3},{3,2},{4,5},{5,4},{6,7},{7,6},{8,9},{9,8},{10,11... | collective-permute-start | bytes 7077896 | tf_op jit(solution)/shard_map/ppermute | solution.py:858
  264.6 4.0 %shard_map.243 = (f32[2,96,768]{2,1,0:T(8,128)}, f32[2,96,768]{2,1,0:T(8,128)}, f32[2,96,768]{2,1,0:T(8,128)}, f32[2,96,768]{2,1,0:T(8,128)}, s32[3]{0:T(128)S(1)}) custom-call(s32[3]{0:T(128)S(1)} %get-tuple-element.256.refs_0_, f32[4,192,768]{2,1,0:T(8,128)} %bitcast.43, f32[4,192,768]{2,1,0:T(8,128)} %bitcast.12.refs_2_.refs_4_.refs_6_.refs_8_, ...), custom_call_target="tpu_custom_call" | custom-call | flops 999999995904 | bytes 1 | tf_op jit(solution)/shard_map/pallas_call | solution.py:519
  279.7 4.1 %collective-permute-done.27.refs_2_ = f32[96,1536]{1,0:T(8,128)} collective-permute-done((f32[96,1536]{1,0:T(8,128)}, f32[96,1536]{1,0:T(8,128)}, u32[]{:S(2)}, u32[]{:S(2)}) %collective-permute-start.27) | collective-permute-done | bytes 589856 | tf_op jit(solution)/shard_map/ppermute | solution.py:858
  294.4 10.0 %shard_map.248 = (f32[4,256,768]{2,1,0:T(8,128)}, s32[3]{0:T(128)S(1)}) custom-call(s32[3]{0:T(128)S(1)} %get-tuple-element.272.refs_0_, bf16[768,1024]{1,0:T(8,128)(2,1)} %get-tuple-element.215.refs_1_, bf16[2,768,1024]{2,1,0:T(8,128)(2,1)} %get-tuple-element.250.refs_2_.refs_4_, f32[768,1024]{1,0:T(8,128)} %get-tuple-element.273.refs_3_, ...), custom_call_target="tpu_custom_call" | custom-call | flops 999999995904 | bytes 1 | tf_op jit(solution)/shard_map/pallas_call | solution.py:519
  307.2 4.4 %collective-permute-done.32.refs_2_ = f32[384,384]{1,0:T(8,128)} collective-permute-done((f32[384,384]{1,0:T(8,128)}, f32[384,384]{1,0:T(8,128)}, u32[]{:S(2)}, u32[]{:S(2)}) %collective-permute-start.32) | collective-permute-done | bytes 589856 | tf_op jit(solution)/shard_map/ppermute | solution.py:858
  332.6 7.6 %collective-permute-done.37.refs_2_ = f32[96,768]{1,0:T(8,128)} collective-permute-done((f32[96,768]{1,0:T(8,128)}, f32[96,768]{1,0:T(8,128)}, u32[]{:S(2)}, u32[]{:S(2)}) %collective-permute-start.37) | collective-permute-done | bytes 294944 | tf_op jit(solution)/shard_map/ppermute | solution.py:858
  342.7 3.8 %shard_map.256 = (f32[768,768]{1,0:T(8,128)}, s32[3]{0:T(128)S(1)}) custom-call(s32[3]{0:T(128)S(1)} %get-tuple-element.293.refs_0_, f32[768,384]{1,0:T(8,128)} %get-tuple-element.294.refs_1_, f32[768,384]{1,0:T(8,128)} %collective-permute-done.38.refs_2_), custom_call_target="tpu_custom_call" | custom-call | flops 999999995904 | bytes 1 | tf_op jit(solution)/shard_map/pallas_call | solution.py:519
  359.6 3.8 %shard_map.260 = (f32[192,3072]{1,0:T(8,128)}, s32[3]{0:T(128)S(1)}) custom-call(s32[3]{0:T(128)S(1)} %get-tuple-element.302.refs_0_, f32[192,1536]{1,0:T(8,128)} %get-tuple-element.303.refs_1_, f32[192,1536]{1,0:T(8,128)} %collective-permute-done.42.refs_2_), custom_call_target="tpu_custom_call" | custom-call | flops 999999995904 | bytes 1 | tf_op jit(solution)/shard_map/pallas_call | solution.py:519
  (181 shorter events, 138.1 us)
Async XLA Ops:
  11.9 22.4 %collective-permute-start = (f32[4,392,128]{2,1,0:T(8,128)}, f32[4,392,128]{2,1,0:T(8,128)}, u32[]{:S(2)}, u32[]{:S(2)}) collective-permute-start(f32[4,392,128]{2,1,0:T(8,128)} %get-tuple-element.168.refs_2_), channel_id=1, source_target_pairs={{0,8},{8,0},{16,24},{24,16},{1,9},{9,1},{17,25},{25,17},{2,10},{10... | collective-permute-start | bytes 2408456 | tf_op jit(solution)/shard_map/ppermute | solution.py:858
  14.0 20.3 %collective-permute-start.1 = (f32[4,392,128]{2,1,0:T(8,128)}, f32[4,392,128]{2,1,0:T(8,128)}, u32[]{:S(2)}, u32[]{:S(2)}) collective-permute-start(f32[4,392,128]{2,1,0:T(8,128)} %get-tuple-element.169.refs_4_), channel_id=1, source_target_pairs={{0,16},{8,24},{16,0},{24,8},{1,17},{9,25},{17,1},{25,9},{2,18},{10... | collective-permute-start | bytes 2408456 | tf_op jit(solution)/shard_map/ppermute | solution.py:858
  37.2 18.2 %collective-permute-start.2 = (f32[4,392,128]{2,1,0:T(8,128)S(1)}, f32[4,392,128]{2,1,0:T(8,128)S(1)}, u32[]{:S(2)}, u32[]{:S(2)}) collective-permute-start(f32[4,392,128]{2,1,0:T(8,128)S(1)} %get-tuple-element.171), channel_id=1, source_target_pairs={{0,16},{8,24},{16,0},{24,8},{1,17},{9,25},{17,1},{25,9},{2,18},{10... | collective-permute-start | bytes 2408456 | tf_op jit(solution)/shard_map/ppermute | solution.py:858
  129.9 40.7 %collective-permute-start.7 = (f32[4,392,128]{2,1,0:T(8,128)}, f32[4,392,128]{2,1,0:T(8,128)}, u32[]{:S(2)}, u32[]{:S(2)}) collective-permute-start(f32[4,392,128]{2,1,0:T(8,128)} %get-tuple-element.202), channel_id=1, source_target_pairs={{0,16},{8,24},{16,0},{24,8},{1,17},{9,25},{17,1},{25,9},{2,18},{10... | collective-permute-start | bytes 2408456 | tf_op jit(solution)/shard_map/ppermute | solution.py:858
  131.0 39.6 %collective-permute-start.8 = (f32[4,392,128]{2,1,0:T(8,128)}, f32[4,392,128]{2,1,0:T(8,128)}, u32[]{:S(2)}, u32[]{:S(2)}) collective-permute-start(f32[4,392,128]{2,1,0:T(8,128)} %get-tuple-element.203), channel_id=1, source_target_pairs={{0,8},{8,0},{16,24},{24,16},{1,9},{9,1},{17,25},{25,17},{2,10},{10... | collective-permute-start | bytes 2408456 | tf_op jit(solution)/shard_map/ppermute | solution.py:858
  138.7 35.8 %collective-permute-start.9 = (f32[2,384,384]{2,1,0:T(8,128)}, f32[2,384,384]{2,1,0:T(8,128)}, u32[]{:S(2)}, u32[]{:S(2)}) collective-permute-start(f32[2,384,384]{2,1,0:T(8,128)} %get-tuple-element.206), channel_id=1, source_target_pairs={{0,8},{8,0},{16,24},{24,16},{1,9},{9,1},{17,25},{25,17},{2,10},{10... | collective-permute-start | bytes 3538952 | tf_op jit(solution)/shard_map/ppermute | solution.py:858
  140.0 34.5 %collective-permute-start.10 = (f32[2,384,384]{2,1,0:T(8,128)}, f32[2,384,384]{2,1,0:T(8,128)}, u32[]{:S(2)}, u32[]{:S(2)}) collective-permute-start(f32[2,384,384]{2,1,0:T(8,128)} %get-tuple-element.208), channel_id=1, source_target_pairs={{0,16},{8,24},{16,0},{24,8},{1,17},{9,25},{17,1},{25,9},{2,18},{10... | collective-permute-start | bytes 3538952 | tf_op jit(solution)/shard_map/ppermute | solution.py:858
  178.0 20.7 %collective-permute-start.12 = (f32[1,384,384]{2,1,0:T(8,128)}, f32[1,384,384]{2,1,0:T(8,128)}, u32[]{:S(2)}, u32[]{:S(2)}) collective-permute-start(f32[1,384,384]{2,1,0:T(8,128)} %get-tuple-element.219), channel_id=1, source_target_pairs={{0,16},{8,24},{16,0},{24,8},{1,17},{9,25},{17,1},{25,9},{2,18},{10... | collective-permute-start | bytes 1769480 | tf_op jit(solution)/shard_map/ppermute | solution.py:858
  179.3 19.4 %collective-permute-start.13 = (f32[1,384,384]{2,1,0:T(8,128)}, f32[1,384,384]{2,1,0:T(8,128)}, u32[]{:S(2)}, u32[]{:S(2)}) collective-permute-start(f32[1,384,384]{2,1,0:T(8,128)} %get-tuple-element.221), channel_id=1, source_target_pairs={{0,8},{8,0},{16,24},{24,16},{1,9},{9,1},{17,25},{25,17},{2,10},{10... | collective-permute-start | bytes 1769480 | tf_op jit(solution)/shard_map/ppermute | solution.py:858
  186.8 50.4 %collective-permute-start.18 = (f32[2,96,1536]{2,1,0:T(8,128)}, f32[2,96,1536]{2,1,0:T(8,128)}, u32[]{:S(2)}, u32[]{:S(2)}) collective-permute-start(f32[2,96,1536]{2,1,0:T(8,128)} %get-tuple-element.241), channel_id=1, source_target_pairs={{0,8},{8,0},{16,24},{24,16},{1,9},{9,1},{17,25},{25,17},{2,10},{10... | collective-permute-start | bytes 3538952 | tf_op jit(solution)/shard_map/ppermute | solution.py:858
  187.2 50.0 %collective-permute-start.19 = (f32[2,96,1536]{2,1,0:T(8,128)}, f32[2,96,1536]{2,1,0:T(8,128)}, u32[]{:S(2)}, u32[]{:S(2)}) collective-permute-start(f32[2,96,1536]{2,1,0:T(8,128)} %get-tuple-element.243), channel_id=1, source_target_pairs={{0,16},{8,24},{16,0},{24,8},{1,17},{9,25},{17,1},{25,9},{2,18},{10... | collective-permute-start | bytes 3538952 | tf_op jit(solution)/shard_map/ppermute | solution.py:858
  208.1 24.4 %collective-permute-start.16 = (f32[2,96,896]{2,1,0:T(8,128)}, f32[2,96,896]{2,1,0:T(8,128)}, u32[]{:S(2)}, u32[]{:S(2)}) collective-permute-start(f32[2,96,896]{2,1,0:T(8,128)} %get-tuple-element.236), channel_id=1, source_target_pairs={{0,8},{8,0},{16,24},{24,16},{1,9},{9,1},{17,25},{25,17},{2,10},{10... | collective-permute-start | bytes 2064392 | tf_op jit(solution)/shard_map/ppermute | solution.py:858
  209.3 23.2 %collective-permute-start.17 = (f32[2,96,896]{2,1,0:T(8,128)}, f32[2,96,896]{2,1,0:T(8,128)}, u32[]{:S(2)}, u32[]{:S(2)}) collective-permute-start(f32[2,96,896]{2,1,0:T(8,128)} %get-tuple-element.238), channel_id=1, source_target_pairs={{0,16},{8,24},{16,0},{24,8},{1,17},{9,25},{17,1},{25,9},{2,18},{10... | collective-permute-start | bytes 2064392 | tf_op jit(solution)/shard_map/ppermute | solution.py:858
  220.2 56.8 %collective-permute-start.26 = (f32[384,384]{1,0:T(8,128)}, f32[384,384]{1,0:T(8,128)}, u32[]{:S(2)}, u32[]{:S(2)}) collective-permute-start(f32[384,384]{1,0:T(8,128)} %get-tuple-element.263.refs_1_), channel_id=1, source_target_pairs={{0,4},{1,5},{2,6},{3,7},{4,0},{5,1},{6,2},{7,3},{8,12},{9,13},{10,... | collective-permute-start | bytes 1769480 | tf_op jit(solution)/shard_map/ppermute | solution.py:858
  240.7 19.4 %collective-permute-start.22 = (f32[1,96,1536]{2,1,0:T(8,128)}, f32[1,96,1536]{2,1,0:T(8,128)}, u32[]{:S(2)}, u32[]{:S(2)}) collective-permute-start(f32[1,96,1536]{2,1,0:T(8,128)} %get-tuple-element.253), channel_id=1, source_target_pairs={{0,16},{8,24},{16,0},{24,8},{1,17},{9,25},{17,1},{25,9},{2,18},{10... | collective-permute-start | bytes 1769480 | tf_op jit(solution)/shard_map/ppermute | solution.py:858
  242.0 18.2 %collective-permute-start.23 = (f32[1,96,1536]{2,1,0:T(8,128)}, f32[1,96,1536]{2,1,0:T(8,128)}, u32[]{:S(2)}, u32[]{:S(2)}) collective-permute-start(f32[1,96,1536]{2,1,0:T(8,128)} %get-tuple-element.255), channel_id=1, source_target_pairs={{0,8},{8,0},{16,24},{24,16},{1,9},{9,1},{17,25},{25,17},{2,10},{10... | collective-permute-start | bytes 1769480 | tf_op jit(solution)/shard_map/ppermute | solution.py:858
  245.1 23.5 %collective-permute-start.25 = (f32[96,896]{1,0:T(8,128)}, f32[96,896]{1,0:T(8,128)}, u32[]{:S(2)}, u32[]{:S(2)}) collective-permute-start(f32[96,896]{1,0:T(8,128)} %get-tuple-element.261), channel_id=1, source_target_pairs={{0,2},{1,3},{2,0},{3,1},{4,6},{5,7},{6,4},{7,5},{8,10},{9,11},{10,... | collective-permute-start | bytes 1032200 | tf_op jit(solution)/shard_map/ppermute | solution.py:858
  262.9 20.9 %collective-permute-start.27 = (f32[96,1536]{1,0:T(8,128)}, f32[96,1536]{1,0:T(8,128)}, u32[]{:S(2)}, u32[]{:S(2)}) collective-permute-start(f32[96,1536]{1,0:T(8,128)} %get-tuple-element.266), channel_id=1, source_target_pairs={{0,2},{1,3},{2,0},{3,1},{4,6},{5,7},{6,4},{7,5},{8,10},{9,11},{10,... | collective-permute-start | bytes 1769480 | tf_op jit(solution)/shard_map/ppermute | solution.py:858
  271.0 43.5 %collective-permute-start.33 = (f32[96,896]{1,0:T(8,128)}, f32[96,896]{1,0:T(8,128)}, u32[]{:S(2)}, u32[]{:S(2)}) collective-permute-start(f32[96,896]{1,0:T(8,128)} %get-tuple-element.283.refs_1_), channel_id=1, source_target_pairs={{0,4},{1,5},{2,6},{3,7},{4,0},{5,1},{6,2},{7,3},{8,12},{9,13},{10,... | collective-permute-start | bytes 1032200 | tf_op jit(solution)/shard_map/ppermute | solution.py:858
  286.3 39.4 %collective-permute-start.35 = (f32[96,1536]{1,0:T(8,128)}, f32[96,1536]{1,0:T(8,128)}, u32[]{:S(2)}, u32[]{:S(2)}) collective-permute-start(f32[96,1536]{1,0:T(8,128)} %get-tuple-element.288.refs_1_), channel_id=1, source_target_pairs={{0,4},{1,5},{2,6},{3,7},{4,0},{5,1},{6,2},{7,3},{8,12},{9,13},{10,... | collective-permute-start | bytes 1769480 | tf_op jit(solution)/shard_map/ppermute | solution.py:858
  286.4 25.2 %collective-permute-start.32 = (f32[384,384]{1,0:T(8,128)}, f32[384,384]{1,0:T(8,128)}, u32[]{:S(2)}, u32[]{:S(2)}) collective-permute-start(f32[384,384]{1,0:T(8,128)} %get-tuple-element.281.refs_1_), channel_id=1, source_target_pairs={{0,2},{1,3},{2,0},{3,1},{4,6},{5,7},{6,4},{7,5},{8,10},{9,11},{10,... | collective-permute-start | bytes 1769480 | tf_op jit(solution)/shard_map/ppermute | solution.py:858
  319.2 23.5 %collective-permute-start.38 = (f32[768,384]{1,0:T(8,128)}, f32[768,384]{1,0:T(8,128)}, u32[]{:S(2)}, u32[]{:S(2)}) collective-permute-start(f32[768,384]{1,0:T(8,128)} %get-tuple-element.294.refs_1_), channel_id=1, source_target_pairs={{0,1},{1,0},{2,3},{3,2},{4,5},{5,4},{6,7},{7,6},{8,9},{9,8},{10,11... | collective-permute-start | bytes 3538952 | tf_op jit(solution)/shard_map/ppermute | solution.py:858
  328.5 19.9 %collective-permute-start.39 = (f32[96,1536]{1,0:T(8,128)}, f32[96,1536]{1,0:T(8,128)}, u32[]{:S(2)}, u32[]{:S(2)}) collective-permute-start(f32[96,1536]{1,0:T(8,128)} %get-tuple-element.296.refs_1_), channel_id=1, source_target_pairs={{0,2},{1,3},{2,0},{3,1},{4,6},{5,7},{6,4},{7,5},{8,10},{9,11},{10,... | collective-permute-start | bytes 1769480 | tf_op jit(solution)/shard_map/ppermute | solution.py:858
  331.3 21.9 %collective-permute-start.40 = (f32[192,896]{1,0:T(8,128)}, f32[192,896]{1,0:T(8,128)}, u32[]{:S(2)}, u32[]{:S(2)}) collective-permute-start(f32[192,896]{1,0:T(8,128)} %get-tuple-element.298.refs_1_), channel_id=1, source_target_pairs={{0,1},{1,0},{2,3},{3,2},{4,5},{5,4},{6,7},{7,6},{8,9},{9,8},{10,11... | collective-permute-start | bytes 2064392 | tf_op jit(solution)/shard_map/ppermute | solution.py:858
  (47 other events, 453.9 us)
